TPU v7x, 32 devices: a whole 2x2x4 slice. The times are simulated.
32 devices in a mesh: pipe: 4 (over y, x), dp: 8 (over z, core).
Axes of the slice: x: 2, y: 2, z: 4, core: 2. Of those that a mesh axis runs over, the one named last changes fastest.
Arguments:
- x_in: bfloat16 [4, 256, 4096], P(None, 'dp'), may hold values from -6 to 6
- cotangent: bfloat16 [4, 256, 4096], P(None, 'dp'), may hold values from -6 to 6
- weights: bfloat16 [4, 64, 64, 2048], P('pipe', 'dp'), as said below
- live_rows: int32 [4, 64, 32], P('pipe'), may hold values from 0 to 63, as said below
- moment: float32 [4, 64, 64, 2048], P('pipe', 'dp'), may hold values from -0.25 to 0.25
- second: float32 [4, 64, 64, 2048], P('pipe', 'dp'), may hold values from 4.8828126e-05 to 0.0009765625
Outputs:
- weights_out: bfloat16 [4, 64, 64, 2048], P('pipe', 'dp')
- moment_out: float32 [4, 64, 64, 2048], P('pipe', 'dp')
- second_out: float32 [4, 64, 64, 2048], P('pipe', 'dp')
Inputs may be any that keep to these rules, and one draw needn't show every extreme that they name: `live_rows`: for each layer and block column the 32 entries are distinct block rows. `weights`: entry [l, j, b, k * 64 + a] is the weight from input feature live_rows[l, j, k] * 64 + a to output feature j * 64 + b; unstored blocks are zero.
All inputs are finite; a program needn't handle non-finite values.
Results may differ from a plain program's by a relative error of at most 0.009.
Values may be sent and summed in bfloat16 or wider, within the bound.
No kernel may reach another device: no remote copies, remote signals or barrier semaphores. Data moves between devices by JAX's collectives and lax.ppermute only.
A program may use at most 256 MiB of HBM per device.

v0:
```python
import math

import jax
import jax.numpy as jnp
from jax import lax
from jax.sharding import PartitionSpec as P

HEAD = 128


column_group = 8


def shifted(value, axis, steps):
    count = lax.axis_size(axis)
    leading, last = (max(0, -steps), min(count, count - steps))
    return lax.ppermute(value, axis, [(source, source + steps) for source in range(leading, last)])


def shrink(magnitude, threshold):
    return jnp.maximum(magnitude - threshold, 0.0) / jnp.maximum(magnitude, threshold)


def column_products(normed, section_weights, live_index):
    tokens, features = normed.shape
    column_count, block_size, wide = section_weights.shape
    live_count = live_index.shape[1]
    group_count = column_count // column_group
    normed_blocks = normed.reshape(tokens, column_count, block_size)

    def column_per_group(members):
        weight_part, index_part = members
        picked = jnp.take(normed_blocks, index_part.reshape(-1), axis=1).reshape(
            tokens, column_group, wide
        )
        return jnp.einsum("tjk,jbk->tjb", picked, weight_part, preferred_element_type=jnp.float32)

    result = lax.map(
        column_per_group,
        (
            section_weights.reshape(group_count, column_group, block_size, wide),
            live_index.reshape(group_count, column_group, live_count),
        ),
    )
    return result.transpose(1, 0, 2, 3).reshape(tokens, features)


def dense_transposed(section_weights, live_index):
    column_count, block_size, wide = section_weights.shape
    live_count = live_index.shape[1]
    group_count = column_count // column_group
    features = column_count * block_size
    targets = jnp.arange(column_count, dtype=jnp.int32)

    def dense_per_group(members):
        weight_part, index_part = members
        chosen = (index_part[:, :, None] == targets[None, None, :]).astype(jnp.bfloat16)
        slab = jnp.einsum(
            "jkr,jbka->jbra",
            chosen,
            weight_part.reshape(column_group, block_size, live_count, block_size),
            preferred_element_type=jnp.float32,
        )
        return slab.astype(jnp.bfloat16).reshape(column_group * block_size, features)

    slabs = lax.map(
        dense_per_group,
        (
            section_weights.reshape(group_count, column_group, block_size, wide),
            live_index.reshape(group_count, column_group, live_count),
        ),
    )
    return slabs.reshape(features, features)


def layer_forward(entering, section_weights, live_index):
    as_float = entering.astype(jnp.float32)
    inverse_rms = lax.rsqrt(jnp.mean(as_float * as_float, axis=-1, keepdims=True) + 1e-05)
    normed = (as_float * inverse_rms).astype(jnp.bfloat16)
    pre_act = column_products(normed, section_weights, live_index)
    return ((as_float + jax.nn.silu(pre_act)).astype(jnp.bfloat16), normed, pre_act)


def layer_backward(arriving, entering, pre_act, dense_weights):
    as_float = entering.astype(jnp.float32)
    inverse_rms = lax.rsqrt(jnp.mean(as_float * as_float, axis=-1, keepdims=True) + 1e-05)
    sigmoid_z = jax.nn.sigmoid(pre_act)
    grad_pre = (
        arriving.astype(jnp.float32) * (sigmoid_z * (1.0 + pre_act * (1.0 - sigmoid_z)))
    ).astype(jnp.bfloat16)
    grad_normed = jnp.dot(grad_pre, dense_weights, preferred_element_type=jnp.float32)
    scaled = as_float * inverse_rms
    leaving = (
        arriving.astype(jnp.float32)
        + inverse_rms
        * (grad_normed - scaled * jnp.mean(grad_normed * scaled, axis=-1, keepdims=True))
    ).astype(jnp.bfloat16)
    return (leaving, grad_pre)


def local(x_in, cotangent, weights, live_rows, moment, second):
    sections = lax.axis_size("pipe")
    section_index = lax.axis_index("pipe")
    micro_count, tokens, features = x_in.shape
    column_count = live_rows.shape[1]
    live_count = live_rows.shape[2]
    own_columns = weights.shape[1]
    block_size = weights.shape[2]
    live_index = live_rows[0]
    section_weights = lax.all_gather(weights[0], "dp", axis=0, tiled=True)
    tick_count = micro_count + sections - 1
    incoming = jnp.zeros((tokens, features), jnp.bfloat16)
    saved_in = jnp.zeros((micro_count, tokens, features), jnp.bfloat16)
    saved_normed = jnp.zeros((micro_count, tokens, features), jnp.bfloat16)
    saved_pre = jnp.zeros((micro_count, tokens, features), jnp.float32)
    for tick_index in range(tick_count):
        slot_raw = tick_index - section_index
        active_now = (slot_raw >= 0) & (slot_raw < micro_count)
        slot_index = jnp.clip(slot_raw, 0, micro_count - 1)
        entering = jnp.where(section_index == 0, x_in[min(tick_index, micro_count - 1)], incoming)

        def forward_work(state, slot_index=slot_index):
            current, store_in, store_normed, store_pre = state
            outgoing, normed, pre_act = layer_forward(current, section_weights, live_index)
            return (
                outgoing,
                store_in.at[slot_index].set(current),
                store_normed.at[slot_index].set(normed),
                store_pre.at[slot_index].set(pre_act),
            )

        def forward_skip(state):
            current, store_in, store_normed, store_pre = state
            return (jnp.zeros_like(current), store_in, store_normed, store_pre)

        outgoing, saved_in, saved_normed, saved_pre = lax.cond(
            active_now, forward_work, forward_skip, (entering, saved_in, saved_normed, saved_pre)
        )
        if tick_index + 1 < tick_count:
            incoming = shifted(outgoing, "pipe", 1)
    dense_weights = dense_transposed(section_weights, live_index)
    incoming_grad = jnp.zeros((tokens, features), jnp.bfloat16)
    saved_grad = jnp.zeros((micro_count, tokens, features), jnp.bfloat16)
    for tick_index in range(tick_count):
        slot_raw = tick_index - (sections - 1 - section_index)
        active_now = (slot_raw >= 0) & (slot_raw < micro_count)
        slot_index = jnp.clip(slot_raw, 0, micro_count - 1)
        arriving = jnp.where(
            section_index == sections - 1,
            cotangent[min(tick_index, micro_count - 1)],
            incoming_grad,
        )

        def backward_work(state, slot_index=slot_index):
            current, store_grad = state
            leaving, grad_pre = layer_backward(
                current, saved_in[slot_index], saved_pre[slot_index], dense_weights
            )
            return (leaving, store_grad.at[slot_index].set(grad_pre))

        def backward_skip(state):
            current, store_grad = state
            return (jnp.zeros_like(current), store_grad)

        leaving, saved_grad = lax.cond(
            active_now, backward_work, backward_skip, (arriving, saved_grad)
        )
        if tick_index + 1 < tick_count:
            incoming_grad = shifted(leaving, "pipe", -1)
    all_rows = micro_count * tokens
    normed_blocks = saved_normed.reshape(all_rows, column_count, block_size)
    grad_blocks = saved_grad.reshape(all_rows, column_count, block_size)
    inverse_tokens = 1.0 / (all_rows * lax.axis_size("dp"))
    cast_type = jnp.bfloat16
    group_size = math.gcd(column_count, column_group)
    group_count = column_count // group_size
    index_part = live_index.reshape(group_count, group_size, live_count)
    grad_part = grad_blocks.reshape(all_rows, group_count, group_size, block_size).transpose(
        1, 0, 2, 3
    )

    def grad_per_group(members):
        index_group, grad_group = members
        picked = jnp.take(normed_blocks, index_group.reshape(-1), axis=1).reshape(
            all_rows, group_size, live_count * block_size
        )
        return (
            jnp.einsum("tjk,tjb->jbk", picked, grad_group, preferred_element_type=jnp.float32)
            * inverse_tokens
        ).astype(cast_type)

    gradient = lax.psum_scatter(
        lax.map(grad_per_group, (index_part, grad_part)).reshape(
            column_count, block_size, live_count * block_size
        ),
        "dp",
        scatter_dimension=0,
        tiled=True,
    ).astype(jnp.float32)
    rate = 0.1 / math.sqrt(live_count * block_size)
    moment_new = 0.9 * moment[0] + 0.1 * gradient
    second_new = 0.95 * second[0] + 0.05 * gradient * gradient
    stepped = weights[0].astype(jnp.float32) - rate * moment_new / (jnp.sqrt(second_new) + 1e-08)
    own_index = lax.dynamic_slice_in_dim(
        live_index, lax.axis_index("dp") * own_columns, own_columns, 0
    )
    blocked = stepped.reshape(own_columns, block_size, live_count, block_size)
    magnitude = jnp.sqrt(jnp.sum(blocked * blocked, axis=(1, 3)))
    leafed = (
        blocked * shrink(magnitude, 0.15 * math.sqrt(block_size / live_count))[:, None, :, None]
    )
    block_squares = jnp.sum(leafed * leafed, axis=(1, 3))
    head_count = features // HEAD
    head_index = own_index // (HEAD // block_size)
    onehot = (
        head_index[:, :, None] == jnp.arange(head_count, dtype=jnp.int32)[None, None, :]
    ).astype(jnp.float32)
    head_squares = lax.psum(jnp.sum(onehot * block_squares[:, :, None], axis=(0, 1)), "dp")
    head_factor = shrink(jnp.sqrt(head_squares), 0.45 * math.sqrt(HEAD))
    headed = leafed * jnp.sum(onehot * head_factor[None, None, :], axis=2)[:, None, :, None]
    layer_squares = jnp.sum(head_factor * head_factor * head_squares)
    layer_factor = shrink(jnp.sqrt(layer_squares), 0.45 * math.sqrt(features))
    weights_out = (
        (headed * layer_factor)
        .astype(jnp.bfloat16)
        .reshape(own_columns, block_size, live_count * block_size)
    )
    return (weights_out[None], moment_new[None], second_new[None])


def solution(mesh):
    placed = (
        P(None, "dp", None),
        P(None, "dp", None),
        P("pipe", "dp", None, None),
        P("pipe", None, None),
        P("pipe", "dp", None, None),
        P("pipe", "dp", None, None),
    )
    return jax.shard_map(
        local,
        mesh=mesh,
        in_specs=placed,
        out_specs=(
            P("pipe", "dp", None, None),
            P("pipe", "dp", None, None),
            P("pipe", "dp", None, None),
        ),
        check_vma=False,
    )
```

profile of v0, /device:TPU:0, one launch (start us, length us, event | category | flops | bytes accessed | tf_op | source)
XLA Modules:
  0.0 1622.1 jit_solution(3121185956785150585)
XLA Ops:
  8.0 155.5 %all-gather.3.cloned.1.call-done = bf16[1,64,64,2048]{3,2,0,1:T(8,128)(2,1)} async-done(((bf16[1,8,64,2048]{3,2,0,1:T(8,128)(2,1)}), bf16[1,64,64,2048]{3,2,0,1:T(8,128)(2,1)}) %all-gather.3.cloned.1.call-update) | async-done | bytes 16777232 | tf_op jit(solution)/shard_map/all_gather | solution.py:110
  164.2 85.1 %conditional.14 = (bf16[32,4096]{1,0:T(8,128)(2,1)S(1)}, bf16[4,32,4096]{2,1,0:T(8,128)(2,1)}, bf16[4,32,4096]{2,1,0:T(8,128)(2,1)}, f32[4,32,4096]{2,1,0:T(8,128)}) conditional(s32[]{:T(128)} %convert_element_type.242, () %tuple.272, (bf16[4,32,4096]{2,1,0:T(8,128)(2,1)}, pred[32,4096]{1,0:T(8,128)(4,1)S(1)}, bf16[32,4096]{1,0:T(8,128)(2,1)S(1)}, ...), branch_computations={%region_0.1_spmd, %region_1.7_spmd} | conditional | flops 69864752 | bytes 28608244 | solution.py:136
  173.0 69.8 %while.112 = (s32[]{:T(128)}, f32[8,32,8,64]{3,1,2,0:T(8,128)}, bf16[8,8,64,2048]{3,2,1,0:T(8,128)(2,1)}, s32[8,8,32]{2,1,0:T(8,128)S(1)}, bf16[32,64,64]{2,0,1:T(8,128)(2,1)S(1)}, /*index=5*/s32[]{:T(128)}) while((s32[]{:T(128)}, f32[8,32,8,64]{3,1,2,0:T(8,128)}, bf16[8,8,64,2048]{3,2,1,0:T(8,128)(2,1)}, s32[8,8,32]{2,1,0:T(8,128)S(1)}, ...), condition=%wide.region_4.5_spmd, body=%wide.region_3.4_spmd.sunk | while | flops 67636480 | bytes 11680329 | solution.py:38
  251.4 6.5 collective-permute-done
  257.9 83.9 %conditional.15 = (bf16[32,4096]{1,0:T(8,128)(2,1)}, bf16[4,32,4096]{2,1,0:T(8,128)(2,1)}, bf16[4,32,4096]{2,1,0:T(8,128)(2,1)}, f32[4,32,4096]{2,1,0:T(8,128)}) conditional(s32[]{:T(128)} %convert_element_type.241, (bf16[4,32,4096]{2,1,0:T(8,128)(2,1)}, bf16[4,32,4096]{2,1,0:T(8,128)(2,1)}, f32[4,32,4096]{2,1,0:T(8,128)}) %tuple.274, ...), branch_computations={%region_6.8_spmd, %region_7.13_spmd} | conditional | flops 69864752 | bytes 21268686 | solution.py:136
  265.9 69.9 %while.113 = (s32[]{:T(128)}, f32[8,32,8,64]{3,1,2,0:T(8,128)}, bf16[8,8,64,2048]{3,2,1,0:T(8,128)(2,1)}, s32[8,8,32]{2,1,0:T(8,128)S(1)}, bf16[32,64,64]{2,0,1:T(8,128)(2,1)S(1)}, /*index=5*/s32[]{:T(128)}) while((s32[]{:T(128)}, f32[8,32,8,64]{3,1,2,0:T(8,128)}, bf16[8,8,64,2048]{3,2,1,0:T(8,128)(2,1)}, s32[8,8,32]{2,1,0:T(8,128)S(1)}, ...), condition=%wide.region_10.11_spmd, body=%wide.region_9.10_spmd.sunk | while | flops 67636480 | bytes 11680329 | solution.py:38
  346.0 5.8 collective-permute-done.1
  351.8 84.1 %conditional.16 = (bf16[32,4096]{1,0:T(8,128)(2,1)}, bf16[4,32,4096]{2,1,0:T(8,128)(2,1)}, bf16[4,32,4096]{2,1,0:T(8,128)(2,1)}, f32[4,32,4096]{2,1,0:T(8,128)}) conditional(s32[]{:T(128)} %convert_element_type.240, (bf16[4,32,4096]{2,1,0:T(8,128)(2,1)}, bf16[4,32,4096]{2,1,0:T(8,128)(2,1)}, f32[4,32,4096]{2,1,0:T(8,128)}) %tuple.276, ...), branch_computations={%region_12.14_spmd, %region_13.19_spmd} | conditional | flops 69864752 | bytes 21268686 | solution.py:136
  360.0 69.9 %while.114 = (s32[]{:T(128)}, f32[8,32,8,64]{3,1,2,0:T(8,128)}, bf16[8,8,64,2048]{3,2,1,0:T(8,128)(2,1)}, s32[8,8,32]{2,1,0:T(8,128)S(1)}, bf16[32,64,64]{2,0,1:T(8,128)(2,1)S(1)}, /*index=5*/s32[]{:T(128)}) while((s32[]{:T(128)}, f32[8,32,8,64]{3,1,2,0:T(8,128)}, bf16[8,8,64,2048]{3,2,1,0:T(8,128)(2,1)}, s32[8,8,32]{2,1,0:T(8,128)S(1)}, ...), condition=%wide.region_16.17_spmd, body=%wide.region_15.16_spmd.sunk | while | flops 67636480 | bytes 11680329 | solution.py:38
  445.1 83.1 %conditional.17 = (bf16[32,4096]{1,0:T(8,128)(2,1)}, bf16[4,32,4096]{2,1,0:T(8,128)(2,1)}, bf16[4,32,4096]{2,1,0:T(8,128)(2,1)}, f32[4,32,4096]{2,1,0:T(8,128)}) conditional(s32[]{:T(128)} %convert_element_type.239, (bf16[4,32,4096]{2,1,0:T(8,128)(2,1)}, bf16[4,32,4096]{2,1,0:T(8,128)(2,1)}, f32[4,32,4096]{2,1,0:T(8,128)}) %tuple.278, ...), branch_computations={%region_18.20_spmd, %region_19.25_spmd} | conditional | flops 69864752 | bytes 21268686 | solution.py:136
  452.4 69.9 %while.115 = (s32[]{:T(128)}, f32[8,32,8,64]{3,1,2,0:T(8,128)}, bf16[8,8,64,2048]{3,2,1,0:T(8,128)(2,1)}, s32[8,8,32]{2,1,0:T(8,128)S(1)}, bf16[32,64,64]{2,0,1:T(8,128)(2,1)S(1)}, /*index=5*/s32[]{:T(128)}) while((s32[]{:T(128)}, f32[8,32,8,64]{3,1,2,0:T(8,128)}, bf16[8,8,64,2048]{3,2,1,0:T(8,128)(2,1)}, s32[8,8,32]{2,1,0:T(8,128)S(1)}, ...), condition=%wide.region_22.23_spmd, body=%wide.region_21.22_spmd.sunk | while | flops 67636480 | bytes 11680329 | solution.py:38
  537.5 87.2 %collective-permute-start.4 = (bf16[32,4096]{1,0:T(8,128)(2,1)}, bf16[32,4096]{1,0:T(8,128)(2,1)S(1)}, u32[]{:S(2)}, u32[]{:S(2)}) collective-permute-start(bf16[32,4096]{1,0:T(8,128)(2,1)} %get-tuple-element.1129), channel_id=1, source_target_pairs={{0,8},{8,16},{16,24},{1,9},{9,17},{17,25},{2,10},{10,18},{18,26},{... | collective-permute-start | bytes 786440 | tf_op jit(solution)/shard_map/ppermute | solution.py:17
  629.9 8.6 collective-permute-start.5
  638.5 356.8 %while.120 = (s32[]{:T(128)}, bf16[8,512,4096]{2,1,0:T(8,128)(2,1)}, bf16[8,8,64,2048]{3,2,1,0:T(8,128)(2,1)}, s32[8,8,32]{2,1,0:T(8,128)}, s32[]{:T(128)}) while((s32[]{:T(128)}, bf16[8,512,4096]{2,1,0:T(8,128)(2,1)}, bf16[8,8,64,2048]{3,2,1,0:T(8,128)(2,1)}, s32[8,8,32]{2,1,0:T(8,128)}, s32[]{:T(128)}) %tuple.552), condition=%wide.region_43.45_spmd.clone, body=%wide.region_42.44_spmd.clone.sunk | while | flops 136331264 | bytes 39849540 | solution.py:66
  640.2 5.3 reshape.1423
  646.2 8.2 convert_bitcast_fusion.2
  654.5 11.9 copy.222
  666.4 12.0 broadcast_in_dim.172
  684.8 5.3 reshape.1423
  690.8 8.2 convert_bitcast_fusion.2
  699.0 11.9 copy.222
  711.0 12.0 broadcast_in_dim.172
  729.4 5.3 reshape.1423
  735.4 8.2 convert_bitcast_fusion.2
  743.6 11.9 copy.222
  755.6 12.0 broadcast_in_dim.172
  780.0 8.2 convert_bitcast_fusion.2
  788.2 11.9 copy.222
  800.2 12.0 broadcast_in_dim.172
  824.6 8.2 convert_bitcast_fusion.2
  832.8 11.9 copy.222
  844.8 12.0 broadcast_in_dim.172
  869.2 8.2 convert_bitcast_fusion.2
  877.4 11.9 copy.222
  889.4 12.0 broadcast_in_dim.172
  913.8 8.2 convert_bitcast_fusion.2
  922.0 11.9 copy.222
  934.0 12.0 broadcast_in_dim.172
  958.4 8.2 convert_bitcast_fusion.2
  966.6 11.9 copy.222
  978.6 12.0 broadcast_in_dim.172
  998.8 87.8 %collective-permute-done.6 = bf16[32,4096]{1,0:T(8,128)(2,1)S(1)} collective-permute-done((bf16[32,4096]{1,0:T(8,128)(2,1)S(1)}, bf16[32,4096]{1,0:T(8,128)(2,1)S(1)}, u32[]{:S(2)}, u32[]{:S(2)}) %collective-permute-start.6) | collective-permute-done | bytes 262176 | tf_op jit(solution)/shard_map/ppermute | solution.py:17
  1088.0 7.9 collective-permute-done.7
  1098.3 139.0 %collective-permute-done.8 = bf16[32,4096]{1,0:T(8,128)(2,1)S(1)} collective-permute-done((bf16[32,4096]{1,0:T(8,128)(2,1)S(1)}, bf16[32,4096]{1,0:T(8,128)(2,1)S(1)}, u32[]{:S(2)}, u32[]{:S(2)}) %collective-permute-start.8) | collective-permute-done | bytes 262176 | tf_op jit(solution)/shard_map/ppermute | solution.py:17
  1237.4 20.3 %conditional.24 = (bf16[32,4096]{1,0:T(8,128)(2,1)S(1)}, bf16[4,32,4096]{2,1,0:T(8,128)(2,1)}) conditional(s32[]{:T(128)} %convert_element_type.232, bf16[4,32,4096]{2,1,0:T(8,128)(2,1)} %get-tuple-element.1141, (pred[32,4096]{1,0:T(8,128)(4,1)S(1)}, bf16[32,4096]{1,0:T(8,128)(2,1)S(1)}, bf16[32,4096]{1,0:T(8,128)(2,1)S(1)}, s32[]{:T(128)}, ...), branch_computations={%region_59.61_spmd, %region_60.65_spmd} | conditional | flops 1077411840 | bytes 38537416 | solution.py:165
  1242.6 13.9 fusion.45
  1259.0 7.9 collective-permute-done.9
  1266.9 20.3 %conditional.25 = (bf16[32,4096]{1,0:T(8,128)(2,1)S(1)}, bf16[4,32,4096]{2,1,0:T(8,128)(2,1)}) conditional(s32[]{:T(128)} %convert_element_type.231, bf16[4,32,4096]{2,1,0:T(8,128)(2,1)} %get-tuple-element.1143, (pred[32,4096]{1,0:T(8,128)(4,1)S(1)}, bf16[32,4096]{1,0:T(8,128)(2,1)S(1)}, bf16[32,4096]{1,0:T(8,128)(2,1)S(1)}, s32[]{:T(128)}, ...), branch_computations={%region_64.66_spmd, %region_65.70_spmd} | conditional | flops 1077411840 | bytes 38537416 | solution.py:165
  1272.1 13.9 fusion.59
  1288.5 7.9 collective-permute-done.10
  1296.3 21.0 %conditional.26 = (bf16[32,4096]{1,0:T(8,128)(2,1)}, bf16[4,32,4096]{2,1,0:T(8,128)(2,1)}) conditional(s32[]{:T(128)} %convert_element_type.230, bf16[4,32,4096]{2,1,0:T(8,128)(2,1)} %get-tuple-element.1145, (pred[32,4096]{1,0:T(8,128)(4,1)S(1)}, bf16[32,4096]{1,0:T(8,128)(2,1)S(1)}, bf16[32,4096]{1,0:T(8,128)(2,1)S(1)}, s32[]{:T(128)}, ...), branch_computations={%region_69.71_spmd, %region_70.75_spmd} | conditional | flops 1077411840 | bytes 38537416 | solution.py:165
  1301.6 13.9 fusion.73
  1337.3 81.3 %while.119 = (s32[]{:T(128)}, bf16[8,8,64,2048]{3,2,1,0:T(8,128)(2,1)}, bf16[8,128,8,64]{1,3,2,0:T(8,128)(2,1)}, s32[8,8,32]{2,1,0:T(8,128)}, bf16[128,64,64]{0,2,1:T(8,128)(2,1)S(1)}, /*index=5*/s32[]{:T(128)}) while((s32[]{:T(128)}, bf16[8,8,64,2048]{3,2,1,0:T(8,128)(2,1)}, bf16[8,128,8,64]{1,3,2,0:T(8,128)(2,1)}, ...), condition=%wide.region_78.80_spmd, body=%wide.region_77.79_spmd.sunk | while | flops 272633088 | bytes 14890569 | solution.py:193
  1341.4 6.1 fusion.283
  1351.5 6.1 fusion.283
  1361.7 6.1 fusion.283
  1371.9 6.1 fusion.283
  1382.1 6.0 fusion.283
  1392.2 6.1 fusion.283
  1402.4 6.0 fusion.283
  1412.5 6.0 fusion.283
  1419.5 164.0 %reduce-scatter.2.cloned.1.call-done = bf16[8,64,2048]{2,1,0:T(8,128)(2,1)} async-done(((bf16[64,64,2048]{2,1,0:T(8,128)(2,1)}), bf16[8,64,2048]{2,1,0:T(8,128)(2,1)}) %reduce-scatter.2.cloned.1.call-update) | async-done | bytes 2097168 | tf_op jit(solution)/shard_map/reduce_scatter | solution.py:192
  1583.4 8.4 multiply_reduce_fusion.1
  1595.4 13.6 psum.7
  (557 shorter events, 547.4 us)
Async XLA Ops:
  7.2 156.4 %copy-start.4 = (s32[1,64,32]{1,2,0:T(8,128)S(1)}, s32[1,64,32]{1,2,0:T(8,128)}, u32[]{:S(2)}) copy-start(s32[1,64,32]{1,2,0:T(8,128)} %param.113) | copy-start | bytes 24580
  7.2 156.3 %all-gather.3.cloned.1.call-start = ((), (), s32[]{:S(2)}) async-start(), calls=%async_computation.2 | async-start | bytes 18874368 | tf_op jit(solution)/shard_map/all_gather | solution.py:110
  7.9 1575.5 %reduce-scatter.2.cloned.1.call-start = ((), (), s32[]{:S(2)}) async-start(), calls=%async_computation.1 | async-start | bytes 18874368 | tf_op jit(solution)/shard_map/reduce_scatter | solution.py:192
  163.5 0.7 copy-start.2
  245.5 2.7 copy-start.1
  249.3 0.7 copy-start.5
  250.0 7.9 collective-permute-start
  341.8 10.1 collective-permute-start.1
  435.9 9.2 collective-permute-start.2
  528.2 8.4 collective-permute-start.3
  537.5 91.4 %collective-permute-start.4 = (bf16[32,4096]{1,0:T(8,128)(2,1)}, bf16[32,4096]{1,0:T(8,128)(2,1)S(1)}, u32[]{:S(2)}, u32[]{:S(2)}) collective-permute-start(bf16[32,4096]{1,0:T(8,128)(2,1)} %get-tuple-element.1129), channel_id=1, source_target_pairs={{0,8},{8,16},{16,24},{1,9},{9,17},{17,25},{2,10},{10,18},{18,26},{... | collective-permute-start | bytes 786440 | tf_op jit(solution)/shard_map/ppermute | solution.py:17
  629.9 365.4 %collective-permute-start.5 = (bf16[32,4096]{1,0:T(8,128)(2,1)}, bf16[32,4096]{1,0:T(8,128)(2,1)S(1)}, u32[]{:S(2)}, u32[]{:S(2)}) collective-permute-start(bf16[32,4096]{1,0:T(8,128)(2,1)} %get-tuple-element.1133), channel_id=1, source_target_pairs={{0,8},{8,16},{16,24},{1,9},{9,17},{17,25},{2,10},{10,18},{18,26},{... | collective-permute-start | bytes 786440 | tf_op jit(solution)/shard_map/ppermute | solution.py:17
  995.3 1.0 copy-start.3
  997.5 89.1 %collective-permute-start.6 = (bf16[32,4096]{1,0:T(8,128)(2,1)S(1)}, bf16[32,4096]{1,0:T(8,128)(2,1)S(1)}, u32[]{:S(2)}, u32[]{:S(2)}) collective-permute-start(bf16[32,4096]{1,0:T(8,128)(2,1)S(1)} %get-tuple-element.1138), channel_id=1, source_target_pairs={{8,0},{16,8},{24,16},{9,1},{17,9},{25,17},{10,2},{18,10},{26,18},{... | collective-permute-start | bytes 786440 | tf_op jit(solution)/shard_map/ppermute | solution.py:17
  1086.7 9.2 collective-permute-start.7
  1095.9 141.5 %collective-permute-start.8 = (bf16[32,4096]{1,0:T(8,128)(2,1)S(1)}, bf16[32,4096]{1,0:T(8,128)(2,1)S(1)}, u32[]{:S(2)}, u32[]{:S(2)}) collective-permute-start(bf16[32,4096]{1,0:T(8,128)(2,1)S(1)} %get-tuple-element.1142), channel_id=1, source_target_pairs={{8,0},{16,8},{24,16},{9,1},{17,9},{25,17},{10,2},{18,10},{26,18},{... | collective-permute-start | bytes 786440 | tf_op jit(solution)/shard_map/ppermute | solution.py:17
  1257.7 9.2 collective-permute-start.9
  1287.2 9.2 collective-permute-start.10
  1317.3 9.5 collective-permute-start.11
  1418.6 164.8 %copy-start = (bf16[1,8,64,2048]{3,2,1,0:T(8,128)(2,1)S(1)}, bf16[1,8,64,2048]{3,2,1,0:T(8,128)(2,1)}, u32[]{:S(2)}) copy-start(bf16[1,8,64,2048]{3,2,1,0:T(8,128)(2,1)} %param.112) | copy-start | bytes 6291460
Sparse Core Ops, SparseCore 0:
  9.6 153.7 all-gather.2
  1418.7 164.6 reduce-scatter.1
where the time goes:
time: 1640 us; the launch traced here: 1620 us
  waiting for transfers between devices  597 us (36%)
  local copies, waits for them, and re-layouts  494 us (30%)
  matrix products  266 us (16%)
  starting transfers between devices  118 us (7%)
  other arithmetic  115 us (7%)
    ppermute x12, waiting for transfers between devices, shifted(): lax.ppermute(value, axis, [(source, source + steps) for source in range(l...  277 us
    reduce_scatter x1, waiting for transfers between devices, local(): lax.psum_scatter(lax.map(grad_per_group, (index_part, grad_part)).reshape...  164 us
    all_gather x1, waiting for transfers between devices, local(): section_weights = lax.all_gather(weights[0], 'dp', axis=0, tiled=True)  155 us
    ppermute x12, starting transfers between devices, shifted(): lax.ppermute(value, axis, [(source, source + steps) for source in range(l...  118 us
    dot_general x32, matrix products, column_per_group(): jnp.einsum('tjk,jbk->tjb', picked, weight_part, preferred_element_type=jn...  110 us
    broadcast_in_dim x8, local copies, waits for them, and re-layouts, dense_transposed(): lax.map(dense_per_group, (section_weights.reshape(group_count, column_gro...  96.4 us
    convert_element_type x8, local copies, waits for them, and re-layouts, dense_per_group(): slab.astype(jnp.bfloat16).reshape(column_group * block_size, features)  95.6 us
    reshape x32, local copies, waits for them, and re-layouts, column_per_group(): jnp.take(normed_blocks, index_part.reshape(-1), axis=1)  77.9 us
  transfers between devices with their start and end apart: 14, of which 13 were waited for; matrix products, arithmetic and copies ran while one was open for 23% of the time, Pallas kernels for 0%

commit v1 on v0

v1 whole, which is shorter than its diff:
```python
import functools
import math

import jax
import jax.numpy as jnp
from jax import lax
from jax.experimental import pallas as pl
from jax.experimental.pallas import tpu as pltpu
from jax.sharding import PartitionSpec as P

HEAD = 128
F32 = jnp.float32
BF16 = jnp.bfloat16
PAD = 16
TILE = 4
VMEM = pl.BlockSpec(memory_space=pltpu.VMEM)
SMEM = pl.BlockSpec(memory_space=pltpu.SMEM)
ANY = pl.BlockSpec(memory_space=pl.ANY)


def shrink(magnitude, threshold):
    return jnp.maximum(magnitude - threshold, 0.0) / jnp.maximum(magnitude, threshold)


def weight_copies(scal, sources, buffer, sems):
    half = buffer.shape[0] // 4
    waits = []
    for group in range(4):
        owner, part = group // 2, group % 2
        target = buffer.at[pl.ds(group * half, half)]
        candidates = sources[owner][part]
        for index, source in enumerate(candidates):

            @pl.when(scal[2 + part] == index)
            def _(source=source, target=target, group=group):
                pltpu.make_async_copy(source, target, sems.at[group]).start()

        waits.append(pltpu.make_async_copy(candidates[0], target, sems.at[group]).wait)
    return waits


def weight_sources(refs):
    sources = []
    for owner in range(2):
        own, x1, x2, x3, y1, y2, y3 = refs[owner * 7 : owner * 7 + 7]
        half = own.shape[0] // 2
        sources.append(
            (
                (own.at[pl.ds(0, half)], x1, y2, y3),
                (own.at[pl.ds(half, half)], x2, x3, y1),
            )
        )
    return sources


def column_loop(scal, half, columns, body, waits):
    for group in range(4):
        waits[group]()
        owner, part = group // 2, group % 2
        first = ((scal[1] + owner) % 2) * (2 * half) + part * half

        @pl.loop(0, half)
        def _(step, group=group, first=first):
            body(group * half + step, first + step, scal[0] * columns + first + step)


def forward_kernel(ways, whole, last, scal, live, *refs):
    count = 1 if whole else ways
    shards, refs = refs[:count], refs[count:]
    sources, refs = weight_sources(refs[:14]), refs[14:]
    outs = 3 if last else 4
    outputs, (buffer, sems) = refs[:outs], refs[outs:]
    z_ref, u_ref, r_ref = outputs[:3]
    waits = weight_copies(scal, sources, buffer, sems)
    features, tokens = u_ref.shape
    rows = z_ref.shape[0]
    block = buffer.shape[1]
    live_count = buffer.shape[2] // block
    total = jnp.zeros((1, tokens), F32)
    for shard in shards:
        value = shard[...].astype(F32)
        total = total + jnp.sum(value * value, axis=0, keepdims=True)
    inverse = lax.rsqrt(total * (1.0 / features) + 1e-05)
    r_ref[...] = jnp.broadcast_to(inverse, r_ref.shape)
    if whole:
        u_ref[...] = (shards[0][...].astype(F32) * inverse).astype(BF16)
    else:
        for step, shard in enumerate(shards):
            u_ref[pl.ds((scal[0] ^ step) * rows, rows), :] = (
                shard[...].astype(F32) * inverse
            ).astype(BF16)

    def column(slot, local, column_index):
        acc = jnp.zeros((block, tokens), F32)
        for tile in range(live_count // TILE):
            picked = jnp.concatenate(
                [
                    u_ref[pl.ds(live[column_index, tile * TILE + i] * block, block), :]
                    for i in range(TILE)
                ],
                axis=0,
            )
            acc = acc + jnp.dot(
                buffer[slot, :, pl.ds(tile * TILE * block, TILE * block)],
                picked,
                preferred_element_type=F32,
            )
        z_ref[pl.ds(local * block, block), :] = acc

    column_loop(scal, buffer.shape[0] // 4, rows // block, column, waits)
    if not last:
        own = shards[0][pl.ds(scal[0] * rows, rows), :] if whole else shards[0][...]
        pre = z_ref[...]
        outputs[3][...] = (own.astype(F32) + pre * jax.nn.sigmoid(pre)).astype(BF16)


def backward_kernel(ways, first, last, scal, live, *refs):
    if first:
        arriving_ref, refs = refs[0], refs[1:]
    else:
        older_ref, h_ref, r_ref = refs[:3]
        shares, refs = refs[3 : 3 + ways], refs[3 + ways :]
    pre_ref, refs = refs[0], refs[1:]
    if not last:
        sources, refs = weight_sources(refs[:14]), refs[14:]
    gz_ref, refs = refs[0], refs[1:]
    if not last:
        outgoing, refs = refs[:ways], refs[ways:]
    if not first:
        g_ref, refs = refs[0], refs[1:]
    rows, tokens = gz_ref.shape
    if not last:
        buffer, sems, du_ref = refs
        waits = weight_copies(scal, sources, buffer, sems)
    if first:
        arriving = arriving_ref[...].astype(F32)
    else:
        total = shares[0][pl.ds(0, rows), :].astype(F32)
        means = shares[0][pl.ds(rows, PAD), :].astype(F32)
        for share in shares[1:]:
            total = total + share[pl.ds(0, rows), :].astype(F32)
            means = means + share[pl.ds(rows, PAD), :].astype(F32)
        mean = jnp.sum(means, axis=0, keepdims=True) * (1.0 / (rows * ways))
        inverse = r_ref[0:1, :]
        scaled = h_ref[...].astype(F32) * inverse
        arriving = (older_ref[...].astype(F32) + inverse * (total - scaled * mean)).astype(BF16)
        g_ref[...] = arriving
        arriving = arriving.astype(F32)
    pre = pre_ref[...]
    sigmoid = jax.nn.sigmoid(pre)
    gz = (arriving * (sigmoid * (1.0 + pre * (1.0 - sigmoid)))).astype(BF16)
    gz_ref[...] = gz
    if last:
        return
    share = jnp.sum(gz.astype(F32) * pre, axis=0, keepdims=True)
    high = share.astype(BF16).astype(F32)
    low = share - high
    row = lax.broadcasted_iota(jnp.int32, (PAD, tokens), 0)
    extra = jnp.where(row == 0, high, jnp.where(row == 1, low, 0.0)).astype(BF16)
    du_ref[...] = jnp.zeros_like(du_ref)
    block = buffer.shape[1]
    live_count = buffer.shape[2] // block

    def column(slot, local, column_index):
        gz_block = gz_ref[pl.ds(local * block, block), :]
        for tile in range(live_count // TILE):
            product = lax.dot_general(
                buffer[slot, :, pl.ds(tile * TILE * block, TILE * block)],
                gz_block,
                (((0,), (0,)), ((), ())),
                preferred_element_type=F32,
            )
            for i in range(TILE):
                at = pl.ds(live[column_index, tile * TILE + i] * block, block)
                du_ref[at, :] += product[i * block : (i + 1) * block]

    column_loop(scal, buffer.shape[0] // 4, rows // block, column, waits)
    for step in range(ways):
        outgoing[step][pl.ds(0, rows), :] = du_ref[
            pl.ds((scal[0] ^ step) * rows, rows), :
        ].astype(BF16)
        outgoing[step][pl.ds(rows, PAD), :] = extra


def segment_sum(row, width):
    lanes = row.shape[-1]
    lane = lax.broadcasted_iota(jnp.int32, row.shape, row.ndim - 1)
    step = 1
    while step < width:
        ahead = pltpu.roll(row, lanes - step, row.ndim - 1)
        behind = pltpu.roll(row, step, row.ndim - 1)
        row = row + jnp.where((lane // step) % 2 == 0, ahead, behind)
        step *= 2
    return row


def update_kernel(chunks, inverse_tokens, first_column, live, *refs):
    gz_refs, u_refs, refs = refs[:chunks], refs[chunks : 2 * chunks], refs[2 * chunks :]
    weight_ref, moment_ref, second_ref = refs[:3]
    moment_out, second_out, stepped_ref, factor_ref, squares_ref = refs[3:]
    column = pl.program_id(0)
    column_index = first_column[0] + column
    block, wide = weight_ref.shape[1:]
    live_count = wide // block
    rate = 0.1 / math.sqrt(wide)
    lhs = jnp.concatenate([gz[...] for gz in gz_refs], axis=1)
    for tile in range(live_count // TILE):
        picked = jnp.concatenate(
            [
                jnp.concatenate(
                    [
                        u[pl.ds(live[column_index, tile * TILE + i] * block, block), :]
                        for u in u_refs
                    ],
                    axis=1,
                )
                for i in range(TILE)
            ],
            axis=0,
        )
        gradient = (
            lax.dot_general(
                lhs, picked, (((1,), (1,)), ((), ())), preferred_element_type=F32
            )
            * inverse_tokens
        )
        at = pl.ds(tile * TILE * block, TILE * block)
        moment = 0.9 * moment_ref[0, :, at] + 0.1 * gradient
        second = 0.95 * second_ref[0, :, at] + 0.05 * gradient * gradient
        stepped = weight_ref[0, :, at].astype(F32) - rate * moment / (jnp.sqrt(second) + 1e-08)
        moment_out[0, :, at] = moment
        second_out[0, :, at] = second
        stepped_ref[0, :, at] = stepped
        squares = segment_sum(jnp.sum(stepped * stepped, axis=0, keepdims=True), block)
        factor = shrink(jnp.sqrt(squares), 0.15 * math.sqrt(block / live_count))
        factor_ref[0, :, at] = factor
        squares_ref[0, :, at] = factor * factor * squares


def kernel_call(kernel, name, outs, in_specs, out_specs, limit_mib, **kwargs):
    return pl.pallas_call(
        kernel,
        out_shape=outs,
        in_specs=in_specs,
        out_specs=out_specs,
        compiler_params=pltpu.CompilerParams(vmem_limit_bytes=limit_mib << 20),
        name=name,
        **kwargs,
    )


def after(value, *others):
    return lax.optimization_barrier((value, *others))[0]


def local(x_in, cotangent, weights, live_rows, moment, second):
    sections = lax.axis_size("pipe")
    devices = lax.axis_size("dp")
    ways = devices // 2
    section = lax.axis_index("pipe")
    place = lax.axis_index("dp")
    line, core = (place // 2, place % 2)
    micro_count, share, features = x_in.shape
    own_columns, block, wide = weights.shape[1:]
    live_count = wide // block
    half = own_columns // 2
    columns = 2 * own_columns
    rows = columns * block
    tokens = ways * share
    column_count = live_rows.shape[1]

    def to_pipe(value, step):
        return lax.ppermute(value, "pipe", [(i, i ^ step) for i in range(sections)])

    def to_line(value, step):
        return lax.ppermute(value, "dp", [(i, i ^ (2 * step)) for i in range(devices)])

    def to_core(value):
        return lax.ppermute(value, "dp", [(i, i ^ 1) for i in range(devices)])

    own_live = live_rows[0]
    by_step = [own_live] + [to_pipe(own_live, step) for step in range(1, sections)]
    live = [lax.select_n(section ^ layer, *by_step) for layer in range(sections)]

    own = weights[0]
    first_half, second_half = own[:half], own[half:]
    x1 = to_pipe(first_half, 1)
    y1 = to_pipe(second_half, 2)
    x2 = to_pipe(jnp.where(section == 2, y1, second_half), 1)
    y2 = to_pipe(jnp.where(section == 1, x1, first_half), 2)
    x3 = to_pipe(after(jnp.where(section == 2, second_half, y1), x2), 1)
    y3 = to_pipe(after(jnp.where(section == 1, first_half, x1), y2), 2)
    mine = [own, x1, x2, x3, y1, y2, y3]
    siblings = [to_core(value) for value in mine]
    odd = (section == sections - 1).astype(jnp.int32)
    scal, held = [], []
    for layer in range(sections):
        step = section ^ layer
        source_first = jnp.where(step < 2, step, (step - 2) ^ odd + 0)
        source_first = jnp.where(step < 2, step, 2 + ((step - 2) ^ odd))
        source_second = jnp.where(
            step == 0, 0, jnp.where(step == 2, 3, 1 + ((step == 3).astype(jnp.int32) ^ odd))
        )
        scal.append(jnp.stack([line, core, source_first, source_second]).astype(jnp.int32))
        if layer == 0:
            pick = [0, 1, 2, 2, 4, 5, 5]
        else:
            pick = [0, 1, 2, 3, 4, 5, 6]
        held.append([mine[i] for i in pick] + [siblings[i] for i in pick])

    x_own = lax.dynamic_index_in_dim(x_in, section, 0, keepdims=False)
    cot_own = lax.dynamic_index_in_dim(cotangent, section, 0, keepdims=False)
    x_all = jnp.zeros((ways, share, features), BF16)
    cot_all = jnp.zeros((ways, share, rows), BF16)
    for step in range(ways):
        x_part = x_own if step == 0 else to_line(x_own, step)
        x_all = lax.dynamic_update_index_in_dim(x_all, x_part, line ^ step, 0)
        cot_part = lax.dynamic_slice_in_dim(cot_own, (line ^ step) * rows, rows, 1)
        cot_part = cot_part if step == 0 else to_line(cot_part, step)
        cot_all = lax.dynamic_update_index_in_dim(cot_all, cot_part, line ^ step, 0)
    x_all = x_all.reshape(tokens, features).T
    cot_all = cot_all.reshape(tokens, rows).T

    def sds(shape, dtype):
        return jax.ShapeDtypeStruct(shape, dtype)

    weight_scratch = [
        pltpu.VMEM((columns, block, wide), BF16),
        pltpu.SemaphoreType.DMA((4,)),
    ]
    limit = 48
    shards = [x_all]
    entering, inverses, normed, pre_acts = [None], [], [], []
    for layer in range(sections):
        last = layer == sections - 1
        outs = [
            sds((rows, tokens), F32),
            sds((features, tokens), BF16),
            sds((8, tokens), F32),
        ] + ([] if last else [sds((rows, tokens), BF16)])
        result = kernel_call(
            functools.partial(forward_kernel, ways, layer == 0, last),
            f"forward{layer}",
            outs,
            [SMEM, SMEM] + [VMEM] * len(shards) + [ANY] * 14,
            [VMEM] * len(outs),
            limit,
            scratch_shapes=weight_scratch,
        )(scal[layer], live[layer], *shards, *held[layer])
        pre_acts.append(result[0])
        normed.append(result[1])
        inverses.append(result[2])
        if not last:
            entering.append(result[3])
            shards = [result[3]] + [to_line(result[3], step) for step in range(1, ways)]

    u_chunks = [lax.select_n(section, *normed)]
    for step in range(1, sections):
        u_chunks.append(to_pipe(lax.select_n(section ^ step, *normed), step))
    u_chunks = u_chunks + [to_core(value) for value in u_chunks]

    gradients = [None] * sections
    arriving = [cot_all]
    for layer in reversed(range(sections)):
        first, last = layer == sections - 1, layer == 0
        outs = [sds((rows, tokens), BF16)]
        if not last:
            outs += [sds((rows + PAD, tokens), BF16)] * ways
        if not first:
            outs += [sds((rows, tokens), BF16)]
        operands = arriving + [pre_acts[layer]]
        weight_operands = [] if last else held[layer]
        result = kernel_call(
            functools.partial(backward_kernel, ways, first, last),
            f"backward{layer}",
            outs,
            [SMEM, SMEM] + [VMEM] * len(operands) + [ANY] * len(weight_operands),
            [VMEM] * len(outs),
            limit,
            scratch_shapes=[]
            if last
            else weight_scratch + [pltpu.VMEM((features, tokens), F32)],
        )(scal[layer], live[layer], *operands, *weight_operands)
        gradients[layer] = result[0]
        if not last:
            outgoing = result[1 : 1 + ways]
            incoming = [outgoing[0]] + [to_line(outgoing[k], k) for k in range(1, ways)]
            older = cot_all if first else result[1 + ways]
            arriving = [older, entering[layer], inverses[layer]] + incoming

    own_rows = own_columns * block
    gz_chunks = []
    for flip in range(2):
        for step in range(sections):
            value = lax.select_n(section ^ step, *gradients)
            value = lax.dynamic_slice_in_dim(value, (core ^ flip) * own_rows, own_rows, 0)
            if step or flip:
                value = lax.ppermute(
                    value,
                    ("pipe", "dp"),
                    [
                        (i * devices + j, (i ^ step) * devices + (j ^ flip))
                        for i in range(sections)
                        for j in range(devices)
                    ],
                )
            gz_chunks.append(value)

    chunks = len(gz_chunks)
    all_tokens = micro_count * devices * share
    per_column = pl.BlockSpec((1, block, wide), lambda j: (j, 0, 0))
    per_row = pl.BlockSpec((1, 1, wide), lambda j: (j, 0, 0))
    held_whole = pl.BlockSpec(
        (features, tokens), lambda j: (0, 0), pipeline_mode=pl.Buffered(1)
    )
    moment_new, second_new, stepped, factor, squares = kernel_call(
        functools.partial(update_kernel, chunks, 1.0 / all_tokens),
        "update",
        [sds((own_columns, block, wide), F32)] * 3 + [sds((own_columns, 1, wide), F32)] * 2,
        [SMEM, SMEM]
        + [pl.BlockSpec((block, tokens), lambda j: (j, 0))] * chunks
        + [held_whole] * chunks
        + [per_column] * 3,
        [per_column] * 3 + [per_row] * 2,
        56,
        grid=(own_columns,),
    )(
        jnp.stack([place * own_columns]).astype(jnp.int32),
        own_live,
        *gz_chunks,
        *u_chunks,
        own,
        moment[0],
        second[0],
    )
    own_index = lax.dynamic_slice_in_dim(own_live, place * own_columns, own_columns, 0)
    head_count = features // HEAD
    onehot = (
        (own_index // (HEAD // block))[:, :, None]
        == jnp.arange(head_count, dtype=jnp.int32)[None, None, :]
    ).astype(F32)
    leaf_squares = squares.reshape(own_columns, live_count, block)[:, :, 0]
    leaf_factor = factor.reshape(own_columns, live_count, block)[:, :, 0]
    head_share = jnp.sum(onehot * leaf_squares[:, :, None], axis=(0, 1))
    head_squares = head_share
    for step in range(1, devices):
        head_squares = head_squares + lax.ppermute(
            head_share, "dp", [(i, i ^ step) for i in range(devices)]
        )
    head_factor = shrink(jnp.sqrt(head_squares), 0.45 * math.sqrt(HEAD))
    layer_squares = jnp.sum(head_factor * head_factor * head_squares)
    layer_factor = shrink(jnp.sqrt(layer_squares), 0.45 * math.sqrt(features))
    scale = leaf_factor * jnp.sum(onehot * head_factor[None, None, :], axis=2) * layer_factor
    scale = jnp.broadcast_to(scale[:, :, None], (own_columns, live_count, block))
    weights_out = (stepped * scale.reshape(own_columns, 1, wide)).astype(BF16)
    return (weights_out[None], moment_new[None], second_new[None])


def solution(mesh):
    placed = (
        P(None, "dp", None),
        P(None, "dp", None),
        P("pipe", "dp", None, None),
        P("pipe", None, None),
        P("pipe", "dp", None, None),
        P("pipe", "dp", None, None),
    )
    return jax.shard_map(
        local,
        mesh=mesh,
        in_specs=placed,
        out_specs=(
            P("pipe", "dp", None, None),
            P("pipe", "dp", None, None),
            P("pipe", "dp", None, None),
        ),
        check_vma=False,
    )
```

time: 1640 us -> 417 us (0.25); the launches traced: 1620 us -> 416 us
  local copies, waits for them, and re-layouts: 494 us -> 28.8 us
  waiting for transfers between devices: 597 us -> 202 us
  matrix products: 266 us -> 0 us
  other arithmetic: 115 us -> 15.4 us
  Pallas kernels: 0 us -> 73.8 us
  starting transfers between devices: 118 us -> 93.9 us
    dot_general x51 -> x0, matrix products: 266 us -> none  [the longest x32 110 us: column_per_group(): jnp.einsum('tjk,jbk->tjb', picked, weight_part, preferred_element_type=jn...]
    reduce_scatter x1 -> x0, waiting for transfers between devices: 164 us -> none  [local(): lax.psum_scatter(lax.map(grad_per_group, (index_part, grad_part)).reshape...]
    all_gather x1 -> x0, waiting for transfers between devices: 155 us -> none  [local(): section_weights = lax.all_gather(weights[0], 'dp', axis=0, tiled=True)]
    reshape x89 -> x4, local copies, waits for them, and re-layouts: 130 us -> 3.55 us  [the longest x1 2.26 us: local(): x_all = x_all.reshape(tokens, features).T]
    broadcast_in_dim x25 -> x3, local copies, waits for them, and re-layouts: 99.7 us -> 1.18 us  [the longest x1 1.07 us: local(): x_all = jnp.zeros((ways, share, features), BF16)]
    convert_element_type x8 -> x0, local copies, waits for them, and re-layouts: 95.6 us -> none  [dense_per_group(): slab.astype(jnp.bfloat16).reshape(column_group * block_size, features)]
    ppermute x12 -> x61, waiting for transfers between devices: 277 us -> 202 us  [the longest x24 120 us: to_line(): lax.ppermute(value, 'dp', [(i, i ^ 2 * step) for i in range(devices)])]
    pallas_call x0 -> x9, Pallas kernels: none -> 73.8 us  [the longest x4 28.1 us: local(): kernel_call(functools.partial(backward_kernel, ways, first, last), f'back...]
  transfers between devices with their start and end apart: 14 -> 61, of which waited for: 13 -> 28; matrix products, arithmetic and copies ran while one was open for 23% -> 4% of each run, Pallas kernels for 0% -> 7%
where the time goes in v1:
time: 417 us; the launch traced here: 416 us
  waiting for transfers between devices  202 us (48%)
  starting transfers between devices  93.9 us (23%)
  Pallas kernels  73.8 us (18%)
  local copies, waits for them, and re-layouts  28.8 us (7%)
  other arithmetic  15.4 us (4%)
    ppermute x24, waiting for transfers between devices, to_line(): lax.ppermute(value, 'dp', [(i, i ^ 2 * step) for i in range(devices)])  120 us
    ppermute x24, starting transfers between devices, to_line(): lax.ppermute(value, 'dp', [(i, i ^ 2 * step) for i in range(devices)])  57.4 us
    ppermute x12, waiting for transfers between devices, to_pipe(): return lax.ppermute(value, 'pipe', [(i, i ^ step) for i in range(sections)])  52 us
    pallas_call x4, Pallas kernels, local(): kernel_call(functools.partial(backward_kernel, ways, first, last), f'back...  28.1 us
    ppermute x7, waiting for transfers between devices, local(): lax.ppermute(value, ('pipe', 'dp'), [(i * devices + j, (i ^ step) * devic...  26.6 us
    pallas_call x4, Pallas kernels, local(): kernel_call(functools.partial(forward_kernel, ways, layer == 0, last), f'...  24.5 us
    pallas_call x1, Pallas kernels, local(): kernel_call(functools.partial(update_kernel, chunks, 1.0 / all_tokens), '...  21.3 us
    ppermute x12, starting transfers between devices, to_pipe(): return lax.ppermute(value, 'pipe', [(i, i ^ step) for i in range(sections)])  16.3 us
  transfers between devices with their start and end apart: 61, of which 28 were waited for; matrix products, arithmetic and copies ran while one was open for 4% of the time, Pallas kernels for 7%

profile of v1, /device:TPU:0, one launch (start us, length us, event | category | flops | bytes accessed | tf_op | source)
XLA Modules:
  0.0 415.8 jit_solution(11912113881133598606)
XLA Ops:
  0.6 2.8 slice_bitcast_fusion
  3.4 2.9 collective-permute-start.9
  6.3 1.5 collective-permute-start.10
  7.9 21.8 %collective-permute-done.9.refs_2_.refs_5_.refs_3_.refs_9_ = bf16[4,64,2048]{2,1,0:T(8,128)(2,1)S(1)} collective-permute-done((bf16[4,64,2048]{2,1,0:T(8,128)(2,1)}, bf16[4,64,2048]{2,1,0:T(8,128)(2,1)S(1)}, u32[]{:S(2)}, u32[]{:S(2)}) %collective-permute-start.9) | collective-permute-done | bytes 1048608 | tf_op jit(solution)/shard_map/ppermute | solution.py:273
  31.0 4.1 broadcast_select_fusion
  35.5 1.6 collective-permute-start.12
  37.7 2.5 collective-permute-start.2
  41.3 1.8 dynamic-slice_bitcast_fusion
  43.0 19.7 %collective-permute-done.1 = s32[64,32]{1,0:T(8,128)S(1)} collective-permute-done((s32[64,32]{1,0:T(8,128)S(1)}, s32[64,32]{1,0:T(8,128)S(1)}, u32[]{:S(2)}, u32[]{:S(2)}) %collective-permute-start.1) | collective-permute-done | bytes 8224 | tf_op jit(solution)/shard_map/ppermute | solution.py:273
  62.7 1.5 collective-permute-start
  64.4 1.6 collective-permute-start.6
  66.6 2.6 collective-permute-start.7
  70.9 6.5 %collective-permute-done.6 = bf16[32,4096]{1,0:T(8,128)(2,1)} collective-permute-done((bf16[32,4096]{1,0:T(8,128)(2,1)}, bf16[32,4096]{1,0:T(8,128)(2,1)}, u32[]{:S(2)}, u32[]{:S(2)}) %collective-permute-start.6) | collective-permute-done | bytes 262176 | tf_op jit(solution)/shard_map/ppermute | solution.py:276
  77.4 9.8 %collective-permute-done.7 = bf16[32,4096]{1,0:T(8,128)(2,1)} collective-permute-done((bf16[32,4096]{1,0:T(8,128)(2,1)}, bf16[32,4096]{1,0:T(8,128)(2,1)}, u32[]{:S(2)}, u32[]{:S(2)}) %collective-permute-start.7) | collective-permute-done | bytes 262176 | tf_op jit(solution)/shard_map/ppermute | solution.py:276
  87.3 1.6 collective-permute-start.22
  88.9 1.7 bitcast_dynamic-update-slice_fusion.2
  92.1 1.7 bitcast_dynamic-update-slice_fusion.1
  93.8 7.6 %collective-permute-done.21.refs_7_.refs_5_.refs_11_ = bf16[4,64,2048]{2,1,0:T(8,128)(2,1)} collective-permute-done((bf16[4,64,2048]{2,1,0:T(8,128)(2,1)}, bf16[4,64,2048]{2,1,0:T(8,128)(2,1)}, u32[]{:S(2)}, u32[]{:S(2)}) %collective-permute-start.21) | collective-permute-done | bytes 1048608 | tf_op jit(solution)/shard_map/ppermute | solution.py:273
  103.1 2.3 copy.31
  106.6 6.5 %forward0.1 = (f32[1024,128]{1,0:T(8,128)S(1)}, bf16[4096,128]{1,0:T(8,128)(2,1)S(1)}, f32[8,128]{1,0:T(8,128)}, bf16[1024,128]{1,0:T(8,128)(2,1)S(1)}) custom-call(s32[4]{0:T(128)S(1)} %get-tuple-element.119.scal, s32[64,32]{1,0:T(8,128)S(1)} %get-tuple-element.118.live, bf16[4096,128]{1,0:T(8,128)(2,1)S(1)} %bitcast.74, ...), custom_call_target="tpu_custom_call" | custom-call | tf_op jit(solution)/shard_map/forward0/pallas_call | solution.py:341
  114.9 7.9 %collective-permute-start.18 = (bf16[1024,128]{1,0:T(8,128)(2,1)S(1)}, bf16[1024,128]{1,0:T(8,128)(2,1)S(1)}, u32[]{:S(2)}, u32[]{:S(2)}) collective-permute-start(bf16[1024,128]{1,0:T(8,128)(2,1)S(1)} %get-tuple-element.42.refs_0_.refs_1_), channel_id=1, source_target_pairs={{0,2},{1,3},{2,0},{3,1},{4,6},{5,7},{6,4},{7,5},{8,10},{9,11},{10,... | collective-permute-start | bytes 786440 | tf_op jit(solution)/shard_map/ppermute | solution.py:276
  122.8 3.5 collective-permute-start.19
  127.5 7.6 %collective-permute-done.18.refs_1_ = bf16[1024,128]{1,0:T(8,128)(2,1)S(1)} collective-permute-done((bf16[1024,128]{1,0:T(8,128)(2,1)S(1)}, bf16[1024,128]{1,0:T(8,128)(2,1)S(1)}, u32[]{:S(2)}, u32[]{:S(2)}) %collective-permute-start.18) | collective-permute-done | bytes 262176 | tf_op jit(solution)/shard_map/ppermute | solution.py:276
  135.1 9.6 %collective-permute-done.19.refs_2_ = bf16[1024,128]{1,0:T(8,128)(2,1)S(1)} collective-permute-done((bf16[1024,128]{1,0:T(8,128)(2,1)S(1)}, bf16[1024,128]{1,0:T(8,128)(2,1)S(1)}, u32[]{:S(2)}, u32[]{:S(2)}) %collective-permute-start.19) | collective-permute-done | bytes 262176 | tf_op jit(solution)/shard_map/ppermute | solution.py:276
  144.7 5.6 %forward1.1 = (f32[1024,128]{1,0:T(8,128)S(1)}, bf16[4096,128]{1,0:T(8,128)(2,1)S(1)}, f32[8,128]{1,0:T(8,128)S(1)}, bf16[1024,128]{1,0:T(8,128)(2,1)S(1)}) custom-call(s32[4]{0:T(128)S(1)} %get-tuple-element.121.scal, s32[64,32]{1,0:T(8,128)S(1)} %get-tuple-element.117.live, bf16[1024,128]{1,0:T(8,128)(2,1)S(1)} %get-tuple-element.42.refs_0_.refs_1_, ...), custom_call_target="tpu_custom_call" | custom-call | tf_op jit(solution)/shard_map/forward1/pallas_call | solution.py:341
  152.1 5.8 %collective-permute-start.25 = (bf16[1024,128]{1,0:T(8,128)(2,1)S(1)}, bf16[1024,128]{1,0:T(8,128)(2,1)S(1)}, u32[]{:S(2)}, u32[]{:S(2)}) collective-permute-start(bf16[1024,128]{1,0:T(8,128)(2,1)S(1)} %get-tuple-element.45.refs_0_.refs_1_), channel_id=1, source_target_pairs={{0,2},{1,3},{2,0},{3,1},{4,6},{5,7},{6,4},{7,5},{8,10},{9,11},{10,... | collective-permute-start | bytes 786440 | tf_op jit(solution)/shard_map/ppermute | solution.py:276
  160.2 2.0 collective-permute-start.4
  163.7 5.1 %collective-permute-done.25.refs_1_ = bf16[1024,128]{1,0:T(8,128)(2,1)S(1)} collective-permute-done((bf16[1024,128]{1,0:T(8,128)(2,1)S(1)}, bf16[1024,128]{1,0:T(8,128)(2,1)S(1)}, u32[]{:S(2)}, u32[]{:S(2)}) %collective-permute-start.25) | collective-permute-done | bytes 262176 | tf_op jit(solution)/shard_map/ppermute | solution.py:276
  168.8 13.3 %collective-permute-done.26.refs_2_ = bf16[1024,128]{1,0:T(8,128)(2,1)S(1)} collective-permute-done((bf16[1024,128]{1,0:T(8,128)(2,1)S(1)}, bf16[1024,128]{1,0:T(8,128)(2,1)S(1)}, u32[]{:S(2)}, u32[]{:S(2)}) %collective-permute-start.26) | collective-permute-done | bytes 262176 | tf_op jit(solution)/shard_map/ppermute | solution.py:276
  182.1 6.2 %forward2.1 = (f32[1024,128]{1,0:T(8,128)S(1)}, bf16[4096,128]{1,0:T(8,128)(2,1)S(1)}, f32[8,128]{1,0:T(8,128)S(1)}, bf16[1024,128]{1,0:T(8,128)(2,1)S(1)}) custom-call(s32[4]{0:T(128)S(1)} %get-tuple-element.120.scal, s32[64,32]{1,0:T(8,128)S(1)} %get-tuple-element.116.live, bf16[1024,128]{1,0:T(8,128)(2,1)S(1)} %get-tuple-element.45.refs_0_.refs_1_, ...), custom_call_target="tpu_custom_call" | custom-call | tf_op jit(solution)/shard_map/forward2/pallas_call | solution.py:341
  190.0 6.1 %collective-permute-start.28 = (bf16[1024,128]{1,0:T(8,128)(2,1)S(1)}, bf16[1024,128]{1,0:T(8,128)(2,1)S(1)}, u32[]{:S(2)}, u32[]{:S(2)}) collective-permute-start(bf16[1024,128]{1,0:T(8,128)(2,1)S(1)} %get-tuple-element.46.refs_0_.refs_1_), channel_id=1, source_target_pairs={{0,2},{1,3},{2,0},{3,1},{4,6},{5,7},{6,4},{7,5},{8,10},{9,11},{10,... | collective-permute-start | bytes 786440 | tf_op jit(solution)/shard_map/ppermute | solution.py:276
  200.3 2.8 collective-permute-done.28.refs_1_
  203.1 13.1 %collective-permute-done.29.refs_2_ = bf16[1024,128]{1,0:T(8,128)(2,1)} collective-permute-done((bf16[1024,128]{1,0:T(8,128)(2,1)S(1)}, bf16[1024,128]{1,0:T(8,128)(2,1)}, u32[]{:S(2)}, u32[]{:S(2)}) %collective-permute-start.29) | collective-permute-done | bytes 262176 | tf_op jit(solution)/shard_map/ppermute | solution.py:276
  216.3 6.2 %forward3.1 = (f32[1024,128]{1,0:T(8,128)S(1)}, bf16[4096,128]{1,0:T(8,128)(2,1)S(1)}, f32[8,128]{1,0:T(8,128)S(1)}) custom-call(s32[4]{0:T(128)S(1)} %get-tuple-element.83.scal, s32[64,32]{1,0:T(8,128)S(1)} %get-tuple-element.115.live, bf16[1024,128]{1,0:T(8,128)(2,1)S(1)} %get-tuple-element.46.refs_0_.refs_1_, ...), custom_call_target="tpu_custom_call" | custom-call | tf_op jit(solution)/shard_map/forward3/pallas_call | solution.py:341
  222.4 8.7 %backward3.1 = (bf16[1024,128]{1,0:T(8,128)(2,1)S(1)}, bf16[1040,128]{1,0:T(8,128)(2,1)S(1)}, bf16[1040,128]{1,0:T(8,128)(2,1)S(1)}, bf16[1040,128]{1,0:T(8,128)(2,1)S(1)}, bf16[1040,128]{1,0:T(8,128)(2,1)S(1)}) custom-call(s32[4]{0:T(128)S(1)} %get-tuple-element.83.scal, s32[64,32]{1,0:T(8,128)S(1)} %get-tuple-element.115.live, ...), custom_call_target="tpu_custom_call" | custom-call | tf_op jit(solution)/shard_map/backward3/pallas_call | solution.py:373
  231.2 3.4 collective-permute-start.31
  237.0 4.6 %collective-permute-done.31.refs_4_ = bf16[1040,128]{1,0:T(8,128)(2,1)S(1)} collective-permute-done((bf16[1040,128]{1,0:T(8,128)(2,1)S(1)}, bf16[1040,128]{1,0:T(8,128)(2,1)S(1)}, u32[]{:S(2)}, u32[]{:S(2)}) %collective-permute-start.31) | collective-permute-done | bytes 266272 | tf_op jit(solution)/shard_map/ppermute | solution.py:276
  241.6 13.2 %collective-permute-done.32.refs_5_ = bf16[1040,128]{1,0:T(8,128)(2,1)S(1)} collective-permute-done((bf16[1040,128]{1,0:T(8,128)(2,1)S(1)}, bf16[1040,128]{1,0:T(8,128)(2,1)S(1)}, u32[]{:S(2)}, u32[]{:S(2)}) %collective-permute-start.32) | collective-permute-done | bytes 266272 | tf_op jit(solution)/shard_map/ppermute | solution.py:276
  254.8 8.5 %backward2.1 = (bf16[1024,128]{1,0:T(8,128)(2,1)S(1)}, bf16[1040,128]{1,0:T(8,128)(2,1)S(1)}, bf16[1040,128]{1,0:T(8,128)(2,1)S(1)}, bf16[1040,128]{1,0:T(8,128)...) custom-call(s32[4]{0:T(128)S(1)} %get-tuple-element.120.scal, ...), custom_call_target="tpu_custom_call" | custom-call | tf_op jit(solution)/shard_map/backward2/pallas_call | solution.py:373
  263.4 3.5 collective-permute-start.34
  266.9 2.3 select_select_fusion
  269.2 2.1 collective-permute-start.47
  272.8 1.7 collective-permute-start.35
  276.0 15.9 %collective-permute-done.35.refs_5_ = bf16[1040,128]{1,0:T(8,128)(2,1)S(1)} collective-permute-done((bf16[1040,128]{1,0:T(8,128)(2,1)S(1)}, bf16[1040,128]{1,0:T(8,128)(2,1)S(1)}, u32[]{:S(2)}, u32[]{:S(2)}) %collective-permute-start.35) | collective-permute-done | bytes 266272 | tf_op jit(solution)/shard_map/ppermute | solution.py:276
  291.9 8.9 %backward1.1 = (bf16[1024,128]{1,0:T(8,128)(2,1)S(1)}, bf16[1040,128]{1,0:T(8,128)(2,1)S(1)}, bf16[1040,128]{1,0:T(8,128)(2,1)S(1)}, bf16[1040,128]{1,0:T(8,128)...) custom-call(s32[4]{0:T(128)S(1)} %get-tuple-element.121.scal, s32[64,32]{1,0:T(8,128)S(1)} %get-tuple-element.117.live, ...), custom_call_target="tpu_custom_call" | custom-call | tf_op jit(solution)/shard_map/backward1/pallas_call | solution.py:373
  302.9 5.1 %collective-permute-start.37 = (bf16[1040,128]{1,0:T(8,128)(2,1)S(1)}, bf16[1040,128]{1,0:T(8,128)(2,1)S(1)}, u32[]{:S(2)}, u32[]{:S(2)}) collective-permute-start(bf16[1040,128]{1,0:T(8,128)(2,1)S(1)} %get-tuple-element.64), channel_id=1, source_target_pairs={{0,2},{1,3},{2,0},{3,1},{4,6},{5,7},{6,4},{7,5},{8,10},{9,11},{10,... | collective-permute-start | bytes 798728 | tf_op jit(solution)/shard_map/ppermute | solution.py:276
  308.0 1.7 collective-permute-start.38
  309.7 10.4 %collective-permute-done.37.refs_4_ = bf16[1040,128]{1,0:T(8,128)(2,1)S(1)} collective-permute-done((bf16[1040,128]{1,0:T(8,128)(2,1)S(1)}, bf16[1040,128]{1,0:T(8,128)(2,1)S(1)}, u32[]{:S(2)}, u32[]{:S(2)}) %collective-permute-start.37) | collective-permute-done | bytes 266272 | tf_op jit(solution)/shard_map/ppermute | solution.py:276
  321.1 8.6 %collective-permute-done.39.refs_6_ = bf16[1040,128]{1,0:T(8,128)(2,1)S(1)} collective-permute-done((bf16[1040,128]{1,0:T(8,128)(2,1)}, bf16[1040,128]{1,0:T(8,128)(2,1)S(1)}, u32[]{:S(2)}, u32[]{:S(2)}) %collective-permute-start.39) | collective-permute-done | bytes 266272 | tf_op jit(solution)/shard_map/ppermute | solution.py:276
  331.6 2.0 backward0.1
  335.4 2.2 collective-permute-start.40
  337.6 4.1 collective-permute-done.40.refs_1_
  342.6 4.4 %collective-permute-done.41.refs_2_ = bf16[512,128]{1,0:T(8,128)(2,1)S(1)} collective-permute-done((bf16[512,128]{1,0:T(8,128)(2,1)S(1)}, bf16[512,128]{1,0:T(8,128)(2,1)S(1)}, u32[]{:S(2)}, u32[]{:S(2)}) %collective-permute-start.41) | collective-permute-done | bytes 131104 | tf_op jit(solution)/shard_map/ppermute | solution.py:398
  347.0 1.8 collective-permute-start.42
  349.4 3.4 collective-permute-done.42.refs_3_
  355.5 4.2 %collective-permute-done.44.refs_5_ = bf16[512,128]{1,0:T(8,128)(2,1)S(1)} collective-permute-done((bf16[512,128]{1,0:T(8,128)(2,1)S(1)}, bf16[512,128]{1,0:T(8,128)(2,1)S(1)}, u32[]{:S(2)}, u32[]{:S(2)}) %collective-permute-start.44) | collective-permute-done | bytes 131104 | tf_op jit(solution)/shard_map/ppermute | solution.py:398
  360.1 5.1 %collective-permute-done.45.refs_6_ = bf16[512,128]{1,0:T(8,128)(2,1)S(1)} collective-permute-done((bf16[512,128]{1,0:T(8,128)(2,1)S(1)}, bf16[512,128]{1,0:T(8,128)(2,1)S(1)}, u32[]{:S(2)}, u32[]{:S(2)}) %collective-permute-start.45) | collective-permute-done | bytes 131104 | tf_op jit(solution)/shard_map/ppermute | solution.py:398
  365.1 1.5 collective-permute-start.46
  367.3 4.2 %collective-permute-done.46.refs_7_ = bf16[512,128]{1,0:T(8,128)(2,1)S(1)} collective-permute-done((bf16[512,128]{1,0:T(8,128)(2,1)S(1)}, bf16[512,128]{1,0:T(8,128)(2,1)S(1)}, u32[]{:S(2)}, u32[]{:S(2)}) %collective-permute-start.46) | collective-permute-done | bytes 131104 | tf_op jit(solution)/shard_map/ppermute | solution.py:398
  372.5 21.3 %update.1 = (f32[8,64,2048]{2,1,0:T(8,128)}, f32[8,64,2048]{2,1,0:T(8,128)}, f32[8,64,2048]{2,1,0:T(8,128)}, f32[8,1,2048]{2,1,0:T(1,128)}, f32[8,1,2048]{2,1,0:T(1,128)}) custom-call(s32[1]{0:T(128)} %bitcast.first_column, s32[64,32]{1,0:T(8,128)} %bitcast.85, bf16[512,128]{1,0:T(8,128)(2,1)} %get-tuple-element.114.refs_0_, bf16[512,128]{1,0:T(8,128)(2,1)} %copy-done.30, ...), custom_call_target="tpu_custom_call" | custom-call | tf_op jit(solution)/shard_map/update/pallas_call | solution.py:416
  395.1 2.9 collective-permute-start.60
  398.8 4.9 %collective-permute-start.58 = (f32[32]{0:T(128)S(1)}, f32[32]{0:T(128)S(1)}, u32[]{:S(2)}, u32[]{:S(2)}) collective-permute-start(f32[32]{0:T(128)S(1)} %select_reduce_fusion.1), channel_id=1, source_target_pairs={{0,5},{1,4},{2,7},{3,6},{4,1},{5,0},{6,3},{7,2},{8,13},{9,12},{10,... | collective-permute-start | bytes 392 | tf_op jit(solution)/shard_map/ppermute | solution.py:447
  408.1 1.9 collective-permute-done.55
  411.8 4.0 fusion
  (181 shorter events, 50.9 us)
Async XLA Ops:
  3.4 26.3 %collective-permute-start.9 = (bf16[4,64,2048]{2,1,0:T(8,128)(2,1)}, bf16[4,64,2048]{2,1,0:T(8,128)(2,1)S(1)}, u32[]{:S(2)}, u32[]{:S(2)}) collective-permute-start(bf16[4,64,2048]{2,1,0:T(8,128)(2,1)} %get-tuple-element.96), channel_id=1, source_target_pairs={{0,8},{8,0},{16,24},{24,16},{1,9},{9,1},{17,25},{25,17},{2,10},{10... | collective-permute-start | bytes 3145736 | tf_op jit(solution)/shard_map/ppermute | solution.py:273
  6.3 24.6 %collective-permute-start.10 = (bf16[4,64,2048]{2,1,0:T(8,128)(2,1)S(1)}, bf16[4,64,2048]{2,1,0:T(8,128)(2,1)S(1)}, u32[]{:S(2)}, u32[]{:S(2)}) collective-permute-start(bf16[4,64,2048]{2,1,0:T(8,128)(2,1)S(1)} %get-tuple-element.95), channel_id=1, source_target_pairs={{0,16},{8,24},{16,0},{24,8},{1,17},{9,25},{17,1},{25,9},{2,18},{10... | collective-permute-start | bytes 3145736 | tf_op jit(solution)/shard_map/ppermute | solution.py:273
  31.0 74.4 %copy-start = (bf16[4,64,2048]{2,1,0:T(8,128)(2,1)}, bf16[4,64,2048]{2,1,0:T(8,128)(2,1)S(1)}, u32[]{:S(2)}) copy-start(bf16[4,64,2048]{2,1,0:T(8,128)(2,1)S(1)} %collective-permute-done.10.refs_5_.refs_8_.refs_6_.refs_12_) | copy-start | bytes 3145732
  35.0 34.3 %collective-permute-start.11 = (bf16[4,64,2048]{2,1,0:T(8,128)(2,1)}, bf16[4,64,2048]{2,1,0:T(8,128)(2,1)S(1)}, u32[]{:S(2)}, u32[]{:S(2)}) collective-permute-start(bf16[4,64,2048]{2,1,0:T(8,128)(2,1)} %get-tuple-element.93), channel_id=1, source_target_pairs={{0,8},{8,0},{16,24},{24,16},{1,9},{9,1},{17,25},{25,17},{2,10},{10... | collective-permute-start | bytes 3145736 | tf_op jit(solution)/shard_map/ppermute | solution.py:273
  35.5 55.0 %collective-permute-start.13 = (bf16[8,64,2048]{2,1,0:T(8,128)(2,1)}, bf16[8,64,2048]{2,1,0:T(8,128)(2,1)}, u32[]{:S(2)}, u32[]{:S(2)}) collective-permute-start(bf16[8,64,2048]{2,1,0:T(8,128)(2,1)} %bitcast.24.refs_1_.refs_4_.refs_2_.refs_8_.refs_16_), channel_id=1, source_target_pairs={{0,1},{1,0},{2,3},{3,2},{4,5},{5,4},{6,7},{7,6},{8,9},{9,8},{10,11... | collective-permute-start | bytes 6291464 | tf_op jit(solution)/shard_map/ppermute | solution.py:279
  35.5 33.9 %collective-permute-start.12 = (bf16[4,64,2048]{2,1,0:T(8,128)(2,1)}, bf16[4,64,2048]{2,1,0:T(8,128)(2,1)}, u32[]{:S(2)}, u32[]{:S(2)}) collective-permute-start(bf16[4,64,2048]{2,1,0:T(8,128)(2,1)} %get-tuple-element.90), channel_id=1, source_target_pairs={{0,16},{8,24},{16,0},{24,8},{1,17},{9,25},{17,1},{25,9},{2,18},{10... | collective-permute-start | bytes 3145736 | tf_op jit(solution)/shard_map/ppermute | solution.py:273
  37.2 68.2 %copy-start.29 = (s32[1,64,32]{2,1,0:T(8,128)}, s32[1,64,32]{2,1,0:T(8,128)S(1)}, u32[]{:S(2)}) copy-start(s32[1,64,32]{2,1,0:T(8,128)S(1)} %copy.29) | copy-start | bytes 24580
  37.2 25.5 %collective-permute-start.1 = (s32[64,32]{1,0:T(8,128)S(1)}, s32[64,32]{1,0:T(8,128)S(1)}, u32[]{:S(2)}, u32[]{:S(2)}) collective-permute-start(s32[64,32]{1,0:T(8,128)S(1)} %bitcast.82), channel_id=1, source_target_pairs={{0,16},{8,24},{16,0},{24,8},{1,17},{9,25},{17,1},{25,9},{2,18},{10... | collective-permute-start | bytes 24584 | tf_op jit(solution)/shard_map/ppermute | solution.py:273
  37.7 26.6 %collective-permute-start.2 = (s32[64,32]{1,0:T(8,128)S(1)}, s32[64,32]{1,0:T(8,128)S(1)}, u32[]{:S(2)}, u32[]{:S(2)}) collective-permute-start(s32[64,32]{1,0:T(8,128)S(1)} %bitcast.83), channel_id=1, source_target_pairs={{0,24},{8,16},{16,8},{24,0},{1,25},{9,17},{17,9},{25,1},{2,26},{10... | collective-permute-start | bytes 24584 | tf_op jit(solution)/shard_map/ppermute | solution.py:273
  62.7 3.9 collective-permute-start
  64.4 13.1 %collective-permute-start.6 = (bf16[32,4096]{1,0:T(8,128)(2,1)}, bf16[32,4096]{1,0:T(8,128)(2,1)}, u32[]{:S(2)}, u32[]{:S(2)}) collective-permute-start(bf16[32,4096]{1,0:T(8,128)(2,1)} %get-tuple-element.101), channel_id=1, source_target_pairs={{0,2},{1,3},{2,0},{3,1},{4,6},{5,7},{6,4},{7,5},{8,10},{9,11},{10,... | collective-permute-start | bytes 786440 | tf_op jit(solution)/shard_map/ppermute | solution.py:276
  66.6 20.6 %collective-permute-start.7 = (bf16[32,4096]{1,0:T(8,128)(2,1)}, bf16[32,4096]{1,0:T(8,128)(2,1)}, u32[]{:S(2)}, u32[]{:S(2)}) collective-permute-start(bf16[32,4096]{1,0:T(8,128)(2,1)} %get-tuple-element.101), channel_id=1, source_target_pairs={{0,4},{1,5},{2,6},{3,7},{4,0},{5,1},{6,2},{7,3},{8,12},{9,13},{10,... | collective-permute-start | bytes 786440 | tf_op jit(solution)/shard_map/ppermute | solution.py:276
  69.4 21.7 %collective-permute-start.14 = (bf16[4,64,2048]{2,1,0:T(8,128)(2,1)S(1)}, bf16[4,64,2048]{2,1,0:T(8,128)(2,1)S(1)}, u32[]{:S(2)}, u32[]{:S(2)}) collective-permute-start(bf16[4,64,2048]{2,1,0:T(8,128)(2,1)S(1)} %collective-permute-done.9.refs_2_.refs_5_.refs_3_.refs_9_), channel_id=1, source_target_pairs={{0,1},{1,0},{2,3},{3,2},{4,5},{5,4},{6,7},{7,6},{8,9},{9,8},{10,11... | collective-permute-start | bytes 3145736 | tf_op jit(solution)/shard_map/ppermute | solution.py:279
  69.5 21.1 %collective-permute-start.8 = (bf16[32,4096]{1,0:T(8,128)(2,1)}, bf16[32,4096]{1,0:T(8,128)(2,1)S(1)}, u32[]{:S(2)}, u32[]{:S(2)}) collective-permute-start(bf16[32,4096]{1,0:T(8,128)(2,1)} %get-tuple-element.101), channel_id=1, source_target_pairs={{0,6},{1,7},{2,4},{3,5},{4,2},{5,3},{6,0},{7,1},{8,14},{9,15},{10,... | collective-permute-start | bytes 786440 | tf_op jit(solution)/shard_map/ppermute | solution.py:276
  77.4 23.9 %collective-permute-start.21 = (bf16[4,64,2048]{2,1,0:T(8,128)(2,1)}, bf16[4,64,2048]{2,1,0:T(8,128)(2,1)}, u32[]{:S(2)}, u32[]{:S(2)}) collective-permute-start(bf16[4,64,2048]{2,1,0:T(8,128)(2,1)} %get-tuple-element.43), channel_id=1, source_target_pairs={{0,8},{8,0},{16,24},{24,16},{1,9},{9,1},{17,25},{25,17},{2,10},{10... | collective-permute-start | bytes 3145736 | tf_op jit(solution)/shard_map/ppermute | solution.py:273
  87.3 15.1 %collective-permute-start.22 = (bf16[4,64,2048]{2,1,0:T(8,128)(2,1)}, bf16[4,64,2048]{2,1,0:T(8,128)(2,1)}, u32[]{:S(2)}, u32[]{:S(2)}) collective-permute-start(bf16[4,64,2048]{2,1,0:T(8,128)(2,1)} %get-tuple-element.44), channel_id=1, source_target_pairs={{0,16},{8,24},{16,0},{24,8},{1,17},{9,25},{17,1},{25,9},{2,18},{10... | collective-permute-start | bytes 3145736 | tf_op jit(solution)/shard_map/ppermute | solution.py:273
  90.5 14.8 %collective-permute-start.16 = (bf16[4,64,2048]{2,1,0:T(8,128)(2,1)S(1)}, bf16[4,64,2048]{2,1,0:T(8,128)(2,1)}, u32[]{:S(2)}, u32[]{:S(2)}) collective-permute-start(bf16[4,64,2048]{2,1,0:T(8,128)(2,1)S(1)} %collective-permute-done.10.refs_5_.refs_8_.refs_6_.refs_12_), channel_id=1, source_target_pairs={{0,1},{1,0},{2,3},{3,2},{4,5},{5,4},{6,7},{7,6},{8,9},{9,8},{10,11... | collective-permute-start | bytes 3145736 | tf_op jit(solution)/shard_map/ppermute | solution.py:279
  90.5 14.8 %collective-permute-start.15 = (bf16[4,64,2048]{2,1,0:T(8,128)(2,1)S(1)}, bf16[4,64,2048]{2,1,0:T(8,128)(2,1)}, u32[]{:S(2)}, u32[]{:S(2)}) collective-permute-start(bf16[4,64,2048]{2,1,0:T(8,128)(2,1)S(1)} %collective-permute-done.11.refs_3_.refs_4_.refs_6_.refs_10_), channel_id=1, source_target_pairs={{0,1},{1,0},{2,3},{3,2},{4,5},{5,4},{6,7},{7,6},{8,9},{9,8},{10,11... | collective-permute-start | bytes 3145736 | tf_op jit(solution)/shard_map/ppermute | solution.py:279
  92.0 13.3 %collective-permute-start.17 = (bf16[4,64,2048]{2,1,0:T(8,128)(2,1)}, bf16[4,64,2048]{2,1,0:T(8,128)(2,1)}, u32[]{:S(2)}, u32[]{:S(2)}) collective-permute-start(bf16[4,64,2048]{2,1,0:T(8,128)(2,1)} %collective-permute-done.12.refs_6_.refs_7_.refs_9_.refs_13_), channel_id=1, source_target_pairs={{0,1},{1,0},{2,3},{3,2},{4,5},{5,4},{6,7},{7,6},{8,9},{9,8},{10,11... | collective-permute-start | bytes 3145736 | tf_op jit(solution)/shard_map/ppermute | solution.py:279
  101.3 43.3 %collective-permute-start.23 = (bf16[4,64,2048]{2,1,0:T(8,128)(2,1)}, bf16[4,64,2048]{2,1,0:T(8,128)(2,1)}, u32[]{:S(2)}, u32[]{:S(2)}) collective-permute-start(bf16[4,64,2048]{2,1,0:T(8,128)(2,1)} %collective-permute-done.21.refs_7_.refs_5_.refs_11_), channel_id=1, source_target_pairs={{0,1},{1,0},{2,3},{3,2},{4,5},{5,4},{6,7},{7,6},{8,9},{9,8},{10,11... | collective-permute-start | bytes 3145736 | tf_op jit(solution)/shard_map/ppermute | solution.py:279
  102.4 42.3 %collective-permute-start.24 = (bf16[4,64,2048]{2,1,0:T(8,128)(2,1)}, bf16[4,64,2048]{2,1,0:T(8,128)(2,1)}, u32[]{:S(2)}, u32[]{:S(2)}) collective-permute-start(bf16[4,64,2048]{2,1,0:T(8,128)(2,1)} %collective-permute-done.22.refs_10_.refs_8_.refs_14_), channel_id=1, source_target_pairs={{0,1},{1,0},{2,3},{3,2},{4,5},{5,4},{6,7},{7,6},{8,9},{9,8},{10,11... | collective-permute-start | bytes 3145736 | tf_op jit(solution)/shard_map/ppermute | solution.py:279
  114.9 20.1 %collective-permute-start.18 = (bf16[1024,128]{1,0:T(8,128)(2,1)S(1)}, bf16[1024,128]{1,0:T(8,128)(2,1)S(1)}, u32[]{:S(2)}, u32[]{:S(2)}) collective-permute-start(bf16[1024,128]{1,0:T(8,128)(2,1)S(1)} %get-tuple-element.42.refs_0_.refs_1_), channel_id=1, source_target_pairs={{0,2},{1,3},{2,0},{3,1},{4,6},{5,7},{6,4},{7,5},{8,10},{9,11},{10,... | collective-permute-start | bytes 786440 | tf_op jit(solution)/shard_map/ppermute | solution.py:276
  122.8 21.9 %collective-permute-start.19 = (bf16[1024,128]{1,0:T(8,128)(2,1)S(1)}, bf16[1024,128]{1,0:T(8,128)(2,1)S(1)}, u32[]{:S(2)}, u32[]{:S(2)}) collective-permute-start(bf16[1024,128]{1,0:T(8,128)(2,1)S(1)} %get-tuple-element.42.refs_0_.refs_1_), channel_id=1, source_target_pairs={{0,4},{1,5},{2,6},{3,7},{4,0},{5,1},{6,2},{7,3},{8,12},{9,13},{10,... | collective-permute-start | bytes 786440 | tf_op jit(solution)/shard_map/ppermute | solution.py:276
  126.3 18.4 %collective-permute-start.20 = (bf16[1024,128]{1,0:T(8,128)(2,1)S(1)}, bf16[1024,128]{1,0:T(8,128)(2,1)S(1)}, u32[]{:S(2)}, u32[]{:S(2)}) collective-permute-start(bf16[1024,128]{1,0:T(8,128)(2,1)S(1)} %get-tuple-element.42.refs_0_.refs_1_), channel_id=1, source_target_pairs={{0,6},{1,7},{2,4},{3,5},{4,2},{5,3},{6,0},{7,1},{8,14},{9,15},{10,... | collective-permute-start | bytes 786440 | tf_op jit(solution)/shard_map/ppermute | solution.py:276
  135.0 27.2 %collective-permute-start.3 = (bf16[32,1024]{1,0:T(8,128)(2,1)S(1)}, bf16[32,1024]{1,0:T(8,128)(2,1)S(1)}, u32[]{:S(2)}, u32[]{:S(2)}) collective-permute-start(bf16[32,1024]{1,0:T(8,128)(2,1)S(1)} %get-tuple-element.104), channel_id=1, source_target_pairs={{0,2},{1,3},{2,0},{3,1},{4,6},{5,7},{6,4},{7,5},{8,10},{9,11},{10,... | collective-permute-start | bytes 196616 | tf_op jit(solution)/shard_map/ppermute | solution.py:276
  152.1 16.7 %collective-permute-start.25 = (bf16[1024,128]{1,0:T(8,128)(2,1)S(1)}, bf16[1024,128]{1,0:T(8,128)(2,1)S(1)}, u32[]{:S(2)}, u32[]{:S(2)}) collective-permute-start(bf16[1024,128]{1,0:T(8,128)(2,1)S(1)} %get-tuple-element.45.refs_0_.refs_1_), channel_id=1, source_target_pairs={{0,2},{1,3},{2,0},{3,1},{4,6},{5,7},{6,4},{7,5},{8,10},{9,11},{10,... | collective-permute-start | bytes 786440 | tf_op jit(solution)/shard_map/ppermute | solution.py:276
  157.9 24.2 %collective-permute-start.26 = (bf16[1024,128]{1,0:T(8,128)(2,1)S(1)}, bf16[1024,128]{1,0:T(8,128)(2,1)S(1)}, u32[]{:S(2)}, u32[]{:S(2)}) collective-permute-start(bf16[1024,128]{1,0:T(8,128)(2,1)S(1)} %get-tuple-element.45.refs_0_.refs_1_), channel_id=1, source_target_pairs={{0,4},{1,5},{2,6},{3,7},{4,0},{5,1},{6,2},{7,3},{8,12},{9,13},{10,... | collective-permute-start | bytes 786440 | tf_op jit(solution)/shard_map/ppermute | solution.py:276
  158.8 23.3 %collective-permute-start.27 = (bf16[1024,128]{1,0:T(8,128)(2,1)S(1)}, bf16[1024,128]{1,0:T(8,128)(2,1)S(1)}, u32[]{:S(2)}, u32[]{:S(2)}) collective-permute-start(bf16[1024,128]{1,0:T(8,128)(2,1)S(1)} %get-tuple-element.45.refs_0_.refs_1_), channel_id=1, source_target_pairs={{0,6},{1,7},{2,4},{3,5},{4,2},{5,3},{6,0},{7,1},{8,14},{9,15},{10,... | collective-permute-start | bytes 786440 | tf_op jit(solution)/shard_map/ppermute | solution.py:276
  160.2 38.2 %collective-permute-start.4 = (bf16[32,1024]{1,0:T(8,128)(2,1)S(1)}, bf16[32,1024]{1,0:T(8,128)(2,1)S(1)}, u32[]{:S(2)}, u32[]{:S(2)}) collective-permute-start(bf16[32,1024]{1,0:T(8,128)(2,1)S(1)} %get-tuple-element.106), channel_id=1, source_target_pairs={{0,4},{1,5},{2,6},{3,7},{4,0},{5,1},{6,2},{7,3},{8,12},{9,13},{10,... | collective-permute-start | bytes 196616 | tf_op jit(solution)/shard_map/ppermute | solution.py:276
  162.3 36.2 %collective-permute-start.5 = (bf16[32,1024]{1,0:T(8,128)(2,1)S(1)}, bf16[32,1024]{1,0:T(8,128)(2,1)S(1)}, u32[]{:S(2)}, u32[]{:S(2)}) collective-permute-start(bf16[32,1024]{1,0:T(8,128)(2,1)S(1)} %get-tuple-element.103), channel_id=1, source_target_pairs={{0,6},{1,7},{2,4},{3,5},{4,2},{5,3},{6,0},{7,1},{8,14},{9,15},{10,... | collective-permute-start | bytes 196616 | tf_op jit(solution)/shard_map/ppermute | solution.py:276
  190.0 13.1 %collective-permute-start.28 = (bf16[1024,128]{1,0:T(8,128)(2,1)S(1)}, bf16[1024,128]{1,0:T(8,128)(2,1)S(1)}, u32[]{:S(2)}, u32[]{:S(2)}) collective-permute-start(bf16[1024,128]{1,0:T(8,128)(2,1)S(1)} %get-tuple-element.46.refs_0_.refs_1_), channel_id=1, source_target_pairs={{0,2},{1,3},{2,0},{3,1},{4,6},{5,7},{6,4},{7,5},{8,10},{9,11},{10,... | collective-permute-start | bytes 786440 | tf_op jit(solution)/shard_map/ppermute | solution.py:276
  196.1 20.2 %collective-permute-start.29 = (bf16[1024,128]{1,0:T(8,128)(2,1)S(1)}, bf16[1024,128]{1,0:T(8,128)(2,1)}, u32[]{:S(2)}, u32[]{:S(2)}) collective-permute-start(bf16[1024,128]{1,0:T(8,128)(2,1)S(1)} %get-tuple-element.46.refs_0_.refs_1_), channel_id=1, source_target_pairs={{0,4},{1,5},{2,6},{3,7},{4,0},{5,1},{6,2},{7,3},{8,12},{9,13},{10,... | collective-permute-start | bytes 786440 | tf_op jit(solution)/shard_map/ppermute | solution.py:276
  197.0 19.3 %collective-permute-start.30 = (bf16[1024,128]{1,0:T(8,128)(2,1)S(1)}, bf16[1024,128]{1,0:T(8,128)(2,1)}, u32[]{:S(2)}, u32[]{:S(2)}) collective-permute-start(bf16[1024,128]{1,0:T(8,128)(2,1)S(1)} %get-tuple-element.46.refs_0_.refs_1_), channel_id=1, source_target_pairs={{0,6},{1,7},{2,4},{3,5},{4,2},{5,3},{6,0},{7,1},{8,14},{9,15},{10,... | collective-permute-start | bytes 786440 | tf_op jit(solution)/shard_map/ppermute | solution.py:276
  231.2 10.4 %collective-permute-start.31 = (bf16[1040,128]{1,0:T(8,128)(2,1)S(1)}, bf16[1040,128]{1,0:T(8,128)(2,1)S(1)}, u32[]{:S(2)}, u32[]{:S(2)}) collective-permute-start(bf16[1040,128]{1,0:T(8,128)(2,1)S(1)} %get-tuple-element.50), channel_id=1, source_target_pairs={{0,2},{1,3},{2,0},{3,1},{4,6},{5,7},{6,4},{7,5},{8,10},{9,11},{10,... | collective-permute-start | bytes 798728 | tf_op jit(solution)/shard_map/ppermute | solution.py:276
  234.6 20.2 %collective-permute-start.32 = (bf16[1040,128]{1,0:T(8,128)(2,1)S(1)}, bf16[1040,128]{1,0:T(8,128)(2,1)S(1)}, u32[]{:S(2)}, u32[]{:S(2)}) collective-permute-start(bf16[1040,128]{1,0:T(8,128)(2,1)S(1)} %get-tuple-element.51), channel_id=1, source_target_pairs={{0,4},{1,5},{2,6},{3,7},{4,0},{5,1},{6,2},{7,3},{8,12},{9,13},{10,... | collective-permute-start | bytes 798728 | tf_op jit(solution)/shard_map/ppermute | solution.py:276
  235.6 19.3 %collective-permute-start.33 = (bf16[1040,128]{1,0:T(8,128)(2,1)S(1)}, bf16[1040,128]{1,0:T(8,128)(2,1)S(1)}, u32[]{:S(2)}, u32[]{:S(2)}) collective-permute-start(bf16[1040,128]{1,0:T(8,128)(2,1)S(1)} %get-tuple-element.52), channel_id=1, source_target_pairs={{0,6},{1,7},{2,4},{3,5},{4,2},{5,3},{6,0},{7,1},{8,14},{9,15},{10,... | collective-permute-start | bytes 798728 | tf_op jit(solution)/shard_map/ppermute | solution.py:276
  263.4 11.1 %collective-permute-start.34 = (bf16[1040,128]{1,0:T(8,128)(2,1)S(1)}, bf16[1040,128]{1,0:T(8,128)(2,1)S(1)}, u32[]{:S(2)}, u32[]{:S(2)}) collective-permute-start(bf16[1040,128]{1,0:T(8,128)(2,1)S(1)} %get-tuple-element.57), channel_id=1, source_target_pairs={{0,2},{1,3},{2,0},{3,1},{4,6},{5,7},{6,4},{7,5},{8,10},{9,11},{10,... | collective-permute-start | bytes 798728 | tf_op jit(solution)/shard_map/ppermute | solution.py:276
  269.2 64.5 %collective-permute-start.47 = (bf16[4096,128]{1,0:T(8,128)(2,1)}, bf16[4096,128]{1,0:T(8,128)(2,1)}, u32[]{:S(2)}, u32[]{:S(2)}) collective-permute-start(bf16[4096,128]{1,0:T(8,128)(2,1)} %get-tuple-element.87), channel_id=1, source_target_pairs={{0,8},{8,0},{16,24},{24,16},{1,9},{9,1},{17,25},{25,17},{2,10},{10... | collective-permute-start | bytes 3145736 | tf_op jit(solution)/shard_map/ppermute | solution.py:273
  271.3 62.3 %collective-permute-start.48 = (bf16[4096,128]{1,0:T(8,128)(2,1)}, bf16[4096,128]{1,0:T(8,128)(2,1)}, u32[]{:S(2)}, u32[]{:S(2)}) collective-permute-start(bf16[4096,128]{1,0:T(8,128)(2,1)} %get-tuple-element.86), channel_id=1, source_target_pairs={{0,16},{8,24},{16,0},{24,8},{1,17},{9,25},{17,1},{25,9},{2,18},{10... | collective-permute-start | bytes 3145736 | tf_op jit(solution)/shard_map/ppermute | solution.py:273
  272.1 62.1 %collective-permute-start.49 = (bf16[4096,128]{1,0:T(8,128)(2,1)}, bf16[4096,128]{1,0:T(8,128)(2,1)}, u32[]{:S(2)}, u32[]{:S(2)}) collective-permute-start(bf16[4096,128]{1,0:T(8,128)(2,1)} %get-tuple-element.85), channel_id=1, source_target_pairs={{0,24},{8,16},{16,8},{24,0},{1,25},{9,17},{17,9},{25,1},{2,26},{10... | collective-permute-start | bytes 3145736 | tf_op jit(solution)/shard_map/ppermute | solution.py:273
  272.8 19.0 %collective-permute-start.35 = (bf16[1040,128]{1,0:T(8,128)(2,1)S(1)}, bf16[1040,128]{1,0:T(8,128)(2,1)S(1)}, u32[]{:S(2)}, u32[]{:S(2)}) collective-permute-start(bf16[1040,128]{1,0:T(8,128)(2,1)S(1)} %get-tuple-element.58), channel_id=1, source_target_pairs={{0,4},{1,5},{2,6},{3,7},{4,0},{5,1},{6,2},{7,3},{8,12},{9,13},{10,... | collective-permute-start | bytes 798728 | tf_op jit(solution)/shard_map/ppermute | solution.py:276
  274.5 17.3 %collective-permute-start.36 = (bf16[1040,128]{1,0:T(8,128)(2,1)S(1)}, bf16[1040,128]{1,0:T(8,128)(2,1)S(1)}, u32[]{:S(2)}, u32[]{:S(2)}) collective-permute-start(bf16[1040,128]{1,0:T(8,128)(2,1)S(1)} %get-tuple-element.59), channel_id=1, source_target_pairs={{0,6},{1,7},{2,4},{3,5},{4,2},{5,3},{6,0},{7,1},{8,14},{9,15},{10,... | collective-permute-start | bytes 798728 | tf_op jit(solution)/shard_map/ppermute | solution.py:276
  291.9 42.3 %copy-start.17 = (bf16[1024,128]{1,0:T(8,128)(2,1)S(1)}, bf16[1024,128]{1,0:T(8,128)(2,1)}, u32[]{:S(2)}) copy-start(bf16[1024,128]{1,0:T(8,128)(2,1)} %copy-done.16) | copy-start | bytes 786436
  302.9 17.2 %collective-permute-start.37 = (bf16[1040,128]{1,0:T(8,128)(2,1)S(1)}, bf16[1040,128]{1,0:T(8,128)(2,1)S(1)}, u32[]{:S(2)}, u32[]{:S(2)}) collective-permute-start(bf16[1040,128]{1,0:T(8,128)(2,1)S(1)} %get-tuple-element.64), channel_id=1, source_target_pairs={{0,2},{1,3},{2,0},{3,1},{4,6},{5,7},{6,4},{7,5},{8,10},{9,11},{10,... | collective-permute-start | bytes 798728 | tf_op jit(solution)/shard_map/ppermute | solution.py:276
  308.0 13.1 %collective-permute-start.38 = (bf16[1040,128]{1,0:T(8,128)(2,1)}, bf16[1040,128]{1,0:T(8,128)(2,1)S(1)}, u32[]{:S(2)}, u32[]{:S(2)}) collective-permute-start(bf16[1040,128]{1,0:T(8,128)(2,1)} %get-tuple-element.65), channel_id=1, source_target_pairs={{0,4},{1,5},{2,6},{3,7},{4,0},{5,1},{6,2},{7,3},{8,12},{9,13},{10,... | collective-permute-start | bytes 798728 | tf_op jit(solution)/shard_map/ppermute | solution.py:276
  320.0 9.6 %collective-permute-start.39 = (bf16[1040,128]{1,0:T(8,128)(2,1)}, bf16[1040,128]{1,0:T(8,128)(2,1)S(1)}, u32[]{:S(2)}, u32[]{:S(2)}) collective-permute-start(bf16[1040,128]{1,0:T(8,128)(2,1)} %get-tuple-element.66), channel_id=1, source_target_pairs={{0,6},{1,7},{2,4},{3,5},{4,2},{5,3},{6,0},{7,1},{8,14},{9,15},{10,... | collective-permute-start | bytes 798728 | tf_op jit(solution)/shard_map/ppermute | solution.py:276
  321.1 50.4 %collective-permute-start.50 = (bf16[4096,128]{1,0:T(8,128)(2,1)}, bf16[4096,128]{1,0:T(8,128)(2,1)}, u32[]{:S(2)}, u32[]{:S(2)}) collective-permute-start(bf16[4096,128]{1,0:T(8,128)(2,1)} %get-tuple-element.88.refs_8_), channel_id=1, source_target_pairs={{0,1},{1,0},{2,3},{3,2},{4,5},{5,4},{6,7},{7,6},{8,9},{9,8},{10,11... | collective-permute-start | bytes 3145736 | tf_op jit(solution)/shard_map/ppermute | solution.py:279
  333.6 37.9 %collective-permute-start.51 = (bf16[4096,128]{1,0:T(8,128)(2,1)}, bf16[4096,128]{1,0:T(8,128)(2,1)S(1)}, u32[]{:S(2)}, u32[]{:S(2)}) collective-permute-start(bf16[4096,128]{1,0:T(8,128)(2,1)} %collective-permute-done.47.refs_9_), channel_id=1, source_target_pairs={{0,1},{1,0},{2,3},{3,2},{4,5},{5,4},{6,7},{7,6},{8,9},{9,8},{10,11... | collective-permute-start | bytes 3145736 | tf_op jit(solution)/shard_map/ppermute | solution.py:279
  333.6 37.9 %collective-permute-start.52 = (bf16[4096,128]{1,0:T(8,128)(2,1)}, bf16[4096,128]{1,0:T(8,128)(2,1)}, u32[]{:S(2)}, u32[]{:S(2)}) collective-permute-start(bf16[4096,128]{1,0:T(8,128)(2,1)} %collective-permute-done.48.refs_10_), channel_id=1, source_target_pairs={{0,1},{1,0},{2,3},{3,2},{4,5},{5,4},{6,7},{7,6},{8,9},{9,8},{10,11... | collective-permute-start | bytes 3145736 | tf_op jit(solution)/shard_map/ppermute | solution.py:279
  334.1 37.4 %collective-permute-start.53 = (bf16[4096,128]{1,0:T(8,128)(2,1)}, bf16[4096,128]{1,0:T(8,128)(2,1)}, u32[]{:S(2)}, u32[]{:S(2)}) collective-permute-start(bf16[4096,128]{1,0:T(8,128)(2,1)} %collective-permute-done.49.refs_11_), channel_id=1, source_target_pairs={{0,1},{1,0},{2,3},{3,2},{4,5},{5,4},{6,7},{7,6},{8,9},{9,8},{10,11... | collective-permute-start | bytes 3145736 | tf_op jit(solution)/shard_map/ppermute | solution.py:279
  335.4 6.3 %collective-permute-start.40 = (bf16[512,128]{1,0:T(8,128)(2,1)S(1)}, bf16[512,128]{1,0:T(8,128)(2,1)S(1)}, u32[]{:S(2)}, u32[]{:S(2)}) collective-permute-start(bf16[512,128]{1,0:T(8,128)(2,1)S(1)} %get-tuple-element.112), channel_id=1, source_target_pairs={{0,8},{1,9},{2,10},{3,11},{4,12},{5,13},{6,14},{7,15},{8,0},{9,1},... | collective-permute-start | bytes 393224 | tf_op jit(solution)/shard_map/ppermute | solution.py:398
  341.7 5.3 %collective-permute-start.41 = (bf16[512,128]{1,0:T(8,128)(2,1)S(1)}, bf16[512,128]{1,0:T(8,128)(2,1)S(1)}, u32[]{:S(2)}, u32[]{:S(2)}) collective-permute-start(bf16[512,128]{1,0:T(8,128)(2,1)S(1)} %get-tuple-element.110), channel_id=1, source_target_pairs={{0,16},{1,17},{2,18},{3,19},{4,20},{5,21},{6,22},{7,23},{8,24},{9,... | collective-permute-start | bytes 393224 | tf_op jit(solution)/shard_map/ppermute | solution.py:398
  347.0 5.9 %collective-permute-start.42 = (bf16[512,128]{1,0:T(8,128)(2,1)S(1)}, bf16[512,128]{1,0:T(8,128)(2,1)S(1)}, u32[]{:S(2)}, u32[]{:S(2)}) collective-permute-start(bf16[512,128]{1,0:T(8,128)(2,1)S(1)} %get-tuple-element.108), channel_id=1, source_target_pairs={{0,24},{1,25},{2,26},{3,27},{4,28},{5,29},{6,30},{7,31},{8,16},{9,... | collective-permute-start | bytes 393224 | tf_op jit(solution)/shard_map/ppermute | solution.py:398
  352.8 1.3 collective-permute-start.43
  354.2 5.5 %collective-permute-start.44 = (bf16[512,128]{1,0:T(8,128)(2,1)S(1)}, bf16[512,128]{1,0:T(8,128)(2,1)S(1)}, u32[]{:S(2)}, u32[]{:S(2)}) collective-permute-start(bf16[512,128]{1,0:T(8,128)(2,1)S(1)} %get-tuple-element.111), channel_id=1, source_target_pairs={{0,9},{1,8},{2,11},{3,10},{4,13},{5,12},{6,15},{7,14},{8,1},{9,0},... | collective-permute-start | bytes 393224 | tf_op jit(solution)/shard_map/ppermute | solution.py:398
  359.7 5.5 %collective-permute-start.45 = (bf16[512,128]{1,0:T(8,128)(2,1)S(1)}, bf16[512,128]{1,0:T(8,128)(2,1)S(1)}, u32[]{:S(2)}, u32[]{:S(2)}) collective-permute-start(bf16[512,128]{1,0:T(8,128)(2,1)S(1)} %get-tuple-element.109), channel_id=1, source_target_pairs={{0,17},{1,16},{2,19},{3,18},{4,21},{5,20},{6,23},{7,22},{8,25},{9,... | collective-permute-start | bytes 393224 | tf_op jit(solution)/shard_map/ppermute | solution.py:398
  365.1 6.4 %collective-permute-start.46 = (bf16[512,128]{1,0:T(8,128)(2,1)S(1)}, bf16[512,128]{1,0:T(8,128)(2,1)S(1)}, u32[]{:S(2)}, u32[]{:S(2)}) collective-permute-start(bf16[512,128]{1,0:T(8,128)(2,1)S(1)} %get-tuple-element.107), channel_id=1, source_target_pairs={{0,25},{1,24},{2,27},{3,26},{4,29},{5,28},{6,31},{7,30},{8,17},{9,... | collective-permute-start | bytes 393224 | tf_op jit(solution)/shard_map/ppermute | solution.py:398
  395.1 11.3 %collective-permute-start.60 = (f32[32]{0:T(128)S(1)}, f32[32]{0:T(128)S(1)}, u32[]{:S(2)}, u32[]{:S(2)}) collective-permute-start(f32[32]{0:T(128)S(1)} %select_reduce_fusion.1), channel_id=1, source_target_pairs={{0,7},{1,6},{2,5},{3,4},{4,3},{5,2},{6,1},{7,0},{8,15},{9,14},{10,... | collective-permute-start | bytes 392 | tf_op jit(solution)/shard_map/ppermute | solution.py:447
  398.0 9.0 %collective-permute-start.59 = (f32[32]{0:T(128)S(1)}, f32[32]{0:T(128)S(1)}, u32[]{:S(2)}, u32[]{:S(2)}) collective-permute-start(f32[32]{0:T(128)S(1)} %select_reduce_fusion.1), channel_id=1, source_target_pairs={{0,6},{1,7},{2,4},{3,5},{4,2},{5,3},{6,0},{7,1},{8,14},{9,15},{10,... | collective-permute-start | bytes 392 | tf_op jit(solution)/shard_map/ppermute | solution.py:447
  398.8 8.4 %collective-permute-start.58 = (f32[32]{0:T(128)S(1)}, f32[32]{0:T(128)S(1)}, u32[]{:S(2)}, u32[]{:S(2)}) collective-permute-start(f32[32]{0:T(128)S(1)} %select_reduce_fusion.1), channel_id=1, source_target_pairs={{0,5},{1,4},{2,7},{3,6},{4,1},{5,0},{6,3},{7,2},{8,13},{9,12},{10,... | collective-permute-start | bytes 392 | tf_op jit(solution)/shard_map/ppermute | solution.py:447
  403.7 4.4 %collective-permute-start.57 = (f32[32]{0:T(128)S(1)}, f32[32]{0:T(128)S(1)}, u32[]{:S(2)}, u32[]{:S(2)}) collective-permute-start(f32[32]{0:T(128)S(1)} %select_reduce_fusion.1), channel_id=1, source_target_pairs={{0,4},{1,5},{2,6},{3,7},{4,0},{5,1},{6,2},{7,3},{8,12},{9,13},{10,... | collective-permute-start | bytes 392 | tf_op jit(solution)/shard_map/ppermute | solution.py:447
  404.0 4.1 collective-permute-start.56
  406.4 3.6 collective-permute-start.55
  407.0 3.0 collective-permute-start.54
  (35 other events, 422.5 us)

commit v2 on v1

v2 whole, which is shorter than its diff:
```python
import functools
import math

import jax
import jax.numpy as jnp
from jax import lax
from jax.experimental import pallas as pl
from jax.experimental.pallas import tpu as pltpu
from jax.sharding import PartitionSpec as P

HEAD = 128
F32 = jnp.float32
BF16 = jnp.bfloat16
PAD = 16
LIMIT = 60
TILE = 4
VMEM = pl.BlockSpec(memory_space=pltpu.VMEM)
SMEM = pl.BlockSpec(memory_space=pltpu.SMEM)
ANY = pl.BlockSpec(memory_space=pl.ANY)


def shrink(magnitude, threshold):
    return jnp.maximum(magnitude - threshold, 0.0) / jnp.maximum(magnitude, threshold)


HOLDS = (
    ("own own", "x1 x2", "y2 y1", "y2 x2"),
    ("x1 x2", "own own", "y3 x3", "y3 y1"),
    ("y2 y1", "y3 x3", "own own", "x1 x3"),
    ("y3 x3", "y2 y1", "x1 x2", "own own"),
)


def holders(layer):
    names = sorted({name for row in HOLDS[layer] for name in row.split()})
    names.remove("own")
    return ["own"] + names


HEADER = 128


def live_row(table, layer, column, number, shape):
    return table[HEADER + (layer * shape[0] + column) * shape[1] + number]


def pick_kernel(layer_round, height, section, own, x1, y1, x_out, y_out, sems):
    half = pl.ds(0, height)
    cases = (
        (x_out.at[half], own.at[pl.ds(height, height)], y1.at[half], 2),
        (y_out.at[half], own.at[half], x1.at[half], 1),
    )
    for number, (out, mine, received, place) in enumerate(cases):
        passes = (section[0] == place) == (layer_round == 2)

        @pl.when(passes)
        def _(out=out, received=received, number=number):
            pltpu.make_async_copy(received, out, sems.at[number]).start()

        @pl.when(jnp.logical_not(passes))
        def _(out=out, mine=mine, number=number):
            pltpu.make_async_copy(mine, out, sems.at[number]).start()

    if layer_round == 2:
        extra = pl.ds(height, PAD)
        pltpu.make_async_copy(y1.at[extra], x_out.at[extra], sems.at[2]).start()
        pltpu.make_async_copy(y1.at[extra], x_out.at[extra], sems.at[2]).wait()
    for number, (out, _, received, _) in enumerate(cases):
        pltpu.make_async_copy(received, out, sems.at[number]).wait()


def weight_copies(layer, table, refs, buffer, sems):
    names = holders(layer)
    height = buffer.shape[0] // 8
    for group in range(8):
        owner, quarter = group // 4, group % 4
        held = dict(zip(names, refs[owner * len(names) : (owner + 1) * len(names)]))
        target = buffer.at[pl.ds(group * height, height)]
        for section, row in enumerate(HOLDS[layer]):
            name = row.split()[quarter // 2]
            first = quarter if name == "own" else quarter % 2
            source = held[name].at[pl.ds(first * height, height)]

            @pl.when(table[2] == section)
            def _(source=source, target=target, group=group):
                pltpu.make_async_copy(source, target, sems.at[group]).start()

    def wait(group):
        target = buffer.at[pl.ds(group * height, height)]
        pltpu.make_async_copy(refs[0].at[pl.ds(0, height)], target, sems.at[group]).wait()

    return wait


def column_loop(scal, own_columns, body, wait):
    taken, count = max(1, 4 // own_columns), max(1, own_columns // 4)

    @pl.loop(0, 8 // taken)
    def _(turn):
        for i in range(taken):
            wait(turn * taken + i)
        for i in range(count):
            slot = turn * count + i
            local = slot ^ (scal[1] * own_columns)
            body(slot, local, scal[0] * 2 * own_columns + local)


def forward_kernel(layer, ways, last, live_shape, scal, *refs):
    whole = layer == 0
    count = 1 if whole else ways
    shards, refs = refs[:count], refs[count:]
    held = 2 * len(holders(layer))
    weight_refs, refs = refs[:held], refs[held:]
    if not whole:
        refs = refs[len(HOLDS) :]
    outs = 2 if last else 3
    outputs, refs = refs[:outs], refs[outs:]
    sends, refs = refs[: len(HOLDS)], refs[len(HOLDS) :]
    buffer, u_ref, sems, send_sem = refs
    z_ref, r_ref = outputs[:2]
    wait = weight_copies(layer, scal, weight_refs, buffer, sems)
    features, tokens = u_ref.shape
    rows = z_ref.shape[0]
    live_count = live_shape[1]
    block = buffer.shape[1] // live_count
    total = jnp.zeros((1, tokens), F32)
    for shard in shards:
        value = shard[...].astype(F32)
        total = total + jnp.sum(value * value, axis=0, keepdims=True)
    inverse = lax.rsqrt(total * (1.0 / features) + 1e-05)
    r_ref[...] = jnp.broadcast_to(inverse, r_ref.shape)
    if whole:
        u_ref[...] = (shards[0][...].astype(F32) * inverse).astype(BF16)
    else:
        for step, shard in enumerate(shards):
            u_ref[pl.ds((scal[0] ^ step) * rows, rows), :] = (
                shard[...].astype(F32) * inverse
            ).astype(BF16)
    for step, send in enumerate(sends):

        @pl.when((scal[2] ^ step) == layer)
        def _(send=send):
            pltpu.make_async_copy(u_ref, send, send_sem.at[0]).start()

    width = TILE * block
    tiles = live_count // TILE

    def picked(column_index, tile):
        return jnp.concatenate(
            [
                u_ref[
                    pl.ds(
                        live_row(scal, layer, column_index, tile * TILE + i, live_shape) * block,
                        block,
                    ),
                    :,
                ]
                for i in range(TILE)
            ],
            axis=0,
        )

    def column(slot, local, column_index):
        acc = jnp.zeros((2 * block, 2 * tokens), F32)
        at = pl.ds(slot * block, block)
        for tile in range(tiles // 2):
            other = tile + tiles // 2
            lhs = jnp.concatenate(
                [
                    buffer[at, pl.ds(tile * width, width)],
                    buffer[at, pl.ds(other * width, width)],
                ],
                axis=0,
            )
            rhs = jnp.concatenate(
                [picked(column_index, tile), picked(column_index, other)], axis=1
            )
            acc = acc + jnp.dot(lhs, rhs, preferred_element_type=F32)
        z_ref[pl.ds(local * block, block), :] = acc[:block, :tokens] + acc[block:, tokens:]

    column_loop(scal, rows // block // 2, column, wait)
    pltpu.make_async_copy(u_ref, sends[0], send_sem.at[0]).wait()
    if not last:
        own = shards[0][pl.ds(scal[0] * rows, rows), :] if whole else shards[0][...]
        pre = z_ref[...]
        outputs[2][...] = (own.astype(F32) + pre * jax.nn.sigmoid(pre)).astype(BF16)


def backward_kernel(layer, ways, live_shape, scal, *refs):
    first, last = layer == len(HOLDS) - 1, layer == 0
    if first:
        arriving_ref, refs = refs[0], refs[1:]
    else:
        older_ref, h_ref, r_ref = refs[:3]
        shares, refs = refs[3 : 3 + ways], refs[3 + ways :]
    pre_ref, refs = refs[0], refs[1:]
    if last:
        others, refs = refs[: len(HOLDS) - 1], refs[len(HOLDS) - 1 :]
        sorted_refs, (gz_ref,) = refs[:-1], refs[-1:]
    else:
        held = 2 * len(holders(layer))
        weight_refs, refs = refs[:held], refs[held:]
        gz_ref, refs = refs[0], refs[1:]
        outgoing, refs = refs[:ways], refs[ways:]
        if not first:
            g_ref, refs = refs[0], refs[1:]
        buffer, sems, du_ref = refs
        wait = weight_copies(layer, scal, weight_refs, buffer, sems)
    rows, tokens = gz_ref.shape
    if first:
        arriving = arriving_ref[...].astype(F32)
    else:
        total = shares[0][pl.ds(0, rows), :].astype(F32)
        means = shares[0][pl.ds(rows, PAD), :].astype(F32)
        for share in shares[1:]:
            total = total + share[pl.ds(0, rows), :].astype(F32)
            means = means + share[pl.ds(rows, PAD), :].astype(F32)
        mean = jnp.sum(means, axis=0, keepdims=True) * (1.0 / (rows * ways))
        inverse = r_ref[0:1, :]
        scaled = h_ref[...].astype(F32) * inverse
        arriving = (older_ref[...].astype(F32) + inverse * (total - scaled * mean)).astype(BF16)
        if not last:
            g_ref[...] = arriving
        arriving = arriving.astype(F32)
    pre = pre_ref[...]
    sigmoid = jax.nn.sigmoid(pre)
    gz = (arriving * (sigmoid * (1.0 + pre * (1.0 - sigmoid)))).astype(BF16)
    gz_ref[...] = gz
    if last:
        half = rows // 2
        for step in range(len(HOLDS)):
            for number, source in enumerate((gz_ref, *others)):

                @pl.when((scal[2] ^ step) == number)
                def _(step=step, source=source):
                    for flip in range(2):
                        sorted_refs[2 * step + flip][...] = source[
                            pl.ds((scal[1] ^ flip) * half, half), :
                        ]

        return
    share = jnp.sum(gz.astype(F32) * pre, axis=0, keepdims=True)
    high = share.astype(BF16).astype(F32)
    low = share - high
    row = lax.broadcasted_iota(jnp.int32, (PAD, tokens), 0)
    extra = jnp.where(row == 0, high, jnp.where(row == 1, low, 0.0)).astype(BF16)
    du_ref[...] = jnp.zeros_like(du_ref)
    live_count = live_shape[1]
    block = buffer.shape[1] // live_count

    width = TILE * block
    tiles = live_count // TILE

    def column(slot, local, column_index):
        gz_block = gz_ref[pl.ds(local * block, block), :]
        empty = jnp.zeros_like(gz_block)
        rhs = jnp.concatenate(
            [
                jnp.concatenate([gz_block, empty], axis=1),
                jnp.concatenate([empty, gz_block], axis=1),
            ],
            axis=0,
        )
        at = pl.ds(slot * block, block)
        for tile in range(tiles // 2):
            other = tile + tiles // 2
            lhs = jnp.concatenate(
                [
                    buffer[at, pl.ds(tile * width, width)],
                    buffer[at, pl.ds(other * width, width)],
                ],
                axis=0,
            )
            product = lax.dot_general(
                lhs, rhs, (((0,), (0,)), ((), ())), preferred_element_type=F32
            )
            for side, first_block in enumerate((tile * TILE, other * TILE)):
                for i in range(TILE):
                    row = live_row(scal, layer, column_index, first_block + i, live_shape)
                    du_ref[pl.ds(row * block, block), :] += product[
                        i * block : (i + 1) * block, side * tokens : (side + 1) * tokens
                    ]

    column_loop(scal, rows // block // 2, column, wait)
    for step in range(ways):
        outgoing[step][pl.ds(0, rows), :] = du_ref[
            pl.ds((scal[0] ^ step) * rows, rows), :
        ].astype(BF16)
        outgoing[step][pl.ds(rows, PAD), :] = extra


def segment_sum(row, width):
    lanes = row.shape[-1]
    lane = lax.broadcasted_iota(jnp.int32, row.shape, row.ndim - 1)
    step = 1
    while step < width:
        ahead = pltpu.roll(row, lanes - step, row.ndim - 1)
        behind = pltpu.roll(row, step, row.ndim - 1)
        row = row + jnp.where((lane // step) % 2 == 0, ahead, behind)
        step *= 2
    return row


def update_kernel(chunks, inverse_tokens, live_shape, table, *refs):
    gz_refs, u_refs, refs = refs[:chunks], refs[chunks : 2 * chunks], refs[2 * chunks :]
    weight_ref, moment_ref, second_ref, head_ref = refs[:4]
    moment_out, second_out, stepped_ref, factor_ref, heads_ref, square_ref = refs[4:]
    column = pl.program_id(0)
    column_index = (table[0] * 2 + table[1]) * pl.num_programs(0) + column
    block, wide = weight_ref.shape[1:]
    live_count = wide // block
    rate = 0.1 / math.sqrt(wide)

    @pl.when(column == 0)
    def _():
        square_ref[...] = jnp.zeros_like(square_ref)

    lhs = jnp.concatenate([gz[...] for gz in gz_refs], axis=1)
    for tile in range(live_count // TILE):
        picked = jnp.concatenate(
            [
                jnp.concatenate(
                    [
                        u[
                            pl.ds(
                                live_row(
                                    table, table[2], column_index, tile * TILE + i, live_shape
                                )
                                * block,
                                block,
                            ),
                            :,
                        ]
                        for u in u_refs
                    ],
                    axis=1,
                )
                for i in range(TILE)
            ],
            axis=0,
        )
        gradient = (
            lax.dot_general(
                lhs, picked, (((1,), (1,)), ((), ())), preferred_element_type=F32
            )
            * inverse_tokens
        )
        at = pl.ds(tile * TILE * block, TILE * block)
        moment = 0.9 * moment_ref[0, :, at] + 0.1 * gradient
        second = 0.95 * second_ref[0, :, at] + 0.05 * gradient * gradient
        stepped = weight_ref[0, :, at].astype(F32) - rate * moment / (jnp.sqrt(second) + 1e-08)
        moment_out[0, :, at] = moment
        second_out[0, :, at] = second
        stepped_ref[0, :, at] = stepped
        square_ref[pl.ds(column, 1), at] = jnp.sum(stepped * stepped, axis=0, keepdims=True)

    @pl.when(column == pl.num_programs(0) - 1)
    def _():
        squares = segment_sum(square_ref[...], block)
        factor = shrink(jnp.sqrt(squares), 0.15 * math.sqrt(block / live_count))
        factor_ref[...] = factor
        leafed = factor * factor * squares * (1.0 / block)
        head = head_ref[...]
        lane = lax.broadcasted_iota(jnp.int32, heads_ref.shape, 1)
        heads = jnp.zeros(heads_ref.shape, F32)
        for number in range(live_shape[0] * block // HEAD):
            share = jnp.sum(jnp.where(head == number, leafed, 0.0), axis=0, keepdims=True)
            heads = jnp.where(lane == number, jnp.sum(share, axis=1, keepdims=True), heads)
        heads_ref[...] = heads


def output_kernel(parts, features, *refs):
    head_refs, refs = refs[:parts], refs[parts:]
    head_ref, factor_ref, stepped_ref, out_ref, scale_ref = refs
    column = pl.program_id(0)

    @pl.when(column == 0)
    def _():
        squares = head_refs[0][0:1, :]
        for ref in head_refs[1:]:
            squares = squares + ref[0:1, :]
        head_factor = shrink(jnp.sqrt(squares), 0.45 * math.sqrt(HEAD))
        layer = jnp.sum(head_factor * head_factor * squares, axis=1, keepdims=True)
        head_factor = head_factor * shrink(jnp.sqrt(layer), 0.45 * math.sqrt(features))
        head = head_ref[...]
        scale = jnp.zeros(head.shape, F32)
        for number in range(features // HEAD):
            scale = jnp.where(head == number, head_factor[:, number : number + 1], scale)
        scale_ref[...] = scale * factor_ref[...]

    out_ref[0] = (stepped_ref[0] * scale_ref[pl.ds(column, 1), :]).astype(BF16)


def kernel_call(kernel, name, outs, in_specs, out_specs, limit_mib, **kwargs):
    return pl.pallas_call(
        kernel,
        out_shape=outs,
        in_specs=in_specs,
        out_specs=out_specs,
        compiler_params=pltpu.CompilerParams(vmem_limit_bytes=limit_mib << 20),
        name=name,
        **kwargs,
    )


def after(value, *others):
    return lax.optimization_barrier((value, *others))[0]


def local(x_in, cotangent, weights, live_rows, moment, second):
    sections = lax.axis_size("pipe")
    devices = lax.axis_size("dp")
    ways = devices // 2
    section = lax.axis_index("pipe")
    place = lax.axis_index("dp")
    line, core = (place // 2, place % 2)
    micro_count, share, features = x_in.shape
    own_columns, block, wide = weights.shape[1:]
    columns = 2 * own_columns
    rows = columns * block
    tokens = ways * share

    def to_pipe(value, step):
        return lax.ppermute(value, "pipe", [(i, i ^ step) for i in range(sections)])

    def to_line(value, step):
        return lax.ppermute(value, "dp", [(i, i ^ (2 * step)) for i in range(devices)])

    def to_core(value):
        return lax.ppermute(value, "dp", [(i, i ^ 1) for i in range(devices)])

    own_live = live_rows[0]

    x_own = lax.dynamic_index_in_dim(x_in, section, 0, keepdims=False)
    own = weights[0].reshape(own_columns * block, wide)
    height = own_columns * block // 2
    extra = jnp.pad(own_live.reshape(1, wide).astype(BF16), ((0, PAD - 1), (0, 0)))
    half1 = jnp.concatenate([own[:height], extra], axis=0)
    half2 = jnp.concatenate([own[height:], extra], axis=0)

    def slot(x_value, y_value, *extra):
        return lax.optimization_barrier((to_pipe(x_value, 1), to_pipe(y_value, 2), *extra))

    def along(value, *deps):
        value = after(value, *deps) if deps else value
        return [to_line(value, step) for step in range(1, ways)]

    def pick(layer_round, first_source, second_source):
        return kernel_call(
            functools.partial(pick_kernel, layer_round, height),
            f"pick{layer_round}",
            [
                jax.ShapeDtypeStruct((height + (PAD if layer_round == 2 else 0), wide), BF16),
                jax.ShapeDtypeStruct((height, wide), BF16),
            ],
            [SMEM] + [ANY] * 3,
            [VMEM] * 2,
            LIMIT,
            scratch_shapes=[pltpu.SemaphoreType.DMA((3,))],
        )(jnp.stack([section]).astype(jnp.int32), own, first_source, second_source)

    x1, y1, *x_parts = slot(half1, half2, *along(x_own, half1, half2))
    x2, y2 = slot(*pick(2, x1, y1))
    by_step = [own_live] + [
        value[height].astype(jnp.int32).reshape(own_live.shape) for value in (x1, y1, x2)
    ]
    mine = dict(own=own, x1=x1, x2=x2, y1=y1, y2=y2)
    siblings = dict(own=to_core(after(own, x1, y1)))
    siblings.update({name: to_core(mine[name]) for name in ("x1", "y1", "x2", "y2")})
    x3, y3 = slot(*pick(3, x1, after(y1, x2, y2)))
    mine.update(x3=x3, y3=y3)
    live = [lax.select_n(section ^ layer, *by_step) for layer in range(sections)]
    live_shape = own_live.shape
    header = jnp.stack([line, core, section]).astype(jnp.int32)
    table = jnp.concatenate(
        [jnp.pad(header, (0, HEADER - header.shape[0]))] + [value.reshape(-1) for value in live]
    )

    def layer_weights(layer):
        names = holders(layer)
        return [mine[name] for name in names] + [siblings[name] for name in names]

    def sds(shape, dtype):
        return jax.ShapeDtypeStruct(shape, dtype)

    x_all = jnp.zeros((ways, share, features), BF16)
    for step, part in enumerate([x_own, *x_parts]):
        x_all = lax.dynamic_update_index_in_dim(x_all, part, line ^ step, 0)
    x_all = x_all.reshape(tokens, features).T

    weight_scratch = [pltpu.VMEM((columns * block, wide), BF16)]
    shards = [x_all]
    entering, inverses, pre_acts, sends = [None], [], [], []
    for layer in range(sections):
        last = layer == sections - 1
        outs = [sds((rows, tokens), F32), sds((8, tokens), F32)]
        outs += [] if last else [sds((rows, tokens), BF16)]
        plain = len(outs)
        outs += [sds((features, tokens), BF16)] * sections
        operands = layer_weights(layer)
        before = 1 + len(shards) + len(operands)
        result = kernel_call(
            functools.partial(forward_kernel, layer, ways, last, live_shape),
            f"forward{layer}",
            outs,
            [SMEM] + [VMEM] * len(shards) + [ANY] * (len(operands) + len(sends)),
            [VMEM] * plain + [ANY] * sections,
            LIMIT,
            scratch_shapes=weight_scratch
            + [
                pltpu.VMEM((features, tokens), BF16),
                pltpu.SemaphoreType.DMA((8,)),
                pltpu.SemaphoreType.DMA((1,)),
            ],
            input_output_aliases={before + i: plain + i for i in range(len(sends))},
        )(table, *shards, *operands, *sends)
        pre_acts.append(result[0])
        inverses.append(result[1])
        sends = result[plain:]
        if not last:
            entering.append(result[2])
            shards = [result[2]] + [to_line(result[2], step) for step in range(1, ways)]
            if layer == 0:
                for name in ("x3", "y3"):
                    siblings[name] = to_core(after(mine[name], *shards[1:]))

    cot_own = after(lax.dynamic_index_in_dim(cotangent, section, 0, keepdims=False), entering[2])
    cot_all = jnp.zeros((ways, share, rows), BF16)
    for step in range(ways):
        cot_part = lax.dynamic_slice_in_dim(cot_own, (line ^ step) * rows, rows, 1)
        cot_part = cot_part if step == 0 else to_line(cot_part, step)
        cot_all = lax.dynamic_update_index_in_dim(cot_all, cot_part, line ^ step, 0)
    cot_all = cot_all.reshape(tokens, rows).T

    u_chunks, u_siblings = [sends[0]] + [None] * (sections - 1), [None] * sections
    u_chunks[1], u_chunks[2] = (to_pipe(sends[1], 1), to_pipe(sends[2], 2))
    gradients = [None] * sections
    arriving = [cot_all]
    for layer in reversed(range(sections)):
        first, last = layer == sections - 1, layer == 0
        if last:
            outs = [sds((rows // 2, tokens), BF16)] * (2 * sections)
            operands = gradients[1:]
            specs, scratch = [VMEM] * len(operands), [pltpu.VMEM((rows, tokens), BF16)]
        else:
            outs = [sds((rows, tokens), BF16)]
            outs += [sds((rows + PAD, tokens), BF16)] * ways
            outs += [] if first else [sds((rows, tokens), BF16)]
            operands = layer_weights(layer)
            specs = [ANY] * len(operands)
            scratch = weight_scratch + [
                pltpu.SemaphoreType.DMA((8,)),
                pltpu.VMEM((features, tokens), F32),
            ]
        operands = arriving + [pre_acts[layer]] + operands
        result = kernel_call(
            functools.partial(backward_kernel, layer, ways, live_shape),
            f"backward{layer}",
            outs,
            [SMEM] + [VMEM] * (len(arriving) + 1) + specs,
            [VMEM] * len(outs),
            LIMIT,
            scratch_shapes=scratch,
        )(table, *operands)
        if last:
            break
        gradients[layer] = result[0]
        outgoing = result[1 : 1 + ways]
        incoming = [outgoing[0]] + [to_line(outgoing[k], k) for k in range(1, ways)]
        older = cot_all if first else result[1 + ways]
        if first:
            incoming[0] = after(incoming[0], u_chunks[1], u_chunks[2])
            u_chunks[3] = to_pipe(after(sends[3], *incoming), 3)
        elif layer == sections - 2:
            for number in (0, 1):
                u_siblings[number] = to_core(after(u_chunks[number], result[0]))
            incoming[0] = after(incoming[0], *u_siblings[:2])
        else:
            for number in (2, 3):
                u_siblings[number] = to_core(after(u_chunks[number], result[0]))
            incoming[0] = after(incoming[0], *u_siblings[2:])
        arriving = [older, entering[layer], inverses[layer]] + incoming
    u_chunks = u_chunks + u_siblings

    gz_chunks = [None] * (2 * sections)
    order = [(step, flip) for step in (3, 1, 2) for flip in range(2)] + [(0, 1), (0, 0)]
    for step, flip in order:
        value = result[2 * step + flip]
        if step or flip:
            value = lax.ppermute(
                value,
                ("pipe", "dp"),
                [
                    (i * devices + j, (i ^ step) * devices + (j ^ flip))
                    for i in range(sections)
                    for j in range(devices)
                ],
            )
        gz_chunks[flip * sections + step] = value

    chunks = len(gz_chunks)
    all_tokens = micro_count * devices * share
    padded = max(8, own_columns)
    own_index = lax.dynamic_slice_in_dim(own_live, place * own_columns, own_columns, 0)
    head = jnp.repeat(own_index // (HEAD // block), block, axis=1)
    head = jnp.concatenate([head, jnp.full((padded - own_columns, wide), -1, jnp.int32)], axis=0)
    per_column = pl.BlockSpec((1, block, wide), lambda j, *_: (j, 0, 0))
    per_lane = pl.BlockSpec((padded, wide), lambda j, *_: (0, 0))
    per_head = pl.BlockSpec((8, 128), lambda j, *_: (0, 0))
    held_whole = pl.BlockSpec(
        (features, tokens), lambda j, *_: (0, 0), pipeline_mode=pl.Buffered(1)
    )
    moment_new, second_new, stepped, factor, heads = pl.pallas_call(
        functools.partial(update_kernel, chunks, 1.0 / all_tokens, live_shape),
        out_shape=[sds((own_columns, block, wide), F32)] * 3
        + [sds((padded, wide), F32), sds((8, 128), F32)],
        grid_spec=pltpu.PrefetchScalarGridSpec(
            num_scalar_prefetch=1,
            grid=(own_columns,),
            in_specs=[pl.BlockSpec((block, tokens), lambda j, *_: (j, 0))] * chunks
            + [held_whole] * chunks
            + [per_column] * 3
            + [per_lane],
            out_specs=[per_column] * 3 + [per_lane, per_head],
            scratch_shapes=[pltpu.VMEM((padded, wide), F32)],
        ),
        compiler_params=pltpu.CompilerParams(vmem_limit_bytes=LIMIT << 20),
        name="update",
    )(
        table,
        *gz_chunks,
        *u_chunks,
        weights[0],
        moment[0],
        second[0],
        head,
    )
    heads = heads + to_core(heads)
    head_parts = [heads] + [to_line(heads, step) for step in range(1, ways)]
    weights_out = kernel_call(
        functools.partial(output_kernel, len(head_parts), features),
        "output",
        sds((own_columns, block, wide), BF16),
        [per_head] * len(head_parts) + [per_lane] * 2 + [per_column],
        per_column,
        LIMIT,
        grid=(own_columns,),
        scratch_shapes=[pltpu.VMEM((padded, wide), F32)],
    )(*head_parts, head, factor, stepped)
    return (weights_out[None], moment_new[None], second_new[None])


def solution(mesh):
    placed = (
        P(None, "dp", None),
        P(None, "dp", None),
        P("pipe", "dp", None, None),
        P("pipe", None, None),
        P("pipe", "dp", None, None),
        P("pipe", "dp", None, None),
    )
    return jax.shard_map(
        local,
        mesh=mesh,
        in_specs=placed,
        out_specs=(
            P("pipe", "dp", None, None),
            P("pipe", "dp", None, None),
            P("pipe", "dp", None, None),
        ),
        check_vma=False,
    )
```

time: 417 us -> 359 us (0.86)
  waiting for transfers between devices: 202 us -> 164 us
  starting transfers between devices: 93.9 us -> 78.5 us
  Pallas kernels: 73.8 us -> 87.2 us
  other arithmetic: 15.4 us -> 3.9 us
  local copies, waits for them, and re-layouts: 28.8 us -> 22.9 us
    ppermute x12 -> x9, waiting for transfers between devices: 52 us -> 29.1 us  [to_pipe(): return lax.ppermute(value, 'pipe', [(i, i ^ step) for i in range(sections)])]
    ppermute x7, waiting for transfers between devices: 26.6 us -> 8.21 us  [local(): lax.ppermute(value, ('pipe', 'dp'), [(i * devices + j, (i ^ step) * devic...]
    pallas_call x9 -> x12, Pallas kernels: 73.8 us -> 87.2 us  [the longest x4 29.4 us: local(): kernel_call(functools.partial(backward_kernel, layer, ways, live_shape),...]
    ppermute x7 -> x0, starting transfers between devices: 10.8 us -> none  [local(): lax.ppermute(head_share, 'dp', [(i, i ^ step) for i in range(devices)])]
    select_n x4 -> x1, other arithmetic: 8.19 us -> 0.01 us  [local(): head = jnp.repeat(own_index // (HEAD // block), block, axis=1)]
    ppermute x12 -> x9, starting transfers between devices: 16.3 us -> 10.2 us  [to_pipe(): return lax.ppermute(value, 'pipe', [(i, i ^ step) for i in range(sections)])]
    ppermute x11 -> x12, waiting for transfers between devices: 0.03 us -> 5.14 us  [to_core(): return lax.ppermute(value, 'dp', [(i, i ^ 1) for i in range(devices)])]
    unnamed x79 -> x96, local copies, waits for them, and re-layouts: 13.5 us -> 8.85 us
  transfers between devices with their start and end apart: 61 -> 55, of which waited for: 28 -> 26; matrix products, arithmetic and copies ran while one was open for 4% -> 4% of each run, Pallas kernels for 7% -> 9%
where the time goes in v2:
time: 359 us; the launch traced here: 358 us
  waiting for transfers between devices  164 us (46%)
  Pallas kernels  87.2 us (24%)
  starting transfers between devices  78.5 us (22%)
  local copies, waits for them, and re-layouts  22.9 us (6%)
  other arithmetic  3.9 us (1%)
    ppermute x27, waiting for transfers between devices, to_line(): lax.ppermute(value, 'dp', [(i, i ^ 2 * step) for i in range(devices)])  122 us
    ppermute x27, starting transfers between devices, to_line(): lax.ppermute(value, 'dp', [(i, i ^ 2 * step) for i in range(devices)])  59 us
    pallas_call x4, Pallas kernels, local(): kernel_call(functools.partial(backward_kernel, layer, ways, live_shape),...  29.4 us
    ppermute x9, waiting for transfers between devices, to_pipe(): return lax.ppermute(value, 'pipe', [(i, i ^ step) for i in range(sections)])  29.1 us
    pallas_call x4, Pallas kernels, local(): kernel_call(functools.partial(forward_kernel, layer, ways, last, live_sha...  23.7 us
    pallas_call x1, Pallas kernels, local(): pl.pallas_call(functools.partial(update_kernel, chunks, 1.0 / all_tokens,...  21.6 us
    ppermute x9, starting transfers between devices, to_pipe(): return lax.ppermute(value, 'pipe', [(i, i ^ step) for i in range(sections)])  10.2 us
    unnamed x96, local copies, waits for them, and re-layouts  8.85 us
  transfers between devices with their start and end apart: 55, of which 26 were waited for; matrix products, arithmetic and copies ran while one was open for 4% of the time, Pallas kernels for 9%

profile of v2, /device:TPU:0, one launch (start us, length us, event | category | flops | bytes accessed | tf_op | source)
XLA Modules:
  0.0 357.9 jit_solution(972966552132438313)
XLA Ops:
  0.7 1.8 fusion.6
  2.6 1.5 fusion.2
  4.2 2.9 collective-permute-start
  7.1 1.5 collective-permute-start.1
  9.8 1.8 dynamic-slice_dynamic-update-slice_fusion
  11.6 1.6 collective-permute-start.2
  13.1 2.6 collective-permute-start.3
  16.2 7.7 %collective-permute-done.2 = bf16[32,4096]{1,0:T(8,128)(2,1)} collective-permute-done((bf16[32,4096]{1,0:T(8,128)(2,1)}, bf16[32,4096]{1,0:T(8,128)(2,1)}, u32[]{:S(2)}, u32[]{:S(2)}) %collective-permute-start.2) | collective-permute-done | bytes 262176 | tf_op jit(solution)/shard_map/ppermute | solution.py:427
  23.9 10.9 %collective-permute-done.3 = bf16[32,4096]{1,0:T(8,128)(2,1)} collective-permute-done((bf16[32,4096]{1,0:T(8,128)(2,1)}, bf16[32,4096]{1,0:T(8,128)(2,1)}, u32[]{:S(2)}, u32[]{:S(2)}) %collective-permute-start.3) | collective-permute-done | bytes 262176 | tf_op jit(solution)/shard_map/ppermute | solution.py:427
  36.8 3.1 pick2.1
  41.5 1.7 bitcast_dynamic-update-slice_fusion.2
  43.2 1.7 bitcast_dynamic-update-slice_fusion.1
  44.9 1.7 bitcast_dynamic-update-slice_fusion
  46.6 2.3 copy.38
  49.6 16.6 %collective-permute-done.6.refs_5_.refs_8_.refs_9_.refs_7_.refs_12_ = bf16[256,2048]{1,0:T(8,128)(2,1)} collective-permute-done((bf16[256,2048]{1,0:T(8,128)(2,1)}, bf16[256,2048]{1,0:T(8,128)(2,1)}, u32[]{:S(2)}, u32[]{:S(2)}) %collective-permute-start.6) | collective-permute-done | bytes 1048608 | tf_op jit(solution)/shard_map/ppermute | solution.py:424
  68.7 2.9 pick3.1
  73.3 5.9 %forward0.1 = (f32[1024,128]{1,0:T(8,128)}, f32[8,128]{1,0:T(8,128)}, bf16[1024,128]{1,0:T(8,128)(2,1)}, bf16[4096,128]{1,0:T(8,128)(2,1)}, bf16[4096,128]{1,0:T...) custom-call(s32[8320]{0:T(1024)} %copy-done.9, bf16[4096,128]{1,0:T(8,128)(2,1)} %bitcast.70, ...), custom_call_target="tpu_custom_call" | custom-call | tf_op jit(solution)/shard_map/forward0/pallas_call | solution.py:502
  79.2 4.3 %collective-permute-start.12 = (bf16[1024,128]{1,0:T(8,128)(2,1)}, bf16[1024,128]{1,0:T(8,128)(2,1)S(1)}, u32[]{:S(2)}, u32[]{:S(2)}) collective-permute-start(bf16[1024,128]{1,0:T(8,128)(2,1)} %get-tuple-element.97.refs_0_.refs_1_), channel_id=1, source_target_pairs={{0,2},{1,3},{2,0},{3,1},{4,6},{5,7},{6,4},{7,5},{8,10},{9,11},{10,... | collective-permute-start | bytes 786440 | tf_op jit(solution)/shard_map/ppermute | solution.py:427
  84.6 1.4 collective-permute-start.14
  86.0 11.1 %collective-permute-done.15.refs_7_.refs_6_.refs_5_.refs_10_.refs_11_ = bf16[256,2048]{1,0:T(8,128)(2,1)} collective-permute-done((bf16[256,2048]{1,0:T(8,128)(2,1)}, bf16[256,2048]{1,0:T(8,128)(2,1)}, u32[]{:S(2)}, u32[]{:S(2)}) %collective-permute-start.15) | collective-permute-done | bytes 1048608 | tf_op jit(solution)/shard_map/ppermute | solution.py:424
  97.3 7.8 %collective-permute-done.13.refs_2_ = bf16[1024,128]{1,0:T(8,128)(2,1)S(1)} collective-permute-done((bf16[1024,128]{1,0:T(8,128)(2,1)}, bf16[1024,128]{1,0:T(8,128)(2,1)S(1)}, u32[]{:S(2)}, u32[]{:S(2)}) %collective-permute-start.13) | collective-permute-done | bytes 262176 | tf_op jit(solution)/shard_map/ppermute | solution.py:427
  105.7 2.4 collective-permute-done.18.refs_15_.refs_17_.refs_19_
  108.0 1.5 collective-permute-done.17.refs_13_.refs_12_.refs_14_.refs_16_.refs_17_
  110.5 6.0 %forward1.1 = (f32[1024,128]{1,0:T(8,128)}, f32[8,128]{1,0:T(8,128)}, bf16[1024,128]{1,0:T(8,128)(2,1)}, bf16[4096,128]{1,0:T(8,128)(2,1)}, bf16[4096,128]{1,0:T...) custom-call(s32[8320]{0:T(1024)} %copy-done.9, ...), custom_call_target="tpu_custom_call", output_to_operand_aliasing={{3}: (17, {}), {4}: (18, {}), {5}: (19, {}), {6}: (20, {})} | custom-call | tf_op jit(solution)/shard_map/forward1/pallas_call | solution.py:502
  116.5 4.4 %collective-permute-start.22 = (bf16[1024,128]{1,0:T(8,128)(2,1)}, bf16[1024,128]{1,0:T(8,128)(2,1)S(1)}, u32[]{:S(2)}, u32[]{:S(2)}) collective-permute-start(bf16[1024,128]{1,0:T(8,128)(2,1)} %get-tuple-element.109.refs_0_.refs_1_), channel_id=1, source_target_pairs={{0,2},{1,3},{2,0},{3,1},{4,6},{5,7},{6,4},{7,5},{8,10},{9,11},{10,... | collective-permute-start | bytes 786440 | tf_op jit(solution)/shard_map/ppermute | solution.py:427
  122.0 1.4 collective-permute-start.24
  123.3 9.4 %collective-permute-done.22.refs_1_ = bf16[1024,128]{1,0:T(8,128)(2,1)S(1)} collective-permute-done((bf16[1024,128]{1,0:T(8,128)(2,1)}, bf16[1024,128]{1,0:T(8,128)(2,1)S(1)}, u32[]{:S(2)}, u32[]{:S(2)}) %collective-permute-start.22) | collective-permute-done | bytes 262176 | tf_op jit(solution)/shard_map/ppermute | solution.py:427
  132.7 9.7 %collective-permute-done.23.refs_2_ = bf16[1024,128]{1,0:T(8,128)(2,1)S(1)} collective-permute-done((bf16[1024,128]{1,0:T(8,128)(2,1)}, bf16[1024,128]{1,0:T(8,128)(2,1)S(1)}, u32[]{:S(2)}, u32[]{:S(2)}) %collective-permute-start.23) | collective-permute-done | bytes 262176 | tf_op jit(solution)/shard_map/ppermute | solution.py:427
  143.2 6.0 %forward2.1 = (f32[1024,128]{1,0:T(8,128)}, f32[8,128]{1,0:T(8,128)}, bf16[1024,128]{1,0:T(8,128)(2,1)}, bf16[4096,128]{1,0:T(8,128)(2,1)}, bf16[4096,128]{1,0:T...) custom-call(s32[8320]{0:T(1024)} %copy-done.9, ...), custom_call_target="tpu_custom_call", output_to_operand_aliasing={{3}: (17, {}), {4}: (18, {}), {5}: (19, {}), {6}: (20, {})} | custom-call | tf_op jit(solution)/shard_map/forward2/pallas_call | solution.py:502
  149.2 5.0 %collective-permute-start.25 = (bf16[1024,128]{1,0:T(8,128)(2,1)}, bf16[1024,128]{1,0:T(8,128)(2,1)S(1)}, u32[]{:S(2)}, u32[]{:S(2)}) collective-permute-start(bf16[1024,128]{1,0:T(8,128)(2,1)} %get-tuple-element.115.refs_0_.refs_1_), channel_id=1, source_target_pairs={{0,2},{1,3},{2,0},{3,1},{4,6},{5,7},{6,4},{7,5},{8,10},{9,11},{10,... | collective-permute-start | bytes 786440 | tf_op jit(solution)/shard_map/ppermute | solution.py:427
  155.3 1.4 collective-permute-start.27
  157.9 2.0 collective-permute-start.20
  159.9 5.2 %collective-permute-done.25.refs_1_ = bf16[1024,128]{1,0:T(8,128)(2,1)S(1)} collective-permute-done((bf16[1024,128]{1,0:T(8,128)(2,1)}, bf16[1024,128]{1,0:T(8,128)(2,1)S(1)}, u32[]{:S(2)}, u32[]{:S(2)}) %collective-permute-start.25) | collective-permute-done | bytes 262176 | tf_op jit(solution)/shard_map/ppermute | solution.py:427
  165.1 1.9 collective-permute-start.21
  167.0 11.6 %collective-permute-done.26.refs_2_ = bf16[1024,128]{1,0:T(8,128)(2,1)S(1)} collective-permute-done((bf16[1024,128]{1,0:T(8,128)(2,1)}, bf16[1024,128]{1,0:T(8,128)(2,1)S(1)}, u32[]{:S(2)}, u32[]{:S(2)}) %collective-permute-start.26) | collective-permute-done | bytes 262176 | tf_op jit(solution)/shard_map/ppermute | solution.py:427
  179.4 5.9 %forward3.1 = (f32[1024,128]{1,0:T(8,128)}, f32[8,128]{1,0:T(8,128)}, bf16[4096,128]{1,0:T(8,128)(2,1)}, bf16[4096,128]{1,0:T(8,128)(2,1)}, bf16[4096,128]{1,0:T(8,128)(2,1)}, /*index=5*/bf16[4096,128]{1,0:T(8,128)(2,1)}) custom-call(s32[8320]{0:T(1024)} %copy-done.9, ...), custom_call_target="tpu_custom_call", output_to_operand_aliasing={{2}: (19, {}), {3}: (20, {}), {4}: (21, {}), {5}: (22, {})} | custom-call | tf_op jit(solution)/shard_map/forward3/pallas_call | solution.py:502
  185.3 1.6 collective-permute-start.28
  186.9 1.5 collective-permute-start.29
  189.4 8.5 %backward3.1 = (bf16[1024,128]{1,0:T(8,128)(2,1)}, bf16[1040,128]{1,0:T(8,128)(2,1)}, bf16[1040,128]{1,0:T(8,128)(2,1)}, bf16[1040,128]{1,0:T(8,128)(2,1)}, bf16[1040,128]{1,0:T(8,128)(2,1)}) custom-call(s32[8320]{0:T(1024)} %copy-done.9, bf16[1024,128]{1,0:T(8,128)(2,1)} %bitcast.71, f32[1024,128]{1,0:T(8,128)} %get-tuple-element.121.refs_1_, ...), custom_call_target="tpu_custom_call" | custom-call | tf_op jit(solution)/shard_map/backward3/pallas_call | solution.py:556
  197.9 5.3 %collective-permute-start.30 = (bf16[1040,128]{1,0:T(8,128)(2,1)}, bf16[1040,128]{1,0:T(8,128)(2,1)S(1)}, u32[]{:S(2)}, u32[]{:S(2)}) collective-permute-start(bf16[1040,128]{1,0:T(8,128)(2,1)} %get-tuple-element.126), channel_id=1, source_target_pairs={{0,2},{1,3},{2,0},{3,1},{4,6},{5,7},{6,4},{7,5},{8,10},{9,11},{10,... | collective-permute-start | bytes 798728 | tf_op jit(solution)/shard_map/ppermute | solution.py:427
  205.7 4.7 %collective-permute-done.30.refs_4_ = bf16[1040,128]{1,0:T(8,128)(2,1)S(1)} collective-permute-done((bf16[1040,128]{1,0:T(8,128)(2,1)}, bf16[1040,128]{1,0:T(8,128)(2,1)S(1)}, u32[]{:S(2)}, u32[]{:S(2)}) %collective-permute-start.30) | collective-permute-done | bytes 266272 | tf_op jit(solution)/shard_map/ppermute | solution.py:427
  210.4 12.2 %collective-permute-done.31.refs_5_ = bf16[1040,128]{1,0:T(8,128)(2,1)S(1)} collective-permute-done((bf16[1040,128]{1,0:T(8,128)(2,1)}, bf16[1040,128]{1,0:T(8,128)(2,1)S(1)}, u32[]{:S(2)}, u32[]{:S(2)}) %collective-permute-start.31) | collective-permute-done | bytes 266272 | tf_op jit(solution)/shard_map/ppermute | solution.py:427
  223.4 8.7 %backward2.1 = (bf16[1024,128]{1,0:T(8,128)(2,1)}, bf16[1040,128]{1,0:T(8,128)(2,1)}, bf16[1040,128]{1,0:T(8,128)(2,1)}, bf16[1040,128]{1,0:T(8,128)(2,1)}, bf16...) custom-call(s32[8320]{0:T(1024)} %copy-done.9, bf16[1024,128]{1,0:T(8,128)(2,1)} %bitcast.72, ...), custom_call_target="tpu_custom_call" | custom-call | tf_op jit(solution)/shard_map/backward2/pallas_call | solution.py:556
  233.2 3.3 collective-permute-start.35
  237.5 1.5 collective-permute-start.37
  239.1 8.9 %collective-permute-done.35.refs_4_ = bf16[1040,128]{1,0:T(8,128)(2,1)S(1)} collective-permute-done((bf16[1040,128]{1,0:T(8,128)(2,1)}, bf16[1040,128]{1,0:T(8,128)(2,1)S(1)}, u32[]{:S(2)}, u32[]{:S(2)}) %collective-permute-start.35) | collective-permute-done | bytes 266272 | tf_op jit(solution)/shard_map/ppermute | solution.py:427
  248.0 10.4 %collective-permute-done.36.refs_5_ = bf16[1040,128]{1,0:T(8,128)(2,1)S(1)} collective-permute-done((bf16[1040,128]{1,0:T(8,128)(2,1)}, bf16[1040,128]{1,0:T(8,128)(2,1)S(1)}, u32[]{:S(2)}, u32[]{:S(2)}) %collective-permute-start.36) | collective-permute-done | bytes 266272 | tf_op jit(solution)/shard_map/ppermute | solution.py:427
  259.2 8.6 %backward1.1 = (bf16[1024,128]{1,0:T(8,128)(2,1)}, bf16[1040,128]{1,0:T(8,128)(2,1)}, bf16[1040,128]{1,0:T(8,128)(2,1)}, bf16[1040,128]{1,0:T(8,128)(2,1)}, bf16...) custom-call(s32[8320]{0:T(1024)} %copy-done.9, bf16[1024,128]{1,0:T(8,128)(2,1)} %get-tuple-element.130.refs_0_, ...), custom_call_target="tpu_custom_call" | custom-call | tf_op jit(solution)/shard_map/backward1/pallas_call | solution.py:556
  268.4 4.7 %collective-permute-start.41 = (bf16[1040,128]{1,0:T(8,128)(2,1)}, bf16[1040,128]{1,0:T(8,128)(2,1)S(1)}, u32[]{:S(2)}, u32[]{:S(2)}) collective-permute-start(bf16[1040,128]{1,0:T(8,128)(2,1)} %get-tuple-element.151), channel_id=1, source_target_pairs={{0,2},{1,3},{2,0},{3,1},{4,6},{5,7},{6,4},{7,5},{8,10},{9,11},{10,... | collective-permute-start | bytes 798728 | tf_op jit(solution)/shard_map/ppermute | solution.py:427
  274.1 1.5 collective-permute-start.43
  275.6 9.4 %collective-permute-done.41.refs_4_ = bf16[1040,128]{1,0:T(8,128)(2,1)S(1)} collective-permute-done((bf16[1040,128]{1,0:T(8,128)(2,1)}, bf16[1040,128]{1,0:T(8,128)(2,1)S(1)}, u32[]{:S(2)}, u32[]{:S(2)}) %collective-permute-start.41) | collective-permute-done | bytes 266272 | tf_op jit(solution)/shard_map/ppermute | solution.py:427
  285.0 9.9 %collective-permute-done.42.refs_5_ = bf16[1040,128]{1,0:T(8,128)(2,1)S(1)} collective-permute-done((bf16[1040,128]{1,0:T(8,128)(2,1)}, bf16[1040,128]{1,0:T(8,128)(2,1)S(1)}, u32[]{:S(2)}, u32[]{:S(2)}) %collective-permute-start.42) | collective-permute-done | bytes 266272 | tf_op jit(solution)/shard_map/ppermute | solution.py:427
  295.7 3.6 %backward0.1 = (bf16[512,128]{1,0:T(8,128)(2,1)}, bf16[512,128]{1,0:T(8,128)(2,1)}, bf16[512,128]{1,0:T(8,128)(2,1)}, bf16[512,128]{1,0:T(8,128)(2,1)}, bf16[512...) custom-call(s32[8320]{0:T(1024)} %copy-done.9, ...), custom_call_target="tpu_custom_call" | custom-call | tf_op jit(solution)/shard_map/backward0/pallas_call | solution.py:556
  299.3 1.6 collective-permute-start.44
  300.9 1.5 collective-permute-start.45
  302.8 1.6 collective-permute-start.48
  308.1 1.8 collective-permute-done.46.refs_3_
  309.8 4.8 %collective-permute-done.49.refs_6_ = bf16[512,128]{1,0:T(8,128)(2,1)S(1)} collective-permute-done((bf16[512,128]{1,0:T(8,128)(2,1)}, bf16[512,128]{1,0:T(8,128)(2,1)S(1)}, u32[]{:S(2)}, u32[]{:S(2)}) %collective-permute-start.49) | collective-permute-done | bytes 131104 | tf_op jit(solution)/shard_map/ppermute | solution.py:590
  315.4 21.6 %update.1 = (f32[8,64,2048]{2,1,0:T(8,128)}, f32[8,64,2048]{2,1,0:T(8,128)}, f32[8,64,2048]{2,1,0:T(8,128)}, f32[8,2048]{1,0:T(8,128)}, f32[8,128]{1,0:T(8,128)}) custom-call(s32[8320]{0:T(1024)} %copy-done.9, bf16[512,128]{1,0:T(8,128)(2,1)} %get-tuple-element.156.refs_0_, bf16[512,128]{1,0:T(8,128)(2,1)} %copy-done.35, bf16[512,128]{1,0:T(8,128)(2,1)} %copy-done.36, ...), custom_call_target="tpu_custom_call" | custom-call | tf_op jit(solution)/shard_map/update/pallas_call | solution.py:613
  339.1 5.2 %collective-permute-start.52 = (f32[8,128]{1,0:T(8,128)S(1)}, f32[8,128]{1,0:T(8,128)S(1)}, u32[]{:S(2)}, u32[]{:S(2)}) collective-permute-start(f32[8,128]{1,0:T(8,128)S(1)} %add.62.refs_0_), channel_id=1, source_target_pairs={{0,2},{1,3},{2,0},{3,1},{4,6},{5,7},{6,4},{7,5},{8,10},{9,11},{10,... | collective-permute-start | bytes 12296 | tf_op jit(solution)/shard_map/ppermute | solution.py:427
  345.3 1.5 collective-permute-start.54
  346.8 2.0 collective-permute-done.53.refs_2_
  348.8 2.0 collective-permute-done.54.refs_3_
  351.3 6.6 %output.1 = bf16[8,64,2048]{2,1,0:T(8,128)(2,1)} custom-call(f32[8,128]{1,0:T(8,128)} %copy-done.43, f32[8,128]{1,0:T(8,128)} %copy-done.44, f32[8,128]{1,0:T(8,128)} %copy-done.45, f32[8,128]{1,0:T(8,128)} %copy-done.46, s32[8,2048]{1,0:T(8,128)} %reshape.71.refs_19_.refs_4_, f32[8,2048]{1,0:T(8,128)} %get-tuple-element.165.refs_5_, ...), custom_call_target="tpu_custom_call" | custom-call | tf_op jit(solution)/shard_map/output/pallas_call | solution.py:640
  (186 shorter events, 36.1 us)
Async XLA Ops:
  0.6 156.1 %copy-start = (bf16[4,32,4096]{2,1,0:T(8,128)(2,1)S(1)}, bf16[4,32,4096]{2,1,0:T(8,128)(2,1)}, u32[]{:S(2)}) copy-start(bf16[4,32,4096]{2,1,0:T(8,128)(2,1)} %param.7) | copy-start | bytes 3145732
  4.2 30.7 %collective-permute-start = (bf16[272,2048]{1,0:T(8,128)(2,1)}, bf16[272,2048]{1,0:T(8,128)(2,1)S(1)}, u32[]{:S(2)}, u32[]{:S(2)}) collective-permute-start(bf16[272,2048]{1,0:T(8,128)(2,1)} %get-tuple-element.181), channel_id=1, source_target_pairs={{0,8},{8,0},{16,24},{24,16},{1,9},{9,1},{17,25},{25,17},{2,10},{10... | collective-permute-start | bytes 3342344 | tf_op jit(solution)/shard_map/ppermute | solution.py:424
  7.1 27.7 %collective-permute-start.1 = (bf16[272,2048]{1,0:T(8,128)(2,1)}, bf16[272,2048]{1,0:T(8,128)(2,1)S(1)}, u32[]{:S(2)}, u32[]{:S(2)}) collective-permute-start(bf16[272,2048]{1,0:T(8,128)(2,1)} %get-tuple-element.180), channel_id=1, source_target_pairs={{0,16},{8,24},{16,0},{24,8},{1,17},{9,25},{17,1},{25,9},{2,18},{10... | collective-permute-start | bytes 3342344 | tf_op jit(solution)/shard_map/ppermute | solution.py:424
  11.6 12.4 %collective-permute-start.2 = (bf16[32,4096]{1,0:T(8,128)(2,1)}, bf16[32,4096]{1,0:T(8,128)(2,1)}, u32[]{:S(2)}, u32[]{:S(2)}) collective-permute-start(bf16[32,4096]{1,0:T(8,128)(2,1)} %get-tuple-element.86), channel_id=1, source_target_pairs={{0,2},{1,3},{2,0},{3,1},{4,6},{5,7},{6,4},{7,5},{8,10},{9,11},{10,... | collective-permute-start | bytes 786440 | tf_op jit(solution)/shard_map/ppermute | solution.py:427
  13.1 21.7 %collective-permute-start.3 = (bf16[32,4096]{1,0:T(8,128)(2,1)}, bf16[32,4096]{1,0:T(8,128)(2,1)}, u32[]{:S(2)}, u32[]{:S(2)}) collective-permute-start(bf16[32,4096]{1,0:T(8,128)(2,1)} %get-tuple-element.86), channel_id=1, source_target_pairs={{0,4},{1,5},{2,6},{3,7},{4,0},{5,1},{6,2},{7,3},{8,12},{9,13},{10,... | collective-permute-start | bytes 786440 | tf_op jit(solution)/shard_map/ppermute | solution.py:427
  15.7 19.1 %collective-permute-start.4 = (bf16[32,4096]{1,0:T(8,128)(2,1)}, bf16[32,4096]{1,0:T(8,128)(2,1)}, u32[]{:S(2)}, u32[]{:S(2)}) collective-permute-start(bf16[32,4096]{1,0:T(8,128)(2,1)} %get-tuple-element.86), channel_id=1, source_target_pairs={{0,6},{1,7},{2,4},{3,5},{4,2},{5,3},{6,0},{7,1},{8,14},{9,15},{10,... | collective-permute-start | bytes 786440 | tf_op jit(solution)/shard_map/ppermute | solution.py:427
  39.9 31.7 %collective-permute-start.10 = (bf16[272,2048]{1,0:T(8,128)(2,1)}, bf16[272,2048]{1,0:T(8,128)(2,1)}, u32[]{:S(2)}, u32[]{:S(2)}) collective-permute-start(bf16[272,2048]{1,0:T(8,128)(2,1)} %copy-done.4), channel_id=1, source_target_pairs={{0,1},{1,0},{2,3},{3,2},{4,5},{5,4},{6,7},{7,6},{8,9},{9,8},{10,11... | collective-permute-start | bytes 3342344 | tf_op jit(solution)/shard_map/ppermute | solution.py:430
  40.0 32.2 %collective-permute-start.8 = (bf16[272,2048]{1,0:T(8,128)(2,1)}, bf16[272,2048]{1,0:T(8,128)(2,1)}, u32[]{:S(2)}, u32[]{:S(2)}) collective-permute-start(bf16[272,2048]{1,0:T(8,128)(2,1)} %copy-done.3), channel_id=1, source_target_pairs={{0,1},{1,0},{2,3},{3,2},{4,5},{5,4},{6,7},{7,6},{8,9},{9,8},{10,11... | collective-permute-start | bytes 3342344 | tf_op jit(solution)/shard_map/ppermute | solution.py:430
  40.5 26.9 %collective-permute-start.5 = (bf16[272,2048]{1,0:T(8,128)(2,1)}, bf16[272,2048]{1,0:T(8,128)(2,1)}, u32[]{:S(2)}, u32[]{:S(2)}) collective-permute-start(bf16[272,2048]{1,0:T(8,128)(2,1)} %get-tuple-element.89), channel_id=1, source_target_pairs={{0,8},{8,0},{16,24},{24,16},{1,9},{9,1},{17,25},{25,17},{2,10},{10... | collective-permute-start | bytes 3342344 | tf_op jit(solution)/shard_map/ppermute | solution.py:424
  41.0 25.2 %collective-permute-start.6 = (bf16[256,2048]{1,0:T(8,128)(2,1)}, bf16[256,2048]{1,0:T(8,128)(2,1)}, u32[]{:S(2)}, u32[]{:S(2)}) collective-permute-start(bf16[256,2048]{1,0:T(8,128)(2,1)} %get-tuple-element.90), channel_id=1, source_target_pairs={{0,16},{8,24},{16,0},{24,8},{1,17},{9,25},{17,1},{25,9},{2,18},{10... | collective-permute-start | bytes 3145736 | tf_op jit(solution)/shard_map/ppermute | solution.py:424
  41.5 31.2 %collective-permute-start.7 = (bf16[512,2048]{1,0:T(8,128)(2,1)S(1)}, bf16[512,2048]{1,0:T(8,128)(2,1)}, u32[]{:S(2)}, u32[]{:S(2)}) collective-permute-start(bf16[512,2048]{1,0:T(8,128)(2,1)S(1)} %bitcast.65), channel_id=1, source_target_pairs={{0,1},{1,0},{2,3},{3,2},{4,5},{5,4},{6,7},{7,6},{8,9},{9,8},{10,11... | collective-permute-start | bytes 6291464 | tf_op jit(solution)/shard_map/ppermute | solution.py:430
  67.3 5.4 %collective-permute-start.9 = (bf16[272,2048]{1,0:T(8,128)(2,1)}, bf16[272,2048]{1,0:T(8,128)(2,1)}, u32[]{:S(2)}, u32[]{:S(2)}) collective-permute-start(bf16[272,2048]{1,0:T(8,128)(2,1)} %collective-permute-done.5.refs_3_.refs_6_.refs_4_.refs_10_), channel_id=1, source_target_pairs={{0,1},{1,0},{2,3},{3,2},{4,5},{5,4},{6,7},{7,6},{8,9},{9,8},{10,11... | collective-permute-start | bytes 3342344 | tf_op jit(solution)/shard_map/ppermute | solution.py:430
  67.3 5.4 %collective-permute-start.11 = (bf16[256,2048]{1,0:T(8,128)(2,1)}, bf16[256,2048]{1,0:T(8,128)(2,1)}, u32[]{:S(2)}, u32[]{:S(2)}) collective-permute-start(bf16[256,2048]{1,0:T(8,128)(2,1)} %collective-permute-done.6.refs_5_.refs_8_.refs_9_.refs_7_.refs_12_), channel_id=1, source_target_pairs={{0,1},{1,0},{2,3},{3,2},{4,5},{5,4},{6,7},{7,6},{8,9},{9,8},{10,11... | collective-permute-start | bytes 3145736 | tf_op jit(solution)/shard_map/ppermute | solution.py:430
  71.6 25.4 %collective-permute-start.15 = (bf16[256,2048]{1,0:T(8,128)(2,1)}, bf16[256,2048]{1,0:T(8,128)(2,1)}, u32[]{:S(2)}, u32[]{:S(2)}) collective-permute-start(bf16[256,2048]{1,0:T(8,128)(2,1)} %get-tuple-element.99), channel_id=1, source_target_pairs={{0,8},{8,0},{16,24},{24,16},{1,9},{9,1},{17,25},{25,17},{2,10},{10... | collective-permute-start | bytes 3145736 | tf_op jit(solution)/shard_map/ppermute | solution.py:424
  72.2 25.1 %collective-permute-start.16 = (bf16[256,2048]{1,0:T(8,128)(2,1)}, bf16[256,2048]{1,0:T(8,128)(2,1)}, u32[]{:S(2)}, u32[]{:S(2)}) collective-permute-start(bf16[256,2048]{1,0:T(8,128)(2,1)} %get-tuple-element.100), channel_id=1, source_target_pairs={{0,16},{8,24},{16,0},{24,8},{1,17},{9,25},{17,1},{25,9},{2,18},{10... | collective-permute-start | bytes 3145736 | tf_op jit(solution)/shard_map/ppermute | solution.py:424
  79.2 18.1 %collective-permute-start.12 = (bf16[1024,128]{1,0:T(8,128)(2,1)}, bf16[1024,128]{1,0:T(8,128)(2,1)S(1)}, u32[]{:S(2)}, u32[]{:S(2)}) collective-permute-start(bf16[1024,128]{1,0:T(8,128)(2,1)} %get-tuple-element.97.refs_0_.refs_1_), channel_id=1, source_target_pairs={{0,2},{1,3},{2,0},{3,1},{4,6},{5,7},{6,4},{7,5},{8,10},{9,11},{10,... | collective-permute-start | bytes 786440 | tf_op jit(solution)/shard_map/ppermute | solution.py:427
  83.5 21.6 %collective-permute-start.13 = (bf16[1024,128]{1,0:T(8,128)(2,1)}, bf16[1024,128]{1,0:T(8,128)(2,1)S(1)}, u32[]{:S(2)}, u32[]{:S(2)}) collective-permute-start(bf16[1024,128]{1,0:T(8,128)(2,1)} %get-tuple-element.97.refs_0_.refs_1_), channel_id=1, source_target_pairs={{0,4},{1,5},{2,6},{3,7},{4,0},{5,1},{6,2},{7,3},{8,12},{9,13},{10,... | collective-permute-start | bytes 786440 | tf_op jit(solution)/shard_map/ppermute | solution.py:427
  84.6 20.5 %collective-permute-start.14 = (bf16[1024,128]{1,0:T(8,128)(2,1)}, bf16[1024,128]{1,0:T(8,128)(2,1)S(1)}, u32[]{:S(2)}, u32[]{:S(2)}) collective-permute-start(bf16[1024,128]{1,0:T(8,128)(2,1)} %get-tuple-element.97.refs_0_.refs_1_), channel_id=1, source_target_pairs={{0,6},{1,7},{2,4},{3,5},{4,2},{5,3},{6,0},{7,1},{8,14},{9,15},{10,... | collective-permute-start | bytes 786440 | tf_op jit(solution)/shard_map/ppermute | solution.py:427
  97.3 12.2 %copy-start.29 = (bf16[1024,128]{1,0:T(8,128)(2,1)}, bf16[1024,128]{1,0:T(8,128)(2,1)S(1)}, u32[]{:S(2)}) copy-start(bf16[1024,128]{1,0:T(8,128)(2,1)S(1)} %collective-permute-done.12.refs_1_) | copy-start | bytes 786436
  105.1 2.9 collective-permute-start.18
  105.2 4.4 %collective-permute-start.17 = (bf16[256,2048]{1,0:T(8,128)(2,1)}, bf16[256,2048]{1,0:T(8,128)(2,1)S(1)}, u32[]{:S(2)}, u32[]{:S(2)}) collective-permute-start(bf16[256,2048]{1,0:T(8,128)(2,1)} %collective-permute-done.15.refs_7_.refs_6_.refs_5_.refs_10_.refs_11_), channel_id=1, source_target_pairs={{0,1},{1,0},{2,3},{3,2},{4,5},{5,4},{6,7},{7,6},{8,9},{9,8},{10,11... | collective-permute-start | bytes 3145736 | tf_op jit(solution)/shard_map/ppermute | solution.py:430
  116.5 16.2 %collective-permute-start.22 = (bf16[1024,128]{1,0:T(8,128)(2,1)}, bf16[1024,128]{1,0:T(8,128)(2,1)S(1)}, u32[]{:S(2)}, u32[]{:S(2)}) collective-permute-start(bf16[1024,128]{1,0:T(8,128)(2,1)} %get-tuple-element.109.refs_0_.refs_1_), channel_id=1, source_target_pairs={{0,2},{1,3},{2,0},{3,1},{4,6},{5,7},{6,4},{7,5},{8,10},{9,11},{10,... | collective-permute-start | bytes 786440 | tf_op jit(solution)/shard_map/ppermute | solution.py:427
  120.9 21.5 %collective-permute-start.23 = (bf16[1024,128]{1,0:T(8,128)(2,1)}, bf16[1024,128]{1,0:T(8,128)(2,1)S(1)}, u32[]{:S(2)}, u32[]{:S(2)}) collective-permute-start(bf16[1024,128]{1,0:T(8,128)(2,1)} %get-tuple-element.109.refs_0_.refs_1_), channel_id=1, source_target_pairs={{0,4},{1,5},{2,6},{3,7},{4,0},{5,1},{6,2},{7,3},{8,12},{9,13},{10,... | collective-permute-start | bytes 786440 | tf_op jit(solution)/shard_map/ppermute | solution.py:427
  122.0 20.5 %collective-permute-start.24 = (bf16[1024,128]{1,0:T(8,128)(2,1)}, bf16[1024,128]{1,0:T(8,128)(2,1)S(1)}, u32[]{:S(2)}, u32[]{:S(2)}) collective-permute-start(bf16[1024,128]{1,0:T(8,128)(2,1)} %get-tuple-element.109.refs_0_.refs_1_), channel_id=1, source_target_pairs={{0,6},{1,7},{2,4},{3,5},{4,2},{5,3},{6,0},{7,1},{8,14},{9,15},{10,... | collective-permute-start | bytes 786440 | tf_op jit(solution)/shard_map/ppermute | solution.py:427
  149.2 15.9 %collective-permute-start.25 = (bf16[1024,128]{1,0:T(8,128)(2,1)}, bf16[1024,128]{1,0:T(8,128)(2,1)S(1)}, u32[]{:S(2)}, u32[]{:S(2)}) collective-permute-start(bf16[1024,128]{1,0:T(8,128)(2,1)} %get-tuple-element.115.refs_0_.refs_1_), channel_id=1, source_target_pairs={{0,2},{1,3},{2,0},{3,1},{4,6},{5,7},{6,4},{7,5},{8,10},{9,11},{10,... | collective-permute-start | bytes 786440 | tf_op jit(solution)/shard_map/ppermute | solution.py:427
  154.3 24.4 %collective-permute-start.26 = (bf16[1024,128]{1,0:T(8,128)(2,1)}, bf16[1024,128]{1,0:T(8,128)(2,1)S(1)}, u32[]{:S(2)}, u32[]{:S(2)}) collective-permute-start(bf16[1024,128]{1,0:T(8,128)(2,1)} %get-tuple-element.115.refs_0_.refs_1_), channel_id=1, source_target_pairs={{0,4},{1,5},{2,6},{3,7},{4,0},{5,1},{6,2},{7,3},{8,12},{9,13},{10,... | collective-permute-start | bytes 786440 | tf_op jit(solution)/shard_map/ppermute | solution.py:427
  155.3 23.3 %collective-permute-start.27 = (bf16[1024,128]{1,0:T(8,128)(2,1)}, bf16[1024,128]{1,0:T(8,128)(2,1)S(1)}, u32[]{:S(2)}, u32[]{:S(2)}) collective-permute-start(bf16[1024,128]{1,0:T(8,128)(2,1)} %get-tuple-element.115.refs_0_.refs_1_), channel_id=1, source_target_pairs={{0,6},{1,7},{2,4},{3,5},{4,2},{5,3},{6,0},{7,1},{8,14},{9,15},{10,... | collective-permute-start | bytes 786440 | tf_op jit(solution)/shard_map/ppermute | solution.py:427
  156.8 31.6 %collective-permute-start.19 = (bf16[32,1024]{1,0:T(8,128)(2,1)S(1)}, bf16[32,1024]{1,0:T(8,128)(2,1)S(1)}, u32[]{:S(2)}, u32[]{:S(2)}) collective-permute-start(bf16[32,1024]{1,0:T(8,128)(2,1)S(1)} %get-tuple-element.179), channel_id=1, source_target_pairs={{0,2},{1,3},{2,0},{3,1},{4,6},{5,7},{6,4},{7,5},{8,10},{9,11},{10,... | collective-permute-start | bytes 196616 | tf_op jit(solution)/shard_map/ppermute | solution.py:427
  157.9 30.6 %collective-permute-start.20 = (bf16[32,1024]{1,0:T(8,128)(2,1)S(1)}, bf16[32,1024]{1,0:T(8,128)(2,1)S(1)}, u32[]{:S(2)}, u32[]{:S(2)}) collective-permute-start(bf16[32,1024]{1,0:T(8,128)(2,1)S(1)} %get-tuple-element.178), channel_id=1, source_target_pairs={{0,4},{1,5},{2,6},{3,7},{4,0},{5,1},{6,2},{7,3},{8,12},{9,13},{10,... | collective-permute-start | bytes 196616 | tf_op jit(solution)/shard_map/ppermute | solution.py:427
  165.1 13.6 %copy-start.26 = (bf16[1024,128]{1,0:T(8,128)(2,1)}, bf16[1024,128]{1,0:T(8,128)(2,1)S(1)}, u32[]{:S(2)}) copy-start(bf16[1024,128]{1,0:T(8,128)(2,1)S(1)} %collective-permute-done.25.refs_1_) | copy-start | bytes 786436
  165.1 23.4 %collective-permute-start.21 = (bf16[32,1024]{1,0:T(8,128)(2,1)S(1)}, bf16[32,1024]{1,0:T(8,128)(2,1)S(1)}, u32[]{:S(2)}, u32[]{:S(2)}) collective-permute-start(bf16[32,1024]{1,0:T(8,128)(2,1)S(1)} %get-tuple-element.177), channel_id=1, source_target_pairs={{0,6},{1,7},{2,4},{3,5},{4,2},{5,3},{6,0},{7,1},{8,14},{9,15},{10,... | collective-permute-start | bytes 196616 | tf_op jit(solution)/shard_map/ppermute | solution.py:427
  185.3 20.4 %collective-permute-start.28 = (bf16[4096,128]{1,0:T(8,128)(2,1)}, bf16[4096,128]{1,0:T(8,128)(2,1)S(1)}, u32[]{:S(2)}, u32[]{:S(2)}) collective-permute-start(bf16[4096,128]{1,0:T(8,128)(2,1)} %get-tuple-element.123), channel_id=1, source_target_pairs={{0,8},{8,0},{16,24},{24,16},{1,9},{9,1},{17,25},{25,17},{2,10},{10... | collective-permute-start | bytes 3145736 | tf_op jit(solution)/shard_map/ppermute | solution.py:424
  186.9 18.8 %collective-permute-start.29 = (bf16[4096,128]{1,0:T(8,128)(2,1)}, bf16[4096,128]{1,0:T(8,128)(2,1)S(1)}, u32[]{:S(2)}, u32[]{:S(2)}) collective-permute-start(bf16[4096,128]{1,0:T(8,128)(2,1)} %get-tuple-element.124), channel_id=1, source_target_pairs={{0,16},{8,24},{16,0},{24,8},{1,17},{9,25},{17,1},{25,9},{2,18},{10... | collective-permute-start | bytes 3145736 | tf_op jit(solution)/shard_map/ppermute | solution.py:424
  197.9 12.5 %collective-permute-start.30 = (bf16[1040,128]{1,0:T(8,128)(2,1)}, bf16[1040,128]{1,0:T(8,128)(2,1)S(1)}, u32[]{:S(2)}, u32[]{:S(2)}) collective-permute-start(bf16[1040,128]{1,0:T(8,128)(2,1)} %get-tuple-element.126), channel_id=1, source_target_pairs={{0,2},{1,3},{2,0},{3,1},{4,6},{5,7},{6,4},{7,5},{8,10},{9,11},{10,... | collective-permute-start | bytes 798728 | tf_op jit(solution)/shard_map/ppermute | solution.py:427
  203.3 19.4 %collective-permute-start.31 = (bf16[1040,128]{1,0:T(8,128)(2,1)}, bf16[1040,128]{1,0:T(8,128)(2,1)S(1)}, u32[]{:S(2)}, u32[]{:S(2)}) collective-permute-start(bf16[1040,128]{1,0:T(8,128)(2,1)} %get-tuple-element.127), channel_id=1, source_target_pairs={{0,4},{1,5},{2,6},{3,7},{4,0},{5,1},{6,2},{7,3},{8,12},{9,13},{10,... | collective-permute-start | bytes 798728 | tf_op jit(solution)/shard_map/ppermute | solution.py:427
  204.3 18.3 %collective-permute-start.32 = (bf16[1040,128]{1,0:T(8,128)(2,1)}, bf16[1040,128]{1,0:T(8,128)(2,1)S(1)}, u32[]{:S(2)}, u32[]{:S(2)}) collective-permute-start(bf16[1040,128]{1,0:T(8,128)(2,1)} %get-tuple-element.128), channel_id=1, source_target_pairs={{0,6},{1,7},{2,4},{3,5},{4,2},{5,3},{6,0},{7,1},{8,14},{9,15},{10,... | collective-permute-start | bytes 798728 | tf_op jit(solution)/shard_map/ppermute | solution.py:427
  205.7 26.4 %copy-start.10 = (bf16[4096,128]{1,0:T(8,128)(2,1)}, bf16[4096,128]{1,0:T(8,128)(2,1)S(1)}, u32[]{:S(2)}) copy-start(bf16[4096,128]{1,0:T(8,128)(2,1)S(1)} %collective-permute-done.28.refs_9_) | copy-start | bytes 3145732
  205.7 16.9 %copy-start.11 = (bf16[4096,128]{1,0:T(8,128)(2,1)}, bf16[4096,128]{1,0:T(8,128)(2,1)S(1)}, u32[]{:S(2)}) copy-start(bf16[4096,128]{1,0:T(8,128)(2,1)S(1)} %collective-permute-done.29.refs_10_) | copy-start | bytes 3145732
  232.1 5.4 %collective-permute-start.34 = (bf16[4096,128]{1,0:T(8,128)(2,1)S(1)}, bf16[4096,128]{1,0:T(8,128)(2,1)S(1)}, u32[]{:S(2)}, u32[]{:S(2)}) collective-permute-start(bf16[4096,128]{1,0:T(8,128)(2,1)S(1)} %collective-permute-done.28.refs_9_), channel_id=1, source_target_pairs={{0,1},{1,0},{2,3},{3,2},{4,5},{5,4},{6,7},{7,6},{8,9},{9,8},{10,11... | collective-permute-start | bytes 3145736 | tf_op jit(solution)/shard_map/ppermute | solution.py:430
  232.2 6.9 %collective-permute-start.33 = (bf16[4096,128]{1,0:T(8,128)(2,1)S(1)}, bf16[4096,128]{1,0:T(8,128)(2,1)S(1)}, u32[]{:S(2)}, u32[]{:S(2)}) collective-permute-start(bf16[4096,128]{1,0:T(8,128)(2,1)S(1)} %copy-done.7), channel_id=1, source_target_pairs={{0,1},{1,0},{2,3},{3,2},{4,5},{5,4},{6,7},{7,6},{8,9},{9,8},{10,11... | collective-permute-start | bytes 3145736 | tf_op jit(solution)/shard_map/ppermute | solution.py:430
  232.7 35.1 %collective-permute-start.39 = (bf16[4096,128]{1,0:T(8,128)(2,1)S(1)}, bf16[4096,128]{1,0:T(8,128)(2,1)}, u32[]{:S(2)}, u32[]{:S(2)}) collective-permute-start(bf16[4096,128]{1,0:T(8,128)(2,1)S(1)} %copy-done.8), channel_id=1, source_target_pairs={{0,24},{8,16},{16,8},{24,0},{1,25},{9,17},{17,9},{25,1},{2,26},{10... | collective-permute-start | bytes 3145736 | tf_op jit(solution)/shard_map/ppermute | solution.py:424
  233.2 14.8 %collective-permute-start.35 = (bf16[1040,128]{1,0:T(8,128)(2,1)}, bf16[1040,128]{1,0:T(8,128)(2,1)S(1)}, u32[]{:S(2)}, u32[]{:S(2)}) collective-permute-start(bf16[1040,128]{1,0:T(8,128)(2,1)} %get-tuple-element.138), channel_id=1, source_target_pairs={{0,2},{1,3},{2,0},{3,1},{4,6},{5,7},{6,4},{7,5},{8,10},{9,11},{10,... | collective-permute-start | bytes 798728 | tf_op jit(solution)/shard_map/ppermute | solution.py:427
  236.5 21.8 %collective-permute-start.36 = (bf16[1040,128]{1,0:T(8,128)(2,1)}, bf16[1040,128]{1,0:T(8,128)(2,1)S(1)}, u32[]{:S(2)}, u32[]{:S(2)}) collective-permute-start(bf16[1040,128]{1,0:T(8,128)(2,1)} %get-tuple-element.139), channel_id=1, source_target_pairs={{0,4},{1,5},{2,6},{3,7},{4,0},{5,1},{6,2},{7,3},{8,12},{9,13},{10,... | collective-permute-start | bytes 798728 | tf_op jit(solution)/shard_map/ppermute | solution.py:427
  237.5 20.8 %copy-start.13 = (bf16[4096,128]{1,0:T(8,128)(2,1)}, bf16[4096,128]{1,0:T(8,128)(2,1)S(1)}, u32[]{:S(2)}) copy-start(bf16[4096,128]{1,0:T(8,128)(2,1)S(1)} %collective-permute-done.34.refs_13_) | copy-start | bytes 3145732
  237.5 20.8 %collective-permute-start.37 = (bf16[1040,128]{1,0:T(8,128)(2,1)}, bf16[1040,128]{1,0:T(8,128)(2,1)S(1)}, u32[]{:S(2)}, u32[]{:S(2)}) collective-permute-start(bf16[1040,128]{1,0:T(8,128)(2,1)} %get-tuple-element.140), channel_id=1, source_target_pairs={{0,6},{1,7},{2,4},{3,5},{4,2},{5,3},{6,0},{7,1},{8,14},{9,15},{10,... | collective-permute-start | bytes 798728 | tf_op jit(solution)/shard_map/ppermute | solution.py:427
  239.1 19.3 %copy-start.14 = (bf16[4096,128]{1,0:T(8,128)(2,1)}, bf16[4096,128]{1,0:T(8,128)(2,1)S(1)}, u32[]{:S(2)}) copy-start(bf16[4096,128]{1,0:T(8,128)(2,1)S(1)} %collective-permute-done.33.refs_12_) | copy-start | bytes 3145732
  267.8 7.8 %collective-permute-start.40 = (bf16[4096,128]{1,0:T(8,128)(2,1)}, bf16[4096,128]{1,0:T(8,128)(2,1)S(1)}, u32[]{:S(2)}, u32[]{:S(2)}) collective-permute-start(bf16[4096,128]{1,0:T(8,128)(2,1)} %collective-permute-done.39.refs_11_), channel_id=1, source_target_pairs={{0,1},{1,0},{2,3},{3,2},{4,5},{5,4},{6,7},{7,6},{8,9},{9,8},{10,11... | collective-permute-start | bytes 3145736 | tf_op jit(solution)/shard_map/ppermute | solution.py:430
  267.9 7.7 %collective-permute-start.38 = (bf16[4096,128]{1,0:T(8,128)(2,1)S(1)}, bf16[4096,128]{1,0:T(8,128)(2,1)S(1)}, u32[]{:S(2)}, u32[]{:S(2)}) collective-permute-start(bf16[4096,128]{1,0:T(8,128)(2,1)S(1)} %copy-done.12), channel_id=1, source_target_pairs={{0,1},{1,0},{2,3},{3,2},{4,5},{5,4},{6,7},{7,6},{8,9},{9,8},{10,11... | collective-permute-start | bytes 3145736 | tf_op jit(solution)/shard_map/ppermute | solution.py:430
  268.4 16.6 %collective-permute-start.41 = (bf16[1040,128]{1,0:T(8,128)(2,1)}, bf16[1040,128]{1,0:T(8,128)(2,1)S(1)}, u32[]{:S(2)}, u32[]{:S(2)}) collective-permute-start(bf16[1040,128]{1,0:T(8,128)(2,1)} %get-tuple-element.151), channel_id=1, source_target_pairs={{0,2},{1,3},{2,0},{3,1},{4,6},{5,7},{6,4},{7,5},{8,10},{9,11},{10,... | collective-permute-start | bytes 798728 | tf_op jit(solution)/shard_map/ppermute | solution.py:427
  273.0 21.8 %collective-permute-start.42 = (bf16[1040,128]{1,0:T(8,128)(2,1)}, bf16[1040,128]{1,0:T(8,128)(2,1)S(1)}, u32[]{:S(2)}, u32[]{:S(2)}) collective-permute-start(bf16[1040,128]{1,0:T(8,128)(2,1)} %get-tuple-element.152), channel_id=1, source_target_pairs={{0,4},{1,5},{2,6},{3,7},{4,0},{5,1},{6,2},{7,3},{8,12},{9,13},{10,... | collective-permute-start | bytes 798728 | tf_op jit(solution)/shard_map/ppermute | solution.py:427
  274.1 20.8 %collective-permute-start.43 = (bf16[1040,128]{1,0:T(8,128)(2,1)}, bf16[1040,128]{1,0:T(8,128)(2,1)S(1)}, u32[]{:S(2)}, u32[]{:S(2)}) collective-permute-start(bf16[1040,128]{1,0:T(8,128)(2,1)} %get-tuple-element.153), channel_id=1, source_target_pairs={{0,6},{1,7},{2,4},{3,5},{4,2},{5,3},{6,0},{7,1},{8,14},{9,15},{10,... | collective-permute-start | bytes 798728 | tf_op jit(solution)/shard_map/ppermute | solution.py:427
  275.5 23.7 %copy-start.15 = (bf16[4096,128]{1,0:T(8,128)(2,1)}, bf16[4096,128]{1,0:T(8,128)(2,1)S(1)}, u32[]{:S(2)}) copy-start(bf16[4096,128]{1,0:T(8,128)(2,1)S(1)} %collective-permute-done.40.refs_15_) | copy-start | bytes 3145732
  275.5 23.7 %copy-start.16 = (bf16[4096,128]{1,0:T(8,128)(2,1)}, bf16[4096,128]{1,0:T(8,128)(2,1)S(1)}, u32[]{:S(2)}) copy-start(bf16[4096,128]{1,0:T(8,128)(2,1)S(1)} %collective-permute-done.38.refs_14_) | copy-start | bytes 3145732
  299.3 5.9 %collective-permute-start.44 = (bf16[512,128]{1,0:T(8,128)(2,1)}, bf16[512,128]{1,0:T(8,128)(2,1)S(1)}, u32[]{:S(2)}, u32[]{:S(2)}) collective-permute-start(bf16[512,128]{1,0:T(8,128)(2,1)} %get-tuple-element.157), channel_id=1, source_target_pairs={{0,8},{1,9},{2,10},{3,11},{4,12},{5,13},{6,14},{7,15},{8,0},{9,1},... | collective-permute-start | bytes 393224 | tf_op jit(solution)/shard_map/ppermute | solution.py:590
  300.9 5.6 %collective-permute-start.45 = (bf16[512,128]{1,0:T(8,128)(2,1)}, bf16[512,128]{1,0:T(8,128)(2,1)S(1)}, u32[]{:S(2)}, u32[]{:S(2)}) collective-permute-start(bf16[512,128]{1,0:T(8,128)(2,1)} %get-tuple-element.158), channel_id=1, source_target_pairs={{0,16},{1,17},{2,18},{3,19},{4,20},{5,21},{6,22},{7,23},{8,24},{9,... | collective-permute-start | bytes 393224 | tf_op jit(solution)/shard_map/ppermute | solution.py:590
  302.3 7.5 %collective-permute-start.46 = (bf16[512,128]{1,0:T(8,128)(2,1)}, bf16[512,128]{1,0:T(8,128)(2,1)S(1)}, u32[]{:S(2)}, u32[]{:S(2)}) collective-permute-start(bf16[512,128]{1,0:T(8,128)(2,1)} %get-tuple-element.159), channel_id=1, source_target_pairs={{0,24},{1,25},{2,26},{3,27},{4,28},{5,29},{6,30},{7,31},{8,16},{9,... | collective-permute-start | bytes 393224 | tf_op jit(solution)/shard_map/ppermute | solution.py:590
  302.8 7.0 %collective-permute-start.47 = (bf16[512,128]{1,0:T(8,128)(2,1)}, bf16[512,128]{1,0:T(8,128)(2,1)S(1)}, u32[]{:S(2)}, u32[]{:S(2)}) collective-permute-start(bf16[512,128]{1,0:T(8,128)(2,1)} %get-tuple-element.160), channel_id=1, source_target_pairs={{0,1},{1,0},{2,3},{3,2},{4,5},{5,4},{6,7},{7,6},{8,9},{9,8},{10,11... | collective-permute-start | bytes 393224 | tf_op jit(solution)/shard_map/ppermute | solution.py:590
  302.8 7.0 %collective-permute-start.48 = (bf16[512,128]{1,0:T(8,128)(2,1)}, bf16[512,128]{1,0:T(8,128)(2,1)S(1)}, u32[]{:S(2)}, u32[]{:S(2)}) collective-permute-start(bf16[512,128]{1,0:T(8,128)(2,1)} %get-tuple-element.161), channel_id=1, source_target_pairs={{0,9},{1,8},{2,11},{3,10},{4,13},{5,12},{6,15},{7,14},{8,1},{9,0},... | collective-permute-start | bytes 393224 | tf_op jit(solution)/shard_map/ppermute | solution.py:590
  305.2 9.5 %collective-permute-start.49 = (bf16[512,128]{1,0:T(8,128)(2,1)}, bf16[512,128]{1,0:T(8,128)(2,1)S(1)}, u32[]{:S(2)}, u32[]{:S(2)}) collective-permute-start(bf16[512,128]{1,0:T(8,128)(2,1)} %get-tuple-element.162), channel_id=1, source_target_pairs={{0,17},{1,16},{2,19},{3,18},{4,21},{5,20},{6,23},{7,22},{8,25},{9,... | collective-permute-start | bytes 393224 | tf_op jit(solution)/shard_map/ppermute | solution.py:590
  306.4 8.2 %collective-permute-start.50 = (bf16[512,128]{1,0:T(8,128)(2,1)}, bf16[512,128]{1,0:T(8,128)(2,1)S(1)}, u32[]{:S(2)}, u32[]{:S(2)}) collective-permute-start(bf16[512,128]{1,0:T(8,128)(2,1)} %get-tuple-element.163), channel_id=1, source_target_pairs={{0,25},{1,24},{2,27},{3,26},{4,29},{5,28},{6,31},{7,30},{8,17},{9,... | collective-permute-start | bytes 393224 | tf_op jit(solution)/shard_map/ppermute | solution.py:590
  336.9 1.4 collective-permute-start.51
  339.1 7.7 %collective-permute-start.52 = (f32[8,128]{1,0:T(8,128)S(1)}, f32[8,128]{1,0:T(8,128)S(1)}, u32[]{:S(2)}, u32[]{:S(2)}) collective-permute-start(f32[8,128]{1,0:T(8,128)S(1)} %add.62.refs_0_), channel_id=1, source_target_pairs={{0,2},{1,3},{2,0},{3,1},{4,6},{5,7},{6,4},{7,5},{8,10},{9,11},{10,... | collective-permute-start | bytes 12296 | tf_op jit(solution)/shard_map/ppermute | solution.py:427
  344.2 4.5 %collective-permute-start.53 = (f32[8,128]{1,0:T(8,128)S(1)}, f32[8,128]{1,0:T(8,128)S(1)}, u32[]{:S(2)}, u32[]{:S(2)}) collective-permute-start(f32[8,128]{1,0:T(8,128)S(1)} %add.62.refs_0_), channel_id=1, source_target_pairs={{0,4},{1,5},{2,6},{3,7},{4,0},{5,1},{6,2},{7,3},{8,12},{9,13},{10,... | collective-permute-start | bytes 12296 | tf_op jit(solution)/shard_map/ppermute | solution.py:427
  345.3 5.4 %collective-permute-start.54 = (f32[8,128]{1,0:T(8,128)S(1)}, f32[8,128]{1,0:T(8,128)S(1)}, u32[]{:S(2)}, u32[]{:S(2)}) collective-permute-start(f32[8,128]{1,0:T(8,128)S(1)} %add.62.refs_0_), channel_id=1, source_target_pairs={{0,6},{1,7},{2,4},{3,5},{4,2},{5,3},{6,0},{7,1},{8,14},{9,15},{10,... | collective-permute-start | bytes 12296 | tf_op jit(solution)/shard_map/ppermute | solution.py:427
  (38 other events, 155.4 us)

commit v3 on v2

v3 whole, which is shorter than its diff:
```python
import functools
import math

import jax
import jax.numpy as jnp
from jax import lax
from jax.experimental import pallas as pl
from jax.experimental.pallas import tpu as pltpu
from jax.sharding import PartitionSpec as P

HEAD = 128
F32 = jnp.float32
BF16 = jnp.bfloat16
PAD = 16
LIMIT = 24
TILE = 4
VMEM = pl.BlockSpec(memory_space=pltpu.VMEM)
SMEM = pl.BlockSpec(memory_space=pltpu.SMEM)
HBM = pl.BlockSpec(memory_space=pltpu.HBM)


def shrink(magnitude, threshold):
    return jnp.maximum(magnitude - threshold, 0.0) / jnp.maximum(magnitude, threshold)


HOLDS = (
    ("own own", "x1 x2", "y2 y1", "y2 x2"),
    ("x1 x2", "own own", "y3 x3", "y3 y1"),
    ("y2 y1", "y3 x3", "own own", "x1 x3"),
    ("y3 x3", "y2 y1", "x1 x2", "own own"),
)


def holders(layer):
    names = sorted({name for row in HOLDS[layer] for name in row.split()})
    names.remove("own")
    return ["own"] + names


def turns(ways):
    return [0] + list(reversed(range(1, ways)))


def places():
    place = lax.axis_index("dp")
    return place // 2, place % 2, lax.axis_index("pipe")


def live_copy(layer, section, live_hbm, live, sem):
    count = live.shape[0]
    start = pl.multiple_of((section ^ layer) * count, count)
    return pltpu.make_async_copy(live_hbm.at[pl.ds(start, count)], live, sem)


def live_row(live, column, number, shape):
    return live[column * shape[1] + number]


def split_kernel(own, extra, first, second, sems):
    height = own.shape[0] // 2
    copies = []
    for number, out in enumerate((first, second)):
        half = own.at[pl.ds(number * height, height)]
        copies.append((half, out.at[pl.ds(0, height)], sems.at[2 * number]))
        copies.append((extra, out.at[pl.ds(height, PAD)], sems.at[2 * number + 1]))
    for source, target, sem in copies:
        pltpu.make_async_copy(source, target, sem).start()
    for source, target, sem in copies:
        pltpu.make_async_copy(source, target, sem).wait()


def pick_kernel(layer_round, height, own, x1, y1, x_out, y_out, sems):
    section = places()[2]
    half = pl.ds(0, height)
    cases = (
        (x_out.at[half], own.at[pl.ds(height, height)], y1.at[half], 2),
        (y_out.at[half], own.at[half], x1.at[half], 1),
    )
    for number, (out, mine, received, place) in enumerate(cases):
        passes = (section == place) == (layer_round == 2)

        @pl.when(passes)
        def _(out=out, received=received, number=number):
            pltpu.make_async_copy(received, out, sems.at[number]).start()

        @pl.when(jnp.logical_not(passes))
        def _(out=out, mine=mine, number=number):
            pltpu.make_async_copy(mine, out, sems.at[number]).start()

    if layer_round == 2:
        extra = pl.ds(height, PAD)
        pltpu.make_async_copy(y1.at[extra], x_out.at[extra], sems.at[2]).start()
        pltpu.make_async_copy(y1.at[extra], x_out.at[extra], sems.at[2]).wait()
    for number, (out, _, received, _) in enumerate(cases):
        pltpu.make_async_copy(received, out, sems.at[number]).wait()


def weight_copies(layer, section_here, refs, buffer, sems):
    names = holders(layer)
    height = buffer.shape[0] // 8
    for group in range(8):
        owner, quarter = group // 4, group % 4
        held = dict(zip(names, refs[owner * len(names) : (owner + 1) * len(names)]))
        target = buffer.at[pl.ds(group * height, height)]
        for section, row in enumerate(HOLDS[layer]):
            name = row.split()[quarter // 2]
            first = quarter if name == "own" else quarter % 2
            source = held[name].at[pl.ds(first * height, height)]

            @pl.when(section_here == section)
            def _(source=source, target=target, group=group):
                pltpu.make_async_copy(source, target, sems.at[group]).start()

    def wait(group):
        target = buffer.at[pl.ds(group * height, height)]
        pltpu.make_async_copy(refs[0].at[pl.ds(0, height)], target, sems.at[group]).wait()

    return wait


def load_kernel(layer, *refs):
    refs, (out, sems) = refs[:-2], refs[-2:]
    wait = weight_copies(layer, places()[2], refs, out, sems)
    for group in range(8):
        wait(group)


def gather_kernel(*refs):
    refs, (out, sems) = refs[:-2], refs[-2:]
    for number, ref in enumerate(refs):
        pltpu.make_async_copy(ref, out.at[number], sems.at[number]).start()
    for number, ref in enumerate(refs):
        pltpu.make_async_copy(ref, out.at[number], sems.at[number]).wait()


def column_loop(line, core, own_columns, body, wait):
    taken, count = max(1, 4 // own_columns), max(1, own_columns // 4)

    @pl.loop(0, 8 // taken)
    def _(turn):
        for i in range(taken if wait else 0):
            wait(turn * taken + i)
        for i in range(count):
            slot = turn * count + i
            local = slot ^ (core * own_columns)
            body(slot, local, line * 2 * own_columns + local)


def forward_kernel(layer, ways, live_shape, live_hbm, *refs):
    line, core, section = places()
    whole, last = layer == 0, layer == len(HOLDS) - 1
    count = 1 if whole else ways
    shards, refs = refs[:count], refs[count:]
    if last:
        arriving_ref, refs = refs[0], refs[1:]
    loaded = layer > 1
    held = 1 if loaded else 2 * len(holders(layer))
    weight_refs, refs = refs[:held], refs[held:]
    if not whole:
        refs = refs[len(HOLDS) :]
    outs = 2 + ways if last else 3
    outputs, refs = refs[:outs], refs[outs:]
    sends, refs = refs[: len(HOLDS)], refs[len(HOLDS) :]
    u_ref, send_sem, live, live_sem = refs[:4]
    refs = refs[4:]
    if loaded:
        buffer, wait = weight_refs[0], None
    else:
        (buffer, sems), refs = refs[:2], refs[2:]
        wait = weight_copies(layer, section, weight_refs, buffer, sems)
    live_copy(layer, section, live_hbm, live, live_sem.at[0]).start()
    r_ref = outputs[0]
    z_ref = refs[0] if last else outputs[1]
    features, tokens = u_ref.shape
    rows = z_ref.shape[0]
    live_count = live_shape[1]
    block = buffer.shape[1] // live_count
    total = jnp.zeros((1, tokens), F32)
    for shard in shards:
        value = shard[...].astype(F32)
        total = total + jnp.sum(value * value, axis=0, keepdims=True)
    inverse = lax.rsqrt(total * (1.0 / features) + 1e-05)
    r_ref[...] = jnp.broadcast_to(inverse, r_ref.shape)
    if whole:
        u_ref[...] = (shards[0][...].astype(F32) * inverse).astype(BF16)
    else:
        for step, shard in zip(turns(ways), shards):
            u_ref[pl.ds((line ^ step) * rows, rows), :] = (
                shard[...].astype(F32) * inverse
            ).astype(BF16)
    for step, send in enumerate(sends):

        @pl.when((section ^ step) == layer)
        def _(send=send):
            pltpu.make_async_copy(u_ref, send, send_sem.at[0]).start()

    width = TILE * block
    tiles = live_count // TILE
    live_copy(layer, section, live_hbm, live, live_sem.at[0]).wait()

    def picked(column_index, tile):
        return jnp.concatenate(
            [
                u_ref[
                    pl.ds(
                        live_row(live, column_index, tile * TILE + i, live_shape) * block,
                        block,
                    ),
                    :,
                ]
                for i in range(TILE)
            ],
            axis=0,
        )

    def column(slot, local, column_index):
        acc = jnp.zeros((2 * block, 2 * tokens), F32)
        at = pl.ds(slot * block, block)
        for tile in range(tiles // 2):
            other = tile + tiles // 2
            lhs = jnp.concatenate(
                [
                    buffer[at, pl.ds(tile * width, width)],
                    buffer[at, pl.ds(other * width, width)],
                ],
                axis=0,
            )
            rhs = jnp.concatenate(
                [picked(column_index, tile), picked(column_index, other)], axis=1
            )
            acc = acc + jnp.dot(lhs, rhs, preferred_element_type=F32)
        z_ref[pl.ds(local * block, block), :] = acc[:block, :tokens] + acc[block:, tokens:]

    column_loop(line, core, rows // block // 2, column, wait)
    if last:
        held_weights = (buffer, live, refs[1])
        backward_products(
            line, core, arriving_ref[...], z_ref[...], held_weights, live_shape, outputs[1], outputs[2:]
        )
    pltpu.make_async_copy(u_ref, sends[0], send_sem.at[0]).wait()
    if not last:
        own = shards[0][pl.ds(line * rows, rows), :] if whole else shards[0][...]
        pre = z_ref[...]
        outputs[2][...] = (own.astype(F32) + pre * jax.nn.sigmoid(pre)).astype(BF16)


def pre_gradient(arriving, pre):
    sigmoid = jax.nn.sigmoid(pre)
    return (arriving.astype(F32) * (sigmoid * (1.0 + pre * (1.0 - sigmoid)))).astype(BF16)


def backward_products(line, core, arriving, pre, held_weights, live_shape, gz_ref, outgoing):
    buffer, live, du_ref = held_weights
    rows, tokens = gz_ref.shape
    gz = pre_gradient(arriving, pre)
    gz_ref[...] = gz
    share = jnp.sum(gz.astype(F32) * pre, axis=0, keepdims=True)
    high = share.astype(BF16).astype(F32)
    low = share - high
    row = lax.broadcasted_iota(jnp.int32, (PAD, tokens), 0)
    extra = jnp.where(row == 0, high, jnp.where(row == 1, low, 0.0)).astype(BF16)
    du_ref[...] = jnp.zeros_like(du_ref)
    live_count = live_shape[1]
    block = buffer.shape[1] // live_count

    width = TILE * block
    tiles = live_count // TILE

    def column(slot, local, column_index):
        gz_block = gz_ref[pl.ds(local * block, block), :]
        empty = jnp.zeros_like(gz_block)
        rhs = jnp.concatenate(
            [
                jnp.concatenate([gz_block, empty], axis=1),
                jnp.concatenate([empty, gz_block], axis=1),
            ],
            axis=0,
        )
        at = pl.ds(slot * block, block)
        for tile in range(tiles // 2):
            other = tile + tiles // 2
            lhs = jnp.concatenate(
                [
                    buffer[at, pl.ds(tile * width, width)],
                    buffer[at, pl.ds(other * width, width)],
                ],
                axis=0,
            )
            product = lax.dot_general(
                lhs, rhs, (((0,), (0,)), ((), ())), preferred_element_type=F32
            )
            for side, first_block in enumerate((tile * TILE, other * TILE)):
                for i in range(TILE):
                    row = live_row(live, column_index, first_block + i, live_shape)
                    du_ref[pl.ds(row * block, block), :] += product[
                        i * block : (i + 1) * block, side * tokens : (side + 1) * tokens
                    ]

    column_loop(line, core, rows // block // 2, column, None)
    for step, share_ref in zip(turns(len(outgoing)), outgoing):
        share_ref[pl.ds(0, rows), :] = du_ref[pl.ds((line ^ step) * rows, rows), :].astype(BF16)
        share_ref[pl.ds(rows, PAD), :] = extra


def backward_kernel(layer, ways, live_shape, live_hbm, *refs):
    line, core, section = places()
    last = layer == 0
    older_ref, h_ref, r_ref = refs[:3]
    shares, refs = refs[3 : 3 + ways], refs[3 + ways :]
    pre_ref, refs = refs[0], refs[1:]
    if last:
        others, refs = refs[: len(HOLDS) - 1], refs[len(HOLDS) - 1 :]
        sorted_refs, (gz_ref,) = refs[:-1], refs[-1:]
    else:
        buffer, refs = refs[0], refs[1:]
        gz_ref, refs = refs[0], refs[1:]
        outgoing, refs = refs[:ways], refs[ways:]
        g_ref, refs = refs[0], refs[1:]
        du_ref, live, live_sem = refs
        live_copy(layer, section, live_hbm, live, live_sem.at[0]).start()
    rows, tokens = gz_ref.shape
    total = shares[0][pl.ds(0, rows), :].astype(F32)
    means = shares[0][pl.ds(rows, PAD), :].astype(F32)
    for share in shares[1:]:
        total = total + share[pl.ds(0, rows), :].astype(F32)
        means = means + share[pl.ds(rows, PAD), :].astype(F32)
    mean = jnp.sum(means, axis=0, keepdims=True) * (1.0 / (rows * ways))
    inverse = r_ref[0:1, :]
    scaled = h_ref[...].astype(F32) * inverse
    arriving = (older_ref[...].astype(F32) + inverse * (total - scaled * mean)).astype(BF16)
    if not last:
        g_ref[...] = arriving
    pre = pre_ref[...]
    if last:
        gz_ref[...] = pre_gradient(arriving, pre)
        half = rows // 2
        for step in range(len(HOLDS)):
            for number, source in enumerate((gz_ref, *others)):

                @pl.when((section ^ step) == number)
                def _(step=step, source=source):
                    for flip in range(2):
                        sorted_refs[2 * step + flip][...] = source[
                            pl.ds((core ^ flip) * half, half), :
                        ]

        return

    live_copy(layer, section, live_hbm, live, live_sem.at[0]).wait()
    held_weights = (buffer, live, du_ref)
    backward_products(line, core, arriving, pre, held_weights, live_shape, gz_ref, outgoing)


def segment_sum(row, width):
    lanes = row.shape[-1]
    lane = lax.broadcasted_iota(jnp.int32, row.shape, row.ndim - 1)
    step = 1
    while step < width:
        ahead = pltpu.roll(row, lanes - step, row.ndim - 1)
        behind = pltpu.roll(row, step, row.ndim - 1)
        row = row + jnp.where((lane // step) % 2 == 0, ahead, behind)
        step *= 2
    return row


def update_kernel(chunks, inverse_tokens, live_shape, live, *refs):
    gz_refs, u_ref, refs = refs[:chunks], refs[chunks], refs[chunks + 1 :]
    weight_ref, moment_ref, second_ref, head_ref = refs[:4]
    moment_out, second_out, stepped_ref, factor_ref, heads_ref, square_ref = refs[4:]
    column = pl.program_id(0)
    column_index = lax.axis_index("dp") * pl.num_programs(0) + column
    block, wide = weight_ref.shape[1:]
    live_count = wide // block
    rate = 0.1 / math.sqrt(wide)

    @pl.when(column == 0)
    def _():
        square_ref[...] = jnp.zeros_like(square_ref)

    lhs = jnp.concatenate([gz[...] for gz in gz_refs], axis=1)
    for tile in range(live_count // TILE):
        picked = jnp.concatenate(
            [
                jnp.concatenate(
                    [
                        u_ref[
                            number,
                            pl.ds(
                                live_row(live, column_index, tile * TILE + i, live_shape) * block,
                                block,
                            ),
                            :,
                        ]
                        for number in range(chunks)
                    ],
                    axis=1,
                )
                for i in range(TILE)
            ],
            axis=0,
        )
        gradient = (
            lax.dot_general(
                lhs, picked, (((1,), (1,)), ((), ())), preferred_element_type=F32
            )
            * inverse_tokens
        )
        at = pl.ds(tile * TILE * block, TILE * block)
        moment = 0.9 * moment_ref[0, :, at] + 0.1 * gradient
        second = 0.95 * second_ref[0, :, at] + 0.05 * gradient * gradient
        stepped = weight_ref[0, :, at].astype(F32) - rate * moment / (jnp.sqrt(second) + 1e-08)
        moment_out[0, :, at] = moment
        second_out[0, :, at] = second
        stepped_ref[0, :, at] = stepped.astype(BF16)
        square_ref[pl.ds(column, 1), at] = jnp.sum(stepped * stepped, axis=0, keepdims=True)

    @pl.when(column == pl.num_programs(0) - 1)
    def _():
        squares = segment_sum(square_ref[...], block)
        factor = shrink(jnp.sqrt(squares), 0.15 * math.sqrt(block / live_count))
        factor_ref[...] = factor
        leafed = factor * factor * squares * (1.0 / block)
        head = head_ref[...]
        lane = lax.broadcasted_iota(jnp.int32, heads_ref.shape, 1)
        heads = jnp.zeros(heads_ref.shape, F32)
        for number in range(live_shape[0] * block // HEAD):
            share = jnp.sum(jnp.where(head == number, leafed, 0.0), axis=0, keepdims=True)
            heads = jnp.where(lane == number, jnp.sum(share, axis=1, keepdims=True), heads)
        heads_ref[...] = heads


def output_kernel(parts, features, *refs):
    head_refs, refs = refs[:parts], refs[parts:]
    head_ref, factor_ref, stepped_ref, out_ref, scale_ref = refs
    column = pl.program_id(0)

    @pl.when(column == 0)
    def _():
        squares = head_refs[0][0:1, :]
        for ref in head_refs[1:]:
            squares = squares + ref[0:1, :]
        head_factor = shrink(jnp.sqrt(squares), 0.45 * math.sqrt(HEAD))
        layer = jnp.sum(head_factor * head_factor * squares, axis=1, keepdims=True)
        head_factor = head_factor * shrink(jnp.sqrt(layer), 0.45 * math.sqrt(features))
        head_factor = jnp.broadcast_to(head_factor, (scale_ref.shape[0], HEAD))
        for at in range(0, scale_ref.shape[1], HEAD):
            chosen = jnp.take_along_axis(
                head_factor, head_ref[:, at : at + HEAD], axis=1, mode="promise_in_bounds"
            )
            scale_ref[:, at : at + HEAD] = chosen * factor_ref[:, at : at + HEAD]

    count = out_ref.shape[0]
    for i in range(count):
        scale = scale_ref[pl.ds(column * count + i, 1), :]
        out_ref[i] = (stepped_ref[i].astype(F32) * scale).astype(BF16)


def kernel_call(kernel, name, outs, in_specs, out_specs, limit_mib, **kwargs):
    return pl.pallas_call(
        kernel,
        out_shape=outs,
        in_specs=in_specs,
        out_specs=out_specs,
        compiler_params=pltpu.CompilerParams(vmem_limit_bytes=limit_mib << 20),
        name=name,
        **kwargs,
    )


def in_hbm(values):
    return [pltpu.with_memory_space_constraint(value, pltpu.HBM) for value in values]


def in_vmem(values):
    return [pltpu.with_memory_space_constraint(value, pltpu.VMEM) for value in values]


def after(value, *others):
    return lax.optimization_barrier((value, *others))[0]


def local(x_in, cotangent, weights, live_rows, moment, second):
    sections = lax.axis_size("pipe")
    devices = lax.axis_size("dp")
    ways = devices // 2
    section = lax.axis_index("pipe")
    place = lax.axis_index("dp")
    line, core = (place // 2, place % 2)
    micro_count, share, features = x_in.shape
    own_columns, block, wide = weights.shape[1:]
    columns = 2 * own_columns
    rows = columns * block
    tokens = ways * share

    def to_pipe(value, step):
        return lax.ppermute(value, "pipe", [(i, i ^ step) for i in range(sections)])

    def to_line(value, step):
        return lax.ppermute(value, "dp", [(i, i ^ (2 * step)) for i in range(devices)])

    def along_line(values):
        pairs = zip(turns(ways), values)
        return [to_line(value, step) if step else value for step, value in pairs]

    def to_core(value):
        return lax.ppermute(value, "dp", [(i, i ^ 1) for i in range(devices)])

    own_live = live_rows[0]
    flat_live = own_live.reshape(-1)

    x_own = lax.dynamic_index_in_dim(x_in, section, 0, keepdims=False)
    own = weights[0].reshape(own_columns * block, wide)
    height = own_columns * block // 2
    extra = jnp.pad(flat_live.astype(BF16).reshape(1, wide), ((0, PAD - 1), (0, 0)))
    half1, half2 = kernel_call(
        split_kernel,
        "split",
        [jax.ShapeDtypeStruct((height + PAD, wide), BF16)] * 2,
        [HBM] * 2,
        [VMEM] * 2,
        LIMIT,
        scratch_shapes=[pltpu.SemaphoreType.DMA((4,))],
    )(*in_hbm((own, extra)))

    def slot(x_value, y_value, *extra):
        return lax.optimization_barrier((to_pipe(x_value, 1), to_pipe(y_value, 2), *extra))

    def pick(layer_round, first_source, second_source):
        return kernel_call(
            functools.partial(pick_kernel, layer_round, height),
            f"pick{layer_round}",
            [
                jax.ShapeDtypeStruct((height + (PAD if layer_round == 2 else 0), wide), BF16),
                jax.ShapeDtypeStruct((height, wide), BF16),
            ],
            [HBM] * 3,
            [VMEM] * 2,
            LIMIT,
            scratch_shapes=[pltpu.SemaphoreType.DMA((3,))],
        )(*in_hbm((own, first_source, second_source)))

    x_parts = {step: to_line(x_own, step) for step in turns(ways)[1:]}
    x1, y1, *sent = slot(half1, half2, *x_parts.values())
    x_parts = dict(zip(x_parts, sent))
    siblings = dict(own=to_core(after(own, x1, y1)), x1=to_core(x1), y1=to_core(y1))
    cot_own = lax.dynamic_index_in_dim(cotangent, section, 0, keepdims=False)
    cot_parts = [
        lax.dynamic_slice_in_dim(cot_own, (line ^ step) * rows, rows, 1) for step in range(ways)
    ]
    cot_held = after(tuple(cot_parts), *siblings.values())
    cot_sent = [to_line(cot_held[step], step) for step in range(1, ways)]
    x_all = jnp.zeros((ways, share, features), BF16)
    for step, part in [(0, x_own), *x_parts.items()]:
        x_all = lax.dynamic_update_index_in_dim(x_all, part, line ^ step, 0)
    x_all = x_all.reshape(tokens, features).T
    third = tuple(pick(3, x1, after(y1, *siblings.values())))
    by_step = [flat_live] + [value[height].astype(jnp.int32) for value in (x1, y1)]
    near_live = jnp.concatenate([*by_step])
    x2, y2, x_all, near_live, *sent = slot(
        *pick(2, x1, y1), x_all, near_live, *third, *cot_sent
    )
    third, cot_sent = sent[:2], sent[2:]
    cot_all = jnp.zeros((ways, share, rows), BF16)
    for step, part in enumerate([cot_parts[0], *cot_sent]):
        cot_all = lax.dynamic_update_index_in_dim(cot_all, part, line ^ step, 0)
    cot_all = cot_all.reshape(tokens, rows).T
    mine = dict(own=own, x1=x1, x2=x2, y1=y1, y2=y2)
    siblings.update(x2=to_core(x2), y2=to_core(y2))
    x3, y3 = slot(*after(tuple(third), x2, y2))
    mine.update(x3=x3, y3=y3)
    live_shape = own_live.shape
    live = jnp.concatenate([near_live, x2[height].astype(jnp.int32)])
    live_scratch = [pltpu.SMEM((own_live.size,), jnp.int32), pltpu.SemaphoreType.DMA((1,))]

    def layer_weights(layer):
        names = holders(layer)
        return in_hbm([mine[name] for name in names] + [siblings[name] for name in names])

    def sds(shape, dtype):
        return jax.ShapeDtypeStruct(shape, dtype)

    def load(layer, ready):
        operands = layer_weights(layer)
        return kernel_call(
            functools.partial(load_kernel, layer),
            f"load{layer}",
            pltpu.VMEM((columns * block, wide), BF16),
            [HBM] * len(operands),
            VMEM,
            LIMIT,
            scratch_shapes=[pltpu.SemaphoreType.DMA((8,))],
            cost_estimate=pl.CostEstimate(
                flops=0, transcendentals=0, bytes_accessed=16 * columns * block * wide
            ),
        )(*in_hbm([after(operands[0], ready)]), *operands[1:])

    loaded = {}
    weight_scratch = [pltpu.VMEM((columns * block, wide), BF16)]
    shards = in_hbm([x_all])
    entering, inverses, pre_acts, sends = [None], [], [], []
    for layer in range(sections):
        last = layer == sections - 1
        outs = [sds((8, tokens), F32)]
        scratch = [
            pltpu.VMEM((features, tokens), BF16),
            pltpu.SemaphoreType.DMA((1,)),
            *live_scratch,
        ]
        if layer < 2:
            scratch += weight_scratch + [pltpu.SemaphoreType.DMA((8,))]
        if last:
            shards.append(cot_all)
            outs += [sds((rows, tokens), BF16)] + [sds((rows + PAD, tokens), BF16)] * ways
            scratch += [pltpu.VMEM((rows, tokens), F32), pltpu.VMEM((features, tokens), F32)]
        else:
            outs += [pltpu.VMEM((rows, tokens), F32), pltpu.VMEM((rows, tokens), BF16)]
        plain = len(outs)
        outs += [pltpu.HBM((features, tokens), BF16)] * sections
        operands = in_vmem([loaded[layer]]) if layer in loaded else layer_weights(layer)
        before = 1 + len(shards) + len(operands)
        result = kernel_call(
            functools.partial(forward_kernel, layer, ways, live_shape),
            f"forward{layer}",
            outs,
            [HBM]
            + [VMEM] * len(shards)
            + [VMEM if layer in loaded else HBM] * len(operands)
            + [HBM] * len(sends),
            [VMEM] * plain + [HBM] * sections,
            LIMIT,
            scratch_shapes=scratch,
            input_output_aliases={before + i: plain + i for i in range(len(sends))},
        )(*in_hbm([live]), *shards, *operands, *in_hbm(sends))
        inverses.append(result[0])
        sends = result[plain:]
        if not last:
            pre_acts.append(result[1])
            entering.append(result[2])
            shards = along_line([result[2]] * ways)
            if layer > 0:
                loaded[layer + 1] = load(layer + 1, result[2])
            if layer == 2:
                loaded[1] = load(1, result[2])
            if layer == 0:
                for name in ("x3", "y3"):
                    siblings[name] = to_core(after(mine[name], *shards[1:]))

    u_chunks, u_siblings = [sends[0]] + [None] * (sections - 1), [None] * sections
    u_chunks[1], u_chunks[2] = (to_pipe(sends[1], 1), to_pipe(sends[2], 2))
    gradients = [None] * sections
    older, result = cot_all, result[1:plain]
    for layer in reversed(range(sections)):
        if layer < sections - 1:
            if layer == 0:
                outs = [sds((rows // 2, tokens), BF16)] * (2 * sections)
                operands = gradients[1:]
                specs, scratch = [VMEM] * len(operands), [pltpu.VMEM((rows, tokens), BF16)]
            else:
                outs = [sds((rows, tokens), BF16)]
                outs += [sds((rows + PAD, tokens), BF16)] * ways
                outs += [sds((rows, tokens), BF16)]
                operands = in_vmem([loaded[layer]])
                specs = [VMEM]
                scratch = [pltpu.VMEM((features, tokens), F32), *live_scratch]
            operands = arriving + in_vmem([pre_acts[layer]]) + operands
            result = kernel_call(
                functools.partial(backward_kernel, layer, ways, live_shape),
                f"backward{layer}",
                outs,
                [HBM] + [VMEM] * (len(arriving) + 1) + specs,
                [VMEM] * len(outs),
                LIMIT,
                scratch_shapes=scratch,
            )(*in_hbm([live]), *operands)
            if layer == 0:
                break
            older = result[1 + ways]
        gradients[layer] = result[0]
        outgoing = result[1 : 1 + ways]
        incoming = along_line(outgoing)
        if layer == sections - 1:
            incoming[0] = after(incoming[0], u_chunks[1], u_chunks[2])
            u_chunks[3] = to_pipe(after(sends[3], *incoming), 3)
        elif layer == sections - 2:
            for number in (0, 1):
                u_siblings[number] = to_core(after(u_chunks[number], result[0]))
            incoming[0] = after(incoming[0], *u_siblings[:2])
        else:
            for number in (2, 3):
                u_siblings[number] = to_core(after(u_chunks[number], result[0]))
            incoming[0] = after(incoming[0], *u_siblings[2:])
        arriving = [older, entering[layer], inverses[layer]] + incoming
    u_chunks = in_hbm(u_chunks + u_siblings)
    held_chunks = kernel_call(
        gather_kernel,
        "gather_u",
        pltpu.VMEM((len(u_chunks), features, tokens), BF16),
        [HBM] * len(u_chunks),
        VMEM,
        LIMIT,
        scratch_shapes=[pltpu.SemaphoreType.DMA((len(u_chunks),))],
        cost_estimate=pl.CostEstimate(
            flops=0, transcendentals=0, bytes_accessed=8 * len(u_chunks) * features * tokens
        ),
    )(*u_chunks)

    gz_chunks = [None] * (2 * sections)
    order = [(step, flip) for step in (3, 1, 2) for flip in range(2)] + [(0, 1), (0, 0)]
    for step, flip in order:
        value = result[2 * step + flip]
        if step or flip:
            value = lax.ppermute(
                value,
                ("pipe", "dp"),
                [
                    (i * devices + j, (i ^ step) * devices + (j ^ flip))
                    for i in range(sections)
                    for j in range(devices)
                ],
            )
        gz_chunks[flip * sections + step] = value

    chunks = len(gz_chunks)
    all_tokens = micro_count * devices * share
    padded = max(8, own_columns)
    own_index = lax.dynamic_slice_in_dim(own_live, place * own_columns, own_columns, 0)
    head = jnp.repeat(own_index // (HEAD // block), block, axis=1)
    head = jnp.concatenate([head, jnp.zeros((padded - own_columns, wide), jnp.int32)], axis=0)
    per_column = pl.BlockSpec((1, block, wide), lambda j, *_: (j, 0, 0))
    per_pair = pl.BlockSpec((2, block, wide), lambda j, *_: (j, 0, 0))
    per_lane = pl.BlockSpec((padded, wide), lambda j, *_: (0, 0))
    per_head = pl.BlockSpec((8, 128), lambda j, *_: (0, 0))
    moment_new, second_new, stepped, factor, heads = pl.pallas_call(
        functools.partial(update_kernel, chunks, 1.0 / all_tokens, live_shape),
        out_shape=[sds((own_columns, block, wide), F32)] * 2
        + [sds((own_columns, block, wide), BF16)]
        + [sds((padded, wide), F32), sds((8, 128), F32)],
        grid_spec=pltpu.PrefetchScalarGridSpec(
            num_scalar_prefetch=1,
            grid=(own_columns,),
            in_specs=[pl.BlockSpec((block, tokens), lambda j, *_: (j, 0))] * chunks
            + [VMEM]
            + [per_column] * 3
            + [per_lane],
            out_specs=[per_column] * 3 + [per_lane, per_head],
            scratch_shapes=[pltpu.VMEM((padded, wide), F32)],
        ),
        compiler_params=pltpu.CompilerParams(vmem_limit_bytes=LIMIT << 20),
        name="update",
    )(
        flat_live,
        *gz_chunks,
        *in_vmem([held_chunks]),
        *in_hbm((weights[0], moment[0], second[0])),
        head,
    )
    heads = heads + to_core(heads)
    head_parts = [heads] + [to_line(heads, step) for step in range(1, ways)]
    weights_out = kernel_call(
        functools.partial(output_kernel, len(head_parts), features),
        "output",
        sds((own_columns, block, wide), BF16),
        [per_head] * len(head_parts) + [per_lane] * 2 + [per_pair],
        per_pair,
        LIMIT,
        grid=(own_columns // 2,),
        scratch_shapes=[pltpu.VMEM((padded, wide), F32)],
    )(*head_parts, head, factor, stepped)
    return (weights_out[None], moment_new[None], second_new[None])


def solution(mesh):
    placed = (
        P(None, "dp", None),
        P(None, "dp", None),
        P("pipe", "dp", None, None),
        P("pipe", None, None),
        P("pipe", "dp", None, None),
        P("pipe", "dp", None, None),
    )
    return jax.shard_map(
        local,
        mesh=mesh,
        in_specs=placed,
        out_specs=(
            P("pipe", "dp", None, None),
            P("pipe", "dp", None, None),
            P("pipe", "dp", None, None),
        ),
        check_vma=False,
    )
```

time: 359 us -> 314 us (0.87)
  waiting for transfers between devices: 164 us -> 147 us
  Pallas kernels: 87.2 us -> 71.8 us
  starting transfers between devices: 78.5 us -> 71.1 us
  local copies, waits for them, and re-layouts: 22.9 us -> 19.3 us
    ppermute x27, waiting for transfers between devices: 122 us -> 105 us  [to_line(): lax.ppermute(value, 'dp', [(i, i ^ 2 * step) for i in range(devices)])]
    pallas_call x4 -> x3, Pallas kernels: 29.4 us -> 13.8 us  [local(): kernel_call(functools.partial(backward_kernel, layer, ways, live_shape),...]
    pallas_call x4 -> x9, Pallas kernels: 23.7 us -> 34.7 us  [the longest x4 23 us: local(): kernel_call(functools.partial(forward_kernel, layer, ways, live_shape), f...]
    ppermute x27, starting transfers between devices: 59 us -> 52.1 us  [to_line(): lax.ppermute(value, 'dp', [(i, i ^ 2 * step) for i in range(devices)])]
    pallas_call x1, Pallas kernels: 21.6 us -> 16.9 us  [local(): pl.pallas_call(functools.partial(update_kernel, chunks, 1.0 / all_tokens,...]
    pallas_call x1, Pallas kernels: 6.56 us -> 2.18 us  [local(): kernel_call(functools.partial(output_kernel, len(head_parts), features),...]
    unnamed x96 -> x47, local copies, waits for them, and re-layouts: 8.85 us -> 5.14 us
  transfers between devices with their start and end apart: 55 -> 55, of which waited for: 26 -> 29; matrix products, arithmetic and copies ran while one was open for 4% -> 5% of each run, Pallas kernels for 9% -> 8%
where the time goes in v3:
time: 314 us; the launch traced here: 313 us
  waiting for transfers between devices  147 us (47%)
  Pallas kernels  71.8 us (23%)
  starting transfers between devices  71.1 us (23%)
  local copies, waits for them, and re-layouts  19.3 us (6%)
    ppermute x27, waiting for transfers between devices, to_line(): lax.ppermute(value, 'dp', [(i, i ^ 2 * step) for i in range(devices)])  105 us
    ppermute x27, starting transfers between devices, to_line(): lax.ppermute(value, 'dp', [(i, i ^ 2 * step) for i in range(devices)])  52.1 us
    ppermute x9, waiting for transfers between devices, to_pipe(): return lax.ppermute(value, 'pipe', [(i, i ^ step) for i in range(sections)])  30.6 us
    pallas_call x4, Pallas kernels, local(): kernel_call(functools.partial(forward_kernel, layer, ways, live_shape), f...  23 us
    pallas_call x1, Pallas kernels, local(): pl.pallas_call(functools.partial(update_kernel, chunks, 1.0 / all_tokens,...  16.9 us
    pallas_call x3, Pallas kernels, local(): kernel_call(functools.partial(backward_kernel, layer, ways, live_shape),...  13.8 us
    ppermute x9, starting transfers between devices, to_pipe(): return lax.ppermute(value, 'pipe', [(i, i ^ step) for i in range(sections)])  11.2 us
    dynamic_update_slice x4, local copies, waits for them, and re-layouts, local(): x_all = lax.dynamic_update_index_in_dim(x_all, part, line ^ step, 0)  6.78 us
  transfers between devices with their start and end apart: 55, of which 29 were waited for; matrix products, arithmetic and copies ran while one was open for 5% of the time, Pallas kernels for 8%

profile of v3, /device:TPU:0, one launch (start us, length us, event | category | flops | bytes accessed | tf_op | source)
XLA Modules:
  0.0 313.1 jit_solution(4926871242281364015)
XLA Ops:
  2.2 1.6 split.1
  3.8 3.0 collective-permute-start
  6.8 1.5 collective-permute-start.1
  9.4 1.8 dynamic-slice_dynamic-update-slice_fusion
  11.2 1.6 collective-permute-start.4
  12.7 2.6 collective-permute-start.3
  15.7 1.7 dynamic-slice_dynamic-update-slice_fusion.1
  17.5 6.1 %collective-permute-done.4 = bf16[32,4096]{1,0:T(8,128)(2,1)} collective-permute-done((bf16[32,4096]{1,0:T(8,128)(2,1)}, bf16[32,4096]{1,0:T(8,128)(2,1)}, u32[]{:S(2)}, u32[]{:S(2)}) %collective-permute-start.4) | collective-permute-done | bytes 262176 | tf_op jit(solution)/shard_map/ppermute | solution.py:499
  23.5 10.9 %collective-permute-done.3 = bf16[32,4096]{1,0:T(8,128)(2,1)} collective-permute-done((bf16[32,4096]{1,0:T(8,128)(2,1)}, bf16[32,4096]{1,0:T(8,128)(2,1)}, u32[]{:S(2)}, u32[]{:S(2)}) %collective-permute-start.3) | collective-permute-done | bytes 262176 | tf_op jit(solution)/shard_map/ppermute | solution.py:499
  35.4 2.5 pick2.1
  39.2 1.7 bitcast_dynamic-update-slice_fusion.2
  40.8 1.7 bitcast_dynamic-update-slice_fusion.1
  42.5 1.7 bitcast_dynamic-update-slice_fusion
  44.2 2.3 copy.37
  47.3 4.3 %collective-permute-start.10 = (bf16[32,1024]{1,0:T(8,128)(2,1)}, bf16[32,1024]{1,0:T(8,128)(2,1)S(1)}, u32[]{:S(2)}, u32[]{:S(2)}) collective-permute-start(bf16[32,1024]{1,0:T(8,128)(2,1)} %get-tuple-element.112), channel_id=1, source_target_pairs={{0,2},{1,3},{2,0},{3,1},{4,6},{5,7},{6,4},{7,5},{8,10},{9,11},{10,... | collective-permute-start | bytes 196616 | tf_op jit(solution)/shard_map/ppermute | solution.py:499
  52.7 1.4 collective-permute-start.12
  54.1 1.6 pick3.1
  55.6 8.3 %collective-permute-done.6.refs_5_.refs_4_ = bf16[256,2048]{1,0:T(8,128)(2,1)} collective-permute-done((bf16[256,2048]{1,0:T(8,128)(2,1)}, bf16[256,2048]{1,0:T(8,128)(2,1)}, u32[]{:S(2)}, u32[]{:S(2)}) %collective-permute-start.6) | collective-permute-done | bytes 1048608 | tf_op jit(solution)/shard_map/ppermute | solution.py:496
  64.0 1.4 collective-permute-done.5.refs_3_.refs_6_.refs_2_
  66.5 1.5 collective-permute-start.19
  71.9 5.5 %forward0.1 = (f32[8,128]{1,0:T(8,128)}, f32[1024,128]{1,0:T(8,128)S(1)}, bf16[1024,128]{1,0:T(8,128)(2,1)S(1)}, bf16[4096,128]{1,0:T(8,128)(2,1)}, bf16[4096,12...) custom-call(s32[8192]{0:T(1024)} %pad_add_fusion.live_hbm, bf16[4096,128]{1,0:T(8,128)(2,1)} %bitcast.54, ...), custom_call_target="tpu_custom_call" | custom-call | tf_op jit(solution)/shard_map/forward0/pallas_call | solution.py:621
  77.4 4.3 %collective-permute-start.17 = (bf16[1024,128]{1,0:T(8,128)(2,1)S(1)}, bf16[1024,128]{1,0:T(8,128)(2,1)S(1)}, u32[]{:S(2)}, u32[]{:S(2)}) collective-permute-start(bf16[1024,128]{1,0:T(8,128)(2,1)S(1)} %get-tuple-element.122.refs_0_.refs_1_), channel_id=1, source_target_pairs={{0,2},{1,3},{2,0},{3,1},{4,6},{5,7},{6,4},{7,5},{8,10},{9,11},{10,... | collective-permute-start | bytes 786440 | tf_op jit(solution)/shard_map/ppermute | solution.py:499
  82.8 1.4 collective-permute-start.15
  84.2 6.9 %collective-permute-done.18.refs_7_.refs_2_.refs_3_ = bf16[256,2048]{1,0:T(8,128)(2,1)S(1)} collective-permute-done((bf16[256,2048]{1,0:T(8,128)(2,1)S(1)}, bf16[256,2048]{1,0:T(8,128)(2,1)S(1)}, u32[]{:S(2)}, u32[]{:S(2)}) %collective-permute-start.18) | collective-permute-done | bytes 1048608 | tf_op jit(solution)/shard_map/ppermute | solution.py:496
  91.4 2.0 collective-permute-done.17.refs_3_
  93.3 9.7 %collective-permute-done.16.refs_2_ = bf16[1024,128]{1,0:T(8,128)(2,1)S(1)} collective-permute-done((bf16[1024,128]{1,0:T(8,128)(2,1)S(1)}, bf16[1024,128]{1,0:T(8,128)(2,1)S(1)}, u32[]{:S(2)}, u32[]{:S(2)}) %collective-permute-start.16) | collective-permute-done | bytes 262176 | tf_op jit(solution)/shard_map/ppermute | solution.py:499
  103.6 2.1 collective-permute-done.20.refs_13_.refs_8_.refs_10_.refs_9_
  105.7 1.5 collective-permute-done.21.refs_15_.refs_11_.refs_13_
  108.2 4.1 %forward1.1 = (f32[8,128]{1,0:T(8,128)S(1)}, f32[1024,128]{1,0:T(8,128)S(1)}, bf16[1024,128]{1,0:T(8,128)(2,1)S(1)}, bf16[4096,128]{1,0:T(8,128)(2,1)}, bf16[409...) custom-call(s32[8192]{0:T(1024)} %pad_add_fusion.live_hbm, ...), custom_call_target="tpu_custom_call", output_to_operand_aliasing={{3}: (17, {}), {4}: (18, {}), {5}: (19, {}), {6}: (20, {})} | custom-call | tf_op jit(solution)/shard_map/forward1/pallas_call | solution.py:621
  112.3 5.2 %collective-permute-start.24 = (bf16[1024,128]{1,0:T(8,128)(2,1)S(1)}, bf16[1024,128]{1,0:T(8,128)(2,1)S(1)}, u32[]{:S(2)}, u32[]{:S(2)}) collective-permute-start(bf16[1024,128]{1,0:T(8,128)(2,1)S(1)} %get-tuple-element.135.refs_0_.refs_1_), channel_id=1, source_target_pairs={{0,2},{1,3},{2,0},{3,1},{4,6},{5,7},{6,4},{7,5},{8,10},{9,11},{10,... | collective-permute-start | bytes 786440 | tf_op jit(solution)/shard_map/ppermute | solution.py:499
  118.5 1.4 collective-permute-start.22
  119.9 2.2 load2.1.refs_4_.refs_8_
  122.2 6.9 %collective-permute-done.24.refs_3_ = bf16[1024,128]{1,0:T(8,128)(2,1)S(1)} collective-permute-done((bf16[1024,128]{1,0:T(8,128)(2,1)S(1)}, bf16[1024,128]{1,0:T(8,128)(2,1)S(1)}, u32[]{:S(2)}, u32[]{:S(2)}) %collective-permute-start.24) | collective-permute-done | bytes 262176 | tf_op jit(solution)/shard_map/ppermute | solution.py:499
  129.1 9.7 %collective-permute-done.23.refs_2_ = bf16[1024,128]{1,0:T(8,128)(2,1)S(1)} collective-permute-done((bf16[1024,128]{1,0:T(8,128)(2,1)S(1)}, bf16[1024,128]{1,0:T(8,128)(2,1)S(1)}, u32[]{:S(2)}, u32[]{:S(2)}) %collective-permute-start.23) | collective-permute-done | bytes 262176 | tf_op jit(solution)/shard_map/ppermute | solution.py:499
  138.8 3.8 %forward2.1 = (f32[8,128]{1,0:T(8,128)S(1)}, f32[1024,128]{1,0:T(8,128)S(1)}, bf16[1024,128]{1,0:T(8,128)(2,1)S(1)}, bf16[4096,128]{1,0:T(8,128)(2,1)}, bf16[409...) custom-call(s32[8192]{0:T(1024)} %pad_add_fusion.live_hbm, ...), custom_call_target="tpu_custom_call", output_to_operand_aliasing={{3}: (6, {}), {4}: (7, {}), {5}: (8, {}), {6}: (9, {})} | custom-call | tf_op jit(solution)/shard_map/forward2/pallas_call | solution.py:621
  142.7 5.2 %collective-permute-start.27 = (bf16[1024,128]{1,0:T(8,128)(2,1)S(1)}, bf16[1024,128]{1,0:T(8,128)(2,1)S(1)}, u32[]{:S(2)}, u32[]{:S(2)}) collective-permute-start(bf16[1024,128]{1,0:T(8,128)(2,1)S(1)} %get-tuple-element.141.refs_0_.refs_1_), channel_id=1, source_target_pairs={{0,2},{1,3},{2,0},{3,1},{4,6},{5,7},{6,4},{7,5},{8,10},{9,11},{10,... | collective-permute-start | bytes 786440 | tf_op jit(solution)/shard_map/ppermute | solution.py:499
  152.1 2.2 load3.1.refs_5_
  154.4 3.4 %collective-permute-done.27.refs_3_ = bf16[1024,128]{1,0:T(8,128)(2,1)S(1)} collective-permute-done((bf16[1024,128]{1,0:T(8,128)(2,1)S(1)}, bf16[1024,128]{1,0:T(8,128)(2,1)S(1)}, u32[]{:S(2)}, u32[]{:S(2)}) %collective-permute-start.27) | collective-permute-done | bytes 262176 | tf_op jit(solution)/shard_map/ppermute | solution.py:499
  157.8 11.4 %collective-permute-done.26.refs_2_ = bf16[1024,128]{1,0:T(8,128)(2,1)S(1)} collective-permute-done((bf16[1024,128]{1,0:T(8,128)(2,1)S(1)}, bf16[1024,128]{1,0:T(8,128)(2,1)S(1)}, u32[]{:S(2)}, u32[]{:S(2)}) %collective-permute-start.26) | collective-permute-done | bytes 262176 | tf_op jit(solution)/shard_map/ppermute | solution.py:499
  169.2 9.5 %forward3.1 = (f32[8,128]{1,0:T(8,128)S(1)}, bf16[1024,128]{1,0:T(8,128)(2,1)S(1)}, bf16[1040,128]{1,0:T(8,128)(2,1)S(1)}, bf16[1040,128]{1,0:T(8,128)(2,1)S(1)}...) custom-call(s32[8192]{0:T(1024)} %pad_add_fusion.live_hbm, ...), custom_call_target="tpu_custom_call", output_to_operand_aliasing={{6}: (7, {}), {7}: (8, {}), {8}: (9, {}), {9}: (10, {})} | custom-call | tf_op jit(solution)/shard_map/forward3/pallas_call | solution.py:621
  179.3 1.5 collective-permute-start.29
  180.8 2.5 collective-permute-start.30
  183.3 2.9 collective-permute-start.31
  186.3 13.4 %collective-permute-done.28.refs_1_ = bf16[4096,128]{1,0:T(8,128)(2,1)S(1)} collective-permute-done((bf16[4096,128]{1,0:T(8,128)(2,1)}, bf16[4096,128]{1,0:T(8,128)(2,1)S(1)}, u32[]{:S(2)}, u32[]{:S(2)}) %collective-permute-start.28) | collective-permute-done | bytes 1048608 | tf_op jit(solution)/shard_map/ppermute | solution.py:496
  200.0 4.1 %collective-permute-done.31.refs_5_ = bf16[1040,128]{1,0:T(8,128)(2,1)S(1)} collective-permute-done((bf16[1040,128]{1,0:T(8,128)(2,1)S(1)}, bf16[1040,128]{1,0:T(8,128)(2,1)S(1)}, u32[]{:S(2)}, u32[]{:S(2)}) %collective-permute-start.31) | collective-permute-done | bytes 266272 | tf_op jit(solution)/shard_map/ppermute | solution.py:499
  204.1 6.6 %backward2.1 = (bf16[1024,128]{1,0:T(8,128)(2,1)S(1)}, bf16[1040,128]{1,0:T(8,128)(2,1)S(1)}, bf16[1040,128]{1,0:T(8,128)(2,1)S(1)}, bf16[1040,128]{1,0:T(8,128)...) custom-call(s32[8192]{0:T(1024)} %pad_add_fusion.live_hbm, bf16[1024,128]{1,0:T(8,128)(2,1)S(1)} %bitcast.51, ...), custom_call_target="tpu_custom_call" | custom-call | tf_op jit(solution)/shard_map/backward2/pallas_call | solution.py:666
  211.3 1.4 collective-permute-start.39
  212.7 2.5 collective-permute-start.35
  215.3 2.0 collective-permute-start.36
  218.4 2.2 load1.1.refs_8_
  220.7 3.3 %collective-permute-done.35.refs_4_ = bf16[1040,128]{1,0:T(8,128)(2,1)S(1)} collective-permute-done((bf16[1040,128]{1,0:T(8,128)(2,1)S(1)}, bf16[1040,128]{1,0:T(8,128)(2,1)S(1)}, u32[]{:S(2)}, u32[]{:S(2)}) %collective-permute-start.35) | collective-permute-done | bytes 266272 | tf_op jit(solution)/shard_map/ppermute | solution.py:499
  223.9 15.8 %collective-permute-done.36.refs_5_ = bf16[1040,128]{1,0:T(8,128)(2,1)S(1)} collective-permute-done((bf16[1040,128]{1,0:T(8,128)(2,1)S(1)}, bf16[1040,128]{1,0:T(8,128)(2,1)S(1)}, u32[]{:S(2)}, u32[]{:S(2)}) %collective-permute-start.36) | collective-permute-done | bytes 266272 | tf_op jit(solution)/shard_map/ppermute | solution.py:499
  239.8 6.5 %backward1.1 = (bf16[1024,128]{1,0:T(8,128)(2,1)S(1)}, bf16[1040,128]{1,0:T(8,128)(2,1)S(1)}, bf16[1040,128]{1,0:T(8,128)(2,1)S(1)}, bf16[1040,128]{1,0:T(8,128)...) custom-call(s32[8192]{0:T(1024)} %pad_add_fusion.live_hbm, ...), custom_call_target="tpu_custom_call" | custom-call | tf_op jit(solution)/shard_map/backward1/pallas_call | solution.py:666
  246.9 2.5 collective-permute-start.41
  249.4 1.9 collective-permute-start.43
  251.3 6.8 %collective-permute-done.41.refs_4_ = bf16[1040,128]{1,0:T(8,128)(2,1)S(1)} collective-permute-done((bf16[1040,128]{1,0:T(8,128)(2,1)S(1)}, bf16[1040,128]{1,0:T(8,128)(2,1)S(1)}, u32[]{:S(2)}, u32[]{:S(2)}) %collective-permute-start.41) | collective-permute-done | bytes 266272 | tf_op jit(solution)/shard_map/ppermute | solution.py:499
  258.1 13.4 %collective-permute-done.42.refs_5_ = bf16[1040,128]{1,0:T(8,128)(2,1)S(1)} collective-permute-done((bf16[1040,128]{1,0:T(8,128)(2,1)S(1)}, bf16[1040,128]{1,0:T(8,128)(2,1)S(1)}, u32[]{:S(2)}, u32[]{:S(2)}) %collective-permute-start.42) | collective-permute-done | bytes 266272 | tf_op jit(solution)/shard_map/ppermute | solution.py:499
  274.0 1.8 collective-permute-start.46
  276.4 2.0 collective-permute-done.44.refs_1_
  280.0 3.5 %gather_u.1.refs_8_ = bf16[8,4096,128]{2,1,0:T(8,128)(2,1)S(1)} custom-call(bf16[4096,128]{1,0:T(8,128)(2,1)} %get-tuple-element.161.refs_0_, bf16[4096,128]{1,0:T(8,128)(2,1)} %copy-done.12, bf16[4096,128]{1,0:T(8,128)(2,1)} %copy-done.13, bf16[4096,128]{1,0:T(8,128)(2,1)} %copy-done.16, bf16[4096,128]{1,0:T(8,128)(2,1)} %copy-done.14, ...), custom_call_target="tpu_custom_call" | custom-call | bytes 33554432 | tf_op jit(solution)/shard_map/gather_u/pallas_call | solution.py:694
  283.5 3.3 %collective-permute-done.49.refs_6_ = bf16[512,128]{1,0:T(8,128)(2,1)S(1)} collective-permute-done((bf16[512,128]{1,0:T(8,128)(2,1)S(1)}, bf16[512,128]{1,0:T(8,128)(2,1)S(1)}, u32[]{:S(2)}, u32[]{:S(2)}) %collective-permute-start.49) | collective-permute-done | bytes 131104 | tf_op jit(solution)/shard_map/ppermute | solution.py:712
  286.8 16.9 %update.1 = (f32[8,64,2048]{2,1,0:T(8,128)}, f32[8,64,2048]{2,1,0:T(8,128)}, bf16[8,64,2048]{2,1,0:T(8,128)(2,1)S(1)}, f32[8,2048]{1,0:T(8,128)S(1)}, f32[8,128]{1,0:T(8,128)S(1)}) custom-call(s32[2048]{0:T(1024)S(1)} %reshape_squeeze.6.live, bf16[512,128]{1,0:T(8,128)(2,1)S(1)} %get-tuple-element.182.refs_0_, ...), custom_call_target="tpu_custom_call" | custom-call | tf_op jit(solution)/shard_map/update/pallas_call | solution.py:733
  306.3 3.0 collective-permute-start.52
  310.9 2.2 output.1
  (134 shorter events, 32.3 us)
Async XLA Ops:
  3.8 30.6 %collective-permute-start = (bf16[272,2048]{1,0:T(8,128)(2,1)S(1)}, bf16[272,2048]{1,0:T(8,128)(2,1)S(1)}, u32[]{:S(2)}, u32[]{:S(2)}) collective-permute-start(bf16[272,2048]{1,0:T(8,128)(2,1)S(1)} %get-tuple-element.99), channel_id=1, source_target_pairs={{0,8},{8,0},{16,24},{24,16},{1,9},{9,1},{17,25},{25,17},{2,10},{10... | collective-permute-start | bytes 3342344 | tf_op jit(solution)/shard_map/ppermute | solution.py:496
  6.8 27.7 %collective-permute-start.1 = (bf16[272,2048]{1,0:T(8,128)(2,1)S(1)}, bf16[272,2048]{1,0:T(8,128)(2,1)}, u32[]{:S(2)}, u32[]{:S(2)}) collective-permute-start(bf16[272,2048]{1,0:T(8,128)(2,1)S(1)} %get-tuple-element.100), channel_id=1, source_target_pairs={{0,16},{8,24},{16,0},{24,8},{1,17},{9,25},{17,1},{25,9},{2,18},{10... | collective-permute-start | bytes 3342344 | tf_op jit(solution)/shard_map/ppermute | solution.py:496
  11.2 12.4 %collective-permute-start.4 = (bf16[32,4096]{1,0:T(8,128)(2,1)}, bf16[32,4096]{1,0:T(8,128)(2,1)}, u32[]{:S(2)}, u32[]{:S(2)}) collective-permute-start(bf16[32,4096]{1,0:T(8,128)(2,1)} %get-tuple-element.200), channel_id=1, source_target_pairs={{0,2},{1,3},{2,0},{3,1},{4,6},{5,7},{6,4},{7,5},{8,10},{9,11},{10,... | collective-permute-start | bytes 786440 | tf_op jit(solution)/shard_map/ppermute | solution.py:499
  12.7 21.7 %collective-permute-start.3 = (bf16[32,4096]{1,0:T(8,128)(2,1)}, bf16[32,4096]{1,0:T(8,128)(2,1)}, u32[]{:S(2)}, u32[]{:S(2)}) collective-permute-start(bf16[32,4096]{1,0:T(8,128)(2,1)} %get-tuple-element.200), channel_id=1, source_target_pairs={{0,4},{1,5},{2,6},{3,7},{4,0},{5,1},{6,2},{7,3},{8,12},{9,13},{10,... | collective-permute-start | bytes 786440 | tf_op jit(solution)/shard_map/ppermute | solution.py:499
  15.3 19.1 %collective-permute-start.2 = (bf16[32,4096]{1,0:T(8,128)(2,1)}, bf16[32,4096]{1,0:T(8,128)(2,1)}, u32[]{:S(2)}, u32[]{:S(2)}) collective-permute-start(bf16[32,4096]{1,0:T(8,128)(2,1)} %get-tuple-element.200), channel_id=1, source_target_pairs={{0,6},{1,7},{2,4},{3,5},{4,2},{5,3},{6,0},{7,1},{8,14},{9,15},{10,... | collective-permute-start | bytes 786440 | tf_op jit(solution)/shard_map/ppermute | solution.py:499
  17.5 17.1 %copy-start.19 = (bf16[4,32,1024]{2,1,0:T(8,128)(2,1)}, bf16[4,32,1024]{2,1,0:T(8,128)(2,1)S(1)}, u32[]{:S(2)}) copy-start(bf16[4,32,1024]{2,1,0:T(8,128)(2,1)S(1)} %get-tuple-element.195) | copy-start | bytes 786436
  34.5 12.8 %collective-permute-start.8 = (bf16[272,2048]{1,0:T(8,128)(2,1)S(1)}, bf16[272,2048]{1,0:T(8,128)(2,1)S(1)}, u32[]{:S(2)}, u32[]{:S(2)}) collective-permute-start(bf16[272,2048]{1,0:T(8,128)(2,1)S(1)} %collective-permute-done.x1.refs_2_.refs_5_.refs_1_), channel_id=1, source_target_pairs={{0,1},{1,0},{2,3},{3,2},{4,5},{5,4},{6,7},{7,6},{8,9},{9,8},{10,11... | collective-permute-start | bytes 3342344 | tf_op jit(solution)/shard_map/ppermute | solution.py:506
  34.6 12.8 %collective-permute-start.9 = (bf16[272,2048]{1,0:T(8,128)(2,1)}, bf16[272,2048]{1,0:T(8,128)(2,1)}, u32[]{:S(2)}, u32[]{:S(2)}) collective-permute-start(bf16[272,2048]{1,0:T(8,128)(2,1)} %collective-permute-done.1.y1.refs_4_.refs_8_.refs_3_), channel_id=1, source_target_pairs={{0,1},{1,0},{2,3},{3,2},{4,5},{5,4},{6,7},{7,6},{8,9},{9,8},{10,11... | collective-permute-start | bytes 3342344 | tf_op jit(solution)/shard_map/ppermute | solution.py:506
  38.0 9.3 %collective-permute-start.7 = (bf16[512,2048]{1,0:T(8,128)(2,1)}, bf16[512,2048]{1,0:T(8,128)(2,1)}, u32[]{:S(2)}, u32[]{:S(2)}) collective-permute-start(bf16[512,2048]{1,0:T(8,128)(2,1)} %bitcast.own.refs_1_.refs_4_.refs_0_), channel_id=1, source_target_pairs={{0,1},{1,0},{2,3},{3,2},{4,5},{5,4},{6,7},{7,6},{8,9},{9,8},{10,11... | collective-permute-start | bytes 6291464 | tf_op jit(solution)/shard_map/ppermute | solution.py:506
  38.1 25.9 %collective-permute-start.6 = (bf16[256,2048]{1,0:T(8,128)(2,1)}, bf16[256,2048]{1,0:T(8,128)(2,1)}, u32[]{:S(2)}, u32[]{:S(2)}) collective-permute-start(bf16[256,2048]{1,0:T(8,128)(2,1)} %get-tuple-element.104), channel_id=1, source_target_pairs={{0,16},{8,24},{16,0},{24,8},{1,17},{9,25},{17,1},{25,9},{2,18},{10... | collective-permute-start | bytes 3145736 | tf_op jit(solution)/shard_map/ppermute | solution.py:496
  38.6 26.7 %collective-permute-start.5 = (bf16[272,2048]{1,0:T(8,128)(2,1)S(1)}, bf16[272,2048]{1,0:T(8,128)(2,1)}, u32[]{:S(2)}, u32[]{:S(2)}) collective-permute-start(bf16[272,2048]{1,0:T(8,128)(2,1)S(1)} %get-tuple-element.103), channel_id=1, source_target_pairs={{0,8},{8,0},{16,24},{24,16},{1,9},{9,1},{17,25},{25,17},{2,10},{10... | collective-permute-start | bytes 3342344 | tf_op jit(solution)/shard_map/ppermute | solution.py:496
  47.3 18.0 %collective-permute-start.10 = (bf16[32,1024]{1,0:T(8,128)(2,1)}, bf16[32,1024]{1,0:T(8,128)(2,1)S(1)}, u32[]{:S(2)}, u32[]{:S(2)}) collective-permute-start(bf16[32,1024]{1,0:T(8,128)(2,1)} %get-tuple-element.112), channel_id=1, source_target_pairs={{0,2},{1,3},{2,0},{3,1},{4,6},{5,7},{6,4},{7,5},{8,10},{9,11},{10,... | collective-permute-start | bytes 196616 | tf_op jit(solution)/shard_map/ppermute | solution.py:499
  51.6 13.8 %collective-permute-start.11 = (bf16[32,1024]{1,0:T(8,128)(2,1)S(1)}, bf16[32,1024]{1,0:T(8,128)(2,1)S(1)}, u32[]{:S(2)}, u32[]{:S(2)}) collective-permute-start(bf16[32,1024]{1,0:T(8,128)(2,1)S(1)} %get-tuple-element.113), channel_id=1, source_target_pairs={{0,4},{1,5},{2,6},{3,7},{4,0},{5,1},{6,2},{7,3},{8,12},{9,13},{10,... | collective-permute-start | bytes 196616 | tf_op jit(solution)/shard_map/ppermute | solution.py:499
  52.7 12.7 %collective-permute-start.12 = (bf16[32,1024]{1,0:T(8,128)(2,1)S(1)}, bf16[32,1024]{1,0:T(8,128)(2,1)S(1)}, u32[]{:S(2)}, u32[]{:S(2)}) collective-permute-start(bf16[32,1024]{1,0:T(8,128)(2,1)S(1)} %get-tuple-element.114), channel_id=1, source_target_pairs={{0,6},{1,7},{2,4},{3,5},{4,2},{5,3},{6,0},{7,1},{8,14},{9,15},{10,... | collective-permute-start | bytes 196616 | tf_op jit(solution)/shard_map/ppermute | solution.py:499
  65.4 4.5 %collective-permute-start.13 = (bf16[272,2048]{1,0:T(8,128)(2,1)}, bf16[272,2048]{1,0:T(8,128)(2,1)S(1)}, u32[]{:S(2)}, u32[]{:S(2)}) collective-permute-start(bf16[272,2048]{1,0:T(8,128)(2,1)} %collective-permute-done.5.refs_3_.refs_6_.refs_2_), channel_id=1, source_target_pairs={{0,1},{1,0},{2,3},{3,2},{4,5},{5,4},{6,7},{7,6},{8,9},{9,8},{10,11... | collective-permute-start | bytes 3342344 | tf_op jit(solution)/shard_map/ppermute | solution.py:506
  65.5 4.5 %collective-permute-start.14 = (bf16[256,2048]{1,0:T(8,128)(2,1)}, bf16[256,2048]{1,0:T(8,128)(2,1)S(1)}, u32[]{:S(2)}, u32[]{:S(2)}) collective-permute-start(bf16[256,2048]{1,0:T(8,128)(2,1)} %collective-permute-done.6.refs_5_.refs_4_), channel_id=1, source_target_pairs={{0,1},{1,0},{2,3},{3,2},{4,5},{5,4},{6,7},{7,6},{8,9},{9,8},{10,11... | collective-permute-start | bytes 3145736 | tf_op jit(solution)/shard_map/ppermute | solution.py:506
  66.0 25.1 %collective-permute-start.18 = (bf16[256,2048]{1,0:T(8,128)(2,1)S(1)}, bf16[256,2048]{1,0:T(8,128)(2,1)S(1)}, u32[]{:S(2)}, u32[]{:S(2)}) collective-permute-start(bf16[256,2048]{1,0:T(8,128)(2,1)S(1)} %get-tuple-element.125), channel_id=1, source_target_pairs={{0,8},{8,0},{16,24},{24,16},{1,9},{9,1},{17,25},{25,17},{2,10},{10... | collective-permute-start | bytes 3145736 | tf_op jit(solution)/shard_map/ppermute | solution.py:496
  66.5 24.9 %collective-permute-start.19 = (bf16[256,2048]{1,0:T(8,128)(2,1)S(1)}, bf16[256,2048]{1,0:T(8,128)(2,1)S(1)}, u32[]{:S(2)}, u32[]{:S(2)}) collective-permute-start(bf16[256,2048]{1,0:T(8,128)(2,1)S(1)} %get-tuple-element.126), channel_id=1, source_target_pairs={{0,16},{8,24},{16,0},{24,8},{1,17},{9,25},{17,1},{25,9},{2,18},{10... | collective-permute-start | bytes 3145736 | tf_op jit(solution)/shard_map/ppermute | solution.py:496
  77.4 15.9 %collective-permute-start.17 = (bf16[1024,128]{1,0:T(8,128)(2,1)S(1)}, bf16[1024,128]{1,0:T(8,128)(2,1)S(1)}, u32[]{:S(2)}, u32[]{:S(2)}) collective-permute-start(bf16[1024,128]{1,0:T(8,128)(2,1)S(1)} %get-tuple-element.122.refs_0_.refs_1_), channel_id=1, source_target_pairs={{0,2},{1,3},{2,0},{3,1},{4,6},{5,7},{6,4},{7,5},{8,10},{9,11},{10,... | collective-permute-start | bytes 786440 | tf_op jit(solution)/shard_map/ppermute | solution.py:499
  81.7 21.3 %collective-permute-start.16 = (bf16[1024,128]{1,0:T(8,128)(2,1)S(1)}, bf16[1024,128]{1,0:T(8,128)(2,1)S(1)}, u32[]{:S(2)}, u32[]{:S(2)}) collective-permute-start(bf16[1024,128]{1,0:T(8,128)(2,1)S(1)} %get-tuple-element.122.refs_0_.refs_1_), channel_id=1, source_target_pairs={{0,4},{1,5},{2,6},{3,7},{4,0},{5,1},{6,2},{7,3},{8,12},{9,13},{10,... | collective-permute-start | bytes 786440 | tf_op jit(solution)/shard_map/ppermute | solution.py:499
  82.8 20.3 %collective-permute-start.15 = (bf16[1024,128]{1,0:T(8,128)(2,1)S(1)}, bf16[1024,128]{1,0:T(8,128)(2,1)S(1)}, u32[]{:S(2)}, u32[]{:S(2)}) collective-permute-start(bf16[1024,128]{1,0:T(8,128)(2,1)S(1)} %get-tuple-element.122.refs_0_.refs_1_), channel_id=1, source_target_pairs={{0,6},{1,7},{2,4},{3,5},{4,2},{5,3},{6,0},{7,1},{8,14},{9,15},{10,... | collective-permute-start | bytes 786440 | tf_op jit(solution)/shard_map/ppermute | solution.py:499
  91.1 16.1 %copy-start.6 = (bf16[256,2048]{1,0:T(8,128)(2,1)}, bf16[256,2048]{1,0:T(8,128)(2,1)S(1)}, u32[]{:S(2)}) copy-start(bf16[256,2048]{1,0:T(8,128)(2,1)S(1)} %collective-permute-done.18.refs_7_.refs_2_.refs_3_) | copy-start | bytes 3145732
  103.1 2.7 collective-permute-start.20
  103.1 4.2 %collective-permute-start.21 = (bf16[256,2048]{1,0:T(8,128)(2,1)S(1)}, bf16[256,2048]{1,0:T(8,128)(2,1)S(1)}, u32[]{:S(2)}, u32[]{:S(2)}) collective-permute-start(bf16[256,2048]{1,0:T(8,128)(2,1)S(1)} %collective-permute-done.19.refs_9_.refs_5_.refs_6_), channel_id=1, source_target_pairs={{0,1},{1,0},{2,3},{3,2},{4,5},{5,4},{6,7},{7,6},{8,9},{9,8},{10,11... | collective-permute-start | bytes 3145736 | tf_op jit(solution)/shard_map/ppermute | solution.py:506
  112.3 16.8 %collective-permute-start.24 = (bf16[1024,128]{1,0:T(8,128)(2,1)S(1)}, bf16[1024,128]{1,0:T(8,128)(2,1)S(1)}, u32[]{:S(2)}, u32[]{:S(2)}) collective-permute-start(bf16[1024,128]{1,0:T(8,128)(2,1)S(1)} %get-tuple-element.135.refs_0_.refs_1_), channel_id=1, source_target_pairs={{0,2},{1,3},{2,0},{3,1},{4,6},{5,7},{6,4},{7,5},{8,10},{9,11},{10,... | collective-permute-start | bytes 786440 | tf_op jit(solution)/shard_map/ppermute | solution.py:499
  117.5 21.3 %collective-permute-start.23 = (bf16[1024,128]{1,0:T(8,128)(2,1)S(1)}, bf16[1024,128]{1,0:T(8,128)(2,1)S(1)}, u32[]{:S(2)}, u32[]{:S(2)}) collective-permute-start(bf16[1024,128]{1,0:T(8,128)(2,1)S(1)} %get-tuple-element.135.refs_0_.refs_1_), channel_id=1, source_target_pairs={{0,4},{1,5},{2,6},{3,7},{4,0},{5,1},{6,2},{7,3},{8,12},{9,13},{10,... | collective-permute-start | bytes 786440 | tf_op jit(solution)/shard_map/ppermute | solution.py:499
  118.5 20.3 %collective-permute-start.22 = (bf16[1024,128]{1,0:T(8,128)(2,1)S(1)}, bf16[1024,128]{1,0:T(8,128)(2,1)S(1)}, u32[]{:S(2)}, u32[]{:S(2)}) collective-permute-start(bf16[1024,128]{1,0:T(8,128)(2,1)S(1)} %get-tuple-element.135.refs_0_.refs_1_), channel_id=1, source_target_pairs={{0,6},{1,7},{2,4},{3,5},{4,2},{5,3},{6,0},{7,1},{8,14},{9,15},{10,... | collective-permute-start | bytes 786440 | tf_op jit(solution)/shard_map/ppermute | solution.py:499
  122.2 20.5 %copy-start = (bf16[1024,2048]{1,0:T(8,128)(2,1)}, bf16[1024,2048]{1,0:T(8,128)(2,1)S(1)}, u32[]{:S(2)}) copy-start(bf16[1024,2048]{1,0:T(8,128)(2,1)S(1)} %load2.1.refs_4_.refs_8_) | copy-start | bytes 12582916
  142.7 15.1 %collective-permute-start.27 = (bf16[1024,128]{1,0:T(8,128)(2,1)S(1)}, bf16[1024,128]{1,0:T(8,128)(2,1)S(1)}, u32[]{:S(2)}, u32[]{:S(2)}) collective-permute-start(bf16[1024,128]{1,0:T(8,128)(2,1)S(1)} %get-tuple-element.141.refs_0_.refs_1_), channel_id=1, source_target_pairs={{0,2},{1,3},{2,0},{3,1},{4,6},{5,7},{6,4},{7,5},{8,10},{9,11},{10,... | collective-permute-start | bytes 786440 | tf_op jit(solution)/shard_map/ppermute | solution.py:499
  147.8 21.4 %collective-permute-start.26 = (bf16[1024,128]{1,0:T(8,128)(2,1)S(1)}, bf16[1024,128]{1,0:T(8,128)(2,1)S(1)}, u32[]{:S(2)}, u32[]{:S(2)}) collective-permute-start(bf16[1024,128]{1,0:T(8,128)(2,1)S(1)} %get-tuple-element.141.refs_0_.refs_1_), channel_id=1, source_target_pairs={{0,4},{1,5},{2,6},{3,7},{4,0},{5,1},{6,2},{7,3},{8,12},{9,13},{10,... | collective-permute-start | bytes 786440 | tf_op jit(solution)/shard_map/ppermute | solution.py:499
  148.9 20.3 %collective-permute-start.25 = (bf16[1024,128]{1,0:T(8,128)(2,1)S(1)}, bf16[1024,128]{1,0:T(8,128)(2,1)S(1)}, u32[]{:S(2)}, u32[]{:S(2)}) collective-permute-start(bf16[1024,128]{1,0:T(8,128)(2,1)S(1)} %get-tuple-element.141.refs_0_.refs_1_), channel_id=1, source_target_pairs={{0,6},{1,7},{2,4},{3,5},{4,2},{5,3},{6,0},{7,1},{8,14},{9,15},{10,... | collective-permute-start | bytes 786440 | tf_op jit(solution)/shard_map/ppermute | solution.py:499
  169.2 34.9 %copy-start.1 = (bf16[1024,2048]{1,0:T(8,128)(2,1)S(1)}, bf16[1024,2048]{1,0:T(8,128)(2,1)}, u32[]{:S(2)}) copy-start(bf16[1024,2048]{1,0:T(8,128)(2,1)} %copy-done) | copy-start | bytes 12582916
  178.7 21.1 %collective-permute-start.28 = (bf16[4096,128]{1,0:T(8,128)(2,1)}, bf16[4096,128]{1,0:T(8,128)(2,1)S(1)}, u32[]{:S(2)}, u32[]{:S(2)}) collective-permute-start(bf16[4096,128]{1,0:T(8,128)(2,1)} %get-tuple-element.149), channel_id=1, source_target_pairs={{0,8},{8,0},{16,24},{24,16},{1,9},{9,1},{17,25},{25,17},{2,10},{10... | collective-permute-start | bytes 3145736 | tf_op jit(solution)/shard_map/ppermute | solution.py:496
  179.3 20.7 %collective-permute-start.29 = (bf16[4096,128]{1,0:T(8,128)(2,1)}, bf16[4096,128]{1,0:T(8,128)(2,1)S(1)}, u32[]{:S(2)}, u32[]{:S(2)}) collective-permute-start(bf16[4096,128]{1,0:T(8,128)(2,1)} %get-tuple-element.150), channel_id=1, source_target_pairs={{0,16},{8,24},{16,0},{24,8},{1,17},{9,25},{17,1},{25,9},{2,18},{10... | collective-permute-start | bytes 3145736 | tf_op jit(solution)/shard_map/ppermute | solution.py:496
  180.8 19.2 %collective-permute-start.30 = (bf16[1040,128]{1,0:T(8,128)(2,1)S(1)}, bf16[1040,128]{1,0:T(8,128)(2,1)S(1)}, u32[]{:S(2)}, u32[]{:S(2)}) collective-permute-start(bf16[1040,128]{1,0:T(8,128)(2,1)S(1)} %get-tuple-element.152), channel_id=1, source_target_pairs={{0,6},{1,7},{2,4},{3,5},{4,2},{5,3},{6,0},{7,1},{8,14},{9,15},{10,... | collective-permute-start | bytes 798728 | tf_op jit(solution)/shard_map/ppermute | solution.py:499
  183.3 20.8 %collective-permute-start.31 = (bf16[1040,128]{1,0:T(8,128)(2,1)S(1)}, bf16[1040,128]{1,0:T(8,128)(2,1)S(1)}, u32[]{:S(2)}, u32[]{:S(2)}) collective-permute-start(bf16[1040,128]{1,0:T(8,128)(2,1)S(1)} %get-tuple-element.153), channel_id=1, source_target_pairs={{0,4},{1,5},{2,6},{3,7},{4,0},{5,1},{6,2},{7,3},{8,12},{9,13},{10,... | collective-permute-start | bytes 798728 | tf_op jit(solution)/shard_map/ppermute | solution.py:499
  186.2 17.9 %collective-permute-start.32 = (bf16[1040,128]{1,0:T(8,128)(2,1)S(1)}, bf16[1040,128]{1,0:T(8,128)(2,1)S(1)}, u32[]{:S(2)}, u32[]{:S(2)}) collective-permute-start(bf16[1040,128]{1,0:T(8,128)(2,1)S(1)} %get-tuple-element.154), channel_id=1, source_target_pairs={{0,2},{1,3},{2,0},{3,1},{4,6},{5,7},{6,4},{7,5},{8,10},{9,11},{10,... | collective-permute-start | bytes 798728 | tf_op jit(solution)/shard_map/ppermute | solution.py:499
  200.0 46.3 %copy-start.13 = (bf16[4096,128]{1,0:T(8,128)(2,1)}, bf16[4096,128]{1,0:T(8,128)(2,1)S(1)}, u32[]{:S(2)}) copy-start(bf16[4096,128]{1,0:T(8,128)(2,1)S(1)} %collective-permute-done.29.refs_2_) | copy-start | bytes 3145732
  210.7 6.5 %collective-permute-start.33 = (bf16[4096,128]{1,0:T(8,128)(2,1)S(1)}, bf16[4096,128]{1,0:T(8,128)(2,1)S(1)}, u32[]{:S(2)}, u32[]{:S(2)}) collective-permute-start(bf16[4096,128]{1,0:T(8,128)(2,1)S(1)} %copy-done.5), channel_id=1, source_target_pairs={{0,1},{1,0},{2,3},{3,2},{4,5},{5,4},{6,7},{7,6},{8,9},{9,8},{10,11... | collective-permute-start | bytes 3145736 | tf_op jit(solution)/shard_map/ppermute | solution.py:506
  210.8 9.9 %collective-permute-start.34 = (bf16[4096,128]{1,0:T(8,128)(2,1)S(1)}, bf16[4096,128]{1,0:T(8,128)(2,1)S(1)}, u32[]{:S(2)}, u32[]{:S(2)}) collective-permute-start(bf16[4096,128]{1,0:T(8,128)(2,1)S(1)} %collective-permute-done.28.refs_1_), channel_id=1, source_target_pairs={{0,1},{1,0},{2,3},{3,2},{4,5},{5,4},{6,7},{7,6},{8,9},{9,8},{10,11... | collective-permute-start | bytes 3145736 | tf_op jit(solution)/shard_map/ppermute | solution.py:506
  211.3 35.0 %collective-permute-start.39 = (bf16[4096,128]{1,0:T(8,128)(2,1)S(1)}, bf16[4096,128]{1,0:T(8,128)(2,1)S(1)}, u32[]{:S(2)}, u32[]{:S(2)}) collective-permute-start(bf16[4096,128]{1,0:T(8,128)(2,1)S(1)} %copy-done.10), channel_id=1, source_target_pairs={{0,24},{8,16},{16,8},{24,0},{1,25},{9,17},{17,9},{25,1},{2,26},{10... | collective-permute-start | bytes 3145736 | tf_op jit(solution)/shard_map/ppermute | solution.py:496
  212.7 11.2 %collective-permute-start.35 = (bf16[1040,128]{1,0:T(8,128)(2,1)S(1)}, bf16[1040,128]{1,0:T(8,128)(2,1)S(1)}, u32[]{:S(2)}, u32[]{:S(2)}) collective-permute-start(bf16[1040,128]{1,0:T(8,128)(2,1)S(1)} %get-tuple-element.164), channel_id=1, source_target_pairs={{0,6},{1,7},{2,4},{3,5},{4,2},{5,3},{6,0},{7,1},{8,14},{9,15},{10,... | collective-permute-start | bytes 798728 | tf_op jit(solution)/shard_map/ppermute | solution.py:499
  215.3 24.5 %collective-permute-start.36 = (bf16[1040,128]{1,0:T(8,128)(2,1)S(1)}, bf16[1040,128]{1,0:T(8,128)(2,1)S(1)}, u32[]{:S(2)}, u32[]{:S(2)}) collective-permute-start(bf16[1040,128]{1,0:T(8,128)(2,1)S(1)} %get-tuple-element.165), channel_id=1, source_target_pairs={{0,4},{1,5},{2,6},{3,7},{4,0},{5,1},{6,2},{7,3},{8,12},{9,13},{10,... | collective-permute-start | bytes 798728 | tf_op jit(solution)/shard_map/ppermute | solution.py:499
  218.2 21.5 %collective-permute-start.37 = (bf16[1040,128]{1,0:T(8,128)(2,1)S(1)}, bf16[1040,128]{1,0:T(8,128)(2,1)S(1)}, u32[]{:S(2)}, u32[]{:S(2)}) collective-permute-start(bf16[1040,128]{1,0:T(8,128)(2,1)S(1)} %get-tuple-element.166), channel_id=1, source_target_pairs={{0,2},{1,3},{2,0},{3,1},{4,6},{5,7},{6,4},{7,5},{8,10},{9,11},{10,... | collective-permute-start | bytes 798728 | tf_op jit(solution)/shard_map/ppermute | solution.py:499
  220.7 25.6 %copy-start.15 = (bf16[4096,128]{1,0:T(8,128)(2,1)}, bf16[4096,128]{1,0:T(8,128)(2,1)S(1)}, u32[]{:S(2)}) copy-start(bf16[4096,128]{1,0:T(8,128)(2,1)S(1)} %collective-permute-done.34.refs_5_) | copy-start | bytes 3145732
  246.3 32.7 %copy-start.16 = (bf16[4096,128]{1,0:T(8,128)(2,1)}, bf16[4096,128]{1,0:T(8,128)(2,1)S(1)}, u32[]{:S(2)}) copy-start(bf16[4096,128]{1,0:T(8,128)(2,1)S(1)} %collective-permute-done.39.refs_3_) | copy-start | bytes 3145732
  246.3 5.0 %collective-permute-start.38 = (bf16[4096,128]{1,0:T(8,128)(2,1)S(1)}, bf16[4096,128]{1,0:T(8,128)(2,1)S(1)}, u32[]{:S(2)}, u32[]{:S(2)}) collective-permute-start(bf16[4096,128]{1,0:T(8,128)(2,1)S(1)} %collective-permute-done.29.refs_2_), channel_id=1, source_target_pairs={{0,1},{1,0},{2,3},{3,2},{4,5},{5,4},{6,7},{7,6},{8,9},{9,8},{10,11... | collective-permute-start | bytes 3145736 | tf_op jit(solution)/shard_map/ppermute | solution.py:506
  246.4 4.9 %collective-permute-start.40 = (bf16[4096,128]{1,0:T(8,128)(2,1)S(1)}, bf16[4096,128]{1,0:T(8,128)(2,1)S(1)}, u32[]{:S(2)}, u32[]{:S(2)}) collective-permute-start(bf16[4096,128]{1,0:T(8,128)(2,1)S(1)} %collective-permute-done.39.refs_3_), channel_id=1, source_target_pairs={{0,1},{1,0},{2,3},{3,2},{4,5},{5,4},{6,7},{7,6},{8,9},{9,8},{10,11... | collective-permute-start | bytes 3145736 | tf_op jit(solution)/shard_map/ppermute | solution.py:506
  246.9 11.2 %collective-permute-start.41 = (bf16[1040,128]{1,0:T(8,128)(2,1)S(1)}, bf16[1040,128]{1,0:T(8,128)(2,1)S(1)}, u32[]{:S(2)}, u32[]{:S(2)}) collective-permute-start(bf16[1040,128]{1,0:T(8,128)(2,1)S(1)} %get-tuple-element.177), channel_id=1, source_target_pairs={{0,6},{1,7},{2,4},{3,5},{4,2},{5,3},{6,0},{7,1},{8,14},{9,15},{10,... | collective-permute-start | bytes 798728 | tf_op jit(solution)/shard_map/ppermute | solution.py:499
  249.4 22.1 %collective-permute-start.42 = (bf16[1040,128]{1,0:T(8,128)(2,1)S(1)}, bf16[1040,128]{1,0:T(8,128)(2,1)S(1)}, u32[]{:S(2)}, u32[]{:S(2)}) collective-permute-start(bf16[1040,128]{1,0:T(8,128)(2,1)S(1)} %get-tuple-element.178), channel_id=1, source_target_pairs={{0,4},{1,5},{2,6},{3,7},{4,0},{5,1},{6,2},{7,3},{8,12},{9,13},{10,... | collective-permute-start | bytes 798728 | tf_op jit(solution)/shard_map/ppermute | solution.py:499
  249.4 22.1 %collective-permute-start.43 = (bf16[1040,128]{1,0:T(8,128)(2,1)S(1)}, bf16[1040,128]{1,0:T(8,128)(2,1)S(1)}, u32[]{:S(2)}, u32[]{:S(2)}) collective-permute-start(bf16[1040,128]{1,0:T(8,128)(2,1)S(1)} %get-tuple-element.179), channel_id=1, source_target_pairs={{0,2},{1,3},{2,0},{3,1},{4,6},{5,7},{6,4},{7,5},{8,10},{9,11},{10,... | collective-permute-start | bytes 798728 | tf_op jit(solution)/shard_map/ppermute | solution.py:499
  251.3 27.8 %copy-start.17 = (bf16[4096,128]{1,0:T(8,128)(2,1)}, bf16[4096,128]{1,0:T(8,128)(2,1)S(1)}, u32[]{:S(2)}) copy-start(bf16[4096,128]{1,0:T(8,128)(2,1)S(1)} %collective-permute-done.38.refs_6_) | copy-start | bytes 3145732
  251.3 27.8 %copy-start.18 = (bf16[4096,128]{1,0:T(8,128)(2,1)}, bf16[4096,128]{1,0:T(8,128)(2,1)S(1)}, u32[]{:S(2)}) copy-start(bf16[4096,128]{1,0:T(8,128)(2,1)S(1)} %collective-permute-done.40.refs_7_) | copy-start | bytes 3145732
  272.2 6.1 %collective-permute-start.44 = (bf16[512,128]{1,0:T(8,128)(2,1)S(1)}, bf16[512,128]{1,0:T(8,128)(2,1)S(1)}, u32[]{:S(2)}, u32[]{:S(2)}) collective-permute-start(bf16[512,128]{1,0:T(8,128)(2,1)S(1)} %get-tuple-element.183), channel_id=1, source_target_pairs={{0,8},{1,9},{2,10},{3,11},{4,12},{5,13},{6,14},{7,15},{8,0},{9,1},... | collective-permute-start | bytes 393224 | tf_op jit(solution)/shard_map/ppermute | solution.py:712
  272.8 6.2 %collective-permute-start.45 = (bf16[512,128]{1,0:T(8,128)(2,1)S(1)}, bf16[512,128]{1,0:T(8,128)(2,1)S(1)}, u32[]{:S(2)}, u32[]{:S(2)}) collective-permute-start(bf16[512,128]{1,0:T(8,128)(2,1)S(1)} %get-tuple-element.184), channel_id=1, source_target_pairs={{0,16},{1,17},{2,18},{3,19},{4,20},{5,21},{6,22},{7,23},{8,24},{9,... | collective-permute-start | bytes 393224 | tf_op jit(solution)/shard_map/ppermute | solution.py:712
  274.0 9.4 %collective-permute-start.46 = (bf16[512,128]{1,0:T(8,128)(2,1)S(1)}, bf16[512,128]{1,0:T(8,128)(2,1)S(1)}, u32[]{:S(2)}, u32[]{:S(2)}) collective-permute-start(bf16[512,128]{1,0:T(8,128)(2,1)S(1)} %get-tuple-element.185), channel_id=1, source_target_pairs={{0,24},{1,25},{2,26},{3,27},{4,28},{5,29},{6,30},{7,31},{8,16},{9,... | collective-permute-start | bytes 393224 | tf_op jit(solution)/shard_map/ppermute | solution.py:712
  275.8 7.7 %collective-permute-start.47 = (bf16[512,128]{1,0:T(8,128)(2,1)S(1)}, bf16[512,128]{1,0:T(8,128)(2,1)S(1)}, u32[]{:S(2)}, u32[]{:S(2)}) collective-permute-start(bf16[512,128]{1,0:T(8,128)(2,1)S(1)} %get-tuple-element.186), channel_id=1, source_target_pairs={{0,1},{1,0},{2,3},{3,2},{4,5},{5,4},{6,7},{7,6},{8,9},{9,8},{10,11... | collective-permute-start | bytes 393224 | tf_op jit(solution)/shard_map/ppermute | solution.py:712
  275.8 7.7 %collective-permute-start.48 = (bf16[512,128]{1,0:T(8,128)(2,1)S(1)}, bf16[512,128]{1,0:T(8,128)(2,1)S(1)}, u32[]{:S(2)}, u32[]{:S(2)}) collective-permute-start(bf16[512,128]{1,0:T(8,128)(2,1)S(1)} %get-tuple-element.187), channel_id=1, source_target_pairs={{0,9},{1,8},{2,11},{3,10},{4,13},{5,12},{6,15},{7,14},{8,1},{9,0},... | collective-permute-start | bytes 393224 | tf_op jit(solution)/shard_map/ppermute | solution.py:712
  278.4 8.5 %collective-permute-start.49 = (bf16[512,128]{1,0:T(8,128)(2,1)S(1)}, bf16[512,128]{1,0:T(8,128)(2,1)S(1)}, u32[]{:S(2)}, u32[]{:S(2)}) collective-permute-start(bf16[512,128]{1,0:T(8,128)(2,1)S(1)} %get-tuple-element.188), channel_id=1, source_target_pairs={{0,17},{1,16},{2,19},{3,18},{4,21},{5,20},{6,23},{7,22},{8,25},{9,... | collective-permute-start | bytes 393224 | tf_op jit(solution)/shard_map/ppermute | solution.py:712
  279.0 7.8 %collective-permute-start.50 = (bf16[512,128]{1,0:T(8,128)(2,1)S(1)}, bf16[512,128]{1,0:T(8,128)(2,1)S(1)}, u32[]{:S(2)}, u32[]{:S(2)}) collective-permute-start(bf16[512,128]{1,0:T(8,128)(2,1)S(1)} %get-tuple-element.189), channel_id=1, source_target_pairs={{0,25},{1,24},{2,27},{3,26},{4,29},{5,28},{6,31},{7,30},{8,17},{9,... | collective-permute-start | bytes 393224 | tf_op jit(solution)/shard_map/ppermute | solution.py:712
  303.8 1.2 collective-permute-start.51
  304.9 5.4 %collective-permute-start.54 = (f32[8,128]{1,0:T(8,128)S(1)}, f32[8,128]{1,0:T(8,128)S(1)}, u32[]{:S(2)}, u32[]{:S(2)}) collective-permute-start(f32[8,128]{1,0:T(8,128)S(1)} %add.67.refs_0_), channel_id=1, source_target_pairs={{0,6},{1,7},{2,4},{3,5},{4,2},{5,3},{6,0},{7,1},{8,14},{9,15},{10,... | collective-permute-start | bytes 12296 | tf_op jit(solution)/shard_map/ppermute | solution.py:499
  306.3 4.5 %collective-permute-start.53 = (f32[8,128]{1,0:T(8,128)S(1)}, f32[8,128]{1,0:T(8,128)S(1)}, u32[]{:S(2)}, u32[]{:S(2)}) collective-permute-start(f32[8,128]{1,0:T(8,128)S(1)} %add.67.refs_0_), channel_id=1, source_target_pairs={{0,4},{1,5},{2,6},{3,7},{4,0},{5,1},{6,2},{7,3},{8,12},{9,13},{10,... | collective-permute-start | bytes 12296 | tf_op jit(solution)/shard_map/ppermute | solution.py:499
  306.3 4.6 %collective-permute-start.52 = (f32[8,128]{1,0:T(8,128)S(1)}, f32[8,128]{1,0:T(8,128)S(1)}, u32[]{:S(2)}, u32[]{:S(2)}) collective-permute-start(f32[8,128]{1,0:T(8,128)S(1)} %add.67.refs_0_), channel_id=1, source_target_pairs={{0,2},{1,3},{2,0},{3,1},{4,6},{5,7},{6,4},{7,5},{8,10},{9,11},{10,... | collective-permute-start | bytes 12296 | tf_op jit(solution)/shard_map/ppermute | solution.py:499
  (14 other events, 80.4 us)

commit v4 on v3

--- a/solution.py
+++ b/solution.py
@@ -39,6 +39,12 @@
 
 def turns(ways):
     return [0] + list(reversed(range(1, ways)))
+
+
+def pieces(ways):
+    if ways == 4:
+        return [(0, None), (3, 0), (3, 1), (2, 0), (2, 1), (1, None)]
+    return [(step, None) for step in turns(ways)]
 
 
 def places():
@@ -149,7 +155,7 @@
 def forward_kernel(layer, ways, live_shape, live_hbm, *refs):
     line, core, section = places()
     whole, last = layer == 0, layer == len(HOLDS) - 1
-    count = 1 if whole else ways
+    count = 1 if whole else len(pieces(ways))
     shards, refs = refs[:count], refs[count:]
     if last:
         arriving_ref, refs = refs[0], refs[1:]
@@ -158,7 +164,7 @@
     weight_refs, refs = refs[:held], refs[held:]
     if not whole:
         refs = refs[len(HOLDS) :]
-    outs = 2 + ways if last else 3
+    outs = 2 + ways if last else 5 if ways == 4 else 3
     outputs, refs = refs[:outs], refs[outs:]
     sends, refs = refs[: len(HOLDS)], refs[len(HOLDS) :]
     u_ref, send_sem, live, live_sem = refs[:4]
@@ -184,8 +190,10 @@
     if whole:
         u_ref[...] = (shards[0][...].astype(F32) * inverse).astype(BF16)
     else:
-        for step, shard in zip(turns(ways), shards):
-            u_ref[pl.ds((line ^ step) * rows, rows), :] = (
+        for (step, half), shard in zip(pieces(ways), shards):
+            height = shard.shape[0]
+            first = (line ^ step) * rows + (half or 0) * height
+            u_ref[pl.ds(pl.multiple_of(first, height), height), :] = (
                 shard[...].astype(F32) * inverse
             ).astype(BF16)
     for step, send in enumerate(sends):
@@ -241,7 +249,11 @@
     if not last:
         own = shards[0][pl.ds(line * rows, rows), :] if whole else shards[0][...]
         pre = z_ref[...]
-        outputs[2][...] = (own.astype(F32) + pre * jax.nn.sigmoid(pre)).astype(BF16)
+        value = (own.astype(F32) + pre * jax.nn.sigmoid(pre)).astype(BF16)
+        outputs[2][...] = value
+        for number, half_ref in enumerate(outputs[3:]):
+            height = half_ref.shape[0]
+            half_ref[...] = value[number * height : (number + 1) * height]
 
 
 def pre_gradient(arriving, pre):
@@ -614,6 +626,7 @@
             scratch += [pltpu.VMEM((rows, tokens), F32), pltpu.VMEM((features, tokens), F32)]
         else:
             outs += [pltpu.VMEM((rows, tokens), F32), pltpu.VMEM((rows, tokens), BF16)]
+            outs += [sds((rows // 2, tokens), BF16)] * (2 if ways == 4 else 0)
         plain = len(outs)
         outs += [pltpu.HBM((features, tokens), BF16)] * sections
         operands = in_vmem([loaded[layer]]) if layer in loaded else layer_weights(layer)
@@ -636,7 +649,12 @@
         if not last:
             pre_acts.append(result[1])
             entering.append(result[2])
-            shards = along_line([result[2]] * ways)
+            if ways == 4:
+                far = [to_line(value, 2) for value in result[3:5]]
+                near = to_line(result[2], 1)
+                shards = [result[2], *[to_line(value, 1) for value in far], *far, near]
+            else:
+                shards = along_line([result[2]] * ways)
             if layer > 0:
                 loaded[layer + 1] = load(layer + 1, result[2])
             if layer == 2:

time: 314 us -> 297 us (0.946)
  waiting for transfers between devices: 147 us -> 138 us
  starting transfers between devices: 71.1 us -> 62.7 us
    ppermute x27 -> x33, starting transfers between devices: 52.1 us -> 43.3 us  [to_line(): lax.ppermute(value, 'dp', [(i, i ^ 2 * step) for i in range(devices)])]
    ppermute x27 -> x33, waiting for transfers between devices: 105 us -> 100 us  [to_line(): lax.ppermute(value, 'dp', [(i, i ^ 2 * step) for i in range(devices)])]
    ppermute x9, waiting for transfers between devices: 30.6 us -> 27.2 us  [to_pipe(): return lax.ppermute(value, 'pipe', [(i, i ^ step) for i in range(sections)])]
  transfers between devices with their start and end apart: 55 -> 61, of which waited for: 29 -> 32; matrix products, arithmetic and copies ran while one was open for 5% -> 5% of each run, Pallas kernels for 8% -> 9%
where the time goes in v4:
time: 297 us; the launch traced here: 296 us
  waiting for transfers between devices  138 us (46%)
  Pallas kernels  71.8 us (24%)
  starting transfers between devices  62.7 us (21%)
  local copies, waits for them, and re-layouts  19.3 us (6%)
    ppermute x33, waiting for transfers between devices, to_line(): lax.ppermute(value, 'dp', [(i, i ^ 2 * step) for i in range(devices)])  100 us
    ppermute x33, starting transfers between devices, to_line(): lax.ppermute(value, 'dp', [(i, i ^ 2 * step) for i in range(devices)])  43.3 us
    ppermute x9, waiting for transfers between devices, to_pipe(): return lax.ppermute(value, 'pipe', [(i, i ^ step) for i in range(sections)])  27.2 us
    pallas_call x4, Pallas kernels, local(): kernel_call(functools.partial(forward_kernel, layer, ways, live_shape), f...  23 us
    pallas_call x1, Pallas kernels, local(): pl.pallas_call(functools.partial(update_kernel, chunks, 1.0 / all_tokens,...  16.9 us
    pallas_call x3, Pallas kernels, local(): kernel_call(functools.partial(backward_kernel, layer, ways, live_shape),...  13.8 us
    ppermute x9, starting transfers between devices, to_pipe(): return lax.ppermute(value, 'pipe', [(i, i ^ step) for i in range(sections)])  11.6 us
    dynamic_update_slice x4, local copies, waits for them, and re-layouts, local(): x_all = lax.dynamic_update_index_in_dim(x_all, part, line ^ step, 0)  6.78 us
  transfers between devices with their start and end apart: 61, of which 32 were waited for; matrix products, arithmetic and copies ran while one was open for 5% of the time, Pallas kernels for 9%

profile of v4, /device:TPU:0, one launch (start us, length us, event | category | flops | bytes accessed | tf_op | source)
XLA Modules:
  0.0 296.2 jit_solution(13503067961906674922)
XLA Ops:
  2.2 1.6 split.1
  3.8 3.0 %collective-permute-start = (bf16[272,2048]{1,0:T(8,128)(2,1)S(1)}, bf16[272,2048]{1,0:T(8,128)(2,1)S(1)}, u32[]{:S(2)}, u32[]{:S(2)}) collective-permute-start(bf16[272,2048]{1,0:T(8,128)(2,1)S(1)} %get-tuple-element.105), channel_id=1, source_target_pairs={{0,8},{8,0},{16,24},{24,16},{1,9},{9,1},{17,25},{25,17},{2,10},{10... | collective-permute-start | bytes 3342344 | tf_op jit(solution)/shard_map/ppermute | solution.py:508
  6.8 1.5 collective-permute-start.1
  9.4 1.8 dynamic-slice_dynamic-update-slice_fusion
  11.2 1.6 collective-permute-start.4
  12.7 2.6 collective-permute-start.3
  15.7 1.7 dynamic-slice_dynamic-update-slice_fusion.1
  17.5 6.0 %collective-permute-done.4 = bf16[32,4096]{1,0:T(8,128)(2,1)} collective-permute-done((bf16[32,4096]{1,0:T(8,128)(2,1)}, bf16[32,4096]{1,0:T(8,128)(2,1)}, u32[]{:S(2)}, u32[]{:S(2)}) %collective-permute-start.4) | collective-permute-done | bytes 262176 | tf_op jit(solution)/shard_map/ppermute | solution.py:511
  23.5 10.9 %collective-permute-done.3 = bf16[32,4096]{1,0:T(8,128)(2,1)} collective-permute-done((bf16[32,4096]{1,0:T(8,128)(2,1)}, bf16[32,4096]{1,0:T(8,128)(2,1)}, u32[]{:S(2)}, u32[]{:S(2)}) %collective-permute-start.3) | collective-permute-done | bytes 262176 | tf_op jit(solution)/shard_map/ppermute | solution.py:511
  35.4 2.5 pick2.1
  39.2 1.7 bitcast_dynamic-update-slice_fusion.2
  40.8 1.7 bitcast_dynamic-update-slice_fusion.1
  42.5 1.7 bitcast_dynamic-update-slice_fusion
  44.2 2.3 copy.37
  47.3 4.3 %collective-permute-start.10 = (bf16[32,1024]{1,0:T(8,128)(2,1)}, bf16[32,1024]{1,0:T(8,128)(2,1)S(1)}, u32[]{:S(2)}, u32[]{:S(2)}) collective-permute-start(bf16[32,1024]{1,0:T(8,128)(2,1)} %get-tuple-element.118), channel_id=1, source_target_pairs={{0,2},{1,3},{2,0},{3,1},{4,6},{5,7},{6,4},{7,5},{8,10},{9,11},{10,... | collective-permute-start | bytes 196616 | tf_op jit(solution)/shard_map/ppermute | solution.py:511
  54.1 1.6 pick3.1
  55.6 8.3 %collective-permute-done.6.refs_5_.refs_4_ = bf16[256,2048]{1,0:T(8,128)(2,1)} collective-permute-done((bf16[256,2048]{1,0:T(8,128)(2,1)}, bf16[256,2048]{1,0:T(8,128)(2,1)}, u32[]{:S(2)}, u32[]{:S(2)}) %collective-permute-start.6) | collective-permute-done | bytes 1048608 | tf_op jit(solution)/shard_map/ppermute | solution.py:508
  64.0 1.4 collective-permute-done.5.refs_3_.refs_8_.refs_2_
  66.5 1.5 collective-permute-start.21
  71.9 5.6 %forward0.1 = (f32[8,128]{1,0:T(8,128)}, f32[1024,128]{1,0:T(8,128)S(1)}, bf16[1024,128]{1,0:T(8,128)(2,1)S(1)}, bf16[512,128]{1,0:T(8,128)(2,1)S(1)}, bf16[512,...) custom-call(s32[8192]{0:T(1024)} %pad_add_fusion.live_hbm, ...), custom_call_target="tpu_custom_call" | custom-call | tf_op jit(solution)/shard_map/forward0/pallas_call | solution.py:634
  77.5 5.3 %collective-permute-start.15 = (bf16[512,128]{1,0:T(8,128)(2,1)S(1)}, bf16[512,128]{1,0:T(8,128)(2,1)S(1)}, u32[]{:S(2)}, u32[]{:S(2)}) collective-permute-start(bf16[512,128]{1,0:T(8,128)(2,1)S(1)} %get-tuple-element.129), channel_id=1, source_target_pairs={{0,4},{1,5},{2,6},{3,7},{4,0},{5,1},{6,2},{7,3},{8,12},{9,13},{10,... | collective-permute-start | bytes 393224 | tf_op jit(solution)/shard_map/ppermute | solution.py:511
  82.8 1.9 collective-permute-start.19
  84.7 8.1 %collective-permute-done.15.refs_3_ = bf16[512,128]{1,0:T(8,128)(2,1)S(1)} collective-permute-done((bf16[512,128]{1,0:T(8,128)(2,1)S(1)}, bf16[512,128]{1,0:T(8,128)(2,1)S(1)}, u32[]{:S(2)}, u32[]{:S(2)}) %collective-permute-start.15) | collective-permute-done | bytes 131104 | tf_op jit(solution)/shard_map/ppermute | solution.py:511
  92.7 2.3 collective-permute-done.17.refs_4_
  95.1 3.9 %collective-permute-done.16.refs_1_ = bf16[512,128]{1,0:T(8,128)(2,1)S(1)} collective-permute-done((bf16[512,128]{1,0:T(8,128)(2,1)S(1)}, bf16[512,128]{1,0:T(8,128)(2,1)S(1)}, u32[]{:S(2)}, u32[]{:S(2)}) %collective-permute-start.16) | collective-permute-done | bytes 131104 | tf_op jit(solution)/shard_map/ppermute | solution.py:511
  99.0 1.9 collective-permute-done.18.refs_2_
  101.4 2.1 collective-permute-done.22.refs_15_.refs_8_.refs_10_.refs_9_
  103.6 1.5 collective-permute-done.23.refs_17_.refs_11_.refs_13_
  106.1 4.0 %forward1.1 = (f32[8,128]{1,0:T(8,128)S(1)}, f32[1024,128]{1,0:T(8,128)S(1)}, bf16[1024,128]{1,0:T(8,128)(2,1)S(1)}, bf16[512,128]{1,0:T(8,128)(2,1)S(1)}, bf16[...) custom-call(s32[8192]{0:T(1024)} %pad_add_fusion.live_hbm, ...), custom_call_target="tpu_custom_call", output_to_operand_aliasing={{5}: (19, {}), {6}: (20, {}), {7}: (21, {}), {8}: (22, {})} | custom-call | tf_op jit(solution)/shard_map/forward1/pallas_call | solution.py:634
  111.5 1.6 collective-permute-start.26
  113.1 1.4 collective-permute-start.28
  114.5 8.6 %collective-permute-done.24.refs_3_ = bf16[512,128]{1,0:T(8,128)(2,1)S(1)} collective-permute-done((bf16[512,128]{1,0:T(8,128)(2,1)S(1)}, bf16[512,128]{1,0:T(8,128)(2,1)S(1)}, u32[]{:S(2)}, u32[]{:S(2)}) %collective-permute-start.24) | collective-permute-done | bytes 131104 | tf_op jit(solution)/shard_map/ppermute | solution.py:511
  123.1 2.0 collective-permute-done.26.refs_4_
  125.2 2.2 load2.1.refs_6_.refs_8_
  127.4 2.1 collective-permute-done.25.refs_1_
  129.6 1.6 collective-permute-done.27.refs_2_
  131.1 3.9 %forward2.1 = (f32[8,128]{1,0:T(8,128)S(1)}, f32[1024,128]{1,0:T(8,128)S(1)}, bf16[1024,128]{1,0:T(8,128)(2,1)S(1)}, bf16[512,128]{1,0:T(8,128)(2,1)S(1)}, bf16[...) custom-call(s32[8192]{0:T(1024)} %pad_add_fusion.live_hbm, ...), custom_call_target="tpu_custom_call", output_to_operand_aliasing={{5}: (8, {}), {6}: (9, {}), {7}: (10, {}), {8}: (11, {})} | custom-call | tf_op jit(solution)/shard_map/forward2/pallas_call | solution.py:634
  136.1 1.9 collective-permute-start.31
  138.0 7.6 %collective-permute-done.29.refs_3_ = bf16[512,128]{1,0:T(8,128)(2,1)S(1)} collective-permute-done((bf16[512,128]{1,0:T(8,128)(2,1)S(1)}, bf16[512,128]{1,0:T(8,128)(2,1)S(1)}, u32[]{:S(2)}, u32[]{:S(2)}) %collective-permute-start.29) | collective-permute-done | bytes 131104 | tf_op jit(solution)/shard_map/ppermute | solution.py:511
  145.7 2.7 collective-permute-done.31.refs_4_
  150.2 2.2 load3.1.refs_7_
  152.5 1.8 collective-permute-done.30.refs_1_
  155.7 9.6 %forward3.1 = (f32[8,128]{1,0:T(8,128)S(1)}, bf16[1024,128]{1,0:T(8,128)(2,1)S(1)}, bf16[1040,128]{1,0:T(8,128)(2,1)S(1)}, bf16[1040,128]{1,0:T(8,128)(2,1)S(1)}...) custom-call(s32[8192]{0:T(1024)} %pad_add_fusion.live_hbm, ...), custom_call_target="tpu_custom_call", output_to_operand_aliasing={{6}: (9, {}), {7}: (10, {}), {8}: (11, {}), {9}: (12, {})} | custom-call | tf_op jit(solution)/shard_map/forward3/pallas_call | solution.py:634
  165.9 1.6 collective-permute-start.35
  168.5 3.4 %collective-permute-start.38 = (bf16[1040,128]{1,0:T(8,128)(2,1)S(1)}, bf16[1040,128]{1,0:T(8,128)(2,1)S(1)}, u32[]{:S(2)}, u32[]{:S(2)}) collective-permute-start(bf16[1040,128]{1,0:T(8,128)(2,1)S(1)} %get-tuple-element.166), channel_id=1, source_target_pairs={{0,2},{1,3},{2,0},{3,1},{4,6},{5,7},{6,4},{7,5},{8,10},{9,11},{10,... | collective-permute-start | bytes 798728 | tf_op jit(solution)/shard_map/ppermute | solution.py:511
  171.9 17.2 %collective-permute-done.34.refs_1_ = bf16[4096,128]{1,0:T(8,128)(2,1)S(1)} collective-permute-done((bf16[4096,128]{1,0:T(8,128)(2,1)}, bf16[4096,128]{1,0:T(8,128)(2,1)S(1)}, u32[]{:S(2)}, u32[]{:S(2)}) %collective-permute-start.34) | collective-permute-done | bytes 1048608 | tf_op jit(solution)/shard_map/ppermute | solution.py:508
  190.2 6.6 %backward2.1 = (bf16[1024,128]{1,0:T(8,128)(2,1)S(1)}, bf16[1040,128]{1,0:T(8,128)(2,1)S(1)}, bf16[1040,128]{1,0:T(8,128)(2,1)S(1)}, bf16[1040,128]{1,0:T(8,128)...) custom-call(s32[8192]{0:T(1024)} %pad_add_fusion.live_hbm, bf16[1024,128]{1,0:T(8,128)(2,1)S(1)} %bitcast.51, ...), custom_call_target="tpu_custom_call" | custom-call | tf_op jit(solution)/shard_map/backward2/pallas_call | solution.py:684
  197.4 1.7 collective-permute-start.45
  201.6 2.9 collective-permute-start.43
  204.5 2.2 load1.1.refs_8_
  206.7 3.6 %collective-permute-done.41.refs_4_ = bf16[1040,128]{1,0:T(8,128)(2,1)S(1)} collective-permute-done((bf16[1040,128]{1,0:T(8,128)(2,1)S(1)}, bf16[1040,128]{1,0:T(8,128)(2,1)S(1)}, u32[]{:S(2)}, u32[]{:S(2)}) %collective-permute-start.41) | collective-permute-done | bytes 266272 | tf_op jit(solution)/shard_map/ppermute | solution.py:511
  210.3 13.5 %collective-permute-done.42.refs_5_ = bf16[1040,128]{1,0:T(8,128)(2,1)S(1)} collective-permute-done((bf16[1040,128]{1,0:T(8,128)(2,1)S(1)}, bf16[1040,128]{1,0:T(8,128)(2,1)S(1)}, u32[]{:S(2)}, u32[]{:S(2)}) %collective-permute-start.42) | collective-permute-done | bytes 266272 | tf_op jit(solution)/shard_map/ppermute | solution.py:511
  223.8 6.5 %backward1.1 = (bf16[1024,128]{1,0:T(8,128)(2,1)S(1)}, bf16[1040,128]{1,0:T(8,128)(2,1)S(1)}, bf16[1040,128]{1,0:T(8,128)(2,1)S(1)}, bf16[1040,128]{1,0:T(8,128)...) custom-call(s32[8192]{0:T(1024)} %pad_add_fusion.live_hbm, ...), custom_call_target="tpu_custom_call" | custom-call | tf_op jit(solution)/shard_map/backward1/pallas_call | solution.py:684
  232.1 3.2 %collective-permute-start.49 = (bf16[1040,128]{1,0:T(8,128)(2,1)S(1)}, bf16[1040,128]{1,0:T(8,128)(2,1)S(1)}, u32[]{:S(2)}, u32[]{:S(2)}) collective-permute-start(bf16[1040,128]{1,0:T(8,128)(2,1)S(1)} %get-tuple-element.191), channel_id=1, source_target_pairs={{0,2},{1,3},{2,0},{3,1},{4,6},{5,7},{6,4},{7,5},{8,10},{9,11},{10,... | collective-permute-start | bytes 798728 | tf_op jit(solution)/shard_map/ppermute | solution.py:511
  235.4 6.8 %collective-permute-done.47.refs_4_ = bf16[1040,128]{1,0:T(8,128)(2,1)S(1)} collective-permute-done((bf16[1040,128]{1,0:T(8,128)(2,1)S(1)}, bf16[1040,128]{1,0:T(8,128)(2,1)S(1)}, u32[]{:S(2)}, u32[]{:S(2)}) %collective-permute-start.47) | collective-permute-done | bytes 266272 | tf_op jit(solution)/shard_map/ppermute | solution.py:511
  242.1 12.1 %collective-permute-done.48.refs_5_ = bf16[1040,128]{1,0:T(8,128)(2,1)S(1)} collective-permute-done((bf16[1040,128]{1,0:T(8,128)(2,1)S(1)}, bf16[1040,128]{1,0:T(8,128)(2,1)S(1)}, u32[]{:S(2)}, u32[]{:S(2)}) %collective-permute-start.48) | collective-permute-done | bytes 266272 | tf_op jit(solution)/shard_map/ppermute | solution.py:511
  256.6 1.9 collective-permute-start.52
  259.1 2.0 collective-permute-done.50.refs_1_
  262.7 3.5 %gather_u.1.refs_8_ = bf16[8,4096,128]{2,1,0:T(8,128)(2,1)S(1)} custom-call(bf16[4096,128]{1,0:T(8,128)(2,1)} %get-tuple-element.173.refs_0_, bf16[4096,128]{1,0:T(8,128)(2,1)} %copy-done.12, bf16[4096,128]{1,0:T(8,128)(2,1)} %copy-done.13, bf16[4096,128]{1,0:T(8,128)(2,1)} %copy-done.16, bf16[4096,128]{1,0:T(8,128)(2,1)} %copy-done.14, ...), custom_call_target="tpu_custom_call" | custom-call | bytes 33554432 | tf_op jit(solution)/shard_map/gather_u/pallas_call | solution.py:712
  266.2 3.3 %collective-permute-done.55.refs_6_ = bf16[512,128]{1,0:T(8,128)(2,1)S(1)} collective-permute-done((bf16[512,128]{1,0:T(8,128)(2,1)S(1)}, bf16[512,128]{1,0:T(8,128)(2,1)S(1)}, u32[]{:S(2)}, u32[]{:S(2)}) %collective-permute-start.55) | collective-permute-done | bytes 131104 | tf_op jit(solution)/shard_map/ppermute | solution.py:730
  269.5 16.9 %update.1 = (f32[8,64,2048]{2,1,0:T(8,128)}, f32[8,64,2048]{2,1,0:T(8,128)}, bf16[8,64,2048]{2,1,0:T(8,128)(2,1)S(1)}, f32[8,2048]{1,0:T(8,128)S(1)}, f32[8,128]{1,0:T(8,128)S(1)}) custom-call(s32[2048]{0:T(1024)S(1)} %reshape_squeeze.6.live, bf16[512,128]{1,0:T(8,128)(2,1)S(1)} %get-tuple-element.194.refs_0_, ...), custom_call_target="tpu_custom_call" | custom-call | tf_op jit(solution)/shard_map/update/pallas_call | solution.py:751
  287.6 2.0 collective-permute-start.60
  289.6 2.4 collective-permute-start.58
  294.1 2.2 output.1
  (146 shorter events, 36.1 us)
Async XLA Ops:
  3.8 30.6 %collective-permute-start = (bf16[272,2048]{1,0:T(8,128)(2,1)S(1)}, bf16[272,2048]{1,0:T(8,128)(2,1)S(1)}, u32[]{:S(2)}, u32[]{:S(2)}) collective-permute-start(bf16[272,2048]{1,0:T(8,128)(2,1)S(1)} %get-tuple-element.105), channel_id=1, source_target_pairs={{0,8},{8,0},{16,24},{24,16},{1,9},{9,1},{17,25},{25,17},{2,10},{10... | collective-permute-start | bytes 3342344 | tf_op jit(solution)/shard_map/ppermute | solution.py:508
  6.8 27.7 %collective-permute-start.1 = (bf16[272,2048]{1,0:T(8,128)(2,1)S(1)}, bf16[272,2048]{1,0:T(8,128)(2,1)}, u32[]{:S(2)}, u32[]{:S(2)}) collective-permute-start(bf16[272,2048]{1,0:T(8,128)(2,1)S(1)} %get-tuple-element.106), channel_id=1, source_target_pairs={{0,16},{8,24},{16,0},{24,8},{1,17},{9,25},{17,1},{25,9},{2,18},{10... | collective-permute-start | bytes 3342344 | tf_op jit(solution)/shard_map/ppermute | solution.py:508
  11.2 12.4 %collective-permute-start.4 = (bf16[32,4096]{1,0:T(8,128)(2,1)}, bf16[32,4096]{1,0:T(8,128)(2,1)}, u32[]{:S(2)}, u32[]{:S(2)}) collective-permute-start(bf16[32,4096]{1,0:T(8,128)(2,1)} %get-tuple-element.212), channel_id=1, source_target_pairs={{0,2},{1,3},{2,0},{3,1},{4,6},{5,7},{6,4},{7,5},{8,10},{9,11},{10,... | collective-permute-start | bytes 786440 | tf_op jit(solution)/shard_map/ppermute | solution.py:511
  12.7 21.7 %collective-permute-start.3 = (bf16[32,4096]{1,0:T(8,128)(2,1)}, bf16[32,4096]{1,0:T(8,128)(2,1)}, u32[]{:S(2)}, u32[]{:S(2)}) collective-permute-start(bf16[32,4096]{1,0:T(8,128)(2,1)} %get-tuple-element.212), channel_id=1, source_target_pairs={{0,4},{1,5},{2,6},{3,7},{4,0},{5,1},{6,2},{7,3},{8,12},{9,13},{10,... | collective-permute-start | bytes 786440 | tf_op jit(solution)/shard_map/ppermute | solution.py:511
  15.3 19.1 %collective-permute-start.2 = (bf16[32,4096]{1,0:T(8,128)(2,1)}, bf16[32,4096]{1,0:T(8,128)(2,1)}, u32[]{:S(2)}, u32[]{:S(2)}) collective-permute-start(bf16[32,4096]{1,0:T(8,128)(2,1)} %get-tuple-element.212), channel_id=1, source_target_pairs={{0,6},{1,7},{2,4},{3,5},{4,2},{5,3},{6,0},{7,1},{8,14},{9,15},{10,... | collective-permute-start | bytes 786440 | tf_op jit(solution)/shard_map/ppermute | solution.py:511
  34.5 12.8 %collective-permute-start.8 = (bf16[272,2048]{1,0:T(8,128)(2,1)S(1)}, bf16[272,2048]{1,0:T(8,128)(2,1)S(1)}, u32[]{:S(2)}, u32[]{:S(2)}) collective-permute-start(bf16[272,2048]{1,0:T(8,128)(2,1)S(1)} %collective-permute-done.x1.refs_2_.refs_7_.refs_1_), channel_id=1, source_target_pairs={{0,1},{1,0},{2,3},{3,2},{4,5},{5,4},{6,7},{7,6},{8,9},{9,8},{10,11... | collective-permute-start | bytes 3342344 | tf_op jit(solution)/shard_map/ppermute | solution.py:518
  34.6 12.8 %collective-permute-start.9 = (bf16[272,2048]{1,0:T(8,128)(2,1)}, bf16[272,2048]{1,0:T(8,128)(2,1)}, u32[]{:S(2)}, u32[]{:S(2)}) collective-permute-start(bf16[272,2048]{1,0:T(8,128)(2,1)} %collective-permute-done.1.y1.refs_4_.refs_10_.refs_3_), channel_id=1, source_target_pairs={{0,1},{1,0},{2,3},{3,2},{4,5},{5,4},{6,7},{7,6},{8,9},{9,8},{10,11... | collective-permute-start | bytes 3342344 | tf_op jit(solution)/shard_map/ppermute | solution.py:518
  38.0 9.3 %collective-permute-start.7 = (bf16[512,2048]{1,0:T(8,128)(2,1)}, bf16[512,2048]{1,0:T(8,128)(2,1)}, u32[]{:S(2)}, u32[]{:S(2)}) collective-permute-start(bf16[512,2048]{1,0:T(8,128)(2,1)} %bitcast.own.refs_1_.refs_6_.refs_0_), channel_id=1, source_target_pairs={{0,1},{1,0},{2,3},{3,2},{4,5},{5,4},{6,7},{7,6},{8,9},{9,8},{10,11... | collective-permute-start | bytes 6291464 | tf_op jit(solution)/shard_map/ppermute | solution.py:518
  38.1 25.9 %collective-permute-start.6 = (bf16[256,2048]{1,0:T(8,128)(2,1)}, bf16[256,2048]{1,0:T(8,128)(2,1)}, u32[]{:S(2)}, u32[]{:S(2)}) collective-permute-start(bf16[256,2048]{1,0:T(8,128)(2,1)} %get-tuple-element.110), channel_id=1, source_target_pairs={{0,16},{8,24},{16,0},{24,8},{1,17},{9,25},{17,1},{25,9},{2,18},{10... | collective-permute-start | bytes 3145736 | tf_op jit(solution)/shard_map/ppermute | solution.py:508
  38.6 26.7 %collective-permute-start.5 = (bf16[272,2048]{1,0:T(8,128)(2,1)S(1)}, bf16[272,2048]{1,0:T(8,128)(2,1)}, u32[]{:S(2)}, u32[]{:S(2)}) collective-permute-start(bf16[272,2048]{1,0:T(8,128)(2,1)S(1)} %get-tuple-element.109), channel_id=1, source_target_pairs={{0,8},{8,0},{16,24},{24,16},{1,9},{9,1},{17,25},{25,17},{2,10},{10... | collective-permute-start | bytes 3342344 | tf_op jit(solution)/shard_map/ppermute | solution.py:508
  47.3 18.1 %collective-permute-start.10 = (bf16[32,1024]{1,0:T(8,128)(2,1)}, bf16[32,1024]{1,0:T(8,128)(2,1)S(1)}, u32[]{:S(2)}, u32[]{:S(2)}) collective-permute-start(bf16[32,1024]{1,0:T(8,128)(2,1)} %get-tuple-element.118), channel_id=1, source_target_pairs={{0,2},{1,3},{2,0},{3,1},{4,6},{5,7},{6,4},{7,5},{8,10},{9,11},{10,... | collective-permute-start | bytes 196616 | tf_op jit(solution)/shard_map/ppermute | solution.py:511
  51.6 13.8 %collective-permute-start.11 = (bf16[32,1024]{1,0:T(8,128)(2,1)S(1)}, bf16[32,1024]{1,0:T(8,128)(2,1)S(1)}, u32[]{:S(2)}, u32[]{:S(2)}) collective-permute-start(bf16[32,1024]{1,0:T(8,128)(2,1)S(1)} %get-tuple-element.119), channel_id=1, source_target_pairs={{0,4},{1,5},{2,6},{3,7},{4,0},{5,1},{6,2},{7,3},{8,12},{9,13},{10,... | collective-permute-start | bytes 196616 | tf_op jit(solution)/shard_map/ppermute | solution.py:511
  52.7 12.7 %collective-permute-start.12 = (bf16[32,1024]{1,0:T(8,128)(2,1)S(1)}, bf16[32,1024]{1,0:T(8,128)(2,1)S(1)}, u32[]{:S(2)}, u32[]{:S(2)}) collective-permute-start(bf16[32,1024]{1,0:T(8,128)(2,1)S(1)} %get-tuple-element.120), channel_id=1, source_target_pairs={{0,6},{1,7},{2,4},{3,5},{4,2},{5,3},{6,0},{7,1},{8,14},{9,15},{10,... | collective-permute-start | bytes 196616 | tf_op jit(solution)/shard_map/ppermute | solution.py:511
  65.4 4.5 %collective-permute-start.13 = (bf16[272,2048]{1,0:T(8,128)(2,1)}, bf16[272,2048]{1,0:T(8,128)(2,1)S(1)}, u32[]{:S(2)}, u32[]{:S(2)}) collective-permute-start(bf16[272,2048]{1,0:T(8,128)(2,1)} %collective-permute-done.5.refs_3_.refs_8_.refs_2_), channel_id=1, source_target_pairs={{0,1},{1,0},{2,3},{3,2},{4,5},{5,4},{6,7},{7,6},{8,9},{9,8},{10,11... | collective-permute-start | bytes 3342344 | tf_op jit(solution)/shard_map/ppermute | solution.py:518
  65.5 4.5 %collective-permute-start.14 = (bf16[256,2048]{1,0:T(8,128)(2,1)}, bf16[256,2048]{1,0:T(8,128)(2,1)S(1)}, u32[]{:S(2)}, u32[]{:S(2)}) collective-permute-start(bf16[256,2048]{1,0:T(8,128)(2,1)} %collective-permute-done.6.refs_5_.refs_4_), channel_id=1, source_target_pairs={{0,1},{1,0},{2,3},{3,2},{4,5},{5,4},{6,7},{7,6},{8,9},{9,8},{10,11... | collective-permute-start | bytes 3145736 | tf_op jit(solution)/shard_map/ppermute | solution.py:518
  66.0 29.1 %collective-permute-start.20 = (bf16[256,2048]{1,0:T(8,128)(2,1)S(1)}, bf16[256,2048]{1,0:T(8,128)(2,1)S(1)}, u32[]{:S(2)}, u32[]{:S(2)}) collective-permute-start(bf16[256,2048]{1,0:T(8,128)(2,1)S(1)} %get-tuple-element.133), channel_id=1, source_target_pairs={{0,8},{8,0},{16,24},{24,16},{1,9},{9,1},{17,25},{25,17},{2,10},{10... | collective-permute-start | bytes 3145736 | tf_op jit(solution)/shard_map/ppermute | solution.py:508
  66.5 28.6 %collective-permute-start.21 = (bf16[256,2048]{1,0:T(8,128)(2,1)S(1)}, bf16[256,2048]{1,0:T(8,128)(2,1)S(1)}, u32[]{:S(2)}, u32[]{:S(2)}) collective-permute-start(bf16[256,2048]{1,0:T(8,128)(2,1)S(1)} %get-tuple-element.134), channel_id=1, source_target_pairs={{0,16},{8,24},{16,0},{24,8},{1,17},{9,25},{17,1},{25,9},{2,18},{10... | collective-permute-start | bytes 3145736 | tf_op jit(solution)/shard_map/ppermute | solution.py:508
  77.5 15.3 %collective-permute-start.15 = (bf16[512,128]{1,0:T(8,128)(2,1)S(1)}, bf16[512,128]{1,0:T(8,128)(2,1)S(1)}, u32[]{:S(2)}, u32[]{:S(2)}) collective-permute-start(bf16[512,128]{1,0:T(8,128)(2,1)S(1)} %get-tuple-element.129), channel_id=1, source_target_pairs={{0,4},{1,5},{2,6},{3,7},{4,0},{5,1},{6,2},{7,3},{8,12},{9,13},{10,... | collective-permute-start | bytes 393224 | tf_op jit(solution)/shard_map/ppermute | solution.py:511
  82.7 12.3 %collective-permute-start.17 = (bf16[512,128]{1,0:T(8,128)(2,1)S(1)}, bf16[512,128]{1,0:T(8,128)(2,1)S(1)}, u32[]{:S(2)}, u32[]{:S(2)}) collective-permute-start(bf16[512,128]{1,0:T(8,128)(2,1)S(1)} %get-tuple-element.130), channel_id=1, source_target_pairs={{0,4},{1,5},{2,6},{3,7},{4,0},{5,1},{6,2},{7,3},{8,12},{9,13},{10,... | collective-permute-start | bytes 393224 | tf_op jit(solution)/shard_map/ppermute | solution.py:511
  82.8 18.1 %collective-permute-start.19 = (bf16[1024,128]{1,0:T(8,128)(2,1)S(1)}, bf16[1024,128]{1,0:T(8,128)(2,1)S(1)}, u32[]{:S(2)}, u32[]{:S(2)}) collective-permute-start(bf16[1024,128]{1,0:T(8,128)(2,1)S(1)} %get-tuple-element.128.refs_0_.refs_1_), channel_id=1, source_target_pairs={{0,2},{1,3},{2,0},{3,1},{4,6},{5,7},{6,4},{7,5},{8,10},{9,11},{10,... | collective-permute-start | bytes 786440 | tf_op jit(solution)/shard_map/ppermute | solution.py:511
  92.7 6.3 %collective-permute-start.16 = (bf16[512,128]{1,0:T(8,128)(2,1)S(1)}, bf16[512,128]{1,0:T(8,128)(2,1)S(1)}, u32[]{:S(2)}, u32[]{:S(2)}) collective-permute-start(bf16[512,128]{1,0:T(8,128)(2,1)S(1)} %collective-permute-done.15.refs_3_), channel_id=1, source_target_pairs={{0,2},{1,3},{2,0},{3,1},{4,6},{5,7},{6,4},{7,5},{8,10},{9,11},{10,... | collective-permute-start | bytes 393224 | tf_op jit(solution)/shard_map/ppermute | solution.py:511
  95.1 5.9 %collective-permute-start.18 = (bf16[512,128]{1,0:T(8,128)(2,1)S(1)}, bf16[512,128]{1,0:T(8,128)(2,1)S(1)}, u32[]{:S(2)}, u32[]{:S(2)}) collective-permute-start(bf16[512,128]{1,0:T(8,128)(2,1)S(1)} %collective-permute-done.17.refs_4_), channel_id=1, source_target_pairs={{0,2},{1,3},{2,0},{3,1},{4,6},{5,7},{6,4},{7,5},{8,10},{9,11},{10,... | collective-permute-start | bytes 393224 | tf_op jit(solution)/shard_map/ppermute | solution.py:511
  100.9 2.7 collective-permute-start.22
  100.9 4.2 %collective-permute-start.23 = (bf16[256,2048]{1,0:T(8,128)(2,1)S(1)}, bf16[256,2048]{1,0:T(8,128)(2,1)S(1)}, u32[]{:S(2)}, u32[]{:S(2)}) collective-permute-start(bf16[256,2048]{1,0:T(8,128)(2,1)S(1)} %collective-permute-done.21.refs_11_.refs_5_.refs_6_), channel_id=1, source_target_pairs={{0,1},{1,0},{2,3},{3,2},{4,5},{5,4},{6,7},{7,6},{8,9},{9,8},{10,11... | collective-permute-start | bytes 3145736 | tf_op jit(solution)/shard_map/ppermute | solution.py:518
  110.1 13.0 %collective-permute-start.24 = (bf16[512,128]{1,0:T(8,128)(2,1)S(1)}, bf16[512,128]{1,0:T(8,128)(2,1)S(1)}, u32[]{:S(2)}, u32[]{:S(2)}) collective-permute-start(bf16[512,128]{1,0:T(8,128)(2,1)S(1)} %get-tuple-element.144), channel_id=1, source_target_pairs={{0,4},{1,5},{2,6},{3,7},{4,0},{5,1},{6,2},{7,3},{8,12},{9,13},{10,... | collective-permute-start | bytes 393224 | tf_op jit(solution)/shard_map/ppermute | solution.py:511
  111.5 13.6 %collective-permute-start.26 = (bf16[512,128]{1,0:T(8,128)(2,1)S(1)}, bf16[512,128]{1,0:T(8,128)(2,1)S(1)}, u32[]{:S(2)}, u32[]{:S(2)}) collective-permute-start(bf16[512,128]{1,0:T(8,128)(2,1)S(1)} %get-tuple-element.145), channel_id=1, source_target_pairs={{0,4},{1,5},{2,6},{3,7},{4,0},{5,1},{6,2},{7,3},{8,12},{9,13},{10,... | collective-permute-start | bytes 393224 | tf_op jit(solution)/shard_map/ppermute | solution.py:511
  113.1 18.1 %collective-permute-start.28 = (bf16[1024,128]{1,0:T(8,128)(2,1)S(1)}, bf16[1024,128]{1,0:T(8,128)(2,1)S(1)}, u32[]{:S(2)}, u32[]{:S(2)}) collective-permute-start(bf16[1024,128]{1,0:T(8,128)(2,1)S(1)} %get-tuple-element.143.refs_0_.refs_1_), channel_id=1, source_target_pairs={{0,2},{1,3},{2,0},{3,1},{4,6},{5,7},{6,4},{7,5},{8,10},{9,11},{10,... | collective-permute-start | bytes 786440 | tf_op jit(solution)/shard_map/ppermute | solution.py:511
  123.1 6.4 %collective-permute-start.25 = (bf16[512,128]{1,0:T(8,128)(2,1)S(1)}, bf16[512,128]{1,0:T(8,128)(2,1)S(1)}, u32[]{:S(2)}, u32[]{:S(2)}) collective-permute-start(bf16[512,128]{1,0:T(8,128)(2,1)S(1)} %collective-permute-done.24.refs_3_), channel_id=1, source_target_pairs={{0,2},{1,3},{2,0},{3,1},{4,6},{5,7},{6,4},{7,5},{8,10},{9,11},{10,... | collective-permute-start | bytes 393224 | tf_op jit(solution)/shard_map/ppermute | solution.py:511
  125.1 6.0 %collective-permute-start.27 = (bf16[512,128]{1,0:T(8,128)(2,1)S(1)}, bf16[512,128]{1,0:T(8,128)(2,1)S(1)}, u32[]{:S(2)}, u32[]{:S(2)}) collective-permute-start(bf16[512,128]{1,0:T(8,128)(2,1)S(1)} %collective-permute-done.26.refs_4_), channel_id=1, source_target_pairs={{0,2},{1,3},{2,0},{3,1},{4,6},{5,7},{6,4},{7,5},{8,10},{9,11},{10,... | collective-permute-start | bytes 393224 | tf_op jit(solution)/shard_map/ppermute | solution.py:511
  135.0 10.6 %collective-permute-start.29 = (bf16[512,128]{1,0:T(8,128)(2,1)S(1)}, bf16[512,128]{1,0:T(8,128)(2,1)S(1)}, u32[]{:S(2)}, u32[]{:S(2)}) collective-permute-start(bf16[512,128]{1,0:T(8,128)(2,1)S(1)} %get-tuple-element.152), channel_id=1, source_target_pairs={{0,4},{1,5},{2,6},{3,7},{4,0},{5,1},{6,2},{7,3},{8,12},{9,13},{10,... | collective-permute-start | bytes 393224 | tf_op jit(solution)/shard_map/ppermute | solution.py:511
  136.1 12.3 %collective-permute-start.31 = (bf16[512,128]{1,0:T(8,128)(2,1)S(1)}, bf16[512,128]{1,0:T(8,128)(2,1)S(1)}, u32[]{:S(2)}, u32[]{:S(2)}) collective-permute-start(bf16[512,128]{1,0:T(8,128)(2,1)S(1)} %get-tuple-element.153), channel_id=1, source_target_pairs={{0,4},{1,5},{2,6},{3,7},{4,0},{5,1},{6,2},{7,3},{8,12},{9,13},{10,... | collective-permute-start | bytes 393224 | tf_op jit(solution)/shard_map/ppermute | solution.py:511
  138.0 17.7 %collective-permute-start.33 = (bf16[1024,128]{1,0:T(8,128)(2,1)S(1)}, bf16[1024,128]{1,0:T(8,128)(2,1)S(1)}, u32[]{:S(2)}, u32[]{:S(2)}) collective-permute-start(bf16[1024,128]{1,0:T(8,128)(2,1)S(1)} %get-tuple-element.151.refs_0_.refs_1_), channel_id=1, source_target_pairs={{0,2},{1,3},{2,0},{3,1},{4,6},{5,7},{6,4},{7,5},{8,10},{9,11},{10,... | collective-permute-start | bytes 786440 | tf_op jit(solution)/shard_map/ppermute | solution.py:511
  145.7 8.6 %collective-permute-start.30 = (bf16[512,128]{1,0:T(8,128)(2,1)S(1)}, bf16[512,128]{1,0:T(8,128)(2,1)S(1)}, u32[]{:S(2)}, u32[]{:S(2)}) collective-permute-start(bf16[512,128]{1,0:T(8,128)(2,1)S(1)} %collective-permute-done.29.refs_3_), channel_id=1, source_target_pairs={{0,2},{1,3},{2,0},{3,1},{4,6},{5,7},{6,4},{7,5},{8,10},{9,11},{10,... | collective-permute-start | bytes 393224 | tf_op jit(solution)/shard_map/ppermute | solution.py:511
  148.4 7.3 %collective-permute-start.32 = (bf16[512,128]{1,0:T(8,128)(2,1)S(1)}, bf16[512,128]{1,0:T(8,128)(2,1)S(1)}, u32[]{:S(2)}, u32[]{:S(2)}) collective-permute-start(bf16[512,128]{1,0:T(8,128)(2,1)S(1)} %collective-permute-done.31.refs_4_), channel_id=1, source_target_pairs={{0,2},{1,3},{2,0},{3,1},{4,6},{5,7},{6,4},{7,5},{8,10},{9,11},{10,... | collective-permute-start | bytes 393224 | tf_op jit(solution)/shard_map/ppermute | solution.py:511
  155.7 34.5 %copy-start.1 = (bf16[1024,2048]{1,0:T(8,128)(2,1)S(1)}, bf16[1024,2048]{1,0:T(8,128)(2,1)}, u32[]{:S(2)}) copy-start(bf16[1024,2048]{1,0:T(8,128)(2,1)} %copy-done) | copy-start | bytes 12582916
  165.3 23.8 %collective-permute-start.34 = (bf16[4096,128]{1,0:T(8,128)(2,1)}, bf16[4096,128]{1,0:T(8,128)(2,1)S(1)}, u32[]{:S(2)}, u32[]{:S(2)}) collective-permute-start(bf16[4096,128]{1,0:T(8,128)(2,1)} %get-tuple-element.161), channel_id=1, source_target_pairs={{0,8},{8,0},{16,24},{24,16},{1,9},{9,1},{17,25},{25,17},{2,10},{10... | collective-permute-start | bytes 3145736 | tf_op jit(solution)/shard_map/ppermute | solution.py:508
  165.9 23.4 %collective-permute-start.35 = (bf16[4096,128]{1,0:T(8,128)(2,1)}, bf16[4096,128]{1,0:T(8,128)(2,1)S(1)}, u32[]{:S(2)}, u32[]{:S(2)}) collective-permute-start(bf16[4096,128]{1,0:T(8,128)(2,1)} %get-tuple-element.162), channel_id=1, source_target_pairs={{0,16},{8,24},{16,0},{24,8},{1,17},{9,25},{17,1},{25,9},{2,18},{10... | collective-permute-start | bytes 3145736 | tf_op jit(solution)/shard_map/ppermute | solution.py:508
  167.5 21.8 %collective-permute-start.36 = (bf16[1040,128]{1,0:T(8,128)(2,1)S(1)}, bf16[1040,128]{1,0:T(8,128)(2,1)S(1)}, u32[]{:S(2)}, u32[]{:S(2)}) collective-permute-start(bf16[1040,128]{1,0:T(8,128)(2,1)S(1)} %get-tuple-element.164), channel_id=1, source_target_pairs={{0,6},{1,7},{2,4},{3,5},{4,2},{5,3},{6,0},{7,1},{8,14},{9,15},{10,... | collective-permute-start | bytes 798728 | tf_op jit(solution)/shard_map/ppermute | solution.py:511
  167.5 22.7 %collective-permute-start.37 = (bf16[1040,128]{1,0:T(8,128)(2,1)S(1)}, bf16[1040,128]{1,0:T(8,128)(2,1)S(1)}, u32[]{:S(2)}, u32[]{:S(2)}) collective-permute-start(bf16[1040,128]{1,0:T(8,128)(2,1)S(1)} %get-tuple-element.165), channel_id=1, source_target_pairs={{0,4},{1,5},{2,6},{3,7},{4,0},{5,1},{6,2},{7,3},{8,12},{9,13},{10,... | collective-permute-start | bytes 798728 | tf_op jit(solution)/shard_map/ppermute | solution.py:511
  168.5 21.7 %collective-permute-start.38 = (bf16[1040,128]{1,0:T(8,128)(2,1)S(1)}, bf16[1040,128]{1,0:T(8,128)(2,1)S(1)}, u32[]{:S(2)}, u32[]{:S(2)}) collective-permute-start(bf16[1040,128]{1,0:T(8,128)(2,1)S(1)} %get-tuple-element.166), channel_id=1, source_target_pairs={{0,2},{1,3},{2,0},{3,1},{4,6},{5,7},{6,4},{7,5},{8,10},{9,11},{10,... | collective-permute-start | bytes 798728 | tf_op jit(solution)/shard_map/ppermute | solution.py:511
  189.3 41.0 %copy-start.13 = (bf16[4096,128]{1,0:T(8,128)(2,1)}, bf16[4096,128]{1,0:T(8,128)(2,1)S(1)}, u32[]{:S(2)}) copy-start(bf16[4096,128]{1,0:T(8,128)(2,1)S(1)} %collective-permute-done.35.refs_2_) | copy-start | bytes 3145732
  196.9 3.8 %collective-permute-start.39 = (bf16[4096,128]{1,0:T(8,128)(2,1)S(1)}, bf16[4096,128]{1,0:T(8,128)(2,1)S(1)}, u32[]{:S(2)}, u32[]{:S(2)}) collective-permute-start(bf16[4096,128]{1,0:T(8,128)(2,1)S(1)} %copy-done.5), channel_id=1, source_target_pairs={{0,1},{1,0},{2,3},{3,2},{4,5},{5,4},{6,7},{7,6},{8,9},{9,8},{10,11... | collective-permute-start | bytes 3145736 | tf_op jit(solution)/shard_map/ppermute | solution.py:518
  197.0 9.8 %collective-permute-start.40 = (bf16[4096,128]{1,0:T(8,128)(2,1)S(1)}, bf16[4096,128]{1,0:T(8,128)(2,1)S(1)}, u32[]{:S(2)}, u32[]{:S(2)}) collective-permute-start(bf16[4096,128]{1,0:T(8,128)(2,1)S(1)} %collective-permute-done.34.refs_1_), channel_id=1, source_target_pairs={{0,1},{1,0},{2,3},{3,2},{4,5},{5,4},{6,7},{7,6},{8,9},{9,8},{10,11... | collective-permute-start | bytes 3145736 | tf_op jit(solution)/shard_map/ppermute | solution.py:518
  197.4 32.9 %collective-permute-start.45 = (bf16[4096,128]{1,0:T(8,128)(2,1)S(1)}, bf16[4096,128]{1,0:T(8,128)(2,1)S(1)}, u32[]{:S(2)}, u32[]{:S(2)}) collective-permute-start(bf16[4096,128]{1,0:T(8,128)(2,1)S(1)} %copy-done.10), channel_id=1, source_target_pairs={{0,24},{8,16},{16,8},{24,0},{1,25},{9,17},{17,9},{25,1},{2,26},{10... | collective-permute-start | bytes 3145736 | tf_op jit(solution)/shard_map/ppermute | solution.py:508
  199.1 11.2 %collective-permute-start.41 = (bf16[1040,128]{1,0:T(8,128)(2,1)S(1)}, bf16[1040,128]{1,0:T(8,128)(2,1)S(1)}, u32[]{:S(2)}, u32[]{:S(2)}) collective-permute-start(bf16[1040,128]{1,0:T(8,128)(2,1)S(1)} %get-tuple-element.176), channel_id=1, source_target_pairs={{0,6},{1,7},{2,4},{3,5},{4,2},{5,3},{6,0},{7,1},{8,14},{9,15},{10,... | collective-permute-start | bytes 798728 | tf_op jit(solution)/shard_map/ppermute | solution.py:511
  200.1 23.7 %collective-permute-start.42 = (bf16[1040,128]{1,0:T(8,128)(2,1)S(1)}, bf16[1040,128]{1,0:T(8,128)(2,1)S(1)}, u32[]{:S(2)}, u32[]{:S(2)}) collective-permute-start(bf16[1040,128]{1,0:T(8,128)(2,1)S(1)} %get-tuple-element.177), channel_id=1, source_target_pairs={{0,4},{1,5},{2,6},{3,7},{4,0},{5,1},{6,2},{7,3},{8,12},{9,13},{10,... | collective-permute-start | bytes 798728 | tf_op jit(solution)/shard_map/ppermute | solution.py:511
  201.6 22.2 %collective-permute-start.43 = (bf16[1040,128]{1,0:T(8,128)(2,1)S(1)}, bf16[1040,128]{1,0:T(8,128)(2,1)S(1)}, u32[]{:S(2)}, u32[]{:S(2)}) collective-permute-start(bf16[1040,128]{1,0:T(8,128)(2,1)S(1)} %get-tuple-element.178), channel_id=1, source_target_pairs={{0,2},{1,3},{2,0},{3,1},{4,6},{5,7},{6,4},{7,5},{8,10},{9,11},{10,... | collective-permute-start | bytes 798728 | tf_op jit(solution)/shard_map/ppermute | solution.py:511
  230.3 31.3 %copy-start.16 = (bf16[4096,128]{1,0:T(8,128)(2,1)}, bf16[4096,128]{1,0:T(8,128)(2,1)S(1)}, u32[]{:S(2)}) copy-start(bf16[4096,128]{1,0:T(8,128)(2,1)S(1)} %collective-permute-done.45.refs_3_) | copy-start | bytes 3145732
  230.4 5.0 %collective-permute-start.44 = (bf16[4096,128]{1,0:T(8,128)(2,1)S(1)}, bf16[4096,128]{1,0:T(8,128)(2,1)S(1)}, u32[]{:S(2)}, u32[]{:S(2)}) collective-permute-start(bf16[4096,128]{1,0:T(8,128)(2,1)S(1)} %collective-permute-done.35.refs_2_), channel_id=1, source_target_pairs={{0,1},{1,0},{2,3},{3,2},{4,5},{5,4},{6,7},{7,6},{8,9},{9,8},{10,11... | collective-permute-start | bytes 3145736 | tf_op jit(solution)/shard_map/ppermute | solution.py:518
  230.4 4.9 %collective-permute-start.46 = (bf16[4096,128]{1,0:T(8,128)(2,1)S(1)}, bf16[4096,128]{1,0:T(8,128)(2,1)S(1)}, u32[]{:S(2)}, u32[]{:S(2)}) collective-permute-start(bf16[4096,128]{1,0:T(8,128)(2,1)S(1)} %collective-permute-done.45.refs_3_), channel_id=1, source_target_pairs={{0,1},{1,0},{2,3},{3,2},{4,5},{5,4},{6,7},{7,6},{8,9},{9,8},{10,11... | collective-permute-start | bytes 3145736 | tf_op jit(solution)/shard_map/ppermute | solution.py:518
  230.9 11.2 %collective-permute-start.47 = (bf16[1040,128]{1,0:T(8,128)(2,1)S(1)}, bf16[1040,128]{1,0:T(8,128)(2,1)S(1)}, u32[]{:S(2)}, u32[]{:S(2)}) collective-permute-start(bf16[1040,128]{1,0:T(8,128)(2,1)S(1)} %get-tuple-element.189), channel_id=1, source_target_pairs={{0,6},{1,7},{2,4},{3,5},{4,2},{5,3},{6,0},{7,1},{8,14},{9,15},{10,... | collective-permute-start | bytes 798728 | tf_op jit(solution)/shard_map/ppermute | solution.py:511
  232.1 22.1 %collective-permute-start.48 = (bf16[1040,128]{1,0:T(8,128)(2,1)S(1)}, bf16[1040,128]{1,0:T(8,128)(2,1)S(1)}, u32[]{:S(2)}, u32[]{:S(2)}) collective-permute-start(bf16[1040,128]{1,0:T(8,128)(2,1)S(1)} %get-tuple-element.190), channel_id=1, source_target_pairs={{0,4},{1,5},{2,6},{3,7},{4,0},{5,1},{6,2},{7,3},{8,12},{9,13},{10,... | collective-permute-start | bytes 798728 | tf_op jit(solution)/shard_map/ppermute | solution.py:511
  232.1 22.1 %collective-permute-start.49 = (bf16[1040,128]{1,0:T(8,128)(2,1)S(1)}, bf16[1040,128]{1,0:T(8,128)(2,1)S(1)}, u32[]{:S(2)}, u32[]{:S(2)}) collective-permute-start(bf16[1040,128]{1,0:T(8,128)(2,1)S(1)} %get-tuple-element.191), channel_id=1, source_target_pairs={{0,2},{1,3},{2,0},{3,1},{4,6},{5,7},{6,4},{7,5},{8,10},{9,11},{10,... | collective-permute-start | bytes 798728 | tf_op jit(solution)/shard_map/ppermute | solution.py:511
  255.0 6.1 %collective-permute-start.50 = (bf16[512,128]{1,0:T(8,128)(2,1)S(1)}, bf16[512,128]{1,0:T(8,128)(2,1)S(1)}, u32[]{:S(2)}, u32[]{:S(2)}) collective-permute-start(bf16[512,128]{1,0:T(8,128)(2,1)S(1)} %get-tuple-element.195), channel_id=1, source_target_pairs={{0,8},{1,9},{2,10},{3,11},{4,12},{5,13},{6,14},{7,15},{8,0},{9,1},... | collective-permute-start | bytes 393224 | tf_op jit(solution)/shard_map/ppermute | solution.py:730
  255.5 6.1 %collective-permute-start.51 = (bf16[512,128]{1,0:T(8,128)(2,1)S(1)}, bf16[512,128]{1,0:T(8,128)(2,1)S(1)}, u32[]{:S(2)}, u32[]{:S(2)}) collective-permute-start(bf16[512,128]{1,0:T(8,128)(2,1)S(1)} %get-tuple-element.196), channel_id=1, source_target_pairs={{0,16},{1,17},{2,18},{3,19},{4,20},{5,21},{6,22},{7,23},{8,24},{9,... | collective-permute-start | bytes 393224 | tf_op jit(solution)/shard_map/ppermute | solution.py:730
  256.6 9.5 %collective-permute-start.52 = (bf16[512,128]{1,0:T(8,128)(2,1)S(1)}, bf16[512,128]{1,0:T(8,128)(2,1)S(1)}, u32[]{:S(2)}, u32[]{:S(2)}) collective-permute-start(bf16[512,128]{1,0:T(8,128)(2,1)S(1)} %get-tuple-element.197), channel_id=1, source_target_pairs={{0,24},{1,25},{2,26},{3,27},{4,28},{5,29},{6,30},{7,31},{8,16},{9,... | collective-permute-start | bytes 393224 | tf_op jit(solution)/shard_map/ppermute | solution.py:730
  258.5 7.6 %collective-permute-start.53 = (bf16[512,128]{1,0:T(8,128)(2,1)S(1)}, bf16[512,128]{1,0:T(8,128)(2,1)S(1)}, u32[]{:S(2)}, u32[]{:S(2)}) collective-permute-start(bf16[512,128]{1,0:T(8,128)(2,1)S(1)} %get-tuple-element.198), channel_id=1, source_target_pairs={{0,1},{1,0},{2,3},{3,2},{4,5},{5,4},{6,7},{7,6},{8,9},{9,8},{10,11... | collective-permute-start | bytes 393224 | tf_op jit(solution)/shard_map/ppermute | solution.py:730
  258.5 7.6 %collective-permute-start.54 = (bf16[512,128]{1,0:T(8,128)(2,1)S(1)}, bf16[512,128]{1,0:T(8,128)(2,1)S(1)}, u32[]{:S(2)}, u32[]{:S(2)}) collective-permute-start(bf16[512,128]{1,0:T(8,128)(2,1)S(1)} %get-tuple-element.199), channel_id=1, source_target_pairs={{0,9},{1,8},{2,11},{3,10},{4,13},{5,12},{6,15},{7,14},{8,1},{9,0},... | collective-permute-start | bytes 393224 | tf_op jit(solution)/shard_map/ppermute | solution.py:730
  261.1 8.4 %collective-permute-start.55 = (bf16[512,128]{1,0:T(8,128)(2,1)S(1)}, bf16[512,128]{1,0:T(8,128)(2,1)S(1)}, u32[]{:S(2)}, u32[]{:S(2)}) collective-permute-start(bf16[512,128]{1,0:T(8,128)(2,1)S(1)} %get-tuple-element.200), channel_id=1, source_target_pairs={{0,17},{1,16},{2,19},{3,18},{4,21},{5,20},{6,23},{7,22},{8,25},{9,... | collective-permute-start | bytes 393224 | tf_op jit(solution)/shard_map/ppermute | solution.py:730
  261.7 7.8 %collective-permute-start.56 = (bf16[512,128]{1,0:T(8,128)(2,1)S(1)}, bf16[512,128]{1,0:T(8,128)(2,1)S(1)}, u32[]{:S(2)}, u32[]{:S(2)}) collective-permute-start(bf16[512,128]{1,0:T(8,128)(2,1)S(1)} %get-tuple-element.201), channel_id=1, source_target_pairs={{0,25},{1,24},{2,27},{3,26},{4,29},{5,28},{6,31},{7,30},{8,17},{9,... | collective-permute-start | bytes 393224 | tf_op jit(solution)/shard_map/ppermute | solution.py:730
  286.4 1.2 collective-permute-start.57
  287.6 5.4 %collective-permute-start.60 = (f32[8,128]{1,0:T(8,128)S(1)}, f32[8,128]{1,0:T(8,128)S(1)}, u32[]{:S(2)}, u32[]{:S(2)}) collective-permute-start(f32[8,128]{1,0:T(8,128)S(1)} %add.67.refs_0_), channel_id=1, source_target_pairs={{0,6},{1,7},{2,4},{3,5},{4,2},{5,3},{6,0},{7,1},{8,14},{9,15},{10,... | collective-permute-start | bytes 12296 | tf_op jit(solution)/shard_map/ppermute | solution.py:511
  289.5 4.5 %collective-permute-start.59 = (f32[8,128]{1,0:T(8,128)S(1)}, f32[8,128]{1,0:T(8,128)S(1)}, u32[]{:S(2)}, u32[]{:S(2)}) collective-permute-start(f32[8,128]{1,0:T(8,128)S(1)} %add.67.refs_0_), channel_id=1, source_target_pairs={{0,4},{1,5},{2,6},{3,7},{4,0},{5,1},{6,2},{7,3},{8,12},{9,13},{10,... | collective-permute-start | bytes 12296 | tf_op jit(solution)/shard_map/ppermute | solution.py:511
  289.6 4.5 %collective-permute-start.58 = (f32[8,128]{1,0:T(8,128)S(1)}, f32[8,128]{1,0:T(8,128)S(1)}, u32[]{:S(2)}, u32[]{:S(2)}) collective-permute-start(f32[8,128]{1,0:T(8,128)S(1)} %add.67.refs_0_), channel_id=1, source_target_pairs={{0,2},{1,3},{2,0},{3,1},{4,6},{5,7},{6,4},{7,5},{8,10},{9,11},{10,... | collective-permute-start | bytes 12296 | tf_op jit(solution)/shard_map/ppermute | solution.py:511
  (20 other events, 189.7 us)

commit v5 on v4

--- a/solution.py
+++ b/solution.py
@@ -17,6 +17,7 @@
 VMEM = pl.BlockSpec(memory_space=pltpu.VMEM)
 SMEM = pl.BlockSpec(memory_space=pltpu.SMEM)
 HBM = pl.BlockSpec(memory_space=pltpu.HBM)
+ANY = pl.BlockSpec(memory_space=pl.ANY)
 
 
 def shrink(magnitude, threshold):
@@ -551,9 +552,13 @@
             scratch_shapes=[pltpu.SemaphoreType.DMA((3,))],
         )(*in_hbm((own, first_source, second_source)))
 
-    x_parts = {step: to_line(x_own, step) for step in turns(ways)[1:]}
-    x1, y1, *sent = slot(half1, half2, *x_parts.values())
-    x_parts = dict(zip(x_parts, sent))
+    if ways == 4:
+        far = [to_line(value, 2) for value in (x_own[: share // 2], x_own[share // 2 :])]
+        near = to_line(x_own, 1)
+        x_parts = [*[to_line(value, 1) for value in far], *far, near]
+    else:
+        x_parts = [to_line(x_own, step) for step in turns(ways)[1:]]
+    x1, y1, *x_parts = slot(half1, half2, *x_parts)
     siblings = dict(own=to_core(after(own, x1, y1)), x1=to_core(x1), y1=to_core(y1))
     cot_own = lax.dynamic_index_in_dim(cotangent, section, 0, keepdims=False)
     cot_parts = [
@@ -562,8 +567,9 @@
     cot_held = after(tuple(cot_parts), *siblings.values())
     cot_sent = [to_line(cot_held[step], step) for step in range(1, ways)]
     x_all = jnp.zeros((ways, share, features), BF16)
-    for step, part in [(0, x_own), *x_parts.items()]:
-        x_all = lax.dynamic_update_index_in_dim(x_all, part, line ^ step, 0)
+    for (step, half), part in zip(pieces(ways), [x_own, *x_parts]):
+        at = (line ^ step, (half or 0) * part.shape[0], 0)
+        x_all = lax.dynamic_update_slice(x_all, part[None], at)
     x_all = x_all.reshape(tokens, features).T
     third = tuple(pick(3, x1, after(y1, *siblings.values())))
     by_step = [flat_live] + [value[height].astype(jnp.int32) for value in (x1, y1)]
@@ -584,20 +590,23 @@
     live = jnp.concatenate([near_live, x2[height].astype(jnp.int32)])
     live_scratch = [pltpu.SMEM((own_live.size,), jnp.int32), pltpu.SemaphoreType.DMA((1,))]
 
-    def layer_weights(layer):
+    def layer_weights(layer, *anywhere):
         names = holders(layer)
-        return in_hbm([mine[name] for name in names] + [siblings[name] for name in names])
+        operands = in_hbm([mine[name] for name in names])
+        for name in names:
+            operands += [siblings[name]] if name in anywhere else in_hbm([siblings[name]])
+        return operands, [HBM] * len(names) + [ANY if name in anywhere else HBM for name in names]
 
     def sds(shape, dtype):
         return jax.ShapeDtypeStruct(shape, dtype)
 
     def load(layer, ready):
-        operands = layer_weights(layer)
+        operands, specs = layer_weights(layer)
         return kernel_call(
             functools.partial(load_kernel, layer),
             f"load{layer}",
             pltpu.VMEM((columns * block, wide), BF16),
-            [HBM] * len(operands),
+            specs,
             VMEM,
             LIMIT,
             scratch_shapes=[pltpu.SemaphoreType.DMA((8,))],
@@ -629,7 +638,10 @@
             outs += [sds((rows // 2, tokens), BF16)] * (2 if ways == 4 else 0)
         plain = len(outs)
         outs += [pltpu.HBM((features, tokens), BF16)] * sections
-        operands = in_vmem([loaded[layer]]) if layer in loaded else layer_weights(layer)
+        if layer in loaded:
+            operands, specs = in_vmem([loaded[layer]]), [VMEM]
+        else:
+            operands, specs = layer_weights(layer, *(("x2", "y2") if layer == 0 else ("x3", "y3")))
         before = 1 + len(shards) + len(operands)
         result = kernel_call(
             functools.partial(forward_kernel, layer, ways, live_shape),
@@ -637,7 +649,7 @@
             outs,
             [HBM]
             + [VMEM] * len(shards)
-            + [VMEM if layer in loaded else HBM] * len(operands)
+            + specs
             + [HBM] * len(sends),
             [VMEM] * plain + [HBM] * sections,
             LIMIT,

time: 297 us -> 294 us (0.990)
  local copies, waits for them, and re-layouts: 19.3 us -> 15.1 us
    ppermute x33 -> x35, waiting for transfers between devices: 100 us -> 92.4 us  [to_line(): lax.ppermute(value, 'dp', [(i, i ^ 2 * step) for i in range(devices)])]
    ppermute x9, waiting for transfers between devices: 27.2 us -> 31.5 us  [to_pipe(): return lax.ppermute(value, 'pipe', [(i, i ^ step) for i in range(sections)])]
    ppermute x33 -> x35, starting transfers between devices: 43.3 us -> 46.3 us  [to_line(): lax.ppermute(value, 'dp', [(i, i ^ 2 * step) for i in range(devices)])]
    dynamic_update_slice x4 -> x6, local copies, waits for them, and re-layouts: 6.78 us -> 6 us  [local(): x_all = lax.dynamic_update_slice(x_all, part[None], at)]
  transfers between devices with their start and end apart: 61 -> 63, of which waited for: 32 -> 37; matrix products, arithmetic and copies ran while one was open for 5% -> 5% of each run, Pallas kernels for 9% -> 9%
where the time goes in v5:
time: 294 us; the launch traced here: 293 us
  waiting for transfers between devices  136 us (46%)
  Pallas kernels  72 us (24%)
  starting transfers between devices  65.1 us (22%)
  local copies, waits for them, and re-layouts  15.1 us (5%)
  other arithmetic  3.66 us (1%)
    ppermute x35, waiting for transfers between devices, to_line(): lax.ppermute(value, 'dp', [(i, i ^ 2 * step) for i in range(devices)])  92.4 us
    ppermute x35, starting transfers between devices, to_line(): lax.ppermute(value, 'dp', [(i, i ^ 2 * step) for i in range(devices)])  46.3 us
    ppermute x9, waiting for transfers between devices, to_pipe(): return lax.ppermute(value, 'pipe', [(i, i ^ step) for i in range(sections)])  31.5 us
    pallas_call x4, Pallas kernels, local(): kernel_call(functools.partial(forward_kernel, layer, ways, live_shape), f...  24 us
    pallas_call x1, Pallas kernels, local(): pl.pallas_call(functools.partial(update_kernel, chunks, 1.0 / all_tokens,...  16.9 us
    pallas_call x3, Pallas kernels, local(): kernel_call(functools.partial(backward_kernel, layer, ways, live_shape),...  14 us
    ppermute x9, starting transfers between devices, to_pipe(): return lax.ppermute(value, 'pipe', [(i, i ^ step) for i in range(sections)])  11 us
    pallas_call x3, Pallas kernels, load(): kernel_call(functools.partial(load_kernel, layer), f'load{layer}', pltpu....  6.68 us
  transfers between devices with their start and end apart: 63, of which 37 were waited for; matrix products, arithmetic and copies ran while one was open for 5% of the time, Pallas kernels for 9%

profile of v5, /device:TPU:0, one launch (start us, length us, event | category | flops | bytes accessed | tf_op | source)
XLA Modules:
  0.0 293.2 jit_solution(7650648204458394508)
XLA Ops:
  2.3 1.6 split.1
  3.9 3.0 %collective-permute-start = (bf16[272,2048]{1,0:T(8,128)(2,1)S(1)}, bf16[272,2048]{1,0:T(8,128)(2,1)}, u32[]{:S(2)}, u32[]{:S(2)}) collective-permute-start(bf16[272,2048]{1,0:T(8,128)(2,1)S(1)} %get-tuple-element.107), channel_id=1, source_target_pairs={{0,8},{8,0},{16,24},{24,16},{1,9},{9,1},{17,25},{25,17},{2,10},{10... | collective-permute-start | bytes 3342344 | tf_op jit(solution)/shard_map/ppermute | solution.py:509
  6.9 1.5 collective-permute-start.1
  8.4 2.7 collective-permute-start.4
  13.3 1.6 collective-permute-start.6
  14.9 6.2 %collective-permute-done.4 = bf16[16,4096]{1,0:T(8,128)(2,1)} collective-permute-done((bf16[16,4096]{1,0:T(8,128)(2,1)S(1)}, bf16[16,4096]{1,0:T(8,128)(2,1)}, u32[]{:S(2)}, u32[]{:S(2)}) %collective-permute-start.4) | collective-permute-done | bytes 131104 | tf_op jit(solution)/shard_map/ppermute | solution.py:512
  21.1 1.6 collective-permute-done.2
  24.2 1.8 dynamic-slice_dynamic-update-slice_fusion.1
  26.0 3.1 %collective-permute-done.5 = bf16[16,4096]{1,0:T(8,128)(2,1)S(1)} collective-permute-done((bf16[16,4096]{1,0:T(8,128)(2,1)}, bf16[16,4096]{1,0:T(8,128)(2,1)S(1)}, u32[]{:S(2)}, u32[]{:S(2)}) %collective-permute-start.5) | collective-permute-done | bytes 131104 | tf_op jit(solution)/shard_map/ppermute | solution.py:512
  33.6 1.6 pick2.1
  35.4 1.5 collective-permute-start.8
  38.8 1.6 bitcast_dynamic-update-slice_fusion.2
  40.4 1.6 bitcast_dynamic-update-slice_fusion.1
  42.6 2.3 copy.39
  45.7 1.6 collective-permute-start.12
  47.4 2.6 collective-permute-start.13
  50.2 1.6 pick3.1
  51.8 9.2 %collective-permute-done.8.refs_5_.refs_4_ = bf16[256,2048]{1,0:T(8,128)(2,1)} collective-permute-done((bf16[256,2048]{1,0:T(8,128)(2,1)S(1)}, bf16[256,2048]{1,0:T(8,128)(2,1)}, u32[]{:S(2)}, u32[]{:S(2)}) %collective-permute-start.8) | collective-permute-done | bytes 1048608 | tf_op jit(solution)/shard_map/ppermute | solution.py:509
  61.0 2.6 collective-permute-done.7.refs_3_.refs_8_.refs_2_
  66.5 1.7 collective-permute-done.16.refs_10_.refs_12_
  68.2 6.3 %forward0.1 = (f32[8,128]{1,0:T(8,128)}, f32[1024,128]{1,0:T(8,128)S(1)}, bf16[1024,128]{1,0:T(8,128)(2,1)S(1)}, bf16[512,128]{1,0:T(8,128)(2,1)S(1)}, bf16[512,...) custom-call(s32[8192]{0:T(1024)} %pad_add_fusion.live_hbm, ...), custom_call_target="tpu_custom_call" | custom-call | tf_op jit(solution)/shard_map/forward0/pallas_call | solution.py:646
  74.5 2.7 collective-permute-start.17
  77.5 1.6 collective-permute-start.21
  79.1 8.5 %collective-permute-done.17.refs_3_ = bf16[512,128]{1,0:T(8,128)(2,1)S(1)} collective-permute-done((bf16[512,128]{1,0:T(8,128)(2,1)S(1)}, bf16[512,128]{1,0:T(8,128)(2,1)S(1)}, u32[]{:S(2)}, u32[]{:S(2)}) %collective-permute-start.17) | collective-permute-done | bytes 131104 | tf_op jit(solution)/shard_map/ppermute | solution.py:512
  87.6 2.0 collective-permute-done.19.refs_4_
  90.2 3.7 %collective-permute-done.18.refs_1_ = bf16[512,128]{1,0:T(8,128)(2,1)S(1)} collective-permute-done((bf16[512,128]{1,0:T(8,128)(2,1)S(1)}, bf16[512,128]{1,0:T(8,128)(2,1)S(1)}, u32[]{:S(2)}, u32[]{:S(2)}) %collective-permute-start.18) | collective-permute-done | bytes 131104 | tf_op jit(solution)/shard_map/ppermute | solution.py:512
  93.9 1.5 collective-permute-done.20.refs_2_
  96.0 2.1 collective-permute-done.24.refs_15_.refs_8_.refs_10_.refs_9_
  98.1 1.5 collective-permute-done.25.refs_17_.refs_11_.refs_13_
  99.6 4.2 %forward1.1 = (f32[8,128]{1,0:T(8,128)S(1)}, f32[1024,128]{1,0:T(8,128)S(1)}, bf16[1024,128]{1,0:T(8,128)(2,1)S(1)}, bf16[512,128]{1,0:T(8,128)(2,1)S(1)}, bf16[...) custom-call(s32[8192]{0:T(1024)} %pad_add_fusion.live_hbm, ...), custom_call_target="tpu_custom_call", output_to_operand_aliasing={{5}: (19, {}), {6}: (20, {}), {7}: (21, {}), {8}: (22, {})} | custom-call | tf_op jit(solution)/shard_map/forward1/pallas_call | solution.py:646
  104.7 2.7 collective-permute-start.26
  107.6 2.3 collective-permute-start.30
  109.9 7.8 %collective-permute-done.26.refs_3_ = bf16[512,128]{1,0:T(8,128)(2,1)S(1)} collective-permute-done((bf16[512,128]{1,0:T(8,128)(2,1)S(1)}, bf16[512,128]{1,0:T(8,128)(2,1)S(1)}, u32[]{:S(2)}, u32[]{:S(2)}) %collective-permute-start.26) | collective-permute-done | bytes 131104 | tf_op jit(solution)/shard_map/ppermute | solution.py:512
  117.7 2.0 collective-permute-done.28.refs_4_
  120.4 2.2 load2.1.refs_6_.refs_8_
  123.8 1.7 collective-permute-done.29.refs_2_
  125.4 3.9 %forward2.1 = (f32[8,128]{1,0:T(8,128)S(1)}, f32[1024,128]{1,0:T(8,128)S(1)}, bf16[1024,128]{1,0:T(8,128)(2,1)S(1)}, bf16[512,128]{1,0:T(8,128)(2,1)S(1)}, bf16[...) custom-call(s32[8192]{0:T(1024)} %pad_add_fusion.live_hbm, ...), custom_call_target="tpu_custom_call", output_to_operand_aliasing={{5}: (8, {}), {6}: (9, {}), {7}: (10, {}), {8}: (11, {})} | custom-call | tf_op jit(solution)/shard_map/forward2/pallas_call | solution.py:646
  129.3 3.8 %collective-permute-start.31 = (bf16[512,128]{1,0:T(8,128)(2,1)S(1)}, bf16[512,128]{1,0:T(8,128)(2,1)S(1)}, u32[]{:S(2)}, u32[]{:S(2)}) collective-permute-start(bf16[512,128]{1,0:T(8,128)(2,1)S(1)} %get-tuple-element.156), channel_id=1, source_target_pairs={{0,4},{1,5},{2,6},{3,7},{4,0},{5,1},{6,2},{7,3},{8,12},{9,13},{10,... | collective-permute-start | bytes 393224 | tf_op jit(solution)/shard_map/ppermute | solution.py:512
  133.2 2.5 collective-permute-start.35
  135.7 7.3 %collective-permute-done.31.refs_3_ = bf16[512,128]{1,0:T(8,128)(2,1)S(1)} collective-permute-done((bf16[512,128]{1,0:T(8,128)(2,1)S(1)}, bf16[512,128]{1,0:T(8,128)(2,1)S(1)}, u32[]{:S(2)}, u32[]{:S(2)}) %collective-permute-start.31) | collective-permute-done | bytes 131104 | tf_op jit(solution)/shard_map/ppermute | solution.py:512
  145.3 2.2 load3.1.refs_7_
  150.4 9.6 %forward3.1 = (f32[8,128]{1,0:T(8,128)S(1)}, bf16[1024,128]{1,0:T(8,128)(2,1)S(1)}, bf16[1040,128]{1,0:T(8,128)(2,1)S(1)}, bf16[1040,128]{1,0:T(8,128)(2,1)S(1)}...) custom-call(s32[8192]{0:T(1024)} %pad_add_fusion.live_hbm, ...), custom_call_target="tpu_custom_call", output_to_operand_aliasing={{6}: (9, {}), {7}: (10, {}), {8}: (11, {}), {9}: (12, {})} | custom-call | tf_op jit(solution)/shard_map/forward3/pallas_call | solution.py:646
  161.1 5.1 %collective-permute-start.38 = (bf16[1040,128]{1,0:T(8,128)(2,1)S(1)}, bf16[1040,128]{1,0:T(8,128)(2,1)S(1)}, u32[]{:S(2)}, u32[]{:S(2)}) collective-permute-start(bf16[1040,128]{1,0:T(8,128)(2,1)S(1)} %get-tuple-element.168), channel_id=1, source_target_pairs={{0,6},{1,7},{2,4},{3,5},{4,2},{5,3},{6,0},{7,1},{8,14},{9,15},{10,... | collective-permute-start | bytes 798728 | tf_op jit(solution)/shard_map/ppermute | solution.py:512
  166.7 16.8 %collective-permute-done.36.refs_1_ = bf16[4096,128]{1,0:T(8,128)(2,1)S(1)} collective-permute-done((bf16[4096,128]{1,0:T(8,128)(2,1)}, bf16[4096,128]{1,0:T(8,128)(2,1)S(1)}, u32[]{:S(2)}, u32[]{:S(2)}) %collective-permute-start.36) | collective-permute-done | bytes 1048608 | tf_op jit(solution)/shard_map/ppermute | solution.py:509
  183.8 1.9 collective-permute-done.39.refs_5_
  185.7 6.6 %backward2.1 = (bf16[1024,128]{1,0:T(8,128)(2,1)S(1)}, bf16[1040,128]{1,0:T(8,128)(2,1)S(1)}, bf16[1040,128]{1,0:T(8,128)(2,1)S(1)}, bf16[1040,128]{1,0:T(8,128)...) custom-call(s32[8192]{0:T(1024)} %pad_add_fusion.live_hbm, bf16[1024,128]{1,0:T(8,128)(2,1)S(1)} %bitcast.47, ...), custom_call_target="tpu_custom_call" | custom-call | tf_op jit(solution)/shard_map/backward2/pallas_call | solution.py:696
  192.9 2.5 collective-permute-start.47
  195.4 2.6 collective-permute-start.43
  199.0 1.7 collective-permute-start.45
  200.7 2.2 load1.1.refs_8_
  203.0 3.6 %collective-permute-done.43.refs_4_ = bf16[1040,128]{1,0:T(8,128)(2,1)S(1)} collective-permute-done((bf16[1040,128]{1,0:T(8,128)(2,1)S(1)}, bf16[1040,128]{1,0:T(8,128)(2,1)S(1)}, u32[]{:S(2)}, u32[]{:S(2)}) %collective-permute-start.43) | collective-permute-done | bytes 266272 | tf_op jit(solution)/shard_map/ppermute | solution.py:512
  206.6 13.3 %collective-permute-done.44.refs_5_ = bf16[1040,128]{1,0:T(8,128)(2,1)S(1)} collective-permute-done((bf16[1040,128]{1,0:T(8,128)(2,1)S(1)}, bf16[1040,128]{1,0:T(8,128)(2,1)S(1)}, u32[]{:S(2)}, u32[]{:S(2)}) %collective-permute-start.44) | collective-permute-done | bytes 266272 | tf_op jit(solution)/shard_map/ppermute | solution.py:512
  219.9 6.6 %backward1.1 = (bf16[1024,128]{1,0:T(8,128)(2,1)S(1)}, bf16[1040,128]{1,0:T(8,128)(2,1)S(1)}, bf16[1040,128]{1,0:T(8,128)(2,1)S(1)}, bf16[1040,128]{1,0:T(8,128)...) custom-call(s32[8192]{0:T(1024)} %pad_add_fusion.live_hbm, ...), custom_call_target="tpu_custom_call" | custom-call | tf_op jit(solution)/shard_map/backward1/pallas_call | solution.py:696
  227.1 2.1 collective-permute-start.49
  229.2 2.3 collective-permute-start.51
  231.5 6.8 %collective-permute-done.49.refs_4_ = bf16[1040,128]{1,0:T(8,128)(2,1)S(1)} collective-permute-done((bf16[1040,128]{1,0:T(8,128)(2,1)S(1)}, bf16[1040,128]{1,0:T(8,128)(2,1)S(1)}, u32[]{:S(2)}, u32[]{:S(2)}) %collective-permute-start.49) | collective-permute-done | bytes 266272 | tf_op jit(solution)/shard_map/ppermute | solution.py:512
  238.3 13.0 %collective-permute-done.50.refs_5_ = bf16[1040,128]{1,0:T(8,128)(2,1)S(1)} collective-permute-done((bf16[1040,128]{1,0:T(8,128)(2,1)S(1)}, bf16[1040,128]{1,0:T(8,128)(2,1)S(1)}, u32[]{:S(2)}, u32[]{:S(2)}) %collective-permute-start.50) | collective-permute-done | bytes 266272 | tf_op jit(solution)/shard_map/ppermute | solution.py:512
  252.6 1.6 collective-permute-start.53
  256.2 2.0 collective-permute-done.52.refs_1_
  260.4 3.5 %gather_u.1.refs_8_ = bf16[8,4096,128]{2,1,0:T(8,128)(2,1)S(1)} custom-call(bf16[4096,128]{1,0:T(8,128)(2,1)} %get-tuple-element.177.refs_0_, bf16[4096,128]{1,0:T(8,128)(2,1)} %copy-done.15, bf16[4096,128]{1,0:T(8,128)(2,1)} %copy-done.16, bf16[4096,128]{1,0:T(8,128)(2,1)} %copy-done.19, bf16[4096,128]{1,0:T(8,128)(2,1)} %copy-done.17, ...), custom_call_target="tpu_custom_call" | custom-call | bytes 33554432 | tf_op jit(solution)/shard_map/gather_u/pallas_call | solution.py:724
  264.0 2.9 %collective-permute-done.57.refs_6_ = bf16[512,128]{1,0:T(8,128)(2,1)S(1)} collective-permute-done((bf16[512,128]{1,0:T(8,128)(2,1)S(1)}, bf16[512,128]{1,0:T(8,128)(2,1)S(1)}, u32[]{:S(2)}, u32[]{:S(2)}) %collective-permute-start.57) | collective-permute-done | bytes 131104 | tf_op jit(solution)/shard_map/ppermute | solution.py:742
  266.9 16.9 %update.1 = (f32[8,64,2048]{2,1,0:T(8,128)}, f32[8,64,2048]{2,1,0:T(8,128)}, bf16[8,64,2048]{2,1,0:T(8,128)(2,1)S(1)}, f32[8,2048]{1,0:T(8,128)S(1)}, f32[8,128]{1,0:T(8,128)S(1)}) custom-call(s32[2048]{0:T(1024)S(1)} %reshape_squeeze.6.live, bf16[512,128]{1,0:T(8,128)(2,1)S(1)} %get-tuple-element.198.refs_0_, ...), custom_call_target="tpu_custom_call" | custom-call | tf_op jit(solution)/shard_map/update/pallas_call | solution.py:763
  286.3 3.1 %collective-permute-start.60 = (f32[8,128]{1,0:T(8,128)S(1)}, f32[8,128]{1,0:T(8,128)S(1)}, u32[]{:S(2)}, u32[]{:S(2)}) collective-permute-start(f32[8,128]{1,0:T(8,128)S(1)} %add.68.refs_0_), channel_id=1, source_target_pairs={{0,2},{1,3},{2,0},{3,1},{4,6},{5,7},{6,4},{7,5},{8,10},{9,11},{10,... | collective-permute-start | bytes 12296 | tf_op jit(solution)/shard_map/ppermute | solution.py:512
  291.0 2.2 output.1
  (167 shorter events, 39.7 us)
Async XLA Ops:
  3.9 27.7 %collective-permute-start = (bf16[272,2048]{1,0:T(8,128)(2,1)S(1)}, bf16[272,2048]{1,0:T(8,128)(2,1)}, u32[]{:S(2)}, u32[]{:S(2)}) collective-permute-start(bf16[272,2048]{1,0:T(8,128)(2,1)S(1)} %get-tuple-element.107), channel_id=1, source_target_pairs={{0,8},{8,0},{16,24},{24,16},{1,9},{9,1},{17,25},{25,17},{2,10},{10... | collective-permute-start | bytes 3342344 | tf_op jit(solution)/shard_map/ppermute | solution.py:509
  6.9 26.1 %collective-permute-start.1 = (bf16[272,2048]{1,0:T(8,128)(2,1)S(1)}, bf16[272,2048]{1,0:T(8,128)(2,1)}, u32[]{:S(2)}, u32[]{:S(2)}) collective-permute-start(bf16[272,2048]{1,0:T(8,128)(2,1)S(1)} %get-tuple-element.108), channel_id=1, source_target_pairs={{0,16},{8,24},{16,0},{24,8},{1,17},{9,25},{17,1},{25,9},{2,18},{10... | collective-permute-start | bytes 3342344 | tf_op jit(solution)/shard_map/ppermute | solution.py:509
  8.4 12.6 %collective-permute-start.4 = (bf16[16,4096]{1,0:T(8,128)(2,1)S(1)}, bf16[16,4096]{1,0:T(8,128)(2,1)}, u32[]{:S(2)}, u32[]{:S(2)}) collective-permute-start(bf16[16,4096]{1,0:T(8,128)(2,1)S(1)} %get-tuple-element.217), channel_id=1, source_target_pairs={{0,4},{1,5},{2,6},{3,7},{4,0},{5,1},{6,2},{7,3},{8,12},{9,13},{10,... | collective-permute-start | bytes 393224 | tf_op jit(solution)/shard_map/ppermute | solution.py:512
  11.1 11.6 %collective-permute-start.2 = (bf16[16,4096]{1,0:T(8,128)(2,1)S(1)}, bf16[16,4096]{1,0:T(8,128)(2,1)}, u32[]{:S(2)}, u32[]{:S(2)}) collective-permute-start(bf16[16,4096]{1,0:T(8,128)(2,1)S(1)} %get-tuple-element.218), channel_id=1, source_target_pairs={{0,4},{1,5},{2,6},{3,7},{4,0},{5,1},{6,2},{7,3},{8,12},{9,13},{10,... | collective-permute-start | bytes 393224 | tf_op jit(solution)/shard_map/ppermute | solution.py:512
  13.3 17.1 %collective-permute-start.6 = (bf16[32,4096]{1,0:T(8,128)(2,1)}, bf16[32,4096]{1,0:T(8,128)(2,1)S(1)}, u32[]{:S(2)}, u32[]{:S(2)}) collective-permute-start(bf16[32,4096]{1,0:T(8,128)(2,1)} %get-tuple-element.216), channel_id=1, source_target_pairs={{0,2},{1,3},{2,0},{3,1},{4,6},{5,7},{6,4},{7,5},{8,10},{9,11},{10,... | collective-permute-start | bytes 786440 | tf_op jit(solution)/shard_map/ppermute | solution.py:512
  21.1 7.9 %collective-permute-start.5 = (bf16[16,4096]{1,0:T(8,128)(2,1)}, bf16[16,4096]{1,0:T(8,128)(2,1)S(1)}, u32[]{:S(2)}, u32[]{:S(2)}) collective-permute-start(bf16[16,4096]{1,0:T(8,128)(2,1)} %collective-permute-done.4), channel_id=1, source_target_pairs={{0,2},{1,3},{2,0},{3,1},{4,6},{5,7},{6,4},{7,5},{8,10},{9,11},{10,... | collective-permute-start | bytes 393224 | tf_op jit(solution)/shard_map/ppermute | solution.py:512
  22.7 7.7 %collective-permute-start.3 = (bf16[16,4096]{1,0:T(8,128)(2,1)}, bf16[16,4096]{1,0:T(8,128)(2,1)S(1)}, u32[]{:S(2)}, u32[]{:S(2)}) collective-permute-start(bf16[16,4096]{1,0:T(8,128)(2,1)} %collective-permute-done.2), channel_id=1, source_target_pairs={{0,2},{1,3},{2,0},{3,1},{4,6},{5,7},{6,4},{7,5},{8,10},{9,11},{10,... | collective-permute-start | bytes 393224 | tf_op jit(solution)/shard_map/ppermute | solution.py:512
  33.0 12.7 %collective-permute-start.10 = (bf16[272,2048]{1,0:T(8,128)(2,1)}, bf16[272,2048]{1,0:T(8,128)(2,1)S(1)}, u32[]{:S(2)}, u32[]{:S(2)}) collective-permute-start(bf16[272,2048]{1,0:T(8,128)(2,1)} %collective-permute-done.x1.refs_2_.refs_7_.refs_1_), channel_id=1, source_target_pairs={{0,1},{1,0},{2,3},{3,2},{4,5},{5,4},{6,7},{7,6},{8,9},{9,8},{10,11... | collective-permute-start | bytes 3342344 | tf_op jit(solution)/shard_map/ppermute | solution.py:519
  33.1 12.7 %collective-permute-start.11 = (bf16[272,2048]{1,0:T(8,128)(2,1)}, bf16[272,2048]{1,0:T(8,128)(2,1)}, u32[]{:S(2)}, u32[]{:S(2)}) collective-permute-start(bf16[272,2048]{1,0:T(8,128)(2,1)} %collective-permute-done.1.y1.refs_4_.refs_10_.refs_3_), channel_id=1, source_target_pairs={{0,1},{1,0},{2,3},{3,2},{4,5},{5,4},{6,7},{7,6},{8,9},{9,8},{10,11... | collective-permute-start | bytes 3342344 | tf_op jit(solution)/shard_map/ppermute | solution.py:519
  35.3 10.5 %collective-permute-start.9 = (bf16[512,2048]{1,0:T(8,128)(2,1)}, bf16[512,2048]{1,0:T(8,128)(2,1)}, u32[]{:S(2)}, u32[]{:S(2)}) collective-permute-start(bf16[512,2048]{1,0:T(8,128)(2,1)} %bitcast.own.refs_1_.refs_6_.refs_0_), channel_id=1, source_target_pairs={{0,1},{1,0},{2,3},{3,2},{4,5},{5,4},{6,7},{7,6},{8,9},{9,8},{10,11... | collective-permute-start | bytes 6291464 | tf_op jit(solution)/shard_map/ppermute | solution.py:519
  35.4 25.6 %collective-permute-start.8 = (bf16[256,2048]{1,0:T(8,128)(2,1)S(1)}, bf16[256,2048]{1,0:T(8,128)(2,1)}, u32[]{:S(2)}, u32[]{:S(2)}) collective-permute-start(bf16[256,2048]{1,0:T(8,128)(2,1)S(1)} %get-tuple-element.112), channel_id=1, source_target_pairs={{0,16},{8,24},{16,0},{24,8},{1,17},{9,25},{17,1},{25,9},{2,18},{10... | collective-permute-start | bytes 3145736 | tf_op jit(solution)/shard_map/ppermute | solution.py:509
  36.9 26.7 %collective-permute-start.7 = (bf16[272,2048]{1,0:T(8,128)(2,1)S(1)}, bf16[272,2048]{1,0:T(8,128)(2,1)}, u32[]{:S(2)}, u32[]{:S(2)}) collective-permute-start(bf16[272,2048]{1,0:T(8,128)(2,1)S(1)} %get-tuple-element.111), channel_id=1, source_target_pairs={{0,8},{8,0},{16,24},{24,16},{1,9},{9,1},{17,25},{25,17},{2,10},{10... | collective-permute-start | bytes 3342344 | tf_op jit(solution)/shard_map/ppermute | solution.py:509
  45.7 17.9 %collective-permute-start.12 = (bf16[32,1024]{1,0:T(8,128)(2,1)}, bf16[32,1024]{1,0:T(8,128)(2,1)S(1)}, u32[]{:S(2)}, u32[]{:S(2)}) collective-permute-start(bf16[32,1024]{1,0:T(8,128)(2,1)} %get-tuple-element.122), channel_id=1, source_target_pairs={{0,2},{1,3},{2,0},{3,1},{4,6},{5,7},{6,4},{7,5},{8,10},{9,11},{10,... | collective-permute-start | bytes 196616 | tf_op jit(solution)/shard_map/ppermute | solution.py:512
  47.4 16.3 %collective-permute-start.13 = (bf16[32,1024]{1,0:T(8,128)(2,1)}, bf16[32,1024]{1,0:T(8,128)(2,1)S(1)}, u32[]{:S(2)}, u32[]{:S(2)}) collective-permute-start(bf16[32,1024]{1,0:T(8,128)(2,1)} %get-tuple-element.123), channel_id=1, source_target_pairs={{0,4},{1,5},{2,6},{3,7},{4,0},{5,1},{6,2},{7,3},{8,12},{9,13},{10,... | collective-permute-start | bytes 196616 | tf_op jit(solution)/shard_map/ppermute | solution.py:512
  50.0 13.7 %collective-permute-start.14 = (bf16[32,1024]{1,0:T(8,128)(2,1)}, bf16[32,1024]{1,0:T(8,128)(2,1)S(1)}, u32[]{:S(2)}, u32[]{:S(2)}) collective-permute-start(bf16[32,1024]{1,0:T(8,128)(2,1)} %get-tuple-element.124), channel_id=1, source_target_pairs={{0,6},{1,7},{2,4},{3,5},{4,2},{5,3},{6,0},{7,1},{8,14},{9,15},{10,... | collective-permute-start | bytes 196616 | tf_op jit(solution)/shard_map/ppermute | solution.py:512
  63.7 4.5 %collective-permute-start.15 = (bf16[272,2048]{1,0:T(8,128)(2,1)}, bf16[272,2048]{1,0:T(8,128)(2,1)S(1)}, u32[]{:S(2)}, u32[]{:S(2)}) collective-permute-start(bf16[272,2048]{1,0:T(8,128)(2,1)} %collective-permute-done.7.refs_3_.refs_8_.refs_2_), channel_id=1, source_target_pairs={{0,1},{1,0},{2,3},{3,2},{4,5},{5,4},{6,7},{7,6},{8,9},{9,8},{10,11... | collective-permute-start | bytes 3342344 | tf_op jit(solution)/shard_map/ppermute | solution.py:519
  63.8 4.5 %collective-permute-start.16 = (bf16[256,2048]{1,0:T(8,128)(2,1)}, bf16[256,2048]{1,0:T(8,128)(2,1)S(1)}, u32[]{:S(2)}, u32[]{:S(2)}) collective-permute-start(bf16[256,2048]{1,0:T(8,128)(2,1)} %collective-permute-done.8.refs_5_.refs_4_), channel_id=1, source_target_pairs={{0,1},{1,0},{2,3},{3,2},{4,5},{5,4},{6,7},{7,6},{8,9},{9,8},{10,11... | collective-permute-start | bytes 3145736 | tf_op jit(solution)/shard_map/ppermute | solution.py:519
  64.2 25.9 %collective-permute-start.22 = (bf16[256,2048]{1,0:T(8,128)(2,1)S(1)}, bf16[256,2048]{1,0:T(8,128)(2,1)S(1)}, u32[]{:S(2)}, u32[]{:S(2)}) collective-permute-start(bf16[256,2048]{1,0:T(8,128)(2,1)S(1)} %get-tuple-element.137), channel_id=1, source_target_pairs={{0,8},{8,0},{16,24},{24,16},{1,9},{9,1},{17,25},{25,17},{2,10},{10... | collective-permute-start | bytes 3145736 | tf_op jit(solution)/shard_map/ppermute | solution.py:509
  64.8 25.4 %collective-permute-start.23 = (bf16[256,2048]{1,0:T(8,128)(2,1)S(1)}, bf16[256,2048]{1,0:T(8,128)(2,1)S(1)}, u32[]{:S(2)}, u32[]{:S(2)}) collective-permute-start(bf16[256,2048]{1,0:T(8,128)(2,1)S(1)} %get-tuple-element.138), channel_id=1, source_target_pairs={{0,16},{8,24},{16,0},{24,8},{1,17},{9,25},{17,1},{25,9},{2,18},{10... | collective-permute-start | bytes 3145736 | tf_op jit(solution)/shard_map/ppermute | solution.py:509
  74.5 13.0 %collective-permute-start.17 = (bf16[512,128]{1,0:T(8,128)(2,1)S(1)}, bf16[512,128]{1,0:T(8,128)(2,1)S(1)}, u32[]{:S(2)}, u32[]{:S(2)}) collective-permute-start(bf16[512,128]{1,0:T(8,128)(2,1)S(1)} %get-tuple-element.133), channel_id=1, source_target_pairs={{0,4},{1,5},{2,6},{3,7},{4,0},{5,1},{6,2},{7,3},{8,12},{9,13},{10,... | collective-permute-start | bytes 393224 | tf_op jit(solution)/shard_map/ppermute | solution.py:512
  77.2 12.3 %collective-permute-start.19 = (bf16[512,128]{1,0:T(8,128)(2,1)S(1)}, bf16[512,128]{1,0:T(8,128)(2,1)S(1)}, u32[]{:S(2)}, u32[]{:S(2)}) collective-permute-start(bf16[512,128]{1,0:T(8,128)(2,1)S(1)} %get-tuple-element.134), channel_id=1, source_target_pairs={{0,4},{1,5},{2,6},{3,7},{4,0},{5,1},{6,2},{7,3},{8,12},{9,13},{10,... | collective-permute-start | bytes 393224 | tf_op jit(solution)/shard_map/ppermute | solution.py:512
  77.5 17.9 %collective-permute-start.21 = (bf16[1024,128]{1,0:T(8,128)(2,1)S(1)}, bf16[1024,128]{1,0:T(8,128)(2,1)S(1)}, u32[]{:S(2)}, u32[]{:S(2)}) collective-permute-start(bf16[1024,128]{1,0:T(8,128)(2,1)S(1)} %get-tuple-element.132.refs_0_.refs_1_), channel_id=1, source_target_pairs={{0,2},{1,3},{2,0},{3,1},{4,6},{5,7},{6,4},{7,5},{8,10},{9,11},{10,... | collective-permute-start | bytes 786440 | tf_op jit(solution)/shard_map/ppermute | solution.py:512
  87.6 6.3 %collective-permute-start.18 = (bf16[512,128]{1,0:T(8,128)(2,1)S(1)}, bf16[512,128]{1,0:T(8,128)(2,1)S(1)}, u32[]{:S(2)}, u32[]{:S(2)}) collective-permute-start(bf16[512,128]{1,0:T(8,128)(2,1)S(1)} %collective-permute-done.17.refs_3_), channel_id=1, source_target_pairs={{0,2},{1,3},{2,0},{3,1},{4,6},{5,7},{6,4},{7,5},{8,10},{9,11},{10,... | collective-permute-start | bytes 393224 | tf_op jit(solution)/shard_map/ppermute | solution.py:512
  89.6 5.9 %collective-permute-start.20 = (bf16[512,128]{1,0:T(8,128)(2,1)S(1)}, bf16[512,128]{1,0:T(8,128)(2,1)S(1)}, u32[]{:S(2)}, u32[]{:S(2)}) collective-permute-start(bf16[512,128]{1,0:T(8,128)(2,1)S(1)} %collective-permute-done.19.refs_4_), channel_id=1, source_target_pairs={{0,2},{1,3},{2,0},{3,1},{4,6},{5,7},{6,4},{7,5},{8,10},{9,11},{10,... | collective-permute-start | bytes 393224 | tf_op jit(solution)/shard_map/ppermute | solution.py:512
  95.5 2.7 collective-permute-start.24
  95.5 4.2 %collective-permute-start.25 = (bf16[256,2048]{1,0:T(8,128)(2,1)S(1)}, bf16[256,2048]{1,0:T(8,128)(2,1)S(1)}, u32[]{:S(2)}, u32[]{:S(2)}) collective-permute-start(bf16[256,2048]{1,0:T(8,128)(2,1)S(1)} %collective-permute-done.23.refs_11_.refs_5_.refs_6_), channel_id=1, source_target_pairs={{0,1},{1,0},{2,3},{3,2},{4,5},{5,4},{6,7},{7,6},{8,9},{9,8},{10,11... | collective-permute-start | bytes 3145736 | tf_op jit(solution)/shard_map/ppermute | solution.py:519
  104.7 13.0 %collective-permute-start.26 = (bf16[512,128]{1,0:T(8,128)(2,1)S(1)}, bf16[512,128]{1,0:T(8,128)(2,1)S(1)}, u32[]{:S(2)}, u32[]{:S(2)}) collective-permute-start(bf16[512,128]{1,0:T(8,128)(2,1)S(1)} %get-tuple-element.148), channel_id=1, source_target_pairs={{0,4},{1,5},{2,6},{3,7},{4,0},{5,1},{6,2},{7,3},{8,12},{9,13},{10,... | collective-permute-start | bytes 393224 | tf_op jit(solution)/shard_map/ppermute | solution.py:512
  107.4 12.3 %collective-permute-start.28 = (bf16[512,128]{1,0:T(8,128)(2,1)S(1)}, bf16[512,128]{1,0:T(8,128)(2,1)S(1)}, u32[]{:S(2)}, u32[]{:S(2)}) collective-permute-start(bf16[512,128]{1,0:T(8,128)(2,1)S(1)} %get-tuple-element.149), channel_id=1, source_target_pairs={{0,4},{1,5},{2,6},{3,7},{4,0},{5,1},{6,2},{7,3},{8,12},{9,13},{10,... | collective-permute-start | bytes 393224 | tf_op jit(solution)/shard_map/ppermute | solution.py:512
  107.6 17.8 %collective-permute-start.30 = (bf16[1024,128]{1,0:T(8,128)(2,1)S(1)}, bf16[1024,128]{1,0:T(8,128)(2,1)S(1)}, u32[]{:S(2)}, u32[]{:S(2)}) collective-permute-start(bf16[1024,128]{1,0:T(8,128)(2,1)S(1)} %get-tuple-element.147.refs_0_.refs_1_), channel_id=1, source_target_pairs={{0,2},{1,3},{2,0},{3,1},{4,6},{5,7},{6,4},{7,5},{8,10},{9,11},{10,... | collective-permute-start | bytes 786440 | tf_op jit(solution)/shard_map/ppermute | solution.py:512
  117.7 6.1 %collective-permute-start.27 = (bf16[512,128]{1,0:T(8,128)(2,1)S(1)}, bf16[512,128]{1,0:T(8,128)(2,1)S(1)}, u32[]{:S(2)}, u32[]{:S(2)}) collective-permute-start(bf16[512,128]{1,0:T(8,128)(2,1)S(1)} %collective-permute-done.26.refs_3_), channel_id=1, source_target_pairs={{0,2},{1,3},{2,0},{3,1},{4,6},{5,7},{6,4},{7,5},{8,10},{9,11},{10,... | collective-permute-start | bytes 393224 | tf_op jit(solution)/shard_map/ppermute | solution.py:512
  119.7 5.7 %collective-permute-start.29 = (bf16[512,128]{1,0:T(8,128)(2,1)S(1)}, bf16[512,128]{1,0:T(8,128)(2,1)S(1)}, u32[]{:S(2)}, u32[]{:S(2)}) collective-permute-start(bf16[512,128]{1,0:T(8,128)(2,1)S(1)} %collective-permute-done.28.refs_4_), channel_id=1, source_target_pairs={{0,2},{1,3},{2,0},{3,1},{4,6},{5,7},{6,4},{7,5},{8,10},{9,11},{10,... | collective-permute-start | bytes 393224 | tf_op jit(solution)/shard_map/ppermute | solution.py:512
  129.3 13.7 %collective-permute-start.31 = (bf16[512,128]{1,0:T(8,128)(2,1)S(1)}, bf16[512,128]{1,0:T(8,128)(2,1)S(1)}, u32[]{:S(2)}, u32[]{:S(2)}) collective-permute-start(bf16[512,128]{1,0:T(8,128)(2,1)S(1)} %get-tuple-element.156), channel_id=1, source_target_pairs={{0,4},{1,5},{2,6},{3,7},{4,0},{5,1},{6,2},{7,3},{8,12},{9,13},{10,... | collective-permute-start | bytes 393224 | tf_op jit(solution)/shard_map/ppermute | solution.py:512
  133.1 11.4 %collective-permute-start.33 = (bf16[512,128]{1,0:T(8,128)(2,1)S(1)}, bf16[512,128]{1,0:T(8,128)(2,1)S(1)}, u32[]{:S(2)}, u32[]{:S(2)}) collective-permute-start(bf16[512,128]{1,0:T(8,128)(2,1)S(1)} %get-tuple-element.157), channel_id=1, source_target_pairs={{0,4},{1,5},{2,6},{3,7},{4,0},{5,1},{6,2},{7,3},{8,12},{9,13},{10,... | collective-permute-start | bytes 393224 | tf_op jit(solution)/shard_map/ppermute | solution.py:512
  133.2 17.2 %collective-permute-start.35 = (bf16[1024,128]{1,0:T(8,128)(2,1)S(1)}, bf16[1024,128]{1,0:T(8,128)(2,1)S(1)}, u32[]{:S(2)}, u32[]{:S(2)}) collective-permute-start(bf16[1024,128]{1,0:T(8,128)(2,1)S(1)} %get-tuple-element.155.refs_0_.refs_1_), channel_id=1, source_target_pairs={{0,2},{1,3},{2,0},{3,1},{4,6},{5,7},{6,4},{7,5},{8,10},{9,11},{10,... | collective-permute-start | bytes 786440 | tf_op jit(solution)/shard_map/ppermute | solution.py:512
  143.1 5.9 %collective-permute-start.32 = (bf16[512,128]{1,0:T(8,128)(2,1)S(1)}, bf16[512,128]{1,0:T(8,128)(2,1)S(1)}, u32[]{:S(2)}, u32[]{:S(2)}) collective-permute-start(bf16[512,128]{1,0:T(8,128)(2,1)S(1)} %collective-permute-done.31.refs_3_), channel_id=1, source_target_pairs={{0,2},{1,3},{2,0},{3,1},{4,6},{5,7},{6,4},{7,5},{8,10},{9,11},{10,... | collective-permute-start | bytes 393224 | tf_op jit(solution)/shard_map/ppermute | solution.py:512
  144.5 5.9 %collective-permute-start.34 = (bf16[512,128]{1,0:T(8,128)(2,1)S(1)}, bf16[512,128]{1,0:T(8,128)(2,1)S(1)}, u32[]{:S(2)}, u32[]{:S(2)}) collective-permute-start(bf16[512,128]{1,0:T(8,128)(2,1)S(1)} %collective-permute-done.33.refs_4_), channel_id=1, source_target_pairs={{0,2},{1,3},{2,0},{3,1},{4,6},{5,7},{6,4},{7,5},{8,10},{9,11},{10,... | collective-permute-start | bytes 393224 | tf_op jit(solution)/shard_map/ppermute | solution.py:512
  160.0 23.5 %collective-permute-start.36 = (bf16[4096,128]{1,0:T(8,128)(2,1)}, bf16[4096,128]{1,0:T(8,128)(2,1)S(1)}, u32[]{:S(2)}, u32[]{:S(2)}) collective-permute-start(bf16[4096,128]{1,0:T(8,128)(2,1)} %get-tuple-element.165), channel_id=1, source_target_pairs={{0,8},{8,0},{16,24},{24,16},{1,9},{9,1},{17,25},{25,17},{2,10},{10... | collective-permute-start | bytes 3145736 | tf_op jit(solution)/shard_map/ppermute | solution.py:509
  160.6 23.2 %collective-permute-start.37 = (bf16[4096,128]{1,0:T(8,128)(2,1)}, bf16[4096,128]{1,0:T(8,128)(2,1)S(1)}, u32[]{:S(2)}, u32[]{:S(2)}) collective-permute-start(bf16[4096,128]{1,0:T(8,128)(2,1)} %get-tuple-element.166), channel_id=1, source_target_pairs={{0,16},{8,24},{16,0},{24,8},{1,17},{9,25},{17,1},{25,9},{2,18},{10... | collective-permute-start | bytes 3145736 | tf_op jit(solution)/shard_map/ppermute | solution.py:509
  161.1 22.7 %collective-permute-start.38 = (bf16[1040,128]{1,0:T(8,128)(2,1)S(1)}, bf16[1040,128]{1,0:T(8,128)(2,1)S(1)}, u32[]{:S(2)}, u32[]{:S(2)}) collective-permute-start(bf16[1040,128]{1,0:T(8,128)(2,1)S(1)} %get-tuple-element.168), channel_id=1, source_target_pairs={{0,6},{1,7},{2,4},{3,5},{4,2},{5,3},{6,0},{7,1},{8,14},{9,15},{10,... | collective-permute-start | bytes 798728 | tf_op jit(solution)/shard_map/ppermute | solution.py:512
  166.2 19.5 %collective-permute-start.39 = (bf16[1040,128]{1,0:T(8,128)(2,1)S(1)}, bf16[1040,128]{1,0:T(8,128)(2,1)S(1)}, u32[]{:S(2)}, u32[]{:S(2)}) collective-permute-start(bf16[1040,128]{1,0:T(8,128)(2,1)S(1)} %get-tuple-element.169), channel_id=1, source_target_pairs={{0,4},{1,5},{2,6},{3,7},{4,0},{5,1},{6,2},{7,3},{8,12},{9,13},{10,... | collective-permute-start | bytes 798728 | tf_op jit(solution)/shard_map/ppermute | solution.py:512
  166.2 19.5 %collective-permute-start.40 = (bf16[1040,128]{1,0:T(8,128)(2,1)S(1)}, bf16[1040,128]{1,0:T(8,128)(2,1)S(1)}, u32[]{:S(2)}, u32[]{:S(2)}) collective-permute-start(bf16[1040,128]{1,0:T(8,128)(2,1)S(1)} %get-tuple-element.170), channel_id=1, source_target_pairs={{0,2},{1,3},{2,0},{3,1},{4,6},{5,7},{6,4},{7,5},{8,10},{9,11},{10,... | collective-permute-start | bytes 798728 | tf_op jit(solution)/shard_map/ppermute | solution.py:512
  183.8 42.7 %copy-start.16 = (bf16[4096,128]{1,0:T(8,128)(2,1)}, bf16[4096,128]{1,0:T(8,128)(2,1)S(1)}, u32[]{:S(2)}) copy-start(bf16[4096,128]{1,0:T(8,128)(2,1)S(1)} %collective-permute-done.37.refs_2_) | copy-start | bytes 3145732
  192.3 5.7 %collective-permute-start.41 = (bf16[4096,128]{1,0:T(8,128)(2,1)S(1)}, bf16[4096,128]{1,0:T(8,128)(2,1)S(1)}, u32[]{:S(2)}, u32[]{:S(2)}) collective-permute-start(bf16[4096,128]{1,0:T(8,128)(2,1)S(1)} %copy-done.11), channel_id=1, source_target_pairs={{0,1},{1,0},{2,3},{3,2},{4,5},{5,4},{6,7},{7,6},{8,9},{9,8},{10,11... | collective-permute-start | bytes 3145736 | tf_op jit(solution)/shard_map/ppermute | solution.py:519
  192.4 10.6 %collective-permute-start.42 = (bf16[4096,128]{1,0:T(8,128)(2,1)S(1)}, bf16[4096,128]{1,0:T(8,128)(2,1)S(1)}, u32[]{:S(2)}, u32[]{:S(2)}) collective-permute-start(bf16[4096,128]{1,0:T(8,128)(2,1)S(1)} %collective-permute-done.36.refs_1_), channel_id=1, source_target_pairs={{0,1},{1,0},{2,3},{3,2},{4,5},{5,4},{6,7},{7,6},{8,9},{9,8},{10,11... | collective-permute-start | bytes 3145736 | tf_op jit(solution)/shard_map/ppermute | solution.py:519
  192.9 33.6 %collective-permute-start.47 = (bf16[4096,128]{1,0:T(8,128)(2,1)S(1)}, bf16[4096,128]{1,0:T(8,128)(2,1)S(1)}, u32[]{:S(2)}, u32[]{:S(2)}) collective-permute-start(bf16[4096,128]{1,0:T(8,128)(2,1)S(1)} %copy-done.14), channel_id=1, source_target_pairs={{0,24},{8,16},{16,8},{24,0},{1,25},{9,17},{17,9},{25,1},{2,26},{10... | collective-permute-start | bytes 3145736 | tf_op jit(solution)/shard_map/ppermute | solution.py:509
  195.4 11.2 %collective-permute-start.43 = (bf16[1040,128]{1,0:T(8,128)(2,1)S(1)}, bf16[1040,128]{1,0:T(8,128)(2,1)S(1)}, u32[]{:S(2)}, u32[]{:S(2)}) collective-permute-start(bf16[1040,128]{1,0:T(8,128)(2,1)S(1)} %get-tuple-element.180), channel_id=1, source_target_pairs={{0,6},{1,7},{2,4},{3,5},{4,2},{5,3},{6,0},{7,1},{8,14},{9,15},{10,... | collective-permute-start | bytes 798728 | tf_op jit(solution)/shard_map/ppermute | solution.py:512
  198.0 21.8 %collective-permute-start.44 = (bf16[1040,128]{1,0:T(8,128)(2,1)S(1)}, bf16[1040,128]{1,0:T(8,128)(2,1)S(1)}, u32[]{:S(2)}, u32[]{:S(2)}) collective-permute-start(bf16[1040,128]{1,0:T(8,128)(2,1)S(1)} %get-tuple-element.181), channel_id=1, source_target_pairs={{0,4},{1,5},{2,6},{3,7},{4,0},{5,1},{6,2},{7,3},{8,12},{9,13},{10,... | collective-permute-start | bytes 798728 | tf_op jit(solution)/shard_map/ppermute | solution.py:512
  199.0 20.9 %collective-permute-start.45 = (bf16[1040,128]{1,0:T(8,128)(2,1)S(1)}, bf16[1040,128]{1,0:T(8,128)(2,1)S(1)}, u32[]{:S(2)}, u32[]{:S(2)}) collective-permute-start(bf16[1040,128]{1,0:T(8,128)(2,1)S(1)} %get-tuple-element.182), channel_id=1, source_target_pairs={{0,2},{1,3},{2,0},{3,1},{4,6},{5,7},{6,4},{7,5},{8,10},{9,11},{10,... | collective-permute-start | bytes 798728 | tf_op jit(solution)/shard_map/ppermute | solution.py:512
  226.5 5.0 %collective-permute-start.46 = (bf16[4096,128]{1,0:T(8,128)(2,1)S(1)}, bf16[4096,128]{1,0:T(8,128)(2,1)S(1)}, u32[]{:S(2)}, u32[]{:S(2)}) collective-permute-start(bf16[4096,128]{1,0:T(8,128)(2,1)S(1)} %collective-permute-done.37.refs_2_), channel_id=1, source_target_pairs={{0,1},{1,0},{2,3},{3,2},{4,5},{5,4},{6,7},{7,6},{8,9},{9,8},{10,11... | collective-permute-start | bytes 3145736 | tf_op jit(solution)/shard_map/ppermute | solution.py:519
  226.6 4.9 %collective-permute-start.48 = (bf16[4096,128]{1,0:T(8,128)(2,1)S(1)}, bf16[4096,128]{1,0:T(8,128)(2,1)S(1)}, u32[]{:S(2)}, u32[]{:S(2)}) collective-permute-start(bf16[4096,128]{1,0:T(8,128)(2,1)S(1)} %collective-permute-done.47.refs_3_), channel_id=1, source_target_pairs={{0,1},{1,0},{2,3},{3,2},{4,5},{5,4},{6,7},{7,6},{8,9},{9,8},{10,11... | collective-permute-start | bytes 3145736 | tf_op jit(solution)/shard_map/ppermute | solution.py:519
  227.1 11.2 %collective-permute-start.49 = (bf16[1040,128]{1,0:T(8,128)(2,1)S(1)}, bf16[1040,128]{1,0:T(8,128)(2,1)S(1)}, u32[]{:S(2)}, u32[]{:S(2)}) collective-permute-start(bf16[1040,128]{1,0:T(8,128)(2,1)S(1)} %get-tuple-element.193), channel_id=1, source_target_pairs={{0,6},{1,7},{2,4},{3,5},{4,2},{5,3},{6,0},{7,1},{8,14},{9,15},{10,... | collective-permute-start | bytes 798728 | tf_op jit(solution)/shard_map/ppermute | solution.py:512
  229.2 22.1 %collective-permute-start.50 = (bf16[1040,128]{1,0:T(8,128)(2,1)S(1)}, bf16[1040,128]{1,0:T(8,128)(2,1)S(1)}, u32[]{:S(2)}, u32[]{:S(2)}) collective-permute-start(bf16[1040,128]{1,0:T(8,128)(2,1)S(1)} %get-tuple-element.194), channel_id=1, source_target_pairs={{0,4},{1,5},{2,6},{3,7},{4,0},{5,1},{6,2},{7,3},{8,12},{9,13},{10,... | collective-permute-start | bytes 798728 | tf_op jit(solution)/shard_map/ppermute | solution.py:512
  229.2 22.1 %collective-permute-start.51 = (bf16[1040,128]{1,0:T(8,128)(2,1)S(1)}, bf16[1040,128]{1,0:T(8,128)(2,1)S(1)}, u32[]{:S(2)}, u32[]{:S(2)}) collective-permute-start(bf16[1040,128]{1,0:T(8,128)(2,1)S(1)} %get-tuple-element.195), channel_id=1, source_target_pairs={{0,2},{1,3},{2,0},{3,1},{4,6},{5,7},{6,4},{7,5},{8,10},{9,11},{10,... | collective-permute-start | bytes 798728 | tf_op jit(solution)/shard_map/ppermute | solution.py:512
  252.1 6.1 %collective-permute-start.52 = (bf16[512,128]{1,0:T(8,128)(2,1)S(1)}, bf16[512,128]{1,0:T(8,128)(2,1)S(1)}, u32[]{:S(2)}, u32[]{:S(2)}) collective-permute-start(bf16[512,128]{1,0:T(8,128)(2,1)S(1)} %get-tuple-element.199), channel_id=1, source_target_pairs={{0,8},{1,9},{2,10},{3,11},{4,12},{5,13},{6,14},{7,15},{8,0},{9,1},... | collective-permute-start | bytes 393224 | tf_op jit(solution)/shard_map/ppermute | solution.py:742
  252.6 6.4 %collective-permute-start.53 = (bf16[512,128]{1,0:T(8,128)(2,1)S(1)}, bf16[512,128]{1,0:T(8,128)(2,1)S(1)}, u32[]{:S(2)}, u32[]{:S(2)}) collective-permute-start(bf16[512,128]{1,0:T(8,128)(2,1)S(1)} %get-tuple-element.200), channel_id=1, source_target_pairs={{0,16},{1,17},{2,18},{3,19},{4,20},{5,21},{6,22},{7,23},{8,24},{9,... | collective-permute-start | bytes 393224 | tf_op jit(solution)/shard_map/ppermute | solution.py:742
  254.2 9.8 %collective-permute-start.54 = (bf16[512,128]{1,0:T(8,128)(2,1)S(1)}, bf16[512,128]{1,0:T(8,128)(2,1)S(1)}, u32[]{:S(2)}, u32[]{:S(2)}) collective-permute-start(bf16[512,128]{1,0:T(8,128)(2,1)S(1)} %get-tuple-element.201), channel_id=1, source_target_pairs={{0,24},{1,25},{2,26},{3,27},{4,28},{5,29},{6,30},{7,31},{8,16},{9,... | collective-permute-start | bytes 393224 | tf_op jit(solution)/shard_map/ppermute | solution.py:742
  255.6 8.3 %collective-permute-start.55 = (bf16[512,128]{1,0:T(8,128)(2,1)S(1)}, bf16[512,128]{1,0:T(8,128)(2,1)S(1)}, u32[]{:S(2)}, u32[]{:S(2)}) collective-permute-start(bf16[512,128]{1,0:T(8,128)(2,1)S(1)} %get-tuple-element.202), channel_id=1, source_target_pairs={{0,1},{1,0},{2,3},{3,2},{4,5},{5,4},{6,7},{7,6},{8,9},{9,8},{10,11... | collective-permute-start | bytes 393224 | tf_op jit(solution)/shard_map/ppermute | solution.py:742
  255.6 8.3 %collective-permute-start.56 = (bf16[512,128]{1,0:T(8,128)(2,1)S(1)}, bf16[512,128]{1,0:T(8,128)(2,1)S(1)}, u32[]{:S(2)}, u32[]{:S(2)}) collective-permute-start(bf16[512,128]{1,0:T(8,128)(2,1)S(1)} %get-tuple-element.203), channel_id=1, source_target_pairs={{0,9},{1,8},{2,11},{3,10},{4,13},{5,12},{6,15},{7,14},{8,1},{9,0},... | collective-permute-start | bytes 393224 | tf_op jit(solution)/shard_map/ppermute | solution.py:742
  258.2 8.7 %collective-permute-start.57 = (bf16[512,128]{1,0:T(8,128)(2,1)S(1)}, bf16[512,128]{1,0:T(8,128)(2,1)S(1)}, u32[]{:S(2)}, u32[]{:S(2)}) collective-permute-start(bf16[512,128]{1,0:T(8,128)(2,1)S(1)} %get-tuple-element.204), channel_id=1, source_target_pairs={{0,17},{1,16},{2,19},{3,18},{4,21},{5,20},{6,23},{7,22},{8,25},{9,... | collective-permute-start | bytes 393224 | tf_op jit(solution)/shard_map/ppermute | solution.py:742
  259.0 7.9 %collective-permute-start.58 = (bf16[512,128]{1,0:T(8,128)(2,1)S(1)}, bf16[512,128]{1,0:T(8,128)(2,1)S(1)}, u32[]{:S(2)}, u32[]{:S(2)}) collective-permute-start(bf16[512,128]{1,0:T(8,128)(2,1)S(1)} %get-tuple-element.205), channel_id=1, source_target_pairs={{0,25},{1,24},{2,27},{3,26},{4,29},{5,28},{6,31},{7,30},{8,17},{9,... | collective-permute-start | bytes 393224 | tf_op jit(solution)/shard_map/ppermute | solution.py:742
  283.8 1.2 collective-permute-start.59
  285.0 5.4 %collective-permute-start.62 = (f32[8,128]{1,0:T(8,128)S(1)}, f32[8,128]{1,0:T(8,128)S(1)}, u32[]{:S(2)}, u32[]{:S(2)}) collective-permute-start(f32[8,128]{1,0:T(8,128)S(1)} %add.68.refs_0_), channel_id=1, source_target_pairs={{0,6},{1,7},{2,4},{3,5},{4,2},{5,3},{6,0},{7,1},{8,14},{9,15},{10,... | collective-permute-start | bytes 12296 | tf_op jit(solution)/shard_map/ppermute | solution.py:512
  286.3 4.5 %collective-permute-start.61 = (f32[8,128]{1,0:T(8,128)S(1)}, f32[8,128]{1,0:T(8,128)S(1)}, u32[]{:S(2)}, u32[]{:S(2)}) collective-permute-start(f32[8,128]{1,0:T(8,128)S(1)} %add.68.refs_0_), channel_id=1, source_target_pairs={{0,4},{1,5},{2,6},{3,7},{4,0},{5,1},{6,2},{7,3},{8,12},{9,13},{10,... | collective-permute-start | bytes 12296 | tf_op jit(solution)/shard_map/ppermute | solution.py:512
  286.3 4.7 %collective-permute-start.60 = (f32[8,128]{1,0:T(8,128)S(1)}, f32[8,128]{1,0:T(8,128)S(1)}, u32[]{:S(2)}, u32[]{:S(2)}) collective-permute-start(f32[8,128]{1,0:T(8,128)S(1)} %add.68.refs_0_), channel_id=1, source_target_pairs={{0,2},{1,3},{2,0},{3,1},{4,6},{5,7},{6,4},{7,5},{8,10},{9,11},{10,... | collective-permute-start | bytes 12296 | tf_op jit(solution)/shard_map/ppermute | solution.py:512
  (29 other events, 341.7 us)
